TPU v7x, 32 devices: a whole 2x2x4 slice. The times are simulated.
32 devices in a mesh: dp: 4 (over y, x), tensor: 8 (over z, core).
Axes of the slice: x: 2, y: 2, z: 4, core: 2. Of those that a mesh axis runs over, the one named last changes fastest.
Arguments:
- inputs: bfloat16 [512, 6144], P('dp'), may hold values from -6 to 6
- targets: bfloat16 [512, 6144], P('dp'), may hold values from -6 to 6
- lengths: int32 [4], P('dp'), may hold values from 1 to 128, 384 in all
- ln_gain: float32 [6144], replicated, may hold values from 0.5 to 1.5
- ln_bias: float32 [6144], replicated, may hold values from -0.8 to 0.8
- query_weight: bfloat16 [6144, 3072], P(None, 'tensor'), may hold values from -0.078125 to 0.078125
- w_key: bfloat16 [6144, 3072], P(None, 'tensor'), may hold values from -0.078125 to 0.078125
- value_weight: bfloat16 [6144, 3072], P(None, 'tensor'), may hold values from -0.078125 to 0.078125
- w_out: bfloat16 [3072, 6144], P('tensor'), may hold values from -0.109375 to 0.109375
- down_query: bfloat16 [6144, 16], replicated, may hold values from -0.078125 to 0.078125
- down_value: bfloat16 [6144, 16], replicated, may hold values from -0.078125 to 0.078125
- query_up_factor: float32 [16, 3072], P(None, 'tensor'), may hold values from -0.6 to 0.6
- value_up_factor: float32 [16, 3072], P(None, 'tensor'), may hold values from -0.6 to 0.6
Outputs:
- step_query: float32 [16, 3072], P(None, 'tensor')
- step_value: float32 [16, 3072], P(None, 'tensor')
- remain_query: float32 [16, 3072], P(None, 'tensor')
- remain_value: float32 [16, 3072], P(None, 'tensor')
Inputs may be any that keep to these rules, and one draw needn't show every extreme that they name: `lengths`: live tokens of each sequence; one sequence has exactly 128.
All inputs are finite; a program needn't handle non-finite values. No bound on the sum of `lengths` on one device may be relied on, other than what follows from the above.
Results may differ from a plain program's by a relative error of at most 0.035.
Values sent between devices are 32-bit elements; how exact they have to be, the bound alone decides.
No kernel may reach another device: no remote copies, remote signals or barrier semaphores. Data moves between devices by JAX's collectives and lax.ppermute only.
A program may use at most 128 MiB of HBM per device.

v0:
```python
import functools

import jax
import jax.numpy as jnp
from jax import lax
from jax.experimental import pallas as pl
from jax.experimental.pallas import tpu as pltpu
from jax.sharding import Mesh
from jax.sharding import PartitionSpec as P

HEAD_DIM = 128
CG_STEPS = 3
CHUNKS = 6
DEPTH = 1024

EPS = 1e-05
ADAPTER_SCALE = 2.0
DAMP = 0.05
NEG = -1e30
F32 = jnp.float32
BF16 = jnp.bfloat16
HIGH = lax.Precision.HIGHEST
SCALE = HEAD_DIM ** (-0.5)
VMEM = pl.BlockSpec(memory_space=pltpu.VMEM)
SMEM = pl.BlockSpec(memory_space=pltpu.SMEM)
LIMIT = 16 * 1024 * 1024
STEP_COST = pl.CostEstimate(flops=10**9, bytes_accessed=10**7, transcendentals=0)
STREAM_LIMIT = 50 * 1024 * 1024


def dot32(first, second):
    return jnp.dot(first, second, preferred_element_type=F32)


def dot_nt(first, second):
    return lax.dot_general(
        first, second, (((1,), (1,)), ((), ())), preferred_element_type=F32
    )


def dot_tn(first, second):
    return lax.dot_general(
        first, second, (((0,), (0,)), ((), ())), preferred_element_type=F32
    )


def high(first, second):
    return jnp.dot(first, second, precision=HIGH, preferred_element_type=F32)


def head(index):
    return slice(index * HEAD_DIM, (index + 1) * HEAD_DIM)


def rows_below(limit, length, width):
    return lax.broadcasted_iota(jnp.int32, (length, width), 0) < limit


def live_pairs(limit, length):
    row = lax.broadcasted_iota(jnp.int32, (length, length), 0)
    column = lax.broadcasted_iota(jnp.int32, (length, length), 1)
    return (column <= row) & (column < limit)


def split_kernel(core_ref, w_ref, *refs):
    own_refs, other_refs = refs[:CHUNKS], refs[CHUNKS : 2 * CHUNKS]
    landed, own_sem, other_sem = refs[2 * CHUNKS :]
    cols = own_refs[0].shape[1]
    half = CHUNKS * cols
    core = core_ref[0]

    def own_copy(k):
        start = pl.multiple_of(core * half + k * cols, HEAD_DIM)
        return pltpu.make_async_copy(
            w_ref.at[:, pl.ds(start, cols)], own_refs[k], own_sem.at[k]
        )

    def other_copy(k):
        start = pl.multiple_of((1 - core) * half + k * cols, HEAD_DIM)
        return pltpu.make_async_copy(
            w_ref.at[:, pl.ds(start, cols)], landed.at[k], other_sem.at[k]
        )

    for k in range(CHUNKS):
        other_copy(k).start()
    for k in range(CHUNKS):
        own_copy(k).start()
    for k in range(CHUNKS):
        other_copy(k).wait()
        other_refs[k][...] = landed[k].astype(F32)
    for k in range(CHUNKS):
        own_copy(k).wait()


def split(core, w_out):
    inner, width = w_out.shape
    cols = width // 2 // CHUNKS
    out = pl.pallas_call(
        split_kernel,
        in_specs=[SMEM, pl.BlockSpec(memory_space=pltpu.HBM)],
        out_specs=[VMEM] * (2 * CHUNKS),
        out_shape=[jax.ShapeDtypeStruct((inner, cols), BF16)] * CHUNKS
        + [jax.ShapeDtypeStruct((inner, cols), F32)] * CHUNKS,
        scratch_shapes=[
            pltpu.VMEM((CHUNKS, inner, cols), BF16),
            pltpu.SemaphoreType.DMA((CHUNKS,)),
            pltpu.SemaphoreType.DMA((CHUNKS,)),
        ],
        compiler_params=pltpu.CompilerParams(vmem_limit_bytes=LIMIT),
    )(core, w_out)
    return out[:CHUNKS], out[CHUNKS:]


def project_kernel(
    limit_ref, x_ref, wq_ref, wk_ref, wv_ref, gain_ref, bias_ref, aq_ref, av_ref, bq_ref, bv_ref,
    soft_ref, key_ref, value_ref, down_q_ref, down_v_ref, mixed_ref,
    rows_in, normed, wq_in, wk_in, wv_in, rows_sem, weight_sem,
):
    length, width = normed.shape
    inner = key_ref.shape[1]
    blocks = [slice(i, i + DEPTH) for i in range(0, width, DEPTH)]
    rows_copy = pltpu.make_async_copy(x_ref, rows_in, rows_sem)
    rows_copy.start()
    copies = []
    for i, block in enumerate(blocks):
        for j, (source, target) in enumerate(
            [(wq_ref, wq_in), (wk_ref, wk_in), (wv_ref, wv_in)]
        ):
            copies.append(
                pltpu.make_async_copy(
                    source.at[block], target.at[block], weight_sem.at[3 * i + j]
                )
            )
            copies[-1].start()
    rows_copy.wait()
    total = jnp.zeros((length, 1), F32)
    for block in blocks:
        total = total + jnp.sum(rows_in[:, block].astype(F32), axis=-1, keepdims=True)
    mean = total / width
    total = jnp.zeros((length, 1), F32)
    for block in blocks:
        centred = rows_in[:, block].astype(F32) - mean
        total = total + jnp.sum(centred * centred, axis=-1, keepdims=True)
    spread = lax.rsqrt(total / width + EPS)
    for block in blocks:
        centred = rows_in[:, block].astype(F32) - mean
        full = centred * spread * gain_ref[:, block] + bias_ref[:, block]
        normed[:, block] = full.astype(BF16)
    query = jnp.zeros((length, inner), F32)
    key = jnp.zeros((length, inner), F32)
    value = jnp.zeros((length, inner), F32)
    for i, block in enumerate(blocks):
        part = normed[:, block]
        for j in range(3):
            copies[3 * i + j].wait()
        query = query + dot32(part, wq_in[block])
        key = key + dot32(part, wk_in[block])
        value = value + dot32(part, wv_in[block])
    down_q = dot_nt(normed[...], aq_ref[...])
    down_v = dot_nt(normed[...], av_ref[...])
    down_q_ref[...] = down_q
    down_v_ref[...] = down_v
    limit = limit_ref[0]
    live = live_pairs(limit, length)
    kept = rows_below(limit, length, HEAD_DIM)
    query = (query + ADAPTER_SCALE * high(down_q, bq_ref[...])).astype(BF16)
    value = (value + ADAPTER_SCALE * high(down_v, bv_ref[...])).astype(BF16)
    key = key.astype(BF16)
    key_ref[...] = key
    value_ref[...] = value
    for h in range(inner // HEAD_DIM):
        scores = dot_nt(query[:, head(h)], key[:, head(h)]) * SCALE
        scores = jnp.where(live, scores, NEG)
        weights = jnp.exp(scores - jnp.max(scores, axis=-1, keepdims=True))
        soft = weights / jnp.sum(weights, axis=-1, keepdims=True)
        soft_ref[h] = soft
        mixed = dot32(soft.astype(BF16), value[:, head(h)]).astype(BF16)
        mixed_ref[:length, head(h)] = jnp.where(kept, mixed.astype(F32), 0.0)
    mixed_ref[length:] = jnp.zeros((8, inner), F32)


def project(limit, x, gain, bias, wq, wk, wv, aq, av, bq, bv):
    length, width = x.shape
    inner = wq.shape[1]
    rank = aq.shape[1]
    heads = inner // HEAD_DIM
    hbm = pl.BlockSpec(memory_space=pltpu.HBM)
    return pl.pallas_call(
        project_kernel,
        in_specs=[SMEM] + [hbm] * 4 + [VMEM] * 6,
        out_specs=[VMEM] * 6,
        out_shape=[
            jax.ShapeDtypeStruct((heads, length, length), F32),
            jax.ShapeDtypeStruct((length, inner), BF16),
            jax.ShapeDtypeStruct((length, inner), BF16),
            jax.ShapeDtypeStruct((length, rank), F32),
            jax.ShapeDtypeStruct((length, rank), F32),
            jax.ShapeDtypeStruct((length + 8, inner), F32),
        ],
        scratch_shapes=[
            pltpu.VMEM((length, width), BF16),
            pltpu.VMEM((length, width), BF16),
            pltpu.VMEM((width, inner), BF16),
            pltpu.VMEM((width, inner), BF16),
            pltpu.VMEM((width, inner), BF16),
            pltpu.SemaphoreType.DMA,
            pltpu.SemaphoreType.DMA((3 * (width // DEPTH),)),
        ],
        compiler_params=pltpu.CompilerParams(vmem_limit_bytes=STREAM_LIMIT),
        cost_estimate=pl.CostEstimate(
            flops=6 * length * width * inner, bytes_accessed=6 * width * inner, transcendentals=0
        ),
    )(limit, x, wq, wk, wv, gain[None], bias[None], aq.T, av.T, bq, bv)


def token_spec():
    return pl.BlockSpec(memory_space=pl.ANY)


def call(kernel, ins, outs, token, scalars=()):
    tokens = [] if token is None else [token]

    def body(*refs):
        count = len(scalars) + len(ins)
        kernel(*refs[:count], *refs[count + len(tokens) :])

    return pl.pallas_call(
        body,
        in_specs=[SMEM] * len(scalars) + [VMEM] * len(ins) + [token_spec()] * len(tokens),
        out_specs=[VMEM] * len(outs),
        out_shape=[jax.ShapeDtypeStruct(shape, kind) for shape, kind in outs],
        compiler_params=pltpu.CompilerParams(vmem_limit_bytes=LIMIT),
        cost_estimate=STEP_COST,
    )(*scalars, *ins, *tokens)


def rows_of(own_ref, got_ref, length):
    return jnp.concatenate(
        [own_ref[:length].astype(BF16), got_ref[:length].astype(BF16)], axis=1
    )


def put_tail(out_ref, own_ref, got_ref, length):
    out_ref[length:] = jnp.zeros((8, out_ref.shape[1]), F32)
    out_ref[length:, :HEAD_DIM] = own_ref[length:, :HEAD_DIM] + got_ref[length:, :HEAD_DIM]


def first_spread(index, length, own, got, own_w, other_w, token):
    inner, cols = own_w.shape
    height = length + (8 if index == 0 else 0)

    def kernel(own_ref, got_ref, own_w_ref, other_w_ref, out_ref, pair_ref):
        pair_ref[:inner] = own_w_ref[...]
        pair_ref[inner:] = other_w_ref[...].astype(BF16)
        out_ref[:length] = dot32(rows_of(own_ref, got_ref, length), pair_ref[...])
        if index == 0:
            put_tail(out_ref, own_ref, got_ref, length)

    outs = [((height, cols), F32), ((2 * inner, cols), BF16)]
    return call(kernel, [own, got, own_w, other_w], outs, token)


def spread(index, length, own, got, pair, token):
    height = length + (8 if index == 0 else 0)

    def kernel(own_ref, got_ref, pair_ref, out_ref):
        out_ref[:length] = dot32(rows_of(own_ref, got_ref, length), pair_ref[...])
        if index == 0:
            put_tail(out_ref, own_ref, got_ref, length)

    return call(kernel, [own, got, pair], [((height, pair.shape[1]), F32)], token)[0]


def add(first, second, token):
    def kernel(first_ref, second_ref, out_ref):
        out_ref[...] = first_ref[...] + second_ref[: first_ref.shape[0]]

    return call(kernel, [first, second], [(first.shape, F32)], token)[0]


def add_and_pick(first, second, ends, outer, token):
    def kernel(ends_ref, first_ref, second_ref, outer_ref, sum_ref, sent_ref):
        total = first_ref[...] + second_ref[...]
        sum_ref[...] = total
        rows = outer_ref.shape[0]
        sent_ref[:rows] = jnp.where(ends_ref[0] > 0, outer_ref[...], total[:rows])
        if total.shape[0] > rows:
            sent_ref[rows:] = total[rows:]

    outs = [(first.shape, F32)] * 2
    return call(kernel, [first, second, outer], outs, token, [ends])


def gather(index, length, ends, got, held, pair, sums, limit, gap, token):
    inner = pair.shape[0] // 2
    extra = [] if gap is None else [gap]

    def kernel(ends_ref, limit_ref, got_ref, held_ref, pair_ref, *refs):
        refs = list(refs)
        gap_ref = refs.pop(0) if gap is not None else None
        before = [refs.pop(0), refs.pop(0)] if index else None
        own_ref, other_ref = refs[:2]
        total = jnp.where(ends_ref[0] > 0, got_ref[...], held_ref[...])
        total = total[: length + (8 if index == 0 else 0)]
        if index == 0:
            refs[2][...] = total[length:, :128]
            total = total[:length]
        if gap_ref is not None:
            kept = rows_below(limit_ref[0], length, total.shape[1])
            total = jnp.where(kept, total + gap_ref[...], 0.0)
        rounded = total.astype(BF16)
        own = dot_nt(rounded, pair_ref[:inner])
        other = dot_nt(rounded, pair_ref[inner:])
        squares = jnp.full((8, inner), jnp.sum(total * total), F32)
        if index:
            own = own + before[0][...]
            other = other + before[1][:length]
            squares = squares + before[1][length:]
        own_ref[...] = own
        other_ref[:length] = other
        other_ref[length:] = squares

    outs = [((length, inner), F32), ((length + 8, inner), F32)]
    if index == 0:
        outs.append(((8, 128), F32))
    return call(kernel, [got, held, pair] + extra + sums, outs, token, [ends, limit])


def cotangent_kernel(
    share, limit_ref, own_ref, other_ref, got_ref, soft_ref, key_ref, value_ref, down_q_ref,
    down_v_ref, out_ref,
):
    length, inner = own_ref.shape
    rank = down_q_ref.shape[1]
    live = live_pairs(limit_ref[0], length)
    pulled = (own_ref[...] + got_ref[:length]).astype(BF16)
    out_ref[2 * rank :] = other_ref[length:] + got_ref[length:]
    for h in range(inner // HEAD_DIM):
        soft = soft_ref[h]
        rows = pulled[:, head(h)]
        d_probs = dot_nt(rows, value_ref[:, head(h)]).astype(BF16).astype(F32)
        d_value = dot_tn(soft.astype(BF16), rows).astype(BF16).astype(F32)
        d_scores = soft * (d_probs - jnp.sum(soft * d_probs, axis=-1, keepdims=True))
        d_scores = jnp.where(live, d_scores, 0.0) * SCALE
        d_query = dot32(d_scores.astype(BF16), key_ref[:, head(h)]).astype(BF16).astype(F32)
        out_ref[:rank, head(h)] = share * lax.dot_general(
            down_q_ref[...], d_query, (((0,), (0,)), ((), ())), precision=HIGH,
            preferred_element_type=F32,
        )
        out_ref[rank : 2 * rank, head(h)] = share * lax.dot_general(
            down_v_ref[...], d_value, (((0,), (0,)), ((), ())), precision=HIGH,
            preferred_element_type=F32,
        )


def cotangent(share, limit, own, other, got, attention):
    inner = own.shape[1]
    rank = attention[3].shape[1]
    return pl.pallas_call(
        functools.partial(cotangent_kernel, share),
        in_specs=[SMEM] + [VMEM] * 8,
        out_specs=VMEM,
        out_shape=jax.ShapeDtypeStruct((2 * rank + 8, inner), F32),
        compiler_params=pltpu.CompilerParams(vmem_limit_bytes=LIMIT),
    )(limit, own, other, got, *attention)


def tangent_of(vector, limit, soft_ref, key_ref, value_ref, down_q_ref, down_v_ref, out_ref):
    length = key_ref.shape[0]
    rank = down_q_ref.shape[1]
    live = live_pairs(limit, length)
    kept = rows_below(limit, length, HEAD_DIM)
    d_query = (ADAPTER_SCALE * high(down_q_ref[...], vector[:rank])).astype(BF16)
    d_value = (ADAPTER_SCALE * high(down_v_ref[...], vector[rank:])).astype(BF16)
    for h in range(key_ref.shape[1] // HEAD_DIM):
        soft = soft_ref[h]
        d_scores = dot_nt(d_query[:, head(h)], key_ref[:, head(h)]) * SCALE
        d_scores = jnp.where(live, d_scores, 0.0)
        d_probs = soft * (d_scores - jnp.sum(soft * d_scores, axis=-1, keepdims=True))
        d_mixed = dot32(d_probs.astype(BF16), value_ref[:, head(h)]) + dot32(
            soft.astype(BF16), d_value[:, head(h)]
        )
        out_ref[:length, head(h)] = jnp.where(kept, d_mixed.astype(BF16).astype(F32), 0.0)


def total_of(terms):
    while len(terms) > 1:
        terms = [terms[i] + terms[i + 1] for i in range(0, len(terms), 2)]
    return terms[0]


def put_sums(out_ref, remain, image):
    lane = lax.broadcasted_iota(jnp.int32, (8, out_ref.shape[1]), 1)
    cross = 0.0 if image is None else jnp.sum(remain * image)
    out_ref[out_ref.shape[0] - 8 :] = jnp.where(lane == 0, jnp.sum(remain * remain), cross)


def first_kernel(n_dp, *refs):
    terms, refs = refs[:n_dp], refs[n_dp:]
    limit_ref, *attention, remain_ref, out_ref = refs
    grads = total_of([term[...] for term in terms])
    remain = -grads[: remain_ref.shape[0]]
    remain_ref[...] = remain
    put_sums(out_ref, remain, None)
    tangent_of(remain, limit_ref[0], *attention, out_ref)


def first_step(terms, limit, attention):
    inner = terms[0].shape[1]
    length = attention[1].shape[0]
    rank = attention[3].shape[1]
    return pl.pallas_call(
        functools.partial(first_kernel, len(terms)),
        in_specs=[VMEM] * len(terms) + [SMEM] + [VMEM] * 5,
        out_specs=[VMEM] * 2,
        out_shape=[
            jax.ShapeDtypeStruct((2 * rank, inner), F32),
            jax.ShapeDtypeStruct((length + 8, inner), F32),
        ],
        compiler_params=pltpu.CompilerParams(vmem_limit_bytes=LIMIT),
    )(*terms, limit, *attention)


def step_kernel(n_dp, token_count, index, last, *refs):
    terms, refs = refs[:n_dp], refs[n_dp:]
    sums_ref, remain_ref, *refs = refs
    if index:
        before_ref, newton_ref, direction_ref, image_ref, *refs = refs
    part = total_of([term[...] for term in terms])
    remain = remain_ref[...]
    rows = remain.shape[0]
    norm, cross = sums_ref[:1, 0:1], sums_ref[:1, 1:2]
    fresh = part[:rows] + DAMP * remain
    curv = part[rows : rows + 1, 0:1] / token_count + DAMP * norm
    if index:
        ratio = norm / before_ref[:1, 0:1]
        curv = curv + 2.0 * ratio * cross + ratio * ratio * before_ref[:1, 1:2]
        direction = remain + ratio * direction_ref[...]
        image = fresh + ratio * image_ref[...]
    else:
        direction, image = remain, fresh
    alpha = norm / curv
    newton = alpha * direction
    if index:
        newton = newton_ref[...] + newton
    remain = remain - alpha * image
    if last:
        step_q_ref, step_v_ref, remain_q_ref, remain_v_ref = refs
        rank = rows // 2
        step_q_ref[...] = newton[:rank]
        step_v_ref[...] = newton[rank:]
        remain_q_ref[...] = remain[:rank]
        remain_v_ref[...] = remain[rank:]
        return
    limit_ref, *refs = refs
    attention, refs = refs[:5], refs[5:]
    next_remain, next_before, next_newton, next_direction, next_image, out_ref = refs
    lane = lax.broadcasted_iota(jnp.int32, next_before.shape, 1)
    next_remain[...] = remain
    next_before[...] = jnp.where(lane == 0, norm, curv)
    next_newton[...] = newton
    next_direction[...] = direction
    next_image[...] = image
    put_sums(out_ref, remain, image)
    tangent_of(remain, limit_ref[0], *attention, out_ref)


def cg_step(index, token_count, terms, sums, remain, state, limit, attention):
    last = index == CG_STEPS - 1
    rows, inner = remain.shape
    matrix = jax.ShapeDtypeStruct((rows, inner), F32)
    scalars = jax.ShapeDtypeStruct((8, 128), F32)
    args = [*terms, sums, remain, *state]
    specs = [VMEM] * len(args)
    if last:
        shapes = [jax.ShapeDtypeStruct((rows // 2, inner), F32)] * 4
    else:
        args += [limit, *attention]
        specs += [SMEM] + [VMEM] * 5
        length = attention[1].shape[0]
        shapes = [matrix, scalars, matrix, matrix, matrix]
        shapes.append(jax.ShapeDtypeStruct((length + 8, inner), F32))
    return pl.pallas_call(
        functools.partial(step_kernel, len(terms), token_count, index, last),
        in_specs=specs,
        out_specs=[VMEM] * len(shapes),
        out_shape=shapes,
        compiler_params=pltpu.CompilerParams(vmem_limit_bytes=LIMIT),
    )(*args)


def on_device(
    inputs,
    targets,
    lengths,
    ln_gain,
    ln_bias,
    query_weight,
    w_key,
    value_weight,
    w_out,
    down_query,
    down_value,
    query_up_factor,
    value_up_factor,
):
    length, width = inputs.shape
    n_dp = lax.axis_size("dp")
    n_chip = lax.axis_size("chip")
    core = lax.axis_index("core")
    chip = lax.axis_index("chip")
    token_count = length * n_dp
    half = width // 2

    def swap(part):
        return lax.ppermute(part, "core", [(0, 1), (1, 0)])

    def data_terms(part):
        step = 1
        while 2 * step < n_dp:
            part = part + lax.ppermute(part, "dp", [(d, d ^ step) for d in range(n_dp)])
            step *= 2
        return [part, lax.ppermute(part, "dp", [(d, d ^ step) for d in range(n_dp)])]

    where = core.astype(jnp.int32)[None]
    own_w, other_w = split(where, w_out)
    other_w = [swap(part) for part in other_w]
    cols = half // CHUNKS
    gap = lax.dynamic_slice_in_dim(inputs, core * half, half, 1).astype(F32)
    gap = gap - lax.dynamic_slice_in_dim(targets, core * half, half, 1).astype(F32)

    soft, key, value, down_q, down_v, mixed = project(
        lengths, inputs, ln_gain, ln_bias, query_weight, w_key, value_weight, down_query,
        down_value, query_up_factor, value_up_factor,
    )
    attention = (soft, key, value, down_q, down_v)

    ends = ((chip == 0) | (chip == n_chip - 1)).astype(jnp.int32)[None]

    def outer_swap(part):
        return lax.ppermute(part, "chip", [(0, 1), (1, 0), (2, 3), (3, 2)])

    def inner_swap(part):
        return lax.ppermute(part, "chip", [(0, 0), (1, 2), (2, 1), (3, 3)])

    def product(rows, pairs):
        got_rows = swap(rows)
        first = not pairs
        pairs.extend([None] * (CHUNKS - len(pairs)))
        parts, scalars = [], None
        own_part, total, outer, inner = {}, {}, {}, {}
        token = None

        def begin(k):
            if first:
                own_part[k], pairs[k] = first_spread(
                    k, length, rows, got_rows, own_w[k], other_w[k], token
                )
            else:
                own_part[k] = spread(k, length, rows, got_rows, pairs[k], token)
            return own_part[k]

        def finish(k, got):
            gap_part = gap[:, k * cols : (k + 1) * cols] if first else None
            return gather(k, length, ends, got, total[k], pairs[k], parts, lengths, gap_part, token)

        if n_chip != 4:
            for k in range(CHUNKS):
                token = begin(k)
            for k in range(CHUNKS):
                total[k] = lax.psum(own_part[k], "chip")
                out = finish(k, total[k])
                parts, scalars = list(out[:2]), out[2] if k == 0 else scalars
        else:
            for k in [0, 1, 2] if first else [0, *range(2, CHUNKS), 1]:
                token = begin(k)
            for k in (0, 1):
                outer[k] = outer_swap(own_part[k])
            for tick in range(CHUNKS + 3):
                if tick < CHUNKS:
                    own_part[tick] = add(own_part[tick], outer[tick], token)
                    token = own_part[tick]
                    inner[tick] = inner_swap(token)
                later = tick + 2
                if tick == CHUNKS:
                    out = finish(tick - 3, outer[tick])
                    parts = list(out[:2])
                    token = parts[0]
                if 1 <= tick <= CHUNKS:
                    k = tick - 1
                    if later < CHUNKS:
                        total[k], sent = add_and_pick(
                            own_part[k], inner[k], ends, own_part[later], token
                        )
                    else:
                        total[k] = sent = add(own_part[k], inner[k], token)
                    token = sent
                    outer[later] = outer_swap(sent)
                elif tick == 0:
                    outer[later] = outer_swap(own_part[later])
                if tick + 3 < CHUNKS and first:
                    token = begin(tick + 3)
                if tick >= 3 and tick != CHUNKS:
                    out = finish(tick - 3, outer[tick])
                    parts, scalars = list(out[:2]), out[2] if tick == 3 else scalars
                    token = parts[0]
        own, other = parts
        share = ADAPTER_SCALE / token_count
        part = cotangent(share, lengths, own, other, swap(other), attention)
        return data_terms(part), scalars

    pairs = []
    terms, _ = product(mixed, pairs)
    remain, rows = first_step(terms, lengths, attention)
    state = ()
    for index in range(CG_STEPS):
        terms, sums = product(rows, pairs)
        out = cg_step(index, token_count, terms, sums, remain, state, lengths, attention)
        if index < CG_STEPS - 1:
            remain, *state, rows = out
    return tuple(out)


def solution(mesh):
    fine = Mesh(mesh.devices.reshape(mesh.shape["dp"], -1, 2), ("dp", "chip", "core"))
    tensor = ("chip", "core")
    in_specs = (
        P("dp", None),
        P("dp", None),
        P("dp"),
        P(),
        P(),
        P(None, tensor),
        P(None, tensor),
        P(None, tensor),
        P(tensor, None),
        P(),
        P(),
        P(None, tensor),
        P(None, tensor),
    )
    out_specs = (P(None, tensor),) * 4
    return jax.shard_map(
        on_device, mesh=fine, in_specs=in_specs, out_specs=out_specs, check_vma=False
    )
```

profile of v0, /device:TPU:0, one launch (start us, length us, event | category | flops | bytes accessed | tf_op | source)
XLA Modules:
  0.0 302.6 jit_solution(1550399012264713755)
XLA Ops:
  0.6 2.3 copy-done
  3.0 2.5 shard_map.157
  8.1 8.8 %shard_map.156 = (f32[3,128,128]{2,1,0:T(8,128)S(1)}, bf16[128,384]{1,0:T(8,128)(2,1)S(1)}, bf16[128,384]{1,0:T(8,128)(2,1)S(1)}, f32[128,16]{1,0:T(8,128)S(1)},...) custom-call(s32[1]{0:T(128)S(6)} %copy.17.limit_ref.refs_1_.refs_2_.refs_4_.refs_8_, bf16[128,6144]{1,0:T(8,128)(2,1)S(1)} %copy-done.1, ...), custom_call_target="tpu_custom_call" | custom-call | flops 1811939328 | bytes 14155776 | tf_op jit(solution)/shard_map/pallas_call | solution.py:188
  21.7 3.0 collective-permute-start.6
  25.0 2.4 shard_map.159
  33.5 4.0 %collective-permute-start.11 = (f32[128,512]{1,0:T(8,128)}, f32[128,512]{1,0:T(8,128)S(1)}, u32[]{:S(2)}, u32[]{:S(2)}) collective-permute-start(f32[128,512]{1,0:T(8,128)} %copy-done.19), channel_id=1, source_target_pairs={{0,2},{2,0},{4,6},{6,4},{1,3},{3,1},{5,7},{7,5},{8,10},{10,8},{12,... | collective-permute-start | bytes 786440 | tf_op jit(solution)/shard_map/ppermute | solution.py:541
  42.0 3.0 collective-permute-start.13
  47.7 3.0 collective-permute-start.15
  53.4 3.5 %collective-permute-start.14 = (f32[128,512]{1,0:T(8,128)S(1)}, f32[128,512]{1,0:T(8,128)S(1)}, u32[]{:S(2)}, u32[]{:S(2)}) collective-permute-start(f32[128,512]{1,0:T(8,128)S(1)} %get-tuple-element.144.refs_6_), channel_id=1, source_target_pairs={{0,2},{2,0},{4,6},{6,4},{1,3},{3,1},{5,7},{7,5},{8,10},{10,8},{12,... | collective-permute-start | bytes 786440 | tf_op jit(solution)/shard_map/ppermute | solution.py:541
  58.7 4.7 %collective-permute-start.18 = (f32[128,512]{1,0:T(8,128)S(1)}, f32[128,512]{1,0:T(8,128)S(1)}, u32[]{:S(2)}, u32[]{:S(2)}) collective-permute-start(f32[128,512]{1,0:T(8,128)S(1)} %shard_map.173.refs_8_.refs_3_), channel_id=1, source_target_pairs={{0,2},{2,0},{4,6},{6,4},{1,3},{3,1},{5,7},{7,5},{8,10},{10,8},{12,... | collective-permute-start | bytes 786440 | tf_op jit(solution)/shard_map/ppermute | solution.py:541
  65.1 4.4 %collective-permute-start.21 = (f32[128,512]{1,0:T(8,128)S(1)}, f32[128,512]{1,0:T(8,128)S(1)}, u32[]{:S(2)}, u32[]{:S(2)}) collective-permute-start(f32[128,512]{1,0:T(8,128)S(1)} %shard_map.176.refs_8_.refs_3_), channel_id=1, source_target_pairs={{0,2},{2,0},{4,6},{6,4},{1,3},{3,1},{5,7},{7,5},{8,10},{10,8},{12,... | collective-permute-start | bytes 786440 | tf_op jit(solution)/shard_map/ppermute | solution.py:541
  70.3 3.9 %collective-permute-start.20 = (f32[128,512]{1,0:T(8,128)S(1)}, f32[128,512]{1,0:T(8,128)S(1)}, u32[]{:S(2)}, u32[]{:S(2)}) collective-permute-start(f32[128,512]{1,0:T(8,128)S(1)} %shard_map.179.refs_8_.refs_3_), channel_id=1, source_target_pairs={{0,2},{2,0},{4,6},{6,4},{1,3},{3,1},{5,7},{7,5},{8,10},{10,8},{12,... | collective-permute-start | bytes 786440 | tf_op jit(solution)/shard_map/ppermute | solution.py:541
  75.8 3.6 %collective-permute-done.20.refs_2_ = f32[128,512]{1,0:T(8,128)S(1)} collective-permute-done((f32[128,512]{1,0:T(8,128)S(1)}, f32[128,512]{1,0:T(8,128)S(1)}, u32[]{:S(2)}, u32[]{:S(2)}) %collective-permute-start.20) | collective-permute-done | bytes 262176 | tf_op jit(solution)/shard_map/ppermute | solution.py:541
  84.4 2.7 collective-permute-done.23
  88.7 2.7 collective-permute-done.24.refs_1_
  97.6 6.0 %collective-permute-done.27.refs_1_ = f32[136,512]{1,0:T(8,128)S(1)} collective-permute-done((f32[136,512]{1,0:T(8,128)S(1)}, f32[136,512]{1,0:T(8,128)S(1)}, u32[]{:S(2)}, u32[]{:S(2)}) %collective-permute-start.27) | collective-permute-done | bytes 278560 | tf_op jit(solution)/shard_map/ppermute | solution.py:541
  104.2 5.6 %collective-permute-start.26 = (f32[128,512]{1,0:T(8,128)S(1)}, f32[128,512]{1,0:T(8,128)S(1)}, u32[]{:S(2)}, u32[]{:S(2)}) collective-permute-start(f32[128,512]{1,0:T(8,128)S(1)} %shard_map.185.refs_3_.refs_0_), channel_id=1, source_target_pairs={{0,2},{2,0},{4,6},{6,4},{1,3},{3,1},{5,7},{7,5},{8,10},{10,8},{12,... | collective-permute-start | bytes 786440 | tf_op jit(solution)/shard_map/ppermute | solution.py:541
  110.7 4.9 %collective-permute-start.31 = (f32[136,512]{1,0:T(8,128)S(1)}, f32[136,512]{1,0:T(8,128)S(1)}, u32[]{:S(2)}, u32[]{:S(2)}) collective-permute-start(f32[136,512]{1,0:T(8,128)S(1)} %get-tuple-element.172.refs_2_), channel_id=1, source_target_pairs={{0,2},{2,0},{4,6},{6,4},{1,3},{3,1},{5,7},{7,5},{8,10},{10,8},{12,... | collective-permute-start | bytes 835592 | tf_op jit(solution)/shard_map/ppermute | solution.py:541
  116.4 4.8 %collective-permute-start.34 = (f32[128,512]{1,0:T(8,128)S(1)}, f32[128,512]{1,0:T(8,128)S(1)}, u32[]{:S(2)}, u32[]{:S(2)}) collective-permute-start(f32[128,512]{1,0:T(8,128)S(1)} %get-tuple-element.173.refs_2_), channel_id=1, source_target_pairs={{0,2},{2,0},{4,6},{6,4},{1,3},{3,1},{5,7},{7,5},{8,10},{10,8},{12,... | collective-permute-start | bytes 786440 | tf_op jit(solution)/shard_map/ppermute | solution.py:541
  122.0 6.2 %collective-permute-start.33 = (f32[128,512]{1,0:T(8,128)S(1)}, f32[128,512]{1,0:T(8,128)S(1)}, u32[]{:S(2)}, u32[]{:S(2)}) collective-permute-start(f32[128,512]{1,0:T(8,128)S(1)} %get-tuple-element.174.refs_5_), channel_id=1, source_target_pairs={{0,2},{2,0},{4,6},{6,4},{1,3},{3,1},{5,7},{7,5},{8,10},{10,8},{12,... | collective-permute-start | bytes 786440 | tf_op jit(solution)/shard_map/ppermute | solution.py:541
  129.4 4.1 %collective-permute-start.37 = (f32[128,512]{1,0:T(8,128)S(1)}, f32[128,512]{1,0:T(8,128)S(1)}, u32[]{:S(2)}, u32[]{:S(2)}) collective-permute-start(f32[128,512]{1,0:T(8,128)S(1)} %shard_map.199.refs_7_.refs_3_), channel_id=1, source_target_pairs={{0,2},{2,0},{4,6},{6,4},{1,3},{3,1},{5,7},{7,5},{8,10},{10,8},{12,... | collective-permute-start | bytes 786440 | tf_op jit(solution)/shard_map/ppermute | solution.py:541
  135.3 5.6 %collective-permute-start.40 = (f32[128,512]{1,0:T(8,128)S(1)}, f32[128,512]{1,0:T(8,128)S(1)}, u32[]{:S(2)}, u32[]{:S(2)}) collective-permute-start(f32[128,512]{1,0:T(8,128)S(1)} %shard_map.202.refs_7_.refs_3_), channel_id=1, source_target_pairs={{0,2},{2,0},{4,6},{6,4},{1,3},{3,1},{5,7},{7,5},{8,10},{10,8},{12,... | collective-permute-start | bytes 786440 | tf_op jit(solution)/shard_map/ppermute | solution.py:541
  141.8 3.6 %collective-permute-start.39 = (f32[128,512]{1,0:T(8,128)S(1)}, f32[128,512]{1,0:T(8,128)S(1)}, u32[]{:S(2)}, u32[]{:S(2)}) collective-permute-start(f32[128,512]{1,0:T(8,128)S(1)} %shard_map.205.refs_7_.refs_3_), channel_id=1, source_target_pairs={{0,2},{2,0},{4,6},{6,4},{1,3},{3,1},{5,7},{7,5},{8,10},{10,8},{12,... | collective-permute-start | bytes 786440 | tf_op jit(solution)/shard_map/ppermute | solution.py:541
  147.5 2.4 collective-permute-done.39.refs_2_
  154.9 2.7 collective-permute-done.42
  159.2 2.7 collective-permute-done.43.refs_1_
  168.0 6.0 %collective-permute-done.46.refs_1_ = f32[136,512]{1,0:T(8,128)S(1)} collective-permute-done((f32[136,512]{1,0:T(8,128)S(1)}, f32[136,512]{1,0:T(8,128)S(1)}, u32[]{:S(2)}, u32[]{:S(2)}) %collective-permute-start.46) | collective-permute-done | bytes 278560 | tf_op jit(solution)/shard_map/ppermute | solution.py:541
  174.8 5.0 %collective-permute-start.45 = (f32[128,512]{1,0:T(8,128)S(1)}, f32[128,512]{1,0:T(8,128)S(1)}, u32[]{:S(2)}, u32[]{:S(2)}) collective-permute-start(f32[128,512]{1,0:T(8,128)S(1)} %shard_map.211.refs_3_.refs_0_), channel_id=1, source_target_pairs={{0,2},{2,0},{4,6},{6,4},{1,3},{3,1},{5,7},{7,5},{8,10},{10,8},{12,... | collective-permute-start | bytes 786440 | tf_op jit(solution)/shard_map/ppermute | solution.py:541
  180.6 4.9 %collective-permute-start.50 = (f32[136,512]{1,0:T(8,128)S(1)}, f32[136,512]{1,0:T(8,128)S(1)}, u32[]{:S(2)}, u32[]{:S(2)}) collective-permute-start(f32[136,512]{1,0:T(8,128)S(1)} %get-tuple-element.193.refs_2_), channel_id=1, source_target_pairs={{0,2},{2,0},{4,6},{6,4},{1,3},{3,1},{5,7},{7,5},{8,10},{10,8},{12,... | collective-permute-start | bytes 835592 | tf_op jit(solution)/shard_map/ppermute | solution.py:541
  186.3 4.9 %collective-permute-start.53 = (f32[128,512]{1,0:T(8,128)S(1)}, f32[128,512]{1,0:T(8,128)S(1)}, u32[]{:S(2)}, u32[]{:S(2)}) collective-permute-start(f32[128,512]{1,0:T(8,128)S(1)} %get-tuple-element.194.refs_2_), channel_id=1, source_target_pairs={{0,2},{2,0},{4,6},{6,4},{1,3},{3,1},{5,7},{7,5},{8,10},{10,8},{12,... | collective-permute-start | bytes 786440 | tf_op jit(solution)/shard_map/ppermute | solution.py:541
  192.0 6.1 %collective-permute-start.52 = (f32[128,512]{1,0:T(8,128)S(1)}, f32[128,512]{1,0:T(8,128)S(1)}, u32[]{:S(2)}, u32[]{:S(2)}) collective-permute-start(f32[128,512]{1,0:T(8,128)S(1)} %get-tuple-element.195.refs_5_), channel_id=1, source_target_pairs={{0,2},{2,0},{4,6},{6,4},{1,3},{3,1},{5,7},{7,5},{8,10},{10,8},{12,... | collective-permute-start | bytes 786440 | tf_op jit(solution)/shard_map/ppermute | solution.py:541
  199.3 4.2 %collective-permute-start.56 = (f32[128,512]{1,0:T(8,128)S(1)}, f32[128,512]{1,0:T(8,128)S(1)}, u32[]{:S(2)}, u32[]{:S(2)}) collective-permute-start(f32[128,512]{1,0:T(8,128)S(1)} %shard_map.225.refs_7_.refs_3_), channel_id=1, source_target_pairs={{0,2},{2,0},{4,6},{6,4},{1,3},{3,1},{5,7},{7,5},{8,10},{10,8},{12,... | collective-permute-start | bytes 786440 | tf_op jit(solution)/shard_map/ppermute | solution.py:541
  205.5 5.6 %collective-permute-start.59 = (f32[128,512]{1,0:T(8,128)S(1)}, f32[128,512]{1,0:T(8,128)S(1)}, u32[]{:S(2)}, u32[]{:S(2)}) collective-permute-start(f32[128,512]{1,0:T(8,128)S(1)} %shard_map.228.refs_7_.refs_3_), channel_id=1, source_target_pairs={{0,2},{2,0},{4,6},{6,4},{1,3},{3,1},{5,7},{7,5},{8,10},{10,8},{12,... | collective-permute-start | bytes 786440 | tf_op jit(solution)/shard_map/ppermute | solution.py:541
  211.9 3.3 %collective-permute-start.58 = (f32[128,512]{1,0:T(8,128)S(1)}, f32[128,512]{1,0:T(8,128)S(1)}, u32[]{:S(2)}, u32[]{:S(2)}) collective-permute-start(f32[128,512]{1,0:T(8,128)S(1)} %shard_map.231.refs_7_.refs_3_), channel_id=1, source_target_pairs={{0,2},{2,0},{4,6},{6,4},{1,3},{3,1},{5,7},{7,5},{8,10},{10,8},{12,... | collective-permute-start | bytes 786440 | tf_op jit(solution)/shard_map/ppermute | solution.py:541
  217.4 2.4 collective-permute-done.58.refs_2_
  224.8 2.7 collective-permute-done.61
  229.1 2.7 collective-permute-done.62.refs_1_
  238.0 6.0 %collective-permute-done.65.refs_1_ = f32[136,512]{1,0:T(8,128)S(1)} collective-permute-done((f32[136,512]{1,0:T(8,128)S(1)}, f32[136,512]{1,0:T(8,128)S(1)}, u32[]{:S(2)}, u32[]{:S(2)}) %collective-permute-start.65) | collective-permute-done | bytes 278560 | tf_op jit(solution)/shard_map/ppermute | solution.py:541
  244.8 5.1 %collective-permute-start.64 = (f32[128,512]{1,0:T(8,128)S(1)}, f32[128,512]{1,0:T(8,128)S(1)}, u32[]{:S(2)}, u32[]{:S(2)}) collective-permute-start(f32[128,512]{1,0:T(8,128)S(1)} %shard_map.237.refs_3_.refs_0_), channel_id=1, source_target_pairs={{0,2},{2,0},{4,6},{6,4},{1,3},{3,1},{5,7},{7,5},{8,10},{10,8},{12,... | collective-permute-start | bytes 786440 | tf_op jit(solution)/shard_map/ppermute | solution.py:541
  250.6 4.9 %collective-permute-start.69 = (f32[136,512]{1,0:T(8,128)S(1)}, f32[136,512]{1,0:T(8,128)S(1)}, u32[]{:S(2)}, u32[]{:S(2)}) collective-permute-start(f32[136,512]{1,0:T(8,128)S(1)} %get-tuple-element.218.refs_2_), channel_id=1, source_target_pairs={{0,2},{2,0},{4,6},{6,4},{1,3},{3,1},{5,7},{7,5},{8,10},{10,8},{12,... | collective-permute-start | bytes 835592 | tf_op jit(solution)/shard_map/ppermute | solution.py:541
  256.3 4.9 %collective-permute-start.72 = (f32[128,512]{1,0:T(8,128)S(1)}, f32[128,512]{1,0:T(8,128)S(1)}, u32[]{:S(2)}, u32[]{:S(2)}) collective-permute-start(f32[128,512]{1,0:T(8,128)S(1)} %get-tuple-element.219.refs_2_), channel_id=1, source_target_pairs={{0,2},{2,0},{4,6},{6,4},{1,3},{3,1},{5,7},{7,5},{8,10},{10,8},{12,... | collective-permute-start | bytes 786440 | tf_op jit(solution)/shard_map/ppermute | solution.py:541
  262.0 6.1 %collective-permute-start.71 = (f32[128,512]{1,0:T(8,128)S(1)}, f32[128,512]{1,0:T(8,128)S(1)}, u32[]{:S(2)}, u32[]{:S(2)}) collective-permute-start(f32[128,512]{1,0:T(8,128)S(1)} %get-tuple-element.220.refs_5_), channel_id=1, source_target_pairs={{0,2},{2,0},{4,6},{6,4},{1,3},{3,1},{5,7},{7,5},{8,10},{10,8},{12,... | collective-permute-start | bytes 786440 | tf_op jit(solution)/shard_map/ppermute | solution.py:541
  269.3 4.2 %collective-permute-start.75 = (f32[128,512]{1,0:T(8,128)S(1)}, f32[128,512]{1,0:T(8,128)S(1)}, u32[]{:S(2)}, u32[]{:S(2)}) collective-permute-start(f32[128,512]{1,0:T(8,128)S(1)} %shard_map.251.refs_7_.refs_3_), channel_id=1, source_target_pairs={{0,2},{2,0},{4,6},{6,4},{1,3},{3,1},{5,7},{7,5},{8,10},{10,8},{12,... | collective-permute-start | bytes 786440 | tf_op jit(solution)/shard_map/ppermute | solution.py:541
  275.3 5.6 %collective-permute-start.78 = (f32[128,512]{1,0:T(8,128)S(1)}, f32[128,512]{1,0:T(8,128)S(1)}, u32[]{:S(2)}, u32[]{:S(2)}) collective-permute-start(f32[128,512]{1,0:T(8,128)S(1)} %shard_map.254.refs_7_.refs_3_), channel_id=1, source_target_pairs={{0,2},{2,0},{4,6},{6,4},{1,3},{3,1},{5,7},{7,5},{8,10},{10,8},{12,... | collective-permute-start | bytes 786440 | tf_op jit(solution)/shard_map/ppermute | solution.py:541
  281.7 3.6 %collective-permute-start.77 = (f32[128,512]{1,0:T(8,128)S(1)}, f32[128,512]{1,0:T(8,128)S(1)}, u32[]{:S(2)}, u32[]{:S(2)}) collective-permute-start(f32[128,512]{1,0:T(8,128)S(1)} %shard_map.257.refs_7_.refs_3_), channel_id=1, source_target_pairs={{0,2},{2,0},{4,6},{6,4},{1,3},{3,1},{5,7},{7,5},{8,10},{10,8},{12,... | collective-permute-start | bytes 786440 | tf_op jit(solution)/shard_map/ppermute | solution.py:541
  287.4 2.4 collective-permute-done.77.refs_2_
  294.8 2.7 collective-permute-done.80
  299.1 2.7 collective-permute-done.81.refs_1_
  (284 shorter events, 100.8 us)
Async XLA Ops:
  6.3 12.6 %collective-permute-start.3 = (f32[384,512]{1,0:T(8,128)}, f32[384,512]{1,0:T(8,128)}, u32[]{:S(2)}, u32[]{:S(2)}) collective-permute-start(f32[384,512]{1,0:T(8,128)} %get-tuple-element.129), channel_id=1, source_target_pairs={{0,1},{1,0},{2,3},{3,2},{4,5},{5,4},{6,7},{7,6},{8,9},{9,8},{10,11... | collective-permute-start | bytes 2359304 | tf_op jit(solution)/shard_map/ppermute | solution.py:516
  6.9 18.1 %collective-permute-start.2 = (f32[384,512]{1,0:T(8,128)}, f32[384,512]{1,0:T(8,128)}, u32[]{:S(2)}, u32[]{:S(2)}) collective-permute-start(f32[384,512]{1,0:T(8,128)} %get-tuple-element.127), channel_id=1, source_target_pairs={{0,1},{1,0},{2,3},{3,2},{4,5},{5,4},{6,7},{7,6},{8,9},{9,8},{10,11... | collective-permute-start | bytes 2359304 | tf_op jit(solution)/shard_map/ppermute | solution.py:516
  6.9 21.3 %collective-permute-start.7 = (f32[384,512]{1,0:T(8,128)}, f32[384,512]{1,0:T(8,128)}, u32[]{:S(2)}, u32[]{:S(2)}) collective-permute-start(f32[384,512]{1,0:T(8,128)} %get-tuple-element.135), channel_id=1, source_target_pairs={{0,1},{1,0},{2,3},{3,2},{4,5},{5,4},{6,7},{7,6},{8,9},{9,8},{10,11... | collective-permute-start | bytes 2359304 | tf_op jit(solution)/shard_map/ppermute | solution.py:516
  17.1 16.4 %collective-permute-start.5 = (f32[384,512]{1,0:T(8,128)}, f32[384,512]{1,0:T(8,128)}, u32[]{:S(2)}, u32[]{:S(2)}) collective-permute-start(f32[384,512]{1,0:T(8,128)} %get-tuple-element.133), channel_id=1, source_target_pairs={{0,1},{1,0},{2,3},{3,2},{4,5},{5,4},{6,7},{7,6},{8,9},{9,8},{10,11... | collective-permute-start | bytes 2359304 | tf_op jit(solution)/shard_map/ppermute | solution.py:516
  18.8 26.3 %collective-permute-start.9 = (f32[384,512]{1,0:T(8,128)}, f32[384,512]{1,0:T(8,128)}, u32[]{:S(2)}, u32[]{:S(2)}) collective-permute-start(f32[384,512]{1,0:T(8,128)} %copy-done.8), channel_id=1, source_target_pairs={{0,1},{1,0},{2,3},{3,2},{4,5},{5,4},{6,7},{7,6},{8,9},{9,8},{10,11... | collective-permute-start | bytes 2359304 | tf_op jit(solution)/shard_map/ppermute | solution.py:516
  21.7 10.0 %collective-permute-start.6 = (f32[136,512]{1,0:T(8,128)S(1)}, f32[136,512]{1,0:T(8,128)S(1)}, u32[]{:S(2)}, u32[]{:S(2)}) collective-permute-start(f32[136,512]{1,0:T(8,128)S(1)} %get-tuple-element.130.refs_4_.refs_0_), channel_id=1, source_target_pairs={{0,2},{2,0},{4,6},{6,4},{1,3},{3,1},{5,7},{7,5},{8,10},{10,8},{12,... | collective-permute-start | bytes 835592 | tf_op jit(solution)/shard_map/ppermute | solution.py:541
  24.9 25.8 %collective-permute-start.1 = (f32[384,512]{1,0:T(8,128)S(1)}, f32[384,512]{1,0:T(8,128)}, u32[]{:S(2)}, u32[]{:S(2)}) collective-permute-start(f32[384,512]{1,0:T(8,128)S(1)} %get-tuple-element.125), channel_id=1, source_target_pairs={{0,1},{1,0},{2,3},{3,2},{4,5},{5,4},{6,7},{7,6},{8,9},{9,8},{10,11... | collective-permute-start | bytes 2359304 | tf_op jit(solution)/shard_map/ppermute | solution.py:516
  28.3 10.9 %collective-permute-start.4 = (f32[128,512]{1,0:T(8,128)}, f32[128,512]{1,0:T(8,128)}, u32[]{:S(2)}, u32[]{:S(2)}) collective-permute-start(f32[128,512]{1,0:T(8,128)} %get-tuple-element.131.refs_4_.refs_0_), channel_id=1, source_target_pairs={{0,2},{2,0},{4,6},{6,4},{1,3},{3,1},{5,7},{7,5},{8,10},{10,8},{12,... | collective-permute-start | bytes 786440 | tf_op jit(solution)/shard_map/ppermute | solution.py:541
  31.9 9.1 %collective-permute-start.10 = (f32[136,512]{1,0:T(8,128)S(1)}, f32[136,512]{1,0:T(8,128)}, u32[]{:S(2)}, u32[]{:S(2)}) collective-permute-start(f32[136,512]{1,0:T(8,128)S(1)} %shard_map.161.refs_4_.refs_1_), channel_id=1, source_target_pairs={{0,0},{2,4},{4,2},{6,6},{1,1},{3,5},{5,3},{7,7},{8,8},{10,12},{12,... | collective-permute-start | bytes 835592 | tf_op jit(solution)/shard_map/ppermute | solution.py:544
  33.5 13.2 %collective-permute-start.11 = (f32[128,512]{1,0:T(8,128)}, f32[128,512]{1,0:T(8,128)S(1)}, u32[]{:S(2)}, u32[]{:S(2)}) collective-permute-start(f32[128,512]{1,0:T(8,128)} %copy-done.19), channel_id=1, source_target_pairs={{0,2},{2,0},{4,6},{6,4},{1,3},{3,1},{5,7},{7,5},{8,10},{10,8},{12,... | collective-permute-start | bytes 786440 | tf_op jit(solution)/shard_map/ppermute | solution.py:541
  40.3 7.4 %collective-permute-start.8 = (f32[128,512]{1,0:T(8,128)S(1)}, f32[128,512]{1,0:T(8,128)S(1)}, u32[]{:S(2)}, u32[]{:S(2)}) collective-permute-start(f32[128,512]{1,0:T(8,128)S(1)} %shard_map.163.refs_4_.refs_1_), channel_id=1, source_target_pairs={{0,0},{2,4},{4,2},{6,6},{1,1},{3,5},{5,3},{7,7},{8,8},{10,12},{12,... | collective-permute-start | bytes 786440 | tf_op jit(solution)/shard_map/ppermute | solution.py:544
  42.0 10.5 %collective-permute-start.13 = (f32[136,512]{1,0:T(8,128)S(1)}, f32[136,512]{1,0:T(8,128)S(1)}, u32[]{:S(2)}, u32[]{:S(2)}) collective-permute-start(f32[136,512]{1,0:T(8,128)S(1)} %get-tuple-element.140.refs_4_), channel_id=1, source_target_pairs={{0,2},{2,0},{4,6},{6,4},{1,3},{3,1},{5,7},{7,5},{8,10},{10,8},{12,... | collective-permute-start | bytes 835592 | tf_op jit(solution)/shard_map/ppermute | solution.py:541
  47.7 10.1 %collective-permute-start.15 = (f32[128,512]{1,0:T(8,128)S(1)}, f32[128,512]{1,0:T(8,128)S(1)}, u32[]{:S(2)}, u32[]{:S(2)}) collective-permute-start(f32[128,512]{1,0:T(8,128)S(1)} %get-tuple-element.142.refs_4_), channel_id=1, source_target_pairs={{0,2},{2,0},{4,6},{6,4},{1,3},{3,1},{5,7},{7,5},{8,10},{10,8},{12,... | collective-permute-start | bytes 786440 | tf_op jit(solution)/shard_map/ppermute | solution.py:541
  53.4 10.5 %collective-permute-start.14 = (f32[128,512]{1,0:T(8,128)S(1)}, f32[128,512]{1,0:T(8,128)S(1)}, u32[]{:S(2)}, u32[]{:S(2)}) collective-permute-start(f32[128,512]{1,0:T(8,128)S(1)} %get-tuple-element.144.refs_6_), channel_id=1, source_target_pairs={{0,2},{2,0},{4,6},{6,4},{1,3},{3,1},{5,7},{7,5},{8,10},{10,8},{12,... | collective-permute-start | bytes 786440 | tf_op jit(solution)/shard_map/ppermute | solution.py:541
  58.7 11.2 %collective-permute-start.18 = (f32[128,512]{1,0:T(8,128)S(1)}, f32[128,512]{1,0:T(8,128)S(1)}, u32[]{:S(2)}, u32[]{:S(2)}) collective-permute-start(f32[128,512]{1,0:T(8,128)S(1)} %shard_map.173.refs_8_.refs_3_), channel_id=1, source_target_pairs={{0,2},{2,0},{4,6},{6,4},{1,3},{3,1},{5,7},{7,5},{8,10},{10,8},{12,... | collective-permute-start | bytes 786440 | tf_op jit(solution)/shard_map/ppermute | solution.py:541
  65.1 10.4 %collective-permute-start.21 = (f32[128,512]{1,0:T(8,128)S(1)}, f32[128,512]{1,0:T(8,128)S(1)}, u32[]{:S(2)}, u32[]{:S(2)}) collective-permute-start(f32[128,512]{1,0:T(8,128)S(1)} %shard_map.176.refs_8_.refs_3_), channel_id=1, source_target_pairs={{0,2},{2,0},{4,6},{6,4},{1,3},{3,1},{5,7},{7,5},{8,10},{10,8},{12,... | collective-permute-start | bytes 786440 | tf_op jit(solution)/shard_map/ppermute | solution.py:541
  70.3 9.1 %collective-permute-start.20 = (f32[128,512]{1,0:T(8,128)S(1)}, f32[128,512]{1,0:T(8,128)S(1)}, u32[]{:S(2)}, u32[]{:S(2)}) collective-permute-start(f32[128,512]{1,0:T(8,128)S(1)} %shard_map.179.refs_8_.refs_3_), channel_id=1, source_target_pairs={{0,2},{2,0},{4,6},{6,4},{1,3},{3,1},{5,7},{7,5},{8,10},{10,8},{12,... | collective-permute-start | bytes 786440 | tf_op jit(solution)/shard_map/ppermute | solution.py:541
  94.0 9.5 %collective-permute-start.27 = (f32[136,512]{1,0:T(8,128)S(1)}, f32[136,512]{1,0:T(8,128)S(1)}, u32[]{:S(2)}, u32[]{:S(2)}) collective-permute-start(f32[136,512]{1,0:T(8,128)S(1)} %shard_map.184.refs_3_.refs_0_), channel_id=1, source_target_pairs={{0,2},{2,0},{4,6},{6,4},{1,3},{3,1},{5,7},{7,5},{8,10},{10,8},{12,... | collective-permute-start | bytes 835592 | tf_op jit(solution)/shard_map/ppermute | solution.py:541
  97.5 12.4 %collective-permute-start.29 = (f32[128,512]{1,0:T(8,128)S(1)}, f32[128,512]{1,0:T(8,128)S(1)}, u32[]{:S(2)}, u32[]{:S(2)}) collective-permute-start(f32[128,512]{1,0:T(8,128)S(1)} %shard_map.189.refs_2_.refs_0_), channel_id=1, source_target_pairs={{0,2},{2,0},{4,6},{6,4},{1,3},{3,1},{5,7},{7,5},{8,10},{10,8},{12,... | collective-permute-start | bytes 786440 | tf_op jit(solution)/shard_map/ppermute | solution.py:541
  104.2 11.3 %collective-permute-start.26 = (f32[128,512]{1,0:T(8,128)S(1)}, f32[128,512]{1,0:T(8,128)S(1)}, u32[]{:S(2)}, u32[]{:S(2)}) collective-permute-start(f32[128,512]{1,0:T(8,128)S(1)} %shard_map.185.refs_3_.refs_0_), channel_id=1, source_target_pairs={{0,2},{2,0},{4,6},{6,4},{1,3},{3,1},{5,7},{7,5},{8,10},{10,8},{12,... | collective-permute-start | bytes 786440 | tf_op jit(solution)/shard_map/ppermute | solution.py:541
  110.7 10.5 %collective-permute-start.31 = (f32[136,512]{1,0:T(8,128)S(1)}, f32[136,512]{1,0:T(8,128)S(1)}, u32[]{:S(2)}, u32[]{:S(2)}) collective-permute-start(f32[136,512]{1,0:T(8,128)S(1)} %get-tuple-element.172.refs_2_), channel_id=1, source_target_pairs={{0,2},{2,0},{4,6},{6,4},{1,3},{3,1},{5,7},{7,5},{8,10},{10,8},{12,... | collective-permute-start | bytes 835592 | tf_op jit(solution)/shard_map/ppermute | solution.py:541
  116.4 12.2 %collective-permute-start.34 = (f32[128,512]{1,0:T(8,128)S(1)}, f32[128,512]{1,0:T(8,128)S(1)}, u32[]{:S(2)}, u32[]{:S(2)}) collective-permute-start(f32[128,512]{1,0:T(8,128)S(1)} %get-tuple-element.173.refs_2_), channel_id=1, source_target_pairs={{0,2},{2,0},{4,6},{6,4},{1,3},{3,1},{5,7},{7,5},{8,10},{10,8},{12,... | collective-permute-start | bytes 786440 | tf_op jit(solution)/shard_map/ppermute | solution.py:541
  121.2 8.1 %collective-permute-start.35 = (f32[128,512]{1,0:T(8,128)S(1)}, f32[128,512]{1,0:T(8,128)S(1)}, u32[]{:S(2)}, u32[]{:S(2)}) collective-permute-start(f32[128,512]{1,0:T(8,128)S(1)} %shard_map.195.refs_4_.refs_0_), channel_id=1, source_target_pairs={{0,0},{2,4},{4,2},{6,6},{1,1},{3,5},{5,3},{7,7},{8,8},{10,12},{12,... | collective-permute-start | bytes 786440 | tf_op jit(solution)/shard_map/ppermute | solution.py:544
  122.0 12.6 %collective-permute-start.33 = (f32[128,512]{1,0:T(8,128)S(1)}, f32[128,512]{1,0:T(8,128)S(1)}, u32[]{:S(2)}, u32[]{:S(2)}) collective-permute-start(f32[128,512]{1,0:T(8,128)S(1)} %get-tuple-element.174.refs_5_), channel_id=1, source_target_pairs={{0,2},{2,0},{4,6},{6,4},{1,3},{3,1},{5,7},{7,5},{8,10},{10,8},{12,... | collective-permute-start | bytes 786440 | tf_op jit(solution)/shard_map/ppermute | solution.py:541
  129.4 12.0 %collective-permute-start.37 = (f32[128,512]{1,0:T(8,128)S(1)}, f32[128,512]{1,0:T(8,128)S(1)}, u32[]{:S(2)}, u32[]{:S(2)}) collective-permute-start(f32[128,512]{1,0:T(8,128)S(1)} %shard_map.199.refs_7_.refs_3_), channel_id=1, source_target_pairs={{0,2},{2,0},{4,6},{6,4},{1,3},{3,1},{5,7},{7,5},{8,10},{10,8},{12,... | collective-permute-start | bytes 786440 | tf_op jit(solution)/shard_map/ppermute | solution.py:541
  135.3 11.7 %collective-permute-start.40 = (f32[128,512]{1,0:T(8,128)S(1)}, f32[128,512]{1,0:T(8,128)S(1)}, u32[]{:S(2)}, u32[]{:S(2)}) collective-permute-start(f32[128,512]{1,0:T(8,128)S(1)} %shard_map.202.refs_7_.refs_3_), channel_id=1, source_target_pairs={{0,2},{2,0},{4,6},{6,4},{1,3},{3,1},{5,7},{7,5},{8,10},{10,8},{12,... | collective-permute-start | bytes 786440 | tf_op jit(solution)/shard_map/ppermute | solution.py:541
  141.8 8.1 %collective-permute-start.39 = (f32[128,512]{1,0:T(8,128)S(1)}, f32[128,512]{1,0:T(8,128)S(1)}, u32[]{:S(2)}, u32[]{:S(2)}) collective-permute-start(f32[128,512]{1,0:T(8,128)S(1)} %shard_map.205.refs_7_.refs_3_), channel_id=1, source_target_pairs={{0,2},{2,0},{4,6},{6,4},{1,3},{3,1},{5,7},{7,5},{8,10},{10,8},{12,... | collective-permute-start | bytes 786440 | tf_op jit(solution)/shard_map/ppermute | solution.py:541
  164.5 9.6 %collective-permute-start.46 = (f32[136,512]{1,0:T(8,128)S(1)}, f32[136,512]{1,0:T(8,128)S(1)}, u32[]{:S(2)}, u32[]{:S(2)}) collective-permute-start(f32[136,512]{1,0:T(8,128)S(1)} %shard_map.210.refs_3_.refs_0_), channel_id=1, source_target_pairs={{0,2},{2,0},{4,6},{6,4},{1,3},{3,1},{5,7},{7,5},{8,10},{10,8},{12,... | collective-permute-start | bytes 835592 | tf_op jit(solution)/shard_map/ppermute | solution.py:541
  167.7 12.1 %collective-permute-start.48 = (f32[128,512]{1,0:T(8,128)S(1)}, f32[128,512]{1,0:T(8,128)S(1)}, u32[]{:S(2)}, u32[]{:S(2)}) collective-permute-start(f32[128,512]{1,0:T(8,128)S(1)} %shard_map.215.refs_2_.refs_0_), channel_id=1, source_target_pairs={{0,2},{2,0},{4,6},{6,4},{1,3},{3,1},{5,7},{7,5},{8,10},{10,8},{12,... | collective-permute-start | bytes 786440 | tf_op jit(solution)/shard_map/ppermute | solution.py:541
  174.8 10.7 %collective-permute-start.45 = (f32[128,512]{1,0:T(8,128)S(1)}, f32[128,512]{1,0:T(8,128)S(1)}, u32[]{:S(2)}, u32[]{:S(2)}) collective-permute-start(f32[128,512]{1,0:T(8,128)S(1)} %shard_map.211.refs_3_.refs_0_), channel_id=1, source_target_pairs={{0,2},{2,0},{4,6},{6,4},{1,3},{3,1},{5,7},{7,5},{8,10},{10,8},{12,... | collective-permute-start | bytes 786440 | tf_op jit(solution)/shard_map/ppermute | solution.py:541
  180.6 10.6 %collective-permute-start.50 = (f32[136,512]{1,0:T(8,128)S(1)}, f32[136,512]{1,0:T(8,128)S(1)}, u32[]{:S(2)}, u32[]{:S(2)}) collective-permute-start(f32[136,512]{1,0:T(8,128)S(1)} %get-tuple-element.193.refs_2_), channel_id=1, source_target_pairs={{0,2},{2,0},{4,6},{6,4},{1,3},{3,1},{5,7},{7,5},{8,10},{10,8},{12,... | collective-permute-start | bytes 835592 | tf_op jit(solution)/shard_map/ppermute | solution.py:541
  186.3 12.2 %collective-permute-start.53 = (f32[128,512]{1,0:T(8,128)S(1)}, f32[128,512]{1,0:T(8,128)S(1)}, u32[]{:S(2)}, u32[]{:S(2)}) collective-permute-start(f32[128,512]{1,0:T(8,128)S(1)} %get-tuple-element.194.refs_2_), channel_id=1, source_target_pairs={{0,2},{2,0},{4,6},{6,4},{1,3},{3,1},{5,7},{7,5},{8,10},{10,8},{12,... | collective-permute-start | bytes 786440 | tf_op jit(solution)/shard_map/ppermute | solution.py:541
  191.2 8.0 %collective-permute-start.54 = (f32[128,512]{1,0:T(8,128)S(1)}, f32[128,512]{1,0:T(8,128)S(1)}, u32[]{:S(2)}, u32[]{:S(2)}) collective-permute-start(f32[128,512]{1,0:T(8,128)S(1)} %shard_map.221.refs_4_.refs_0_), channel_id=1, source_target_pairs={{0,0},{2,4},{4,2},{6,6},{1,1},{3,5},{5,3},{7,7},{8,8},{10,12},{12,... | collective-permute-start | bytes 786440 | tf_op jit(solution)/shard_map/ppermute | solution.py:544
  192.0 12.5 %collective-permute-start.52 = (f32[128,512]{1,0:T(8,128)S(1)}, f32[128,512]{1,0:T(8,128)S(1)}, u32[]{:S(2)}, u32[]{:S(2)}) collective-permute-start(f32[128,512]{1,0:T(8,128)S(1)} %get-tuple-element.195.refs_5_), channel_id=1, source_target_pairs={{0,2},{2,0},{4,6},{6,4},{1,3},{3,1},{5,7},{7,5},{8,10},{10,8},{12,... | collective-permute-start | bytes 786440 | tf_op jit(solution)/shard_map/ppermute | solution.py:541
  199.3 12.2 %collective-permute-start.56 = (f32[128,512]{1,0:T(8,128)S(1)}, f32[128,512]{1,0:T(8,128)S(1)}, u32[]{:S(2)}, u32[]{:S(2)}) collective-permute-start(f32[128,512]{1,0:T(8,128)S(1)} %shard_map.225.refs_7_.refs_3_), channel_id=1, source_target_pairs={{0,2},{2,0},{4,6},{6,4},{1,3},{3,1},{5,7},{7,5},{8,10},{10,8},{12,... | collective-permute-start | bytes 786440 | tf_op jit(solution)/shard_map/ppermute | solution.py:541
  204.6 7.3 %collective-permute-start.55 = (f32[128,512]{1,0:T(8,128)S(1)}, f32[128,512]{1,0:T(8,128)S(1)}, u32[]{:S(2)}, u32[]{:S(2)}) collective-permute-start(f32[128,512]{1,0:T(8,128)S(1)} %shard_map.227.refs_2_.refs_0_), channel_id=1, source_target_pairs={{0,0},{2,4},{4,2},{6,6},{1,1},{3,5},{5,3},{7,7},{8,8},{10,12},{12,... | collective-permute-start | bytes 786440 | tf_op jit(solution)/shard_map/ppermute | solution.py:544
  205.5 11.5 %collective-permute-start.59 = (f32[128,512]{1,0:T(8,128)S(1)}, f32[128,512]{1,0:T(8,128)S(1)}, u32[]{:S(2)}, u32[]{:S(2)}) collective-permute-start(f32[128,512]{1,0:T(8,128)S(1)} %shard_map.228.refs_7_.refs_3_), channel_id=1, source_target_pairs={{0,2},{2,0},{4,6},{6,4},{1,3},{3,1},{5,7},{7,5},{8,10},{10,8},{12,... | collective-permute-start | bytes 786440 | tf_op jit(solution)/shard_map/ppermute | solution.py:541
  211.9 7.9 %collective-permute-start.58 = (f32[128,512]{1,0:T(8,128)S(1)}, f32[128,512]{1,0:T(8,128)S(1)}, u32[]{:S(2)}, u32[]{:S(2)}) collective-permute-start(f32[128,512]{1,0:T(8,128)S(1)} %shard_map.231.refs_7_.refs_3_), channel_id=1, source_target_pairs={{0,2},{2,0},{4,6},{6,4},{1,3},{3,1},{5,7},{7,5},{8,10},{10,8},{12,... | collective-permute-start | bytes 786440 | tf_op jit(solution)/shard_map/ppermute | solution.py:541
  234.5 9.6 %collective-permute-start.65 = (f32[136,512]{1,0:T(8,128)S(1)}, f32[136,512]{1,0:T(8,128)S(1)}, u32[]{:S(2)}, u32[]{:S(2)}) collective-permute-start(f32[136,512]{1,0:T(8,128)S(1)} %shard_map.236.refs_3_.refs_0_), channel_id=1, source_target_pairs={{0,2},{2,0},{4,6},{6,4},{1,3},{3,1},{5,7},{7,5},{8,10},{10,8},{12,... | collective-permute-start | bytes 835592 | tf_op jit(solution)/shard_map/ppermute | solution.py:541
  237.7 12.1 %collective-permute-start.67 = (f32[128,512]{1,0:T(8,128)S(1)}, f32[128,512]{1,0:T(8,128)S(1)}, u32[]{:S(2)}, u32[]{:S(2)}) collective-permute-start(f32[128,512]{1,0:T(8,128)S(1)} %shard_map.241.refs_2_.refs_0_), channel_id=1, source_target_pairs={{0,2},{2,0},{4,6},{6,4},{1,3},{3,1},{5,7},{7,5},{8,10},{10,8},{12,... | collective-permute-start | bytes 786440 | tf_op jit(solution)/shard_map/ppermute | solution.py:541
  244.8 10.8 %collective-permute-start.64 = (f32[128,512]{1,0:T(8,128)S(1)}, f32[128,512]{1,0:T(8,128)S(1)}, u32[]{:S(2)}, u32[]{:S(2)}) collective-permute-start(f32[128,512]{1,0:T(8,128)S(1)} %shard_map.237.refs_3_.refs_0_), channel_id=1, source_target_pairs={{0,2},{2,0},{4,6},{6,4},{1,3},{3,1},{5,7},{7,5},{8,10},{10,8},{12,... | collective-permute-start | bytes 786440 | tf_op jit(solution)/shard_map/ppermute | solution.py:541
  250.6 10.6 %collective-permute-start.69 = (f32[136,512]{1,0:T(8,128)S(1)}, f32[136,512]{1,0:T(8,128)S(1)}, u32[]{:S(2)}, u32[]{:S(2)}) collective-permute-start(f32[136,512]{1,0:T(8,128)S(1)} %get-tuple-element.218.refs_2_), channel_id=1, source_target_pairs={{0,2},{2,0},{4,6},{6,4},{1,3},{3,1},{5,7},{7,5},{8,10},{10,8},{12,... | collective-permute-start | bytes 835592 | tf_op jit(solution)/shard_map/ppermute | solution.py:541
  256.3 12.2 %collective-permute-start.72 = (f32[128,512]{1,0:T(8,128)S(1)}, f32[128,512]{1,0:T(8,128)S(1)}, u32[]{:S(2)}, u32[]{:S(2)}) collective-permute-start(f32[128,512]{1,0:T(8,128)S(1)} %get-tuple-element.219.refs_2_), channel_id=1, source_target_pairs={{0,2},{2,0},{4,6},{6,4},{1,3},{3,1},{5,7},{7,5},{8,10},{10,8},{12,... | collective-permute-start | bytes 786440 | tf_op jit(solution)/shard_map/ppermute | solution.py:541
  261.3 8.0 %collective-permute-start.73 = (f32[128,512]{1,0:T(8,128)S(1)}, f32[128,512]{1,0:T(8,128)S(1)}, u32[]{:S(2)}, u32[]{:S(2)}) collective-permute-start(f32[128,512]{1,0:T(8,128)S(1)} %shard_map.247.refs_4_.refs_0_), channel_id=1, source_target_pairs={{0,0},{2,4},{4,2},{6,6},{1,1},{3,5},{5,3},{7,7},{8,8},{10,12},{12,... | collective-permute-start | bytes 786440 | tf_op jit(solution)/shard_map/ppermute | solution.py:544
  262.0 12.5 %collective-permute-start.71 = (f32[128,512]{1,0:T(8,128)S(1)}, f32[128,512]{1,0:T(8,128)S(1)}, u32[]{:S(2)}, u32[]{:S(2)}) collective-permute-start(f32[128,512]{1,0:T(8,128)S(1)} %get-tuple-element.220.refs_5_), channel_id=1, source_target_pairs={{0,2},{2,0},{4,6},{6,4},{1,3},{3,1},{5,7},{7,5},{8,10},{10,8},{12,... | collective-permute-start | bytes 786440 | tf_op jit(solution)/shard_map/ppermute | solution.py:541
  269.3 12.0 %collective-permute-start.75 = (f32[128,512]{1,0:T(8,128)S(1)}, f32[128,512]{1,0:T(8,128)S(1)}, u32[]{:S(2)}, u32[]{:S(2)}) collective-permute-start(f32[128,512]{1,0:T(8,128)S(1)} %shard_map.251.refs_7_.refs_3_), channel_id=1, source_target_pairs={{0,2},{2,0},{4,6},{6,4},{1,3},{3,1},{5,7},{7,5},{8,10},{10,8},{12,... | collective-permute-start | bytes 786440 | tf_op jit(solution)/shard_map/ppermute | solution.py:541
  275.3 11.7 %collective-permute-start.78 = (f32[128,512]{1,0:T(8,128)S(1)}, f32[128,512]{1,0:T(8,128)S(1)}, u32[]{:S(2)}, u32[]{:S(2)}) collective-permute-start(f32[128,512]{1,0:T(8,128)S(1)} %shard_map.254.refs_7_.refs_3_), channel_id=1, source_target_pairs={{0,2},{2,0},{4,6},{6,4},{1,3},{3,1},{5,7},{7,5},{8,10},{10,8},{12,... | collective-permute-start | bytes 786440 | tf_op jit(solution)/shard_map/ppermute | solution.py:541
  281.7 8.1 %collective-permute-start.77 = (f32[128,512]{1,0:T(8,128)S(1)}, f32[128,512]{1,0:T(8,128)S(1)}, u32[]{:S(2)}, u32[]{:S(2)}) collective-permute-start(f32[128,512]{1,0:T(8,128)S(1)} %shard_map.257.refs_7_.refs_3_), channel_id=1, source_target_pairs={{0,2},{2,0},{4,6},{6,4},{1,3},{3,1},{5,7},{7,5},{8,10},{10,8},{12,... | collective-permute-start | bytes 786440 | tf_op jit(solution)/shard_map/ppermute | solution.py:541
  (62 other events, 302.8 us)
where the time goes:
time: 304 us; the launch traced here: 303 us
  starting transfers between devices  173 us (57%)
  waiting for transfers between devices  71.8 us (24%)
  Pallas kernels  50 us (16%)
  local copies, waits for them, and re-layouts  5.26 us (2%)
    ppermute x36, starting transfers between devices, outer_swap(): return lax.ppermute(part, 'chip', [(0, 1), (1, 0), (2, 3), (3, 2)])  140 us
    ppermute x36, waiting for transfers between devices, outer_swap(): return lax.ppermute(part, 'chip', [(0, 1), (1, 0), (2, 3), (3, 2)])  38.6 us
    pallas_call x96, Pallas kernels, call(): pl.pallas_call(body, in_specs=[SMEM] * len(scalars) + [VMEM] * len(ins) +...  29.4 us
    ppermute x24, starting transfers between devices, inner_swap(): return lax.ppermute(part, 'chip', [(0, 0), (1, 2), (2, 1), (3, 3)])  18 us
    ppermute x14, waiting for transfers between devices, swap(): return lax.ppermute(part, 'core', [(0, 1), (1, 0)])  11.4 us
    ppermute x4, waiting for transfers between devices, data_terms(): lax.ppermute(part, 'dp', [(d, d ^ step) for d in range(n_dp)])  10.8 us
    ppermute x4, waiting for transfers between devices, data_terms(): part = part + lax.ppermute(part, 'dp', [(d, d ^ step) for d in range(n_dp)])  10.8 us
    pallas_call x1, Pallas kernels, project(): pl.pallas_call(project_kernel, in_specs=[SMEM] + [hbm] * 4 + [VMEM] * 6,...  8.78 us
  transfers between devices with their start and end apart: 82, of which 33 were waited for; matrix products, arithmetic and copies ran while one was open for 0% of the time, Pallas kernels for 12%

commit v1 on v0

--- a/solution.py
+++ b/solution.py
@@ -11,6 +11,7 @@
 HEAD_DIM = 128
 CG_STEPS = 3
 CHUNKS = 6
+LAG = 4
 DEPTH = 1024
 
 EPS = 1e-05
@@ -278,11 +279,19 @@
     return call(kernel, [first, second], [(first.shape, F32)], token)[0]
 
 
+def copy(part, token):
+    def kernel(part_ref, out_ref):
+        out_ref[...] = part_ref[...]
+
+    return call(kernel, [part], [(part.shape, F32)], token)[0]
+
+
 def add_and_pick(first, second, ends, outer, token):
+    rows = outer.shape[0]
+
     def kernel(ends_ref, first_ref, second_ref, outer_ref, sum_ref, sent_ref):
         total = first_ref[...] + second_ref[...]
         sum_ref[...] = total
-        rows = outer_ref.shape[0]
         sent_ref[:rows] = jnp.where(ends_ref[0] > 0, outer_ref[...], total[:rows])
         if total.shape[0] > rows:
             sent_ref[rows:] = total[rows:]
@@ -560,50 +569,52 @@
                 own_part[k] = spread(k, length, rows, got_rows, pairs[k], token)
             return own_part[k]
 
-        def finish(k, got):
+        def take_in(k, got):
+            nonlocal parts, scalars
             gap_part = gap[:, k * cols : (k + 1) * cols] if first else None
-            return gather(k, length, ends, got, total[k], pairs[k], parts, lengths, gap_part, token)
+            out = gather(k, length, ends, got, total[k], pairs[k], parts, lengths, gap_part, token)
+            parts = list(out[:2])
+            scalars = out[2] if k == 0 else scalars
+            return parts[0]
 
         if n_chip != 4:
             for k in range(CHUNKS):
                 token = begin(k)
             for k in range(CHUNKS):
                 total[k] = lax.psum(own_part[k], "chip")
-                out = finish(k, total[k])
-                parts, scalars = list(out[:2]), out[2] if k == 0 else scalars
+                token = take_in(k, total[k])
         else:
-            for k in [0, 1, 2] if first else [0, *range(2, CHUNKS), 1]:
+            for k in (0, 2, 1):
                 token = begin(k)
             for k in (0, 1):
                 outer[k] = outer_swap(own_part[k])
-            for tick in range(CHUNKS + 3):
+            for tick in range(CHUNKS + LAG):
+                if LAG <= tick != CHUNKS + 1:
+                    token = take_in(tick - LAG, outer[tick])
+                else:
+                    token = outer.get(tick, token)
                 if tick < CHUNKS:
-                    own_part[tick] = add(own_part[tick], outer[tick], token)
+                    later, back = tick + 2, tick - 2
+                    if back < 0:
+                        sent = copy(own_part[later], token)
+                    elif later < CHUNKS:
+                        total[back], sent = add_and_pick(
+                            own_part[back], inner[back], ends, own_part[later], token
+                        )
+                    else:
+                        sent = total[back] = add(own_part[back], inner[back], token)
+                    outer[later] = outer_swap(sent)
+                    own_part[tick] = add(own_part[tick], outer[tick], sent)
                     token = own_part[tick]
                     inner[tick] = inner_swap(token)
-                later = tick + 2
+                    if tick + 3 < CHUNKS:
+                        token = begin(tick + 3)
                 if tick == CHUNKS:
-                    out = finish(tick - 3, outer[tick])
-                    parts = list(out[:2])
-                    token = parts[0]
-                if 1 <= tick <= CHUNKS:
+                    token = take_in(tick + 1 - LAG, outer[tick + 1])
+                if tick in (CHUNKS - 1, CHUNKS):
                     k = tick - 1
-                    if later < CHUNKS:
-                        total[k], sent = add_and_pick(
-                            own_part[k], inner[k], ends, own_part[later], token
-                        )
-                    else:
-                        total[k] = sent = add(own_part[k], inner[k], token)
-                    token = sent
-                    outer[later] = outer_swap(sent)
-                elif tick == 0:
-                    outer[later] = outer_swap(own_part[later])
-                if tick + 3 < CHUNKS and first:
-                    token = begin(tick + 3)
-                if tick >= 3 and tick != CHUNKS:
-                    out = finish(tick - 3, outer[tick])
-                    parts, scalars = list(out[:2]), out[2] if tick == 3 else scalars
-                    token = parts[0]
+                    token = total[k] = add(own_part[k], inner[k], token)
+                    outer[k + LAG] = outer_swap(token)
         own, other = parts
         share = ADAPTER_SCALE / token_count
         part = cotangent(share, lengths, own, other, swap(other), attention)

time: 304 us -> 324 us (1.066)
  waiting for transfers between devices: 71.8 us -> 186 us
  starting transfers between devices: 173 us -> 75.9 us
  local copies, waits for them, and re-layouts: 5.26 us -> 9.99 us
  Pallas kernels: 50 us -> 46.7 us
    ppermute x36 -> x40, waiting for transfers between devices: 38.6 us -> 154 us  [outer_swap(): return lax.ppermute(part, 'chip', [(0, 1), (1, 0), (2, 3), (3, 2)])]
    ppermute x36 -> x40, starting transfers between devices: 140 us -> 44.7 us  [outer_swap(): return lax.ppermute(part, 'chip', [(0, 1), (1, 0), (2, 3), (3, 2)])]
    unnamed x56 -> x48, local copies, waits for them, and re-layouts: 5.14 us -> 9.87 us
    pallas_call x96 -> x104, Pallas kernels: 29.4 us -> 26.6 us  [call(): pl.pallas_call(body, in_specs=[SMEM] * len(scalars) + [VMEM] * len(ins) +...]
  transfers between devices with their start and end apart: 82 -> 86, of which waited for: 33 -> 51; matrix products, arithmetic and copies ran while one was open for 0% -> 0% of each run, Pallas kernels for 12% -> 10%
where the time goes in v1:
time: 324 us; the launch traced here: 323 us
  waiting for transfers between devices  186 us (57%)
  starting transfers between devices  75.9 us (23%)
  Pallas kernels  46.7 us (14%)
  local copies, waits for them, and re-layouts  9.99 us (3%)
    ppermute x40, waiting for transfers between devices, outer_swap(): return lax.ppermute(part, 'chip', [(0, 1), (1, 0), (2, 3), (3, 2)])  154 us
    ppermute x40, starting transfers between devices, outer_swap(): return lax.ppermute(part, 'chip', [(0, 1), (1, 0), (2, 3), (3, 2)])  44.7 us
    pallas_call x104, Pallas kernels, call(): pl.pallas_call(body, in_specs=[SMEM] * len(scalars) + [VMEM] * len(ins) +...  26.6 us
    ppermute x24, starting transfers between devices, inner_swap(): return lax.ppermute(part, 'chip', [(0, 0), (1, 2), (2, 1), (3, 3)])  16.7 us
    ppermute x4, waiting for transfers between devices, data_terms(): part = part + lax.ppermute(part, 'dp', [(d, d ^ step) for d in range(n_dp)])  11 us
    ppermute x4, waiting for transfers between devices, data_terms(): lax.ppermute(part, 'dp', [(d, d ^ step) for d in range(n_dp)])  10.8 us
    ppermute x14, waiting for transfers between devices, swap(): return lax.ppermute(part, 'core', [(0, 1), (1, 0)])  10.1 us
    unnamed x48, local copies, waits for them, and re-layouts  9.87 us
  transfers between devices with their start and end apart: 86, of which 51 were waited for; matrix products, arithmetic and copies ran while one was open for 0% of the time, Pallas kernels for 10%

profile of v1, /device:TPU:0, one launch (start us, length us, event | category | flops | bytes accessed | tf_op | source)
XLA Modules:
  0.0 322.8 jit_solution(9553390216210751879)
XLA Ops:
  3.0 2.7 shard_map.157
  10.7 8.1 %shard_map.156 = (f32[3,128,128]{2,1,0:T(8,128)S(1)}, bf16[128,384]{1,0:T(8,128)(2,1)S(1)}, bf16[128,384]{1,0:T(8,128)(2,1)S(1)}, f32[128,16]{1,0:T(8,128)S(1)},...) custom-call(s32[1]{0:T(128)S(6)} %copy.17.limit_ref.refs_1_.refs_2_.refs_4_.refs_8_, bf16[128,6144]{1,0:T(8,128)(2,1)S(1)} %copy-done.1, ...), custom_call_target="tpu_custom_call" | custom-call | flops 1811939328 | bytes 14155776 | tf_op jit(solution)/shard_map/pallas_call | solution.py:189
  24.8 3.0 collective-permute-start.4
  39.9 2.4 collective-permute-done.9.refs_1_
  55.7 3.8 %collective-permute-done.15.refs_2_.refs_1_ = f32[136,512]{1,0:T(8,128)S(1)} collective-permute-done((f32[136,512]{1,0:T(8,128)S(1)}, f32[136,512]{1,0:T(8,128)S(1)}, u32[]{:S(2)}, u32[]{:S(2)}) %collective-permute-start.15) | collective-permute-done | bytes 278560 | tf_op jit(solution)/shard_map/ppermute | solution.py:550
  61.3 3.8 %collective-permute-done.13.refs_2_.refs_1_ = f32[128,512]{1,0:T(8,128)S(1)} collective-permute-done((f32[128,512]{1,0:T(8,128)S(1)}, f32[128,512]{1,0:T(8,128)S(1)}, u32[]{:S(2)}, u32[]{:S(2)}) %collective-permute-start.13) | collective-permute-done | bytes 262176 | tf_op jit(solution)/shard_map/ppermute | solution.py:550
  67.5 4.6 %collective-permute-start.22 = (f32[128,512]{1,0:T(8,128)S(1)}, f32[128,512]{1,0:T(8,128)S(1)}, u32[]{:S(2)}, u32[]{:S(2)}) collective-permute-start(f32[128,512]{1,0:T(8,128)S(1)} %shard_map.178.refs_8_.refs_3_), channel_id=1, source_target_pairs={{0,2},{2,0},{4,6},{6,4},{1,3},{3,1},{5,7},{7,5},{8,10},{10,8},{12,... | collective-permute-start | bytes 786440 | tf_op jit(solution)/shard_map/ppermute | solution.py:550
  72.5 3.9 %collective-permute-done.18.refs_2_.refs_8_ = f32[128,512]{1,0:T(8,128)S(1)} collective-permute-done((f32[128,512]{1,0:T(8,128)S(1)}, f32[128,512]{1,0:T(8,128)S(1)}, u32[]{:S(2)}, u32[]{:S(2)}) %collective-permute-start.18) | collective-permute-done | bytes 262176 | tf_op jit(solution)/shard_map/ppermute | solution.py:550
  77.4 4.6 %collective-permute-done.22.refs_2_ = f32[128,512]{1,0:T(8,128)S(1)} collective-permute-done((f32[128,512]{1,0:T(8,128)S(1)}, f32[128,512]{1,0:T(8,128)S(1)}, u32[]{:S(2)}, u32[]{:S(2)}) %collective-permute-start.22) | collective-permute-done | bytes 262176 | tf_op jit(solution)/shard_map/ppermute | solution.py:550
  82.4 4.8 %collective-permute-done.21.refs_2_ = f32[128,512]{1,0:T(8,128)S(1)} collective-permute-done((f32[128,512]{1,0:T(8,128)S(1)}, f32[128,512]{1,0:T(8,128)S(1)}, u32[]{:S(2)}, u32[]{:S(2)}) %collective-permute-start.21) | collective-permute-done | bytes 262176 | tf_op jit(solution)/shard_map/ppermute | solution.py:550
  92.2 2.7 collective-permute-done.24
  96.5 2.7 collective-permute-done.25.refs_1_
  104.5 6.8 %collective-permute-done.27.refs_1_ = f32[136,512]{1,0:T(8,128)S(1)} collective-permute-done((f32[136,512]{1,0:T(8,128)S(1)}, f32[136,512]{1,0:T(8,128)S(1)}, u32[]{:S(2)}, u32[]{:S(2)}) %collective-permute-start.27) | collective-permute-done | bytes 278560 | tf_op jit(solution)/shard_map/ppermute | solution.py:550
  112.7 4.2 %collective-permute-done.30.refs_1_ = f32[128,512]{1,0:T(8,128)S(1)} collective-permute-done((f32[128,512]{1,0:T(8,128)S(1)}, f32[128,512]{1,0:T(8,128)S(1)}, u32[]{:S(2)}, u32[]{:S(2)}) %collective-permute-start.30) | collective-permute-done | bytes 262176 | tf_op jit(solution)/shard_map/ppermute | solution.py:550
  118.3 4.2 %collective-permute-done.28.refs_4_.refs_1_ = f32[128,512]{1,0:T(8,128)S(1)} collective-permute-done((f32[128,512]{1,0:T(8,128)S(1)}, f32[128,512]{1,0:T(8,128)S(1)}, u32[]{:S(2)}, u32[]{:S(2)}) %collective-permute-start.28) | collective-permute-done | bytes 262176 | tf_op jit(solution)/shard_map/ppermute | solution.py:550
  124.0 4.1 %collective-permute-done.32.refs_4_.refs_1_ = f32[128,512]{1,0:T(8,128)S(1)} collective-permute-done((f32[128,512]{1,0:T(8,128)S(1)}, f32[128,512]{1,0:T(8,128)S(1)}, u32[]{:S(2)}, u32[]{:S(2)}) %collective-permute-start.32) | collective-permute-done | bytes 262176 | tf_op jit(solution)/shard_map/ppermute | solution.py:550
  129.4 4.8 %collective-permute-done.35.refs_2_.refs_1_ = f32[136,512]{1,0:T(8,128)S(1)} collective-permute-done((f32[136,512]{1,0:T(8,128)S(1)}, f32[136,512]{1,0:T(8,128)S(1)}, u32[]{:S(2)}, u32[]{:S(2)}) %collective-permute-start.35) | collective-permute-done | bytes 278560 | tf_op jit(solution)/shard_map/ppermute | solution.py:550
  135.6 4.1 %collective-permute-done.33.refs_2_.refs_1_ = f32[128,512]{1,0:T(8,128)S(1)} collective-permute-done((f32[128,512]{1,0:T(8,128)S(1)}, f32[128,512]{1,0:T(8,128)S(1)}, u32[]{:S(2)}, u32[]{:S(2)}) %collective-permute-start.33) | collective-permute-done | bytes 262176 | tf_op jit(solution)/shard_map/ppermute | solution.py:550
  141.5 4.4 %collective-permute-start.42 = (f32[128,512]{1,0:T(8,128)S(1)}, f32[128,512]{1,0:T(8,128)S(1)}, u32[]{:S(2)}, u32[]{:S(2)}) collective-permute-start(f32[128,512]{1,0:T(8,128)S(1)} %shard_map.206.refs_7_.refs_3_), channel_id=1, source_target_pairs={{0,2},{2,0},{4,6},{6,4},{1,3},{3,1},{5,7},{7,5},{8,10},{10,8},{12,... | collective-permute-start | bytes 786440 | tf_op jit(solution)/shard_map/ppermute | solution.py:550
  146.3 4.7 %collective-permute-done.38.refs_2_.refs_7_ = f32[128,512]{1,0:T(8,128)S(1)} collective-permute-done((f32[128,512]{1,0:T(8,128)S(1)}, f32[128,512]{1,0:T(8,128)S(1)}, u32[]{:S(2)}, u32[]{:S(2)}) %collective-permute-start.38) | collective-permute-done | bytes 262176 | tf_op jit(solution)/shard_map/ppermute | solution.py:550
  151.8 4.8 %collective-permute-done.42.refs_2_ = f32[128,512]{1,0:T(8,128)S(1)} collective-permute-done((f32[128,512]{1,0:T(8,128)S(1)}, f32[128,512]{1,0:T(8,128)S(1)}, u32[]{:S(2)}, u32[]{:S(2)}) %collective-permute-start.42) | collective-permute-done | bytes 262176 | tf_op jit(solution)/shard_map/ppermute | solution.py:550
  157.0 4.4 %collective-permute-done.41.refs_2_ = f32[128,512]{1,0:T(8,128)S(1)} collective-permute-done((f32[128,512]{1,0:T(8,128)S(1)}, f32[128,512]{1,0:T(8,128)S(1)}, u32[]{:S(2)}, u32[]{:S(2)}) %collective-permute-start.41) | collective-permute-done | bytes 262176 | tf_op jit(solution)/shard_map/ppermute | solution.py:550
  166.4 2.7 collective-permute-done.44
  170.7 2.7 collective-permute-done.45.refs_1_
  178.7 6.9 %collective-permute-done.47.refs_1_ = f32[136,512]{1,0:T(8,128)S(1)} collective-permute-done((f32[136,512]{1,0:T(8,128)S(1)}, f32[136,512]{1,0:T(8,128)S(1)}, u32[]{:S(2)}, u32[]{:S(2)}) %collective-permute-start.47) | collective-permute-done | bytes 278560 | tf_op jit(solution)/shard_map/ppermute | solution.py:550
  187.0 4.2 %collective-permute-done.50.refs_1_ = f32[128,512]{1,0:T(8,128)S(1)} collective-permute-done((f32[128,512]{1,0:T(8,128)S(1)}, f32[128,512]{1,0:T(8,128)S(1)}, u32[]{:S(2)}, u32[]{:S(2)}) %collective-permute-start.50) | collective-permute-done | bytes 262176 | tf_op jit(solution)/shard_map/ppermute | solution.py:550
  192.6 4.2 %collective-permute-done.48.refs_4_.refs_1_ = f32[128,512]{1,0:T(8,128)S(1)} collective-permute-done((f32[128,512]{1,0:T(8,128)S(1)}, f32[128,512]{1,0:T(8,128)S(1)}, u32[]{:S(2)}, u32[]{:S(2)}) %collective-permute-start.48) | collective-permute-done | bytes 262176 | tf_op jit(solution)/shard_map/ppermute | solution.py:550
  198.3 4.1 %collective-permute-done.52.refs_4_.refs_1_ = f32[128,512]{1,0:T(8,128)S(1)} collective-permute-done((f32[128,512]{1,0:T(8,128)S(1)}, f32[128,512]{1,0:T(8,128)S(1)}, u32[]{:S(2)}, u32[]{:S(2)}) %collective-permute-start.52) | collective-permute-done | bytes 262176 | tf_op jit(solution)/shard_map/ppermute | solution.py:550
  203.7 4.7 %collective-permute-done.55.refs_2_.refs_1_ = f32[136,512]{1,0:T(8,128)S(1)} collective-permute-done((f32[136,512]{1,0:T(8,128)S(1)}, f32[136,512]{1,0:T(8,128)S(1)}, u32[]{:S(2)}, u32[]{:S(2)}) %collective-permute-start.55) | collective-permute-done | bytes 278560 | tf_op jit(solution)/shard_map/ppermute | solution.py:550
  209.9 4.1 %collective-permute-done.53.refs_2_.refs_1_ = f32[128,512]{1,0:T(8,128)S(1)} collective-permute-done((f32[128,512]{1,0:T(8,128)S(1)}, f32[128,512]{1,0:T(8,128)S(1)}, u32[]{:S(2)}, u32[]{:S(2)}) %collective-permute-start.53) | collective-permute-done | bytes 262176 | tf_op jit(solution)/shard_map/ppermute | solution.py:550
  216.0 4.4 %collective-permute-start.62 = (f32[128,512]{1,0:T(8,128)S(1)}, f32[128,512]{1,0:T(8,128)S(1)}, u32[]{:S(2)}, u32[]{:S(2)}) collective-permute-start(f32[128,512]{1,0:T(8,128)S(1)} %shard_map.234.refs_7_.refs_3_), channel_id=1, source_target_pairs={{0,2},{2,0},{4,6},{6,4},{1,3},{3,1},{5,7},{7,5},{8,10},{10,8},{12,... | collective-permute-start | bytes 786440 | tf_op jit(solution)/shard_map/ppermute | solution.py:550
  220.8 4.4 %collective-permute-done.58.refs_2_.refs_7_ = f32[128,512]{1,0:T(8,128)S(1)} collective-permute-done((f32[128,512]{1,0:T(8,128)S(1)}, f32[128,512]{1,0:T(8,128)S(1)}, u32[]{:S(2)}, u32[]{:S(2)}) %collective-permute-start.58) | collective-permute-done | bytes 262176 | tf_op jit(solution)/shard_map/ppermute | solution.py:550
  226.1 4.8 %collective-permute-done.62.refs_2_ = f32[128,512]{1,0:T(8,128)S(1)} collective-permute-done((f32[128,512]{1,0:T(8,128)S(1)}, f32[128,512]{1,0:T(8,128)S(1)}, u32[]{:S(2)}, u32[]{:S(2)}) %collective-permute-start.62) | collective-permute-done | bytes 262176 | tf_op jit(solution)/shard_map/ppermute | solution.py:550
  231.3 4.4 %collective-permute-done.61.refs_2_ = f32[128,512]{1,0:T(8,128)S(1)} collective-permute-done((f32[128,512]{1,0:T(8,128)S(1)}, f32[128,512]{1,0:T(8,128)S(1)}, u32[]{:S(2)}, u32[]{:S(2)}) %collective-permute-start.61) | collective-permute-done | bytes 262176 | tf_op jit(solution)/shard_map/ppermute | solution.py:550
  240.6 2.7 collective-permute-done.64
  245.0 2.7 collective-permute-done.65.refs_1_
  253.1 6.8 %collective-permute-done.67.refs_1_ = f32[136,512]{1,0:T(8,128)S(1)} collective-permute-done((f32[136,512]{1,0:T(8,128)S(1)}, f32[136,512]{1,0:T(8,128)S(1)}, u32[]{:S(2)}, u32[]{:S(2)}) %collective-permute-start.67) | collective-permute-done | bytes 278560 | tf_op jit(solution)/shard_map/ppermute | solution.py:550
  261.3 4.2 %collective-permute-done.70.refs_1_ = f32[128,512]{1,0:T(8,128)S(1)} collective-permute-done((f32[128,512]{1,0:T(8,128)S(1)}, f32[128,512]{1,0:T(8,128)S(1)}, u32[]{:S(2)}, u32[]{:S(2)}) %collective-permute-start.70) | collective-permute-done | bytes 262176 | tf_op jit(solution)/shard_map/ppermute | solution.py:550
  266.9 4.2 %collective-permute-done.68.refs_4_.refs_1_ = f32[128,512]{1,0:T(8,128)S(1)} collective-permute-done((f32[128,512]{1,0:T(8,128)S(1)}, f32[128,512]{1,0:T(8,128)S(1)}, u32[]{:S(2)}, u32[]{:S(2)}) %collective-permute-start.68) | collective-permute-done | bytes 262176 | tf_op jit(solution)/shard_map/ppermute | solution.py:550
  272.6 4.1 %collective-permute-done.72.refs_4_.refs_1_ = f32[128,512]{1,0:T(8,128)S(1)} collective-permute-done((f32[128,512]{1,0:T(8,128)S(1)}, f32[128,512]{1,0:T(8,128)S(1)}, u32[]{:S(2)}, u32[]{:S(2)}) %collective-permute-start.72) | collective-permute-done | bytes 262176 | tf_op jit(solution)/shard_map/ppermute | solution.py:550
  278.0 4.8 %collective-permute-done.75.refs_2_.refs_1_ = f32[136,512]{1,0:T(8,128)S(1)} collective-permute-done((f32[136,512]{1,0:T(8,128)S(1)}, f32[136,512]{1,0:T(8,128)S(1)}, u32[]{:S(2)}, u32[]{:S(2)}) %collective-permute-start.75) | collective-permute-done | bytes 278560 | tf_op jit(solution)/shard_map/ppermute | solution.py:550
  284.2 4.1 %collective-permute-done.73.refs_2_.refs_1_ = f32[128,512]{1,0:T(8,128)S(1)} collective-permute-done((f32[128,512]{1,0:T(8,128)S(1)}, f32[128,512]{1,0:T(8,128)S(1)}, u32[]{:S(2)}, u32[]{:S(2)}) %collective-permute-start.73) | collective-permute-done | bytes 262176 | tf_op jit(solution)/shard_map/ppermute | solution.py:550
  290.1 4.4 %collective-permute-start.82 = (f32[128,512]{1,0:T(8,128)S(1)}, f32[128,512]{1,0:T(8,128)S(1)}, u32[]{:S(2)}, u32[]{:S(2)}) collective-permute-start(f32[128,512]{1,0:T(8,128)S(1)} %shard_map.262.refs_7_.refs_3_), channel_id=1, source_target_pairs={{0,2},{2,0},{4,6},{6,4},{1,3},{3,1},{5,7},{7,5},{8,10},{10,8},{12,... | collective-permute-start | bytes 786440 | tf_op jit(solution)/shard_map/ppermute | solution.py:550
  294.9 4.7 %collective-permute-done.78.refs_2_.refs_7_ = f32[128,512]{1,0:T(8,128)S(1)} collective-permute-done((f32[128,512]{1,0:T(8,128)S(1)}, f32[128,512]{1,0:T(8,128)S(1)}, u32[]{:S(2)}, u32[]{:S(2)}) %collective-permute-start.78) | collective-permute-done | bytes 262176 | tf_op jit(solution)/shard_map/ppermute | solution.py:550
  300.4 4.8 %collective-permute-done.82.refs_2_ = f32[128,512]{1,0:T(8,128)S(1)} collective-permute-done((f32[128,512]{1,0:T(8,128)S(1)}, f32[128,512]{1,0:T(8,128)S(1)}, u32[]{:S(2)}, u32[]{:S(2)}) %collective-permute-start.82) | collective-permute-done | bytes 262176 | tf_op jit(solution)/shard_map/ppermute | solution.py:550
  305.6 4.4 %collective-permute-done.81.refs_2_ = f32[128,512]{1,0:T(8,128)S(1)} collective-permute-done((f32[128,512]{1,0:T(8,128)S(1)}, f32[128,512]{1,0:T(8,128)S(1)}, u32[]{:S(2)}, u32[]{:S(2)}) %collective-permute-start.81) | collective-permute-done | bytes 262176 | tf_op jit(solution)/shard_map/ppermute | solution.py:550
  315.0 2.7 collective-permute-done.84
  319.3 2.7 collective-permute-done.85.refs_1_
  (292 shorter events, 117.1 us)
Async XLA Ops:
  9.5 11.9 %collective-permute-start.3 = (f32[384,512]{1,0:T(8,128)}, f32[384,512]{1,0:T(8,128)}, u32[]{:S(2)}, u32[]{:S(2)}) collective-permute-start(f32[384,512]{1,0:T(8,128)} %get-tuple-element.121), channel_id=1, source_target_pairs={{0,1},{1,0},{2,3},{3,2},{4,5},{5,4},{6,7},{7,6},{8,9},{9,8},{10,11... | collective-permute-start | bytes 2359304 | tf_op jit(solution)/shard_map/ppermute | solution.py:525
  10.0 18.0 %collective-permute-start.2 = (f32[384,512]{1,0:T(8,128)}, f32[384,512]{1,0:T(8,128)}, u32[]{:S(2)}, u32[]{:S(2)}) collective-permute-start(f32[384,512]{1,0:T(8,128)} %get-tuple-element.119), channel_id=1, source_target_pairs={{0,1},{1,0},{2,3},{3,2},{4,5},{5,4},{6,7},{7,6},{8,9},{9,8},{10,11... | collective-permute-start | bytes 2359304 | tf_op jit(solution)/shard_map/ppermute | solution.py:525
  19.4 18.3 %collective-permute-start.10 = (f32[384,512]{1,0:T(8,128)}, f32[384,512]{1,0:T(8,128)}, u32[]{:S(2)}, u32[]{:S(2)}) collective-permute-start(f32[384,512]{1,0:T(8,128)} %get-tuple-element.130), channel_id=1, source_target_pairs={{0,1},{1,0},{2,3},{3,2},{4,5},{5,4},{6,7},{7,6},{8,9},{9,8},{10,11... | collective-permute-start | bytes 2359304 | tf_op jit(solution)/shard_map/ppermute | solution.py:525
  19.5 12.1 %collective-permute-start.8 = (f32[384,512]{1,0:T(8,128)}, f32[384,512]{1,0:T(8,128)}, u32[]{:S(2)}, u32[]{:S(2)}) collective-permute-start(f32[384,512]{1,0:T(8,128)} %get-tuple-element.127), channel_id=1, source_target_pairs={{0,1},{1,0},{2,3},{3,2},{4,5},{5,4},{6,7},{7,6},{8,9},{9,8},{10,11... | collective-permute-start | bytes 2359304 | tf_op jit(solution)/shard_map/ppermute | solution.py:525
  21.3 23.2 %collective-permute-start.7 = (f32[384,512]{1,0:T(8,128)}, f32[384,512]{1,0:T(8,128)}, u32[]{:S(2)}, u32[]{:S(2)}) collective-permute-start(f32[384,512]{1,0:T(8,128)} %get-tuple-element.125), channel_id=1, source_target_pairs={{0,1},{1,0},{2,3},{3,2},{4,5},{5,4},{6,7},{7,6},{8,9},{9,8},{10,11... | collective-permute-start | bytes 2359304 | tf_op jit(solution)/shard_map/ppermute | solution.py:525
  28.0 22.4 %collective-permute-start.1 = (f32[384,512]{1,0:T(8,128)S(1)}, f32[384,512]{1,0:T(8,128)S(1)}, u32[]{:S(2)}, u32[]{:S(2)}) collective-permute-start(f32[384,512]{1,0:T(8,128)S(1)} %get-tuple-element.117), channel_id=1, source_target_pairs={{0,1},{1,0},{2,3},{3,2},{4,5},{5,4},{6,7},{7,6},{8,9},{9,8},{10,11... | collective-permute-start | bytes 2359304 | tf_op jit(solution)/shard_map/ppermute | solution.py:525
  34.9 13.1 %collective-permute-start.5 = (f32[128,512]{1,0:T(8,128)S(1)}, f32[128,512]{1,0:T(8,128)S(1)}, u32[]{:S(2)}, u32[]{:S(2)}) collective-permute-start(f32[128,512]{1,0:T(8,128)S(1)} %shard_map.160.refs_2_), channel_id=1, source_target_pairs={{0,2},{2,0},{4,6},{6,4},{1,3},{3,1},{5,7},{7,5},{8,10},{10,8},{12,... | collective-permute-start | bytes 786440 | tf_op jit(solution)/shard_map/ppermute | solution.py:550
  42.3 11.2 %collective-permute-start.12 = (f32[128,512]{1,0:T(8,128)S(1)}, f32[128,512]{1,0:T(8,128)S(1)}, u32[]{:S(2)}, u32[]{:S(2)}) collective-permute-start(f32[128,512]{1,0:T(8,128)S(1)} %shard_map.164.refs_2_), channel_id=1, source_target_pairs={{0,2},{2,0},{4,6},{6,4},{1,3},{3,1},{5,7},{7,5},{8,10},{10,8},{12,... | collective-permute-start | bytes 786440 | tf_op jit(solution)/shard_map/ppermute | solution.py:550
  48.0 11.5 %collective-permute-start.15 = (f32[136,512]{1,0:T(8,128)S(1)}, f32[136,512]{1,0:T(8,128)S(1)}, u32[]{:S(2)}, u32[]{:S(2)}) collective-permute-start(f32[136,512]{1,0:T(8,128)S(1)} %get-tuple-element.133.refs_2_), channel_id=1, source_target_pairs={{0,2},{2,0},{4,6},{6,4},{1,3},{3,1},{5,7},{7,5},{8,10},{10,8},{12,... | collective-permute-start | bytes 835592 | tf_op jit(solution)/shard_map/ppermute | solution.py:550
  53.6 11.5 %collective-permute-start.13 = (f32[128,512]{1,0:T(8,128)S(1)}, f32[128,512]{1,0:T(8,128)S(1)}, u32[]{:S(2)}, u32[]{:S(2)}) collective-permute-start(f32[128,512]{1,0:T(8,128)S(1)} %get-tuple-element.135.refs_2_), channel_id=1, source_target_pairs={{0,2},{2,0},{4,6},{6,4},{1,3},{3,1},{5,7},{7,5},{8,10},{10,8},{12,... | collective-permute-start | bytes 786440 | tf_op jit(solution)/shard_map/ppermute | solution.py:550
  60.4 11.7 %collective-permute-start.19 = (f32[128,512]{1,0:T(8,128)S(1)}, f32[128,512]{1,0:T(8,128)S(1)}, u32[]{:S(2)}, u32[]{:S(2)}) collective-permute-start(f32[128,512]{1,0:T(8,128)S(1)} %shard_map.173.refs_2_.refs_3_), channel_id=1, source_target_pairs={{0,2},{2,0},{4,6},{6,4},{1,3},{3,1},{5,7},{7,5},{8,10},{10,8},{12,... | collective-permute-start | bytes 786440 | tf_op jit(solution)/shard_map/ppermute | solution.py:550
  65.6 10.8 %collective-permute-start.18 = (f32[128,512]{1,0:T(8,128)S(1)}, f32[128,512]{1,0:T(8,128)S(1)}, u32[]{:S(2)}, u32[]{:S(2)}) collective-permute-start(f32[128,512]{1,0:T(8,128)S(1)} %shard_map.176.refs_2_.refs_3_), channel_id=1, source_target_pairs={{0,2},{2,0},{4,6},{6,4},{1,3},{3,1},{5,7},{7,5},{8,10},{10,8},{12,... | collective-permute-start | bytes 786440 | tf_op jit(solution)/shard_map/ppermute | solution.py:550
  67.5 14.5 %collective-permute-start.22 = (f32[128,512]{1,0:T(8,128)S(1)}, f32[128,512]{1,0:T(8,128)S(1)}, u32[]{:S(2)}, u32[]{:S(2)}) collective-permute-start(f32[128,512]{1,0:T(8,128)S(1)} %shard_map.178.refs_8_.refs_3_), channel_id=1, source_target_pairs={{0,2},{2,0},{4,6},{6,4},{1,3},{3,1},{5,7},{7,5},{8,10},{10,8},{12,... | collective-permute-start | bytes 786440 | tf_op jit(solution)/shard_map/ppermute | solution.py:550
  102.7 14.3 %collective-permute-start.30 = (f32[128,512]{1,0:T(8,128)S(1)}, f32[128,512]{1,0:T(8,128)S(1)}, u32[]{:S(2)}, u32[]{:S(2)}) collective-permute-start(f32[128,512]{1,0:T(8,128)S(1)} %shard_map.190.refs_0_), channel_id=1, source_target_pairs={{0,2},{2,0},{4,6},{6,4},{1,3},{3,1},{5,7},{7,5},{8,10},{10,8},{12,... | collective-permute-start | bytes 786440 | tf_op jit(solution)/shard_map/ppermute | solution.py:550
  111.3 11.2 %collective-permute-start.28 = (f32[128,512]{1,0:T(8,128)S(1)}, f32[128,512]{1,0:T(8,128)S(1)}, u32[]{:S(2)}, u32[]{:S(2)}) collective-permute-start(f32[128,512]{1,0:T(8,128)S(1)} %shard_map.188.refs_2_), channel_id=1, source_target_pairs={{0,2},{2,0},{4,6},{6,4},{1,3},{3,1},{5,7},{7,5},{8,10},{10,8},{12,... | collective-permute-start | bytes 786440 | tf_op jit(solution)/shard_map/ppermute | solution.py:550
  111.7 10.8 %collective-permute-start.29 = (f32[136,512]{1,0:T(8,128)S(1)}, f32[136,512]{1,0:T(8,128)S(1)}, u32[]{:S(2)}, u32[]{:S(2)}) collective-permute-start(f32[136,512]{1,0:T(8,128)S(1)} %shard_map.189.refs_3_.refs_1_), channel_id=1, source_target_pairs={{0,0},{2,4},{4,2},{6,6},{1,1},{3,5},{5,3},{7,7},{8,8},{10,12},{12,... | collective-permute-start | bytes 835592 | tf_op jit(solution)/shard_map/ppermute | solution.py:553
  117.0 11.2 %collective-permute-start.32 = (f32[128,512]{1,0:T(8,128)S(1)}, f32[128,512]{1,0:T(8,128)S(1)}, u32[]{:S(2)}, u32[]{:S(2)}) collective-permute-start(f32[128,512]{1,0:T(8,128)S(1)} %shard_map.192.refs_2_), channel_id=1, source_target_pairs={{0,2},{2,0},{4,6},{6,4},{1,3},{3,1},{5,7},{7,5},{8,10},{10,8},{12,... | collective-permute-start | bytes 786440 | tf_op jit(solution)/shard_map/ppermute | solution.py:550
  122.6 11.5 %collective-permute-start.35 = (f32[136,512]{1,0:T(8,128)S(1)}, f32[136,512]{1,0:T(8,128)S(1)}, u32[]{:S(2)}, u32[]{:S(2)}) collective-permute-start(f32[136,512]{1,0:T(8,128)S(1)} %get-tuple-element.162.refs_2_), channel_id=1, source_target_pairs={{0,2},{2,0},{4,6},{6,4},{1,3},{3,1},{5,7},{7,5},{8,10},{10,8},{12,... | collective-permute-start | bytes 835592 | tf_op jit(solution)/shard_map/ppermute | solution.py:550
  123.0 11.5 %collective-permute-start.36 = (f32[128,512]{1,0:T(8,128)S(1)}, f32[128,512]{1,0:T(8,128)S(1)}, u32[]{:S(2)}, u32[]{:S(2)}) collective-permute-start(f32[128,512]{1,0:T(8,128)S(1)} %shard_map.196.refs_3_.refs_0_), channel_id=1, source_target_pairs={{0,0},{2,4},{4,2},{6,6},{1,1},{3,5},{5,3},{7,7},{8,8},{10,12},{12,... | collective-permute-start | bytes 786440 | tf_op jit(solution)/shard_map/ppermute | solution.py:553
  128.2 11.5 %collective-permute-start.33 = (f32[128,512]{1,0:T(8,128)S(1)}, f32[128,512]{1,0:T(8,128)S(1)}, u32[]{:S(2)}, u32[]{:S(2)}) collective-permute-start(f32[128,512]{1,0:T(8,128)S(1)} %get-tuple-element.163.refs_2_), channel_id=1, source_target_pairs={{0,2},{2,0},{4,6},{6,4},{1,3},{3,1},{5,7},{7,5},{8,10},{10,8},{12,... | collective-permute-start | bytes 786440 | tf_op jit(solution)/shard_map/ppermute | solution.py:550
  128.7 11.5 %collective-permute-start.34 = (f32[128,512]{1,0:T(8,128)S(1)}, f32[128,512]{1,0:T(8,128)S(1)}, u32[]{:S(2)}, u32[]{:S(2)}) collective-permute-start(f32[128,512]{1,0:T(8,128)S(1)} %shard_map.199.refs_5_.refs_0_), channel_id=1, source_target_pairs={{0,0},{2,4},{4,2},{6,6},{1,1},{3,5},{5,3},{7,7},{8,8},{10,12},{12,... | collective-permute-start | bytes 786440 | tf_op jit(solution)/shard_map/ppermute | solution.py:553
  134.6 11.4 %collective-permute-start.39 = (f32[128,512]{1,0:T(8,128)S(1)}, f32[128,512]{1,0:T(8,128)S(1)}, u32[]{:S(2)}, u32[]{:S(2)}) collective-permute-start(f32[128,512]{1,0:T(8,128)S(1)} %shard_map.201.refs_2_.refs_3_), channel_id=1, source_target_pairs={{0,2},{2,0},{4,6},{6,4},{1,3},{3,1},{5,7},{7,5},{8,10},{10,8},{12,... | collective-permute-start | bytes 786440 | tf_op jit(solution)/shard_map/ppermute | solution.py:550
  140.2 10.8 %collective-permute-start.38 = (f32[128,512]{1,0:T(8,128)S(1)}, f32[128,512]{1,0:T(8,128)S(1)}, u32[]{:S(2)}, u32[]{:S(2)}) collective-permute-start(f32[128,512]{1,0:T(8,128)S(1)} %shard_map.204.refs_2_.refs_3_), channel_id=1, source_target_pairs={{0,2},{2,0},{4,6},{6,4},{1,3},{3,1},{5,7},{7,5},{8,10},{10,8},{12,... | collective-permute-start | bytes 786440 | tf_op jit(solution)/shard_map/ppermute | solution.py:550
  140.8 10.6 %collective-permute-start.37 = (f32[128,512]{1,0:T(8,128)S(1)}, f32[128,512]{1,0:T(8,128)S(1)}, u32[]{:S(2)}, u32[]{:S(2)}) collective-permute-start(f32[128,512]{1,0:T(8,128)S(1)} %shard_map.205.refs_2_.refs_0_), channel_id=1, source_target_pairs={{0,0},{2,4},{4,2},{6,6},{1,1},{3,5},{5,3},{7,7},{8,8},{10,12},{12,... | collective-permute-start | bytes 786440 | tf_op jit(solution)/shard_map/ppermute | solution.py:553
  141.5 15.1 %collective-permute-start.42 = (f32[128,512]{1,0:T(8,128)S(1)}, f32[128,512]{1,0:T(8,128)S(1)}, u32[]{:S(2)}, u32[]{:S(2)}) collective-permute-start(f32[128,512]{1,0:T(8,128)S(1)} %shard_map.206.refs_7_.refs_3_), channel_id=1, source_target_pairs={{0,2},{2,0},{4,6},{6,4},{1,3},{3,1},{5,7},{7,5},{8,10},{10,8},{12,... | collective-permute-start | bytes 786440 | tf_op jit(solution)/shard_map/ppermute | solution.py:550
  176.9 14.3 %collective-permute-start.50 = (f32[128,512]{1,0:T(8,128)S(1)}, f32[128,512]{1,0:T(8,128)S(1)}, u32[]{:S(2)}, u32[]{:S(2)}) collective-permute-start(f32[128,512]{1,0:T(8,128)S(1)} %shard_map.218.refs_0_), channel_id=1, source_target_pairs={{0,2},{2,0},{4,6},{6,4},{1,3},{3,1},{5,7},{7,5},{8,10},{10,8},{12,... | collective-permute-start | bytes 786440 | tf_op jit(solution)/shard_map/ppermute | solution.py:550
  185.6 11.2 %collective-permute-start.48 = (f32[128,512]{1,0:T(8,128)S(1)}, f32[128,512]{1,0:T(8,128)S(1)}, u32[]{:S(2)}, u32[]{:S(2)}) collective-permute-start(f32[128,512]{1,0:T(8,128)S(1)} %shard_map.216.refs_2_), channel_id=1, source_target_pairs={{0,2},{2,0},{4,6},{6,4},{1,3},{3,1},{5,7},{7,5},{8,10},{10,8},{12,... | collective-permute-start | bytes 786440 | tf_op jit(solution)/shard_map/ppermute | solution.py:550
  186.0 10.8 %collective-permute-start.49 = (f32[136,512]{1,0:T(8,128)S(1)}, f32[136,512]{1,0:T(8,128)S(1)}, u32[]{:S(2)}, u32[]{:S(2)}) collective-permute-start(f32[136,512]{1,0:T(8,128)S(1)} %shard_map.217.refs_3_.refs_1_), channel_id=1, source_target_pairs={{0,0},{2,4},{4,2},{6,6},{1,1},{3,5},{5,3},{7,7},{8,8},{10,12},{12,... | collective-permute-start | bytes 835592 | tf_op jit(solution)/shard_map/ppermute | solution.py:553
  191.2 11.2 %collective-permute-start.52 = (f32[128,512]{1,0:T(8,128)S(1)}, f32[128,512]{1,0:T(8,128)S(1)}, u32[]{:S(2)}, u32[]{:S(2)}) collective-permute-start(f32[128,512]{1,0:T(8,128)S(1)} %shard_map.220.refs_2_), channel_id=1, source_target_pairs={{0,2},{2,0},{4,6},{6,4},{1,3},{3,1},{5,7},{7,5},{8,10},{10,8},{12,... | collective-permute-start | bytes 786440 | tf_op jit(solution)/shard_map/ppermute | solution.py:550
  196.9 11.5 %collective-permute-start.55 = (f32[136,512]{1,0:T(8,128)S(1)}, f32[136,512]{1,0:T(8,128)S(1)}, u32[]{:S(2)}, u32[]{:S(2)}) collective-permute-start(f32[136,512]{1,0:T(8,128)S(1)} %get-tuple-element.181.refs_2_), channel_id=1, source_target_pairs={{0,2},{2,0},{4,6},{6,4},{1,3},{3,1},{5,7},{7,5},{8,10},{10,8},{12,... | collective-permute-start | bytes 835592 | tf_op jit(solution)/shard_map/ppermute | solution.py:550
  197.3 11.5 %collective-permute-start.56 = (f32[128,512]{1,0:T(8,128)S(1)}, f32[128,512]{1,0:T(8,128)S(1)}, u32[]{:S(2)}, u32[]{:S(2)}) collective-permute-start(f32[128,512]{1,0:T(8,128)S(1)} %shard_map.224.refs_3_.refs_0_), channel_id=1, source_target_pairs={{0,0},{2,4},{4,2},{6,6},{1,1},{3,5},{5,3},{7,7},{8,8},{10,12},{12,... | collective-permute-start | bytes 786440 | tf_op jit(solution)/shard_map/ppermute | solution.py:553
  202.5 11.5 %collective-permute-start.53 = (f32[128,512]{1,0:T(8,128)S(1)}, f32[128,512]{1,0:T(8,128)S(1)}, u32[]{:S(2)}, u32[]{:S(2)}) collective-permute-start(f32[128,512]{1,0:T(8,128)S(1)} %get-tuple-element.182.refs_2_), channel_id=1, source_target_pairs={{0,2},{2,0},{4,6},{6,4},{1,3},{3,1},{5,7},{7,5},{8,10},{10,8},{12,... | collective-permute-start | bytes 786440 | tf_op jit(solution)/shard_map/ppermute | solution.py:550
  203.0 11.4 %collective-permute-start.54 = (f32[128,512]{1,0:T(8,128)S(1)}, f32[128,512]{1,0:T(8,128)S(1)}, u32[]{:S(2)}, u32[]{:S(2)}) collective-permute-start(f32[128,512]{1,0:T(8,128)S(1)} %shard_map.227.refs_5_.refs_0_), channel_id=1, source_target_pairs={{0,0},{2,4},{4,2},{6,6},{1,1},{3,5},{5,3},{7,7},{8,8},{10,12},{12,... | collective-permute-start | bytes 786440 | tf_op jit(solution)/shard_map/ppermute | solution.py:553
  208.8 11.6 %collective-permute-start.59 = (f32[128,512]{1,0:T(8,128)S(1)}, f32[128,512]{1,0:T(8,128)S(1)}, u32[]{:S(2)}, u32[]{:S(2)}) collective-permute-start(f32[128,512]{1,0:T(8,128)S(1)} %shard_map.229.refs_2_.refs_3_), channel_id=1, source_target_pairs={{0,2},{2,0},{4,6},{6,4},{1,3},{3,1},{5,7},{7,5},{8,10},{10,8},{12,... | collective-permute-start | bytes 786440 | tf_op jit(solution)/shard_map/ppermute | solution.py:550
  214.5 10.8 %collective-permute-start.58 = (f32[128,512]{1,0:T(8,128)S(1)}, f32[128,512]{1,0:T(8,128)S(1)}, u32[]{:S(2)}, u32[]{:S(2)}) collective-permute-start(f32[128,512]{1,0:T(8,128)S(1)} %shard_map.232.refs_2_.refs_3_), channel_id=1, source_target_pairs={{0,2},{2,0},{4,6},{6,4},{1,3},{3,1},{5,7},{7,5},{8,10},{10,8},{12,... | collective-permute-start | bytes 786440 | tf_op jit(solution)/shard_map/ppermute | solution.py:550
  215.0 10.6 %collective-permute-start.57 = (f32[128,512]{1,0:T(8,128)S(1)}, f32[128,512]{1,0:T(8,128)S(1)}, u32[]{:S(2)}, u32[]{:S(2)}) collective-permute-start(f32[128,512]{1,0:T(8,128)S(1)} %shard_map.233.refs_2_.refs_0_), channel_id=1, source_target_pairs={{0,0},{2,4},{4,2},{6,6},{1,1},{3,5},{5,3},{7,7},{8,8},{10,12},{12,... | collective-permute-start | bytes 786440 | tf_op jit(solution)/shard_map/ppermute | solution.py:553
  216.0 14.9 %collective-permute-start.62 = (f32[128,512]{1,0:T(8,128)S(1)}, f32[128,512]{1,0:T(8,128)S(1)}, u32[]{:S(2)}, u32[]{:S(2)}) collective-permute-start(f32[128,512]{1,0:T(8,128)S(1)} %shard_map.234.refs_7_.refs_3_), channel_id=1, source_target_pairs={{0,2},{2,0},{4,6},{6,4},{1,3},{3,1},{5,7},{7,5},{8,10},{10,8},{12,... | collective-permute-start | bytes 786440 | tf_op jit(solution)/shard_map/ppermute | solution.py:550
  251.3 14.3 %collective-permute-start.70 = (f32[128,512]{1,0:T(8,128)S(1)}, f32[128,512]{1,0:T(8,128)S(1)}, u32[]{:S(2)}, u32[]{:S(2)}) collective-permute-start(f32[128,512]{1,0:T(8,128)S(1)} %shard_map.246.refs_0_), channel_id=1, source_target_pairs={{0,2},{2,0},{4,6},{6,4},{1,3},{3,1},{5,7},{7,5},{8,10},{10,8},{12,... | collective-permute-start | bytes 786440 | tf_op jit(solution)/shard_map/ppermute | solution.py:550
  259.9 11.2 %collective-permute-start.68 = (f32[128,512]{1,0:T(8,128)S(1)}, f32[128,512]{1,0:T(8,128)S(1)}, u32[]{:S(2)}, u32[]{:S(2)}) collective-permute-start(f32[128,512]{1,0:T(8,128)S(1)} %shard_map.244.refs_2_), channel_id=1, source_target_pairs={{0,2},{2,0},{4,6},{6,4},{1,3},{3,1},{5,7},{7,5},{8,10},{10,8},{12,... | collective-permute-start | bytes 786440 | tf_op jit(solution)/shard_map/ppermute | solution.py:550
  260.3 10.8 %collective-permute-start.69 = (f32[136,512]{1,0:T(8,128)S(1)}, f32[136,512]{1,0:T(8,128)S(1)}, u32[]{:S(2)}, u32[]{:S(2)}) collective-permute-start(f32[136,512]{1,0:T(8,128)S(1)} %shard_map.245.refs_3_.refs_1_), channel_id=1, source_target_pairs={{0,0},{2,4},{4,2},{6,6},{1,1},{3,5},{5,3},{7,7},{8,8},{10,12},{12,... | collective-permute-start | bytes 835592 | tf_op jit(solution)/shard_map/ppermute | solution.py:553
  265.6 11.2 %collective-permute-start.72 = (f32[128,512]{1,0:T(8,128)S(1)}, f32[128,512]{1,0:T(8,128)S(1)}, u32[]{:S(2)}, u32[]{:S(2)}) collective-permute-start(f32[128,512]{1,0:T(8,128)S(1)} %shard_map.248.refs_2_), channel_id=1, source_target_pairs={{0,2},{2,0},{4,6},{6,4},{1,3},{3,1},{5,7},{7,5},{8,10},{10,8},{12,... | collective-permute-start | bytes 786440 | tf_op jit(solution)/shard_map/ppermute | solution.py:550
  271.2 11.5 %collective-permute-start.75 = (f32[136,512]{1,0:T(8,128)S(1)}, f32[136,512]{1,0:T(8,128)S(1)}, u32[]{:S(2)}, u32[]{:S(2)}) collective-permute-start(f32[136,512]{1,0:T(8,128)S(1)} %get-tuple-element.204.refs_2_), channel_id=1, source_target_pairs={{0,2},{2,0},{4,6},{6,4},{1,3},{3,1},{5,7},{7,5},{8,10},{10,8},{12,... | collective-permute-start | bytes 835592 | tf_op jit(solution)/shard_map/ppermute | solution.py:550
  271.6 11.5 %collective-permute-start.76 = (f32[128,512]{1,0:T(8,128)S(1)}, f32[128,512]{1,0:T(8,128)S(1)}, u32[]{:S(2)}, u32[]{:S(2)}) collective-permute-start(f32[128,512]{1,0:T(8,128)S(1)} %shard_map.252.refs_3_.refs_0_), channel_id=1, source_target_pairs={{0,0},{2,4},{4,2},{6,6},{1,1},{3,5},{5,3},{7,7},{8,8},{10,12},{12,... | collective-permute-start | bytes 786440 | tf_op jit(solution)/shard_map/ppermute | solution.py:553
  276.8 11.5 %collective-permute-start.73 = (f32[128,512]{1,0:T(8,128)S(1)}, f32[128,512]{1,0:T(8,128)S(1)}, u32[]{:S(2)}, u32[]{:S(2)}) collective-permute-start(f32[128,512]{1,0:T(8,128)S(1)} %get-tuple-element.205.refs_2_), channel_id=1, source_target_pairs={{0,2},{2,0},{4,6},{6,4},{1,3},{3,1},{5,7},{7,5},{8,10},{10,8},{12,... | collective-permute-start | bytes 786440 | tf_op jit(solution)/shard_map/ppermute | solution.py:550
  277.3 11.5 %collective-permute-start.74 = (f32[128,512]{1,0:T(8,128)S(1)}, f32[128,512]{1,0:T(8,128)S(1)}, u32[]{:S(2)}, u32[]{:S(2)}) collective-permute-start(f32[128,512]{1,0:T(8,128)S(1)} %shard_map.255.refs_5_.refs_0_), channel_id=1, source_target_pairs={{0,0},{2,4},{4,2},{6,6},{1,1},{3,5},{5,3},{7,7},{8,8},{10,12},{12,... | collective-permute-start | bytes 786440 | tf_op jit(solution)/shard_map/ppermute | solution.py:553
  283.2 11.4 %collective-permute-start.79 = (f32[128,512]{1,0:T(8,128)S(1)}, f32[128,512]{1,0:T(8,128)S(1)}, u32[]{:S(2)}, u32[]{:S(2)}) collective-permute-start(f32[128,512]{1,0:T(8,128)S(1)} %shard_map.257.refs_2_.refs_3_), channel_id=1, source_target_pairs={{0,2},{2,0},{4,6},{6,4},{1,3},{3,1},{5,7},{7,5},{8,10},{10,8},{12,... | collective-permute-start | bytes 786440 | tf_op jit(solution)/shard_map/ppermute | solution.py:550
  288.8 10.8 %collective-permute-start.78 = (f32[128,512]{1,0:T(8,128)S(1)}, f32[128,512]{1,0:T(8,128)S(1)}, u32[]{:S(2)}, u32[]{:S(2)}) collective-permute-start(f32[128,512]{1,0:T(8,128)S(1)} %shard_map.260.refs_2_.refs_3_), channel_id=1, source_target_pairs={{0,2},{2,0},{4,6},{6,4},{1,3},{3,1},{5,7},{7,5},{8,10},{10,8},{12,... | collective-permute-start | bytes 786440 | tf_op jit(solution)/shard_map/ppermute | solution.py:550
  290.1 15.1 %collective-permute-start.82 = (f32[128,512]{1,0:T(8,128)S(1)}, f32[128,512]{1,0:T(8,128)S(1)}, u32[]{:S(2)}, u32[]{:S(2)}) collective-permute-start(f32[128,512]{1,0:T(8,128)S(1)} %shard_map.262.refs_7_.refs_3_), channel_id=1, source_target_pairs={{0,2},{2,0},{4,6},{6,4},{1,3},{3,1},{5,7},{7,5},{8,10},{10,8},{12,... | collective-permute-start | bytes 786440 | tf_op jit(solution)/shard_map/ppermute | solution.py:550
  (62 other events, 326.4 us)

commit v2 on v0

--- a/solution.py
+++ b/solution.py
@@ -10,7 +10,8 @@
 
 HEAD_DIM = 128
 CG_STEPS = 3
-CHUNKS = 6
+WIDTHS = (2, 5, 4, 4, 5, 4)
+CHUNKS = len(WIDTHS)
 DEPTH = 1024
 
 EPS = 1e-05
@@ -48,6 +49,12 @@
     return jnp.dot(first, second, precision=HIGH, preferred_element_type=F32)
 
 
+def chunks_of(half):
+    unit = half // sum(WIDTHS)
+    ends = [unit * sum(WIDTHS[:k]) for k in range(CHUNKS + 1)]
+    return [slice(first, last) for first, last in zip(ends[:-1], ends[1:])]
+
+
 def head(index):
     return slice(index * HEAD_DIM, (index + 1) * HEAD_DIM)
 
@@ -65,20 +72,22 @@
 def split_kernel(core_ref, w_ref, *refs):
     own_refs, other_refs = refs[:CHUNKS], refs[CHUNKS : 2 * CHUNKS]
     landed, own_sem, other_sem = refs[2 * CHUNKS :]
-    cols = own_refs[0].shape[1]
-    half = CHUNKS * cols
+    half = w_ref.shape[1] // 2
+    places = chunks_of(half)
     core = core_ref[0]
 
     def own_copy(k):
-        start = pl.multiple_of(core * half + k * cols, HEAD_DIM)
+        start = pl.multiple_of(core * half + places[k].start, HEAD_DIM)
         return pltpu.make_async_copy(
-            w_ref.at[:, pl.ds(start, cols)], own_refs[k], own_sem.at[k]
+            w_ref.at[:, pl.ds(start, own_refs[k].shape[1])], own_refs[k], own_sem.at[k]
         )
 
     def other_copy(k):
-        start = pl.multiple_of((1 - core) * half + k * cols, HEAD_DIM)
+        start = pl.multiple_of((1 - core) * half + places[k].start, HEAD_DIM)
         return pltpu.make_async_copy(
-            w_ref.at[:, pl.ds(start, cols)], landed.at[k], other_sem.at[k]
+            w_ref.at[:, pl.ds(start, other_refs[k].shape[1])],
+            landed.at[:, places[k]],
+            other_sem.at[k],
         )
 
     for k in range(CHUNKS):
@@ -87,22 +96,23 @@
         own_copy(k).start()
     for k in range(CHUNKS):
         other_copy(k).wait()
-        other_refs[k][...] = landed[k].astype(F32)
+        other_refs[k][...] = landed[:, places[k]].astype(F32)
     for k in range(CHUNKS):
         own_copy(k).wait()
 
 
 def split(core, w_out):
     inner, width = w_out.shape
-    cols = width // 2 // CHUNKS
+    half = width // 2
+    cols = [place.stop - place.start for place in chunks_of(half)]
     out = pl.pallas_call(
         split_kernel,
         in_specs=[SMEM, pl.BlockSpec(memory_space=pltpu.HBM)],
         out_specs=[VMEM] * (2 * CHUNKS),
-        out_shape=[jax.ShapeDtypeStruct((inner, cols), BF16)] * CHUNKS
-        + [jax.ShapeDtypeStruct((inner, cols), F32)] * CHUNKS,
+        out_shape=[jax.ShapeDtypeStruct((inner, wide), BF16) for wide in cols]
+        + [jax.ShapeDtypeStruct((inner, wide), F32) for wide in cols],
         scratch_shapes=[
-            pltpu.VMEM((CHUNKS, inner, cols), BF16),
+            pltpu.VMEM((inner, half), BF16),
             pltpu.SemaphoreType.DMA((CHUNKS,)),
             pltpu.SemaphoreType.DMA((CHUNKS,)),
         ],
@@ -272,22 +282,36 @@
 
 
 def add(first, second, token):
+    rows, cols = first.shape
+
     def kernel(first_ref, second_ref, out_ref):
-        out_ref[...] = first_ref[...] + second_ref[: first_ref.shape[0]]
+        out_ref[...] = first_ref[...] + second_ref[:rows, :cols]
 
     return call(kernel, [first, second], [(first.shape, F32)], token)[0]
 
 
+def copy(part, token):
+    def kernel(part_ref, out_ref):
+        out_ref[...] = part_ref[...]
+
+    return call(kernel, [part], [(part.shape, F32)], token)[0]
+
+
 def add_and_pick(first, second, ends, outer, token):
+    rows, cols = first.shape
+    high, wide = outer.shape
+
     def kernel(ends_ref, first_ref, second_ref, outer_ref, sum_ref, sent_ref):
         total = first_ref[...] + second_ref[...]
         sum_ref[...] = total
-        rows = outer_ref.shape[0]
-        sent_ref[:rows] = jnp.where(ends_ref[0] > 0, outer_ref[...], total[:rows])
-        if total.shape[0] > rows:
-            sent_ref[rows:] = total[rows:]
-
-    outs = [(first.shape, F32)] * 2
+        sent_ref[:high, :cols] = jnp.where(ends_ref[0] > 0, outer_ref[:, :cols], total[:high])
+        if wide > cols:
+            sent_ref[:high, cols:] = outer_ref[:, cols:]
+        if rows > high:
+            sent_ref[high:] = jnp.zeros((rows - high, wide), F32)
+            sent_ref[high:, :cols] = total[high:]
+
+    outs = [(first.shape, F32), ((rows, wide), F32)]
     return call(kernel, [first, second, outer], outs, token, [ends])
 
 
@@ -300,7 +324,7 @@
         gap_ref = refs.pop(0) if gap is not None else None
         before = [refs.pop(0), refs.pop(0)] if index else None
         own_ref, other_ref = refs[:2]
-        total = jnp.where(ends_ref[0] > 0, got_ref[...], held_ref[...])
+        total = jnp.where(ends_ref[0] > 0, got_ref[:, : held.shape[1]], held_ref[...])
         total = total[: length + (8 if index == 0 else 0)]
         if index == 0:
             refs[2][...] = total[length:, :128]
@@ -525,7 +549,7 @@
     where = core.astype(jnp.int32)[None]
     own_w, other_w = split(where, w_out)
     other_w = [swap(part) for part in other_w]
-    cols = half // CHUNKS
+    places = chunks_of(half)
     gap = lax.dynamic_slice_in_dim(inputs, core * half, half, 1).astype(F32)
     gap = gap - lax.dynamic_slice_in_dim(targets, core * half, half, 1).astype(F32)
 
@@ -560,50 +584,52 @@
                 own_part[k] = spread(k, length, rows, got_rows, pairs[k], token)
             return own_part[k]
 
-        def finish(k, got):
-            gap_part = gap[:, k * cols : (k + 1) * cols] if first else None
-            return gather(k, length, ends, got, total[k], pairs[k], parts, lengths, gap_part, token)
+        def take_in(k, got):
+            nonlocal parts, scalars
+            gap_part = gap[:, places[k]] if first else None
+            out = gather(k, length, ends, got, total[k], pairs[k], parts, lengths, gap_part, token)
+            parts = list(out[:2])
+            scalars = out[2] if k == 0 else scalars
+            return parts[0]
 
         if n_chip != 4:
             for k in range(CHUNKS):
                 token = begin(k)
             for k in range(CHUNKS):
                 total[k] = lax.psum(own_part[k], "chip")
-                out = finish(k, total[k])
-                parts, scalars = list(out[:2]), out[2] if k == 0 else scalars
+                token = take_in(k, total[k])
         else:
-            for k in [0, 1, 2] if first else [0, *range(2, CHUNKS), 1]:
+            for k in (0, 1, 2) if first else (0,):
                 token = begin(k)
-            for k in (0, 1):
-                outer[k] = outer_swap(own_part[k])
+            outer[0] = outer_swap(own_part[0])
             for tick in range(CHUNKS + 3):
+                later = tick + 2
+                if tick == 0:
+                    token = outer[0]
+                    token = copy(own_part[1], token) if first else begin(1)
+                    outer[1] = outer_swap(token)
                 if tick < CHUNKS:
                     own_part[tick] = add(own_part[tick], outer[tick], token)
                     token = own_part[tick]
                     inner[tick] = inner_swap(token)
-                later = tick + 2
                 if tick == CHUNKS:
-                    out = finish(tick - 3, outer[tick])
-                    parts = list(out[:2])
-                    token = parts[0]
-                if 1 <= tick <= CHUNKS:
+                    token = take_in(tick - 3, outer[tick])
+                if tick == 0:
+                    token = copy(own_part[2], token) if first else begin(2)
+                    outer[2] = outer_swap(token)
+                elif tick <= CHUNKS:
                     k = tick - 1
                     if later < CHUNKS:
-                        total[k], sent = add_and_pick(
+                        total[k], token = add_and_pick(
                             own_part[k], inner[k], ends, own_part[later], token
                         )
                     else:
-                        total[k] = sent = add(own_part[k], inner[k], token)
-                    token = sent
-                    outer[later] = outer_swap(sent)
-                elif tick == 0:
-                    outer[later] = outer_swap(own_part[later])
-                if tick + 3 < CHUNKS and first:
+                        token = total[k] = add(own_part[k], inner[k], token)
+                    outer[later] = outer_swap(token)
+                if tick + 3 < CHUNKS:
                     token = begin(tick + 3)
                 if tick >= 3 and tick != CHUNKS:
-                    out = finish(tick - 3, outer[tick])
-                    parts, scalars = list(out[:2]), out[2] if tick == 3 else scalars
-                    token = parts[0]
+                    token = take_in(tick - 3, outer[tick])
         own, other = parts
         share = ADAPTER_SCALE / token_count
         part = cotangent(share, lengths, own, other, swap(other), attention)

time: 304 us -> 325 us (1.069)
  waiting for transfers between devices: 71.8 us -> 91.6 us
  starting transfers between devices: 173 us -> 164 us
  local copies, waits for them, and re-layouts: 5.26 us -> 12.9 us
    ppermute x36, waiting for transfers between devices: 38.6 us -> 59 us  [outer_swap(): return lax.ppermute(part, 'chip', [(0, 1), (1, 0), (2, 3), (3, 2)])]
    ppermute x36, starting transfers between devices: 140 us -> 129 us  [outer_swap(): return lax.ppermute(part, 'chip', [(0, 1), (1, 0), (2, 3), (3, 2)])]
    unnamed x56 -> x66, local copies, waits for them, and re-layouts: 5.14 us -> 10.8 us
    pallas_call x96 -> x98, Pallas kernels: 29.4 us -> 31.6 us  [call(): pl.pallas_call(body, in_specs=[SMEM] * len(scalars) + [VMEM] * len(ins) +...]
  transfers between devices with their start and end apart: 82 -> 82, of which waited for: 33 -> 38; matrix products, arithmetic and copies ran while one was open for 0% -> 1% of each run, Pallas kernels for 12% -> 11%
where the time goes in v2:
time: 325 us; the launch traced here: 324 us
  starting transfers between devices  164 us (50%)
  waiting for transfers between devices  91.6 us (28%)
  Pallas kernels  52.5 us (16%)
  local copies, waits for them, and re-layouts  12.9 us (4%)
    ppermute x36, starting transfers between devices, outer_swap(): return lax.ppermute(part, 'chip', [(0, 1), (1, 0), (2, 3), (3, 2)])  129 us
    ppermute x36, waiting for transfers between devices, outer_swap(): return lax.ppermute(part, 'chip', [(0, 1), (1, 0), (2, 3), (3, 2)])  59 us
    pallas_call x98, Pallas kernels, call(): pl.pallas_call(body, in_specs=[SMEM] * len(scalars) + [VMEM] * len(ins) +...  31.6 us
    ppermute x24, starting transfers between devices, inner_swap(): return lax.ppermute(part, 'chip', [(0, 0), (1, 2), (2, 1), (3, 3)])  19.7 us
    ppermute x14, waiting for transfers between devices, swap(): return lax.ppermute(part, 'core', [(0, 1), (1, 0)])  11.1 us
    unnamed x66, local copies, waits for them, and re-layouts  10.8 us
    ppermute x4, waiting for transfers between devices, data_terms(): lax.ppermute(part, 'dp', [(d, d ^ step) for d in range(n_dp)])  10.8 us
    ppermute x4, waiting for transfers between devices, data_terms(): part = part + lax.ppermute(part, 'dp', [(d, d ^ step) for d in range(n_dp)])  10.7 us
  transfers between devices with their start and end apart: 82, of which 38 were waited for; matrix products, arithmetic and copies ran while one was open for 1% of the time, Pallas kernels for 11%

profile of v2, /device:TPU:0, one launch (start us, length us, event | category | flops | bytes accessed | tf_op | source)
XLA Modules:
  0.0 323.8 jit_solution(71314392076021232)
XLA Ops:
  3.0 2.8 shard_map.157
  10.8 8.8 %shard_map.156 = (f32[3,128,128]{2,1,0:T(8,128)S(1)}, bf16[128,384]{1,0:T(8,128)(2,1)S(1)}, bf16[128,384]{1,0:T(8,128)(2,1)S(1)}, f32[128,16]{1,0:T(8,128)S(1)},...) custom-call(s32[1]{0:T(128)S(6)} %copy.17.limit_ref.refs_1_.refs_2_.refs_4_.refs_8_, bf16[128,6144]{1,0:T(8,128)(2,1)S(1)} %copy-done.1, ...), custom_call_target="tpu_custom_call" | custom-call | flops 1811939328 | bytes 14155776 | tf_op jit(solution)/shard_map/pallas_call | solution.py:198
  25.2 2.7 collective-permute-start.4
  34.6 2.8 collective-permute-start.10
  61.0 2.5 collective-permute-start.14
  64.2 2.6 collective-permute-done.15.refs_1_.refs_2_
  68.7 4.2 %collective-permute-start.18 = (f32[128,512]{1,0:T(8,128)S(1)}, f32[128,512]{1,0:T(8,128)S(1)}, u32[]{:S(2)}, u32[]{:S(2)}) collective-permute-start(f32[128,512]{1,0:T(8,128)S(1)} %shard_map.175.refs_8_.refs_3_), channel_id=1, source_target_pairs={{0,2},{2,0},{4,6},{6,4},{1,3},{3,1},{5,7},{7,5},{8,10},{10,8},{12,... | collective-permute-start | bytes 786440 | tf_op jit(solution)/shard_map/ppermute | solution.py:565
  74.5 6.0 %collective-permute-start.21 = (f32[128,640]{1,0:T(8,128)S(1)}, f32[128,640]{1,0:T(8,128)S(1)}, u32[]{:S(2)}, u32[]{:S(2)}) collective-permute-start(f32[128,640]{1,0:T(8,128)S(1)} %shard_map.178.refs_8_.refs_3_), channel_id=1, source_target_pairs={{0,2},{2,0},{4,6},{6,4},{1,3},{3,1},{5,7},{7,5},{8,10},{10,8},{12,... | collective-permute-start | bytes 983048 | tf_op jit(solution)/shard_map/ppermute | solution.py:565
  83.3 4.2 %collective-permute-done.21.refs_2_ = f32[128,640]{1,0:T(8,128)S(1)} collective-permute-done((f32[128,640]{1,0:T(8,128)S(1)}, f32[128,640]{1,0:T(8,128)S(1)}, u32[]{:S(2)}, u32[]{:S(2)}) %collective-permute-start.21) | collective-permute-done | bytes 327712 | tf_op jit(solution)/shard_map/ppermute | solution.py:565
  88.0 2.3 collective-permute-done.20.refs_2_
  95.3 2.7 collective-permute-done.23
  99.6 2.7 collective-permute-done.24.refs_1_
  106.6 4.0 %collective-permute-done.26.refs_3_.refs_1_ = f32[136,256]{1,0:T(8,128)S(1)} collective-permute-done((f32[136,256]{1,0:T(8,128)S(1)}, f32[136,256]{1,0:T(8,128)S(1)}, u32[]{:S(2)}, u32[]{:S(2)}) %collective-permute-start.26) | collective-permute-done | bytes 139296 | tf_op jit(solution)/shard_map/ppermute | solution.py:565
  113.7 2.6 collective-permute-start.30
  116.6 5.0 %collective-permute-done.27.refs_1_ = f32[128,640]{1,0:T(8,128)S(1)} collective-permute-done((f32[128,640]{1,0:T(8,128)S(1)}, f32[128,640]{1,0:T(8,128)S(1)}, u32[]{:S(2)}, u32[]{:S(2)}) %collective-permute-start.27) | collective-permute-done | bytes 327712 | tf_op jit(solution)/shard_map/ppermute | solution.py:565
  122.4 4.1 %collective-permute-start.32 = (f32[136,512]{1,0:T(8,128)S(1)}, f32[136,512]{1,0:T(8,128)S(1)}, u32[]{:S(2)}, u32[]{:S(2)}) collective-permute-start(f32[136,512]{1,0:T(8,128)S(1)} %get-tuple-element.172.refs_3_), channel_id=1, source_target_pairs={{0,2},{2,0},{4,6},{6,4},{1,3},{3,1},{5,7},{7,5},{8,10},{10,8},{12,... | collective-permute-start | bytes 835592 | tf_op jit(solution)/shard_map/ppermute | solution.py:565
  128.1 6.6 %collective-permute-start.34 = (f32[128,640]{1,0:T(8,128)S(1)}, f32[128,640]{1,0:T(8,128)S(1)}, u32[]{:S(2)}, u32[]{:S(2)}) collective-permute-start(f32[128,640]{1,0:T(8,128)S(1)} %get-tuple-element.173.refs_3_), channel_id=1, source_target_pairs={{0,2},{2,0},{4,6},{6,4},{1,3},{3,1},{5,7},{7,5},{8,10},{10,8},{12,... | collective-permute-start | bytes 983048 | tf_op jit(solution)/shard_map/ppermute | solution.py:565
  135.8 4.5 %collective-permute-start.33 = (f32[128,512]{1,0:T(8,128)S(1)}, f32[128,512]{1,0:T(8,128)S(1)}, u32[]{:S(2)}, u32[]{:S(2)}) collective-permute-start(f32[128,512]{1,0:T(8,128)S(1)} %get-tuple-element.174.refs_5_), channel_id=1, source_target_pairs={{0,2},{2,0},{4,6},{6,4},{1,3},{3,1},{5,7},{7,5},{8,10},{10,8},{12,... | collective-permute-start | bytes 786440 | tf_op jit(solution)/shard_map/ppermute | solution.py:565
  143.4 4.7 %collective-permute-start.37 = (f32[128,512]{1,0:T(8,128)S(1)}, f32[128,512]{1,0:T(8,128)S(1)}, u32[]{:S(2)}, u32[]{:S(2)}) collective-permute-start(f32[128,512]{1,0:T(8,128)S(1)} %shard_map.201.refs_7_.refs_3_), channel_id=1, source_target_pairs={{0,2},{2,0},{4,6},{6,4},{1,3},{3,1},{5,7},{7,5},{8,10},{10,8},{12,... | collective-permute-start | bytes 786440 | tf_op jit(solution)/shard_map/ppermute | solution.py:565
  149.3 6.0 %collective-permute-start.40 = (f32[128,640]{1,0:T(8,128)S(1)}, f32[128,640]{1,0:T(8,128)S(1)}, u32[]{:S(2)}, u32[]{:S(2)}) collective-permute-start(f32[128,640]{1,0:T(8,128)S(1)} %shard_map.204.refs_7_.refs_3_), channel_id=1, source_target_pairs={{0,2},{2,0},{4,6},{6,4},{1,3},{3,1},{5,7},{7,5},{8,10},{10,8},{12,... | collective-permute-start | bytes 983048 | tf_op jit(solution)/shard_map/ppermute | solution.py:565
  156.1 2.6 collective-permute-start.39
  161.4 2.3 collective-permute-done.39.refs_2_
  168.7 2.7 collective-permute-done.42
  173.0 2.7 collective-permute-done.43.refs_1_
  180.2 4.0 %collective-permute-done.45.refs_3_.refs_1_ = f32[136,256]{1,0:T(8,128)S(1)} collective-permute-done((f32[136,256]{1,0:T(8,128)S(1)}, f32[136,256]{1,0:T(8,128)S(1)}, u32[]{:S(2)}, u32[]{:S(2)}) %collective-permute-start.45) | collective-permute-done | bytes 139296 | tf_op jit(solution)/shard_map/ppermute | solution.py:565
  187.3 2.6 collective-permute-start.49
  190.2 5.0 %collective-permute-done.46.refs_1_ = f32[128,640]{1,0:T(8,128)S(1)} collective-permute-done((f32[128,640]{1,0:T(8,128)S(1)}, f32[128,640]{1,0:T(8,128)S(1)}, u32[]{:S(2)}, u32[]{:S(2)}) %collective-permute-start.46) | collective-permute-done | bytes 327712 | tf_op jit(solution)/shard_map/ppermute | solution.py:565
  196.0 4.1 %collective-permute-start.51 = (f32[136,512]{1,0:T(8,128)S(1)}, f32[136,512]{1,0:T(8,128)S(1)}, u32[]{:S(2)}, u32[]{:S(2)}) collective-permute-start(f32[136,512]{1,0:T(8,128)S(1)} %get-tuple-element.193.refs_3_), channel_id=1, source_target_pairs={{0,2},{2,0},{4,6},{6,4},{1,3},{3,1},{5,7},{7,5},{8,10},{10,8},{12,... | collective-permute-start | bytes 835592 | tf_op jit(solution)/shard_map/ppermute | solution.py:565
  201.7 6.6 %collective-permute-start.53 = (f32[128,640]{1,0:T(8,128)S(1)}, f32[128,640]{1,0:T(8,128)S(1)}, u32[]{:S(2)}, u32[]{:S(2)}) collective-permute-start(f32[128,640]{1,0:T(8,128)S(1)} %get-tuple-element.194.refs_3_), channel_id=1, source_target_pairs={{0,2},{2,0},{4,6},{6,4},{1,3},{3,1},{5,7},{7,5},{8,10},{10,8},{12,... | collective-permute-start | bytes 983048 | tf_op jit(solution)/shard_map/ppermute | solution.py:565
  209.4 4.5 %collective-permute-start.52 = (f32[128,512]{1,0:T(8,128)S(1)}, f32[128,512]{1,0:T(8,128)S(1)}, u32[]{:S(2)}, u32[]{:S(2)}) collective-permute-start(f32[128,512]{1,0:T(8,128)S(1)} %get-tuple-element.195.refs_5_), channel_id=1, source_target_pairs={{0,2},{2,0},{4,6},{6,4},{1,3},{3,1},{5,7},{7,5},{8,10},{10,8},{12,... | collective-permute-start | bytes 786440 | tf_op jit(solution)/shard_map/ppermute | solution.py:565
  217.0 4.7 %collective-permute-start.56 = (f32[128,512]{1,0:T(8,128)S(1)}, f32[128,512]{1,0:T(8,128)S(1)}, u32[]{:S(2)}, u32[]{:S(2)}) collective-permute-start(f32[128,512]{1,0:T(8,128)S(1)} %shard_map.227.refs_7_.refs_3_), channel_id=1, source_target_pairs={{0,2},{2,0},{4,6},{6,4},{1,3},{3,1},{5,7},{7,5},{8,10},{10,8},{12,... | collective-permute-start | bytes 786440 | tf_op jit(solution)/shard_map/ppermute | solution.py:565
  223.1 5.8 %collective-permute-start.59 = (f32[128,640]{1,0:T(8,128)S(1)}, f32[128,640]{1,0:T(8,128)S(1)}, u32[]{:S(2)}, u32[]{:S(2)}) collective-permute-start(f32[128,640]{1,0:T(8,128)S(1)} %shard_map.230.refs_7_.refs_3_), channel_id=1, source_target_pairs={{0,2},{2,0},{4,6},{6,4},{1,3},{3,1},{5,7},{7,5},{8,10},{10,8},{12,... | collective-permute-start | bytes 983048 | tf_op jit(solution)/shard_map/ppermute | solution.py:565
  229.7 2.6 collective-permute-start.58
  235.0 2.4 collective-permute-done.58.refs_2_
  242.3 2.7 collective-permute-done.61
  246.6 2.7 collective-permute-done.62.refs_1_
  253.9 4.0 %collective-permute-done.64.refs_3_.refs_1_ = f32[136,256]{1,0:T(8,128)S(1)} collective-permute-done((f32[136,256]{1,0:T(8,128)S(1)}, f32[136,256]{1,0:T(8,128)S(1)}, u32[]{:S(2)}, u32[]{:S(2)}) %collective-permute-start.64) | collective-permute-done | bytes 139296 | tf_op jit(solution)/shard_map/ppermute | solution.py:565
  261.0 2.6 collective-permute-start.68
  263.9 5.0 %collective-permute-done.65.refs_1_ = f32[128,640]{1,0:T(8,128)S(1)} collective-permute-done((f32[128,640]{1,0:T(8,128)S(1)}, f32[128,640]{1,0:T(8,128)S(1)}, u32[]{:S(2)}, u32[]{:S(2)}) %collective-permute-start.65) | collective-permute-done | bytes 327712 | tf_op jit(solution)/shard_map/ppermute | solution.py:565
  269.7 4.1 %collective-permute-start.70 = (f32[136,512]{1,0:T(8,128)S(1)}, f32[136,512]{1,0:T(8,128)S(1)}, u32[]{:S(2)}, u32[]{:S(2)}) collective-permute-start(f32[136,512]{1,0:T(8,128)S(1)} %get-tuple-element.218.refs_3_), channel_id=1, source_target_pairs={{0,2},{2,0},{4,6},{6,4},{1,3},{3,1},{5,7},{7,5},{8,10},{10,8},{12,... | collective-permute-start | bytes 835592 | tf_op jit(solution)/shard_map/ppermute | solution.py:565
  275.4 6.6 %collective-permute-start.72 = (f32[128,640]{1,0:T(8,128)S(1)}, f32[128,640]{1,0:T(8,128)S(1)}, u32[]{:S(2)}, u32[]{:S(2)}) collective-permute-start(f32[128,640]{1,0:T(8,128)S(1)} %get-tuple-element.219.refs_3_), channel_id=1, source_target_pairs={{0,2},{2,0},{4,6},{6,4},{1,3},{3,1},{5,7},{7,5},{8,10},{10,8},{12,... | collective-permute-start | bytes 983048 | tf_op jit(solution)/shard_map/ppermute | solution.py:565
  283.1 4.5 %collective-permute-start.71 = (f32[128,512]{1,0:T(8,128)S(1)}, f32[128,512]{1,0:T(8,128)S(1)}, u32[]{:S(2)}, u32[]{:S(2)}) collective-permute-start(f32[128,512]{1,0:T(8,128)S(1)} %get-tuple-element.220.refs_5_), channel_id=1, source_target_pairs={{0,2},{2,0},{4,6},{6,4},{1,3},{3,1},{5,7},{7,5},{8,10},{10,8},{12,... | collective-permute-start | bytes 786440 | tf_op jit(solution)/shard_map/ppermute | solution.py:565
  290.7 4.7 %collective-permute-start.75 = (f32[128,512]{1,0:T(8,128)S(1)}, f32[128,512]{1,0:T(8,128)S(1)}, u32[]{:S(2)}, u32[]{:S(2)}) collective-permute-start(f32[128,512]{1,0:T(8,128)S(1)} %shard_map.253.refs_7_.refs_3_), channel_id=1, source_target_pairs={{0,2},{2,0},{4,6},{6,4},{1,3},{3,1},{5,7},{7,5},{8,10},{10,8},{12,... | collective-permute-start | bytes 786440 | tf_op jit(solution)/shard_map/ppermute | solution.py:565
  296.6 6.0 %collective-permute-start.78 = (f32[128,640]{1,0:T(8,128)S(1)}, f32[128,640]{1,0:T(8,128)S(1)}, u32[]{:S(2)}, u32[]{:S(2)}) collective-permute-start(f32[128,640]{1,0:T(8,128)S(1)} %shard_map.256.refs_7_.refs_3_), channel_id=1, source_target_pairs={{0,2},{2,0},{4,6},{6,4},{1,3},{3,1},{5,7},{7,5},{8,10},{10,8},{12,... | collective-permute-start | bytes 983048 | tf_op jit(solution)/shard_map/ppermute | solution.py:565
  303.4 2.6 collective-permute-start.77
  308.7 2.3 collective-permute-done.77.refs_2_
  316.1 2.6 collective-permute-done.80
  320.3 2.7 collective-permute-done.81.refs_1_
  (298 shorter events, 133.6 us)
Async XLA Ops:
  9.6 18.5 %collective-permute-start.2 = (f32[384,640]{1,0:T(8,128)}, f32[384,640]{1,0:T(8,128)}, u32[]{:S(2)}, u32[]{:S(2)}) collective-permute-start(f32[384,640]{1,0:T(8,128)} %get-tuple-element.127), channel_id=1, source_target_pairs={{0,1},{1,0},{2,3},{3,2},{4,5},{5,4},{6,7},{7,6},{8,9},{9,8},{10,11... | collective-permute-start | bytes 2949128 | tf_op jit(solution)/shard_map/ppermute | solution.py:540
  10.0 11.9 %collective-permute-start.3 = (f32[384,256]{1,0:T(8,128)}, f32[384,256]{1,0:T(8,128)}, u32[]{:S(2)}, u32[]{:S(2)}) collective-permute-start(f32[384,256]{1,0:T(8,128)} %get-tuple-element.129), channel_id=1, source_target_pairs={{0,1},{1,0},{2,3},{3,2},{4,5},{5,4},{6,7},{7,6},{8,9},{9,8},{10,11... | collective-permute-start | bytes 1179656 | tf_op jit(solution)/shard_map/ppermute | solution.py:540
  20.1 14.5 %collective-permute-start.7 = (f32[384,512]{1,0:T(8,128)}, f32[384,512]{1,0:T(8,128)}, u32[]{:S(2)}, u32[]{:S(2)}) collective-permute-start(f32[384,512]{1,0:T(8,128)} %get-tuple-element.135), channel_id=1, source_target_pairs={{0,1},{1,0},{2,3},{3,2},{4,5},{5,4},{6,7},{7,6},{8,9},{9,8},{10,11... | collective-permute-start | bytes 2359304 | tf_op jit(solution)/shard_map/ppermute | solution.py:540
  20.2 19.9 %collective-permute-start.6 = (f32[384,512]{1,0:T(8,128)}, f32[384,512]{1,0:T(8,128)}, u32[]{:S(2)}, u32[]{:S(2)}) collective-permute-start(f32[384,512]{1,0:T(8,128)} %get-tuple-element.133), channel_id=1, source_target_pairs={{0,1},{1,0},{2,3},{3,2},{4,5},{5,4},{6,7},{7,6},{8,9},{9,8},{10,11... | collective-permute-start | bytes 2359304 | tf_op jit(solution)/shard_map/ppermute | solution.py:540
  21.5 29.9 %collective-permute-start.9 = (f32[384,640]{1,0:T(8,128)S(1)}, f32[384,640]{1,0:T(8,128)}, u32[]{:S(2)}, u32[]{:S(2)}) collective-permute-start(f32[384,640]{1,0:T(8,128)S(1)} %get-tuple-element.139), channel_id=1, source_target_pairs={{0,1},{1,0},{2,3},{3,2},{4,5},{5,4},{6,7},{7,6},{8,9},{9,8},{10,11... | collective-permute-start | bytes 2949128 | tf_op jit(solution)/shard_map/ppermute | solution.py:540
  28.1 30.2 %collective-permute-start.1 = (f32[384,512]{1,0:T(8,128)}, f32[384,512]{1,0:T(8,128)}, u32[]{:S(2)}, u32[]{:S(2)}) collective-permute-start(f32[384,512]{1,0:T(8,128)} %get-tuple-element.125), channel_id=1, source_target_pairs={{0,1},{1,0},{2,3},{3,2},{4,5},{5,4},{6,7},{7,6},{8,9},{9,8},{10,11... | collective-permute-start | bytes 2359304 | tf_op jit(solution)/shard_map/ppermute | solution.py:540
  32.1 12.0 %collective-permute-start.5 = (f32[128,640]{1,0:T(8,128)S(1)}, f32[128,640]{1,0:T(8,128)S(1)}, u32[]{:S(2)}, u32[]{:S(2)}) collective-permute-start(f32[128,640]{1,0:T(8,128)S(1)} %shard_map.160.refs_2_), channel_id=1, source_target_pairs={{0,2},{2,0},{4,6},{6,4},{1,3},{3,1},{5,7},{7,5},{8,10},{10,8},{12,... | collective-permute-start | bytes 983048 | tf_op jit(solution)/shard_map/ppermute | solution.py:565
  34.6 12.9 %collective-permute-start.10 = (f32[136,256]{1,0:T(8,128)}, f32[136,256]{1,0:T(8,128)}, u32[]{:S(2)}, u32[]{:S(2)}) collective-permute-start(f32[136,256]{1,0:T(8,128)} %shard_map.162.refs_1_), channel_id=1, source_target_pairs={{0,0},{2,4},{4,2},{6,6},{1,1},{3,5},{5,3},{7,7},{8,8},{10,12},{12,... | collective-permute-start | bytes 417800 | tf_op jit(solution)/shard_map/ppermute | solution.py:568
  40.1 13.2 %collective-permute-start.11 = (f32[128,512]{1,0:T(8,128)}, f32[128,512]{1,0:T(8,128)}, u32[]{:S(2)}, u32[]{:S(2)}) collective-permute-start(f32[128,512]{1,0:T(8,128)} %shard_map.163.refs_4_), channel_id=1, source_target_pairs={{0,2},{2,0},{4,6},{6,4},{1,3},{3,1},{5,7},{7,5},{8,10},{10,8},{12,... | collective-permute-start | bytes 786440 | tf_op jit(solution)/shard_map/ppermute | solution.py:565
  45.1 9.9 %collective-permute-start.8 = (f32[128,640]{1,0:T(8,128)S(1)}, f32[128,640]{1,0:T(8,128)}, u32[]{:S(2)}, u32[]{:S(2)}) collective-permute-start(f32[128,640]{1,0:T(8,128)S(1)} %shard_map.165.refs_4_.refs_1_), channel_id=1, source_target_pairs={{0,0},{2,4},{4,2},{6,6},{1,1},{3,5},{5,3},{7,7},{8,8},{10,12},{12,... | collective-permute-start | bytes 983048 | tf_op jit(solution)/shard_map/ppermute | solution.py:568
  49.5 10.5 %collective-permute-start.13 = (f32[136,512]{1,0:T(8,128)S(1)}, f32[136,512]{1,0:T(8,128)S(1)}, u32[]{:S(2)}, u32[]{:S(2)}) collective-permute-start(f32[136,512]{1,0:T(8,128)S(1)} %get-tuple-element.140.refs_4_), channel_id=1, source_target_pairs={{0,2},{2,0},{4,6},{6,4},{1,3},{3,1},{5,7},{7,5},{8,10},{10,8},{12,... | collective-permute-start | bytes 835592 | tf_op jit(solution)/shard_map/ppermute | solution.py:565
  56.0 10.8 %collective-permute-start.15 = (f32[128,640]{1,0:T(8,128)S(1)}, f32[128,640]{1,0:T(8,128)S(1)}, u32[]{:S(2)}, u32[]{:S(2)}) collective-permute-start(f32[128,640]{1,0:T(8,128)S(1)} %get-tuple-element.142.refs_4_), channel_id=1, source_target_pairs={{0,2},{2,0},{4,6},{6,4},{1,3},{3,1},{5,7},{7,5},{8,10},{10,8},{12,... | collective-permute-start | bytes 983048 | tf_op jit(solution)/shard_map/ppermute | solution.py:565
  60.1 8.6 %collective-permute-start.16 = (f32[128,512]{1,0:T(8,128)S(1)}, f32[128,512]{1,0:T(8,128)S(1)}, u32[]{:S(2)}, u32[]{:S(2)}) collective-permute-start(f32[128,512]{1,0:T(8,128)S(1)} %shard_map.171.refs_4_.refs_0_), channel_id=1, source_target_pairs={{0,0},{2,4},{4,2},{6,6},{1,1},{3,5},{5,3},{7,7},{8,8},{10,12},{12,... | collective-permute-start | bytes 786440 | tf_op jit(solution)/shard_map/ppermute | solution.py:568
  61.0 12.4 %collective-permute-start.14 = (f32[128,512]{1,0:T(8,128)S(1)}, f32[128,512]{1,0:T(8,128)S(1)}, u32[]{:S(2)}, u32[]{:S(2)}) collective-permute-start(f32[128,512]{1,0:T(8,128)S(1)} %get-tuple-element.144.refs_6_), channel_id=1, source_target_pairs={{0,2},{2,0},{4,6},{6,4},{1,3},{3,1},{5,7},{7,5},{8,10},{10,8},{12,... | collective-permute-start | bytes 786440 | tf_op jit(solution)/shard_map/ppermute | solution.py:565
  68.7 12.2 %collective-permute-start.18 = (f32[128,512]{1,0:T(8,128)S(1)}, f32[128,512]{1,0:T(8,128)S(1)}, u32[]{:S(2)}, u32[]{:S(2)}) collective-permute-start(f32[128,512]{1,0:T(8,128)S(1)} %shard_map.175.refs_8_.refs_3_), channel_id=1, source_target_pairs={{0,2},{2,0},{4,6},{6,4},{1,3},{3,1},{5,7},{7,5},{8,10},{10,8},{12,... | collective-permute-start | bytes 786440 | tf_op jit(solution)/shard_map/ppermute | solution.py:565
  73.5 8.6 %collective-permute-start.17 = (f32[128,512]{1,0:T(8,128)S(1)}, f32[128,512]{1,0:T(8,128)S(1)}, u32[]{:S(2)}, u32[]{:S(2)}) collective-permute-start(f32[128,512]{1,0:T(8,128)S(1)} %shard_map.177.refs_2_.refs_0_), channel_id=1, source_target_pairs={{0,0},{2,4},{4,2},{6,6},{1,1},{3,5},{5,3},{7,7},{8,8},{10,12},{12,... | collective-permute-start | bytes 786440 | tf_op jit(solution)/shard_map/ppermute | solution.py:568
  74.5 13.0 %collective-permute-start.21 = (f32[128,640]{1,0:T(8,128)S(1)}, f32[128,640]{1,0:T(8,128)S(1)}, u32[]{:S(2)}, u32[]{:S(2)}) collective-permute-start(f32[128,640]{1,0:T(8,128)S(1)} %shard_map.178.refs_8_.refs_3_), channel_id=1, source_target_pairs={{0,2},{2,0},{4,6},{6,4},{1,3},{3,1},{5,7},{7,5},{8,10},{10,8},{12,... | collective-permute-start | bytes 983048 | tf_op jit(solution)/shard_map/ppermute | solution.py:565
  82.1 8.2 %collective-permute-start.20 = (f32[128,512]{1,0:T(8,128)S(1)}, f32[128,512]{1,0:T(8,128)S(1)}, u32[]{:S(2)}, u32[]{:S(2)}) collective-permute-start(f32[128,512]{1,0:T(8,128)S(1)} %shard_map.181.refs_8_.refs_3_), channel_id=1, source_target_pairs={{0,2},{2,0},{4,6},{6,4},{1,3},{3,1},{5,7},{7,5},{8,10},{10,8},{12,... | collective-permute-start | bytes 786440 | tf_op jit(solution)/shard_map/ppermute | solution.py:565
  110.9 10.7 %collective-permute-start.27 = (f32[128,640]{1,0:T(8,128)S(1)}, f32[128,640]{1,0:T(8,128)S(1)}, u32[]{:S(2)}, u32[]{:S(2)}) collective-permute-start(f32[128,640]{1,0:T(8,128)S(1)} %shard_map.187.refs_2_.refs_0_), channel_id=1, source_target_pairs={{0,2},{2,0},{4,6},{6,4},{1,3},{3,1},{5,7},{7,5},{8,10},{10,8},{12,... | collective-permute-start | bytes 983048 | tf_op jit(solution)/shard_map/ppermute | solution.py:565
  112.8 9.6 %collective-permute-start.29 = (f32[136,256]{1,0:T(8,128)S(1)}, f32[136,256]{1,0:T(8,128)S(1)}, u32[]{:S(2)}, u32[]{:S(2)}) collective-permute-start(f32[136,256]{1,0:T(8,128)S(1)} %shard_map.188.refs_3_.refs_1_), channel_id=1, source_target_pairs={{0,0},{2,4},{4,2},{6,6},{1,1},{3,5},{5,3},{7,7},{8,8},{10,12},{12,... | collective-permute-start | bytes 417800 | tf_op jit(solution)/shard_map/ppermute | solution.py:568
  113.7 13.6 %collective-permute-start.30 = (f32[128,512]{1,0:T(8,128)S(1)}, f32[128,512]{1,0:T(8,128)S(1)}, u32[]{:S(2)}, u32[]{:S(2)}) collective-permute-start(f32[128,512]{1,0:T(8,128)S(1)} %shard_map.189.refs_3_.refs_0_), channel_id=1, source_target_pairs={{0,2},{2,0},{4,6},{6,4},{1,3},{3,1},{5,7},{7,5},{8,10},{10,8},{12,... | collective-permute-start | bytes 786440 | tf_op jit(solution)/shard_map/ppermute | solution.py:565
  122.4 12.5 %collective-permute-start.32 = (f32[136,512]{1,0:T(8,128)S(1)}, f32[136,512]{1,0:T(8,128)S(1)}, u32[]{:S(2)}, u32[]{:S(2)}) collective-permute-start(f32[136,512]{1,0:T(8,128)S(1)} %get-tuple-element.172.refs_3_), channel_id=1, source_target_pairs={{0,2},{2,0},{4,6},{6,4},{1,3},{3,1},{5,7},{7,5},{8,10},{10,8},{12,... | collective-permute-start | bytes 835592 | tf_op jit(solution)/shard_map/ppermute | solution.py:565
  127.3 8.4 %collective-permute-start.31 = (f32[128,512]{1,0:T(8,128)S(1)}, f32[128,512]{1,0:T(8,128)S(1)}, u32[]{:S(2)}, u32[]{:S(2)}) collective-permute-start(f32[128,512]{1,0:T(8,128)S(1)} %shard_map.194.refs_4_.refs_1_), channel_id=1, source_target_pairs={{0,0},{2,4},{4,2},{6,6},{1,1},{3,5},{5,3},{7,7},{8,8},{10,12},{12,... | collective-permute-start | bytes 786440 | tf_op jit(solution)/shard_map/ppermute | solution.py:568
  128.1 14.5 %collective-permute-start.34 = (f32[128,640]{1,0:T(8,128)S(1)}, f32[128,640]{1,0:T(8,128)S(1)}, u32[]{:S(2)}, u32[]{:S(2)}) collective-permute-start(f32[128,640]{1,0:T(8,128)S(1)} %get-tuple-element.173.refs_3_), channel_id=1, source_target_pairs={{0,2},{2,0},{4,6},{6,4},{1,3},{3,1},{5,7},{7,5},{8,10},{10,8},{12,... | collective-permute-start | bytes 983048 | tf_op jit(solution)/shard_map/ppermute | solution.py:565
  135.0 8.3 %collective-permute-start.35 = (f32[128,512]{1,0:T(8,128)S(1)}, f32[128,512]{1,0:T(8,128)S(1)}, u32[]{:S(2)}, u32[]{:S(2)}) collective-permute-start(f32[128,512]{1,0:T(8,128)S(1)} %shard_map.197.refs_4_.refs_0_), channel_id=1, source_target_pairs={{0,0},{2,4},{4,2},{6,6},{1,1},{3,5},{5,3},{7,7},{8,8},{10,12},{12,... | collective-permute-start | bytes 786440 | tf_op jit(solution)/shard_map/ppermute | solution.py:568
  135.8 12.7 %collective-permute-start.33 = (f32[128,512]{1,0:T(8,128)S(1)}, f32[128,512]{1,0:T(8,128)S(1)}, u32[]{:S(2)}, u32[]{:S(2)}) collective-permute-start(f32[128,512]{1,0:T(8,128)S(1)} %get-tuple-element.174.refs_5_), channel_id=1, source_target_pairs={{0,2},{2,0},{4,6},{6,4},{1,3},{3,1},{5,7},{7,5},{8,10},{10,8},{12,... | collective-permute-start | bytes 786440 | tf_op jit(solution)/shard_map/ppermute | solution.py:565
  143.4 12.3 %collective-permute-start.37 = (f32[128,512]{1,0:T(8,128)S(1)}, f32[128,512]{1,0:T(8,128)S(1)}, u32[]{:S(2)}, u32[]{:S(2)}) collective-permute-start(f32[128,512]{1,0:T(8,128)S(1)} %shard_map.201.refs_7_.refs_3_), channel_id=1, source_target_pairs={{0,2},{2,0},{4,6},{6,4},{1,3},{3,1},{5,7},{7,5},{8,10},{10,8},{12,... | collective-permute-start | bytes 786440 | tf_op jit(solution)/shard_map/ppermute | solution.py:565
  149.3 11.6 %collective-permute-start.40 = (f32[128,640]{1,0:T(8,128)S(1)}, f32[128,640]{1,0:T(8,128)S(1)}, u32[]{:S(2)}, u32[]{:S(2)}) collective-permute-start(f32[128,640]{1,0:T(8,128)S(1)} %shard_map.204.refs_7_.refs_3_), channel_id=1, source_target_pairs={{0,2},{2,0},{4,6},{6,4},{1,3},{3,1},{5,7},{7,5},{8,10},{10,8},{12,... | collective-permute-start | bytes 983048 | tf_op jit(solution)/shard_map/ppermute | solution.py:565
  184.5 10.7 %collective-permute-start.46 = (f32[128,640]{1,0:T(8,128)S(1)}, f32[128,640]{1,0:T(8,128)S(1)}, u32[]{:S(2)}, u32[]{:S(2)}) collective-permute-start(f32[128,640]{1,0:T(8,128)S(1)} %shard_map.213.refs_2_.refs_0_), channel_id=1, source_target_pairs={{0,2},{2,0},{4,6},{6,4},{1,3},{3,1},{5,7},{7,5},{8,10},{10,8},{12,... | collective-permute-start | bytes 983048 | tf_op jit(solution)/shard_map/ppermute | solution.py:565
  186.4 9.6 %collective-permute-start.48 = (f32[136,256]{1,0:T(8,128)S(1)}, f32[136,256]{1,0:T(8,128)S(1)}, u32[]{:S(2)}, u32[]{:S(2)}) collective-permute-start(f32[136,256]{1,0:T(8,128)S(1)} %shard_map.214.refs_3_.refs_1_), channel_id=1, source_target_pairs={{0,0},{2,4},{4,2},{6,6},{1,1},{3,5},{5,3},{7,7},{8,8},{10,12},{12,... | collective-permute-start | bytes 417800 | tf_op jit(solution)/shard_map/ppermute | solution.py:568
  187.3 13.5 %collective-permute-start.49 = (f32[128,512]{1,0:T(8,128)S(1)}, f32[128,512]{1,0:T(8,128)S(1)}, u32[]{:S(2)}, u32[]{:S(2)}) collective-permute-start(f32[128,512]{1,0:T(8,128)S(1)} %shard_map.215.refs_3_.refs_0_), channel_id=1, source_target_pairs={{0,2},{2,0},{4,6},{6,4},{1,3},{3,1},{5,7},{7,5},{8,10},{10,8},{12,... | collective-permute-start | bytes 786440 | tf_op jit(solution)/shard_map/ppermute | solution.py:565
  196.0 12.5 %collective-permute-start.51 = (f32[136,512]{1,0:T(8,128)S(1)}, f32[136,512]{1,0:T(8,128)S(1)}, u32[]{:S(2)}, u32[]{:S(2)}) collective-permute-start(f32[136,512]{1,0:T(8,128)S(1)} %get-tuple-element.193.refs_3_), channel_id=1, source_target_pairs={{0,2},{2,0},{4,6},{6,4},{1,3},{3,1},{5,7},{7,5},{8,10},{10,8},{12,... | collective-permute-start | bytes 835592 | tf_op jit(solution)/shard_map/ppermute | solution.py:565
  200.9 8.4 %collective-permute-start.50 = (f32[128,512]{1,0:T(8,128)S(1)}, f32[128,512]{1,0:T(8,128)S(1)}, u32[]{:S(2)}, u32[]{:S(2)}) collective-permute-start(f32[128,512]{1,0:T(8,128)S(1)} %shard_map.220.refs_4_.refs_1_), channel_id=1, source_target_pairs={{0,0},{2,4},{4,2},{6,6},{1,1},{3,5},{5,3},{7,7},{8,8},{10,12},{12,... | collective-permute-start | bytes 786440 | tf_op jit(solution)/shard_map/ppermute | solution.py:568
  201.7 14.5 %collective-permute-start.53 = (f32[128,640]{1,0:T(8,128)S(1)}, f32[128,640]{1,0:T(8,128)S(1)}, u32[]{:S(2)}, u32[]{:S(2)}) collective-permute-start(f32[128,640]{1,0:T(8,128)S(1)} %get-tuple-element.194.refs_3_), channel_id=1, source_target_pairs={{0,2},{2,0},{4,6},{6,4},{1,3},{3,1},{5,7},{7,5},{8,10},{10,8},{12,... | collective-permute-start | bytes 983048 | tf_op jit(solution)/shard_map/ppermute | solution.py:565
  208.6 8.3 %collective-permute-start.54 = (f32[128,512]{1,0:T(8,128)S(1)}, f32[128,512]{1,0:T(8,128)S(1)}, u32[]{:S(2)}, u32[]{:S(2)}) collective-permute-start(f32[128,512]{1,0:T(8,128)S(1)} %shard_map.223.refs_4_.refs_0_), channel_id=1, source_target_pairs={{0,0},{2,4},{4,2},{6,6},{1,1},{3,5},{5,3},{7,7},{8,8},{10,12},{12,... | collective-permute-start | bytes 786440 | tf_op jit(solution)/shard_map/ppermute | solution.py:568
  209.4 12.7 %collective-permute-start.52 = (f32[128,512]{1,0:T(8,128)S(1)}, f32[128,512]{1,0:T(8,128)S(1)}, u32[]{:S(2)}, u32[]{:S(2)}) collective-permute-start(f32[128,512]{1,0:T(8,128)S(1)} %get-tuple-element.195.refs_5_), channel_id=1, source_target_pairs={{0,2},{2,0},{4,6},{6,4},{1,3},{3,1},{5,7},{7,5},{8,10},{10,8},{12,... | collective-permute-start | bytes 786440 | tf_op jit(solution)/shard_map/ppermute | solution.py:565
  217.0 12.3 %collective-permute-start.56 = (f32[128,512]{1,0:T(8,128)S(1)}, f32[128,512]{1,0:T(8,128)S(1)}, u32[]{:S(2)}, u32[]{:S(2)}) collective-permute-start(f32[128,512]{1,0:T(8,128)S(1)} %shard_map.227.refs_7_.refs_3_), channel_id=1, source_target_pairs={{0,2},{2,0},{4,6},{6,4},{1,3},{3,1},{5,7},{7,5},{8,10},{10,8},{12,... | collective-permute-start | bytes 786440 | tf_op jit(solution)/shard_map/ppermute | solution.py:565
  223.1 11.4 %collective-permute-start.59 = (f32[128,640]{1,0:T(8,128)S(1)}, f32[128,640]{1,0:T(8,128)S(1)}, u32[]{:S(2)}, u32[]{:S(2)}) collective-permute-start(f32[128,640]{1,0:T(8,128)S(1)} %shard_map.230.refs_7_.refs_3_), channel_id=1, source_target_pairs={{0,2},{2,0},{4,6},{6,4},{1,3},{3,1},{5,7},{7,5},{8,10},{10,8},{12,... | collective-permute-start | bytes 983048 | tf_op jit(solution)/shard_map/ppermute | solution.py:565
  258.2 10.7 %collective-permute-start.65 = (f32[128,640]{1,0:T(8,128)S(1)}, f32[128,640]{1,0:T(8,128)S(1)}, u32[]{:S(2)}, u32[]{:S(2)}) collective-permute-start(f32[128,640]{1,0:T(8,128)S(1)} %shard_map.239.refs_2_.refs_0_), channel_id=1, source_target_pairs={{0,2},{2,0},{4,6},{6,4},{1,3},{3,1},{5,7},{7,5},{8,10},{10,8},{12,... | collective-permute-start | bytes 983048 | tf_op jit(solution)/shard_map/ppermute | solution.py:565
  260.1 9.6 %collective-permute-start.67 = (f32[136,256]{1,0:T(8,128)S(1)}, f32[136,256]{1,0:T(8,128)S(1)}, u32[]{:S(2)}, u32[]{:S(2)}) collective-permute-start(f32[136,256]{1,0:T(8,128)S(1)} %shard_map.240.refs_3_.refs_1_), channel_id=1, source_target_pairs={{0,0},{2,4},{4,2},{6,6},{1,1},{3,5},{5,3},{7,7},{8,8},{10,12},{12,... | collective-permute-start | bytes 417800 | tf_op jit(solution)/shard_map/ppermute | solution.py:568
  261.0 13.5 %collective-permute-start.68 = (f32[128,512]{1,0:T(8,128)S(1)}, f32[128,512]{1,0:T(8,128)S(1)}, u32[]{:S(2)}, u32[]{:S(2)}) collective-permute-start(f32[128,512]{1,0:T(8,128)S(1)} %shard_map.241.refs_3_.refs_0_), channel_id=1, source_target_pairs={{0,2},{2,0},{4,6},{6,4},{1,3},{3,1},{5,7},{7,5},{8,10},{10,8},{12,... | collective-permute-start | bytes 786440 | tf_op jit(solution)/shard_map/ppermute | solution.py:565
  269.7 12.5 %collective-permute-start.70 = (f32[136,512]{1,0:T(8,128)S(1)}, f32[136,512]{1,0:T(8,128)S(1)}, u32[]{:S(2)}, u32[]{:S(2)}) collective-permute-start(f32[136,512]{1,0:T(8,128)S(1)} %get-tuple-element.218.refs_3_), channel_id=1, source_target_pairs={{0,2},{2,0},{4,6},{6,4},{1,3},{3,1},{5,7},{7,5},{8,10},{10,8},{12,... | collective-permute-start | bytes 835592 | tf_op jit(solution)/shard_map/ppermute | solution.py:565
  274.6 8.4 %collective-permute-start.69 = (f32[128,512]{1,0:T(8,128)S(1)}, f32[128,512]{1,0:T(8,128)S(1)}, u32[]{:S(2)}, u32[]{:S(2)}) collective-permute-start(f32[128,512]{1,0:T(8,128)S(1)} %shard_map.246.refs_4_.refs_1_), channel_id=1, source_target_pairs={{0,0},{2,4},{4,2},{6,6},{1,1},{3,5},{5,3},{7,7},{8,8},{10,12},{12,... | collective-permute-start | bytes 786440 | tf_op jit(solution)/shard_map/ppermute | solution.py:568
  275.4 14.5 %collective-permute-start.72 = (f32[128,640]{1,0:T(8,128)S(1)}, f32[128,640]{1,0:T(8,128)S(1)}, u32[]{:S(2)}, u32[]{:S(2)}) collective-permute-start(f32[128,640]{1,0:T(8,128)S(1)} %get-tuple-element.219.refs_3_), channel_id=1, source_target_pairs={{0,2},{2,0},{4,6},{6,4},{1,3},{3,1},{5,7},{7,5},{8,10},{10,8},{12,... | collective-permute-start | bytes 983048 | tf_op jit(solution)/shard_map/ppermute | solution.py:565
  282.3 8.3 %collective-permute-start.73 = (f32[128,512]{1,0:T(8,128)S(1)}, f32[128,512]{1,0:T(8,128)S(1)}, u32[]{:S(2)}, u32[]{:S(2)}) collective-permute-start(f32[128,512]{1,0:T(8,128)S(1)} %shard_map.249.refs_4_.refs_0_), channel_id=1, source_target_pairs={{0,0},{2,4},{4,2},{6,6},{1,1},{3,5},{5,3},{7,7},{8,8},{10,12},{12,... | collective-permute-start | bytes 786440 | tf_op jit(solution)/shard_map/ppermute | solution.py:568
  283.1 12.7 %collective-permute-start.71 = (f32[128,512]{1,0:T(8,128)S(1)}, f32[128,512]{1,0:T(8,128)S(1)}, u32[]{:S(2)}, u32[]{:S(2)}) collective-permute-start(f32[128,512]{1,0:T(8,128)S(1)} %get-tuple-element.220.refs_5_), channel_id=1, source_target_pairs={{0,2},{2,0},{4,6},{6,4},{1,3},{3,1},{5,7},{7,5},{8,10},{10,8},{12,... | collective-permute-start | bytes 786440 | tf_op jit(solution)/shard_map/ppermute | solution.py:565
  290.7 12.3 %collective-permute-start.75 = (f32[128,512]{1,0:T(8,128)S(1)}, f32[128,512]{1,0:T(8,128)S(1)}, u32[]{:S(2)}, u32[]{:S(2)}) collective-permute-start(f32[128,512]{1,0:T(8,128)S(1)} %shard_map.253.refs_7_.refs_3_), channel_id=1, source_target_pairs={{0,2},{2,0},{4,6},{6,4},{1,3},{3,1},{5,7},{7,5},{8,10},{10,8},{12,... | collective-permute-start | bytes 786440 | tf_op jit(solution)/shard_map/ppermute | solution.py:565
  296.6 11.6 %collective-permute-start.78 = (f32[128,640]{1,0:T(8,128)S(1)}, f32[128,640]{1,0:T(8,128)S(1)}, u32[]{:S(2)}, u32[]{:S(2)}) collective-permute-start(f32[128,640]{1,0:T(8,128)S(1)} %shard_map.256.refs_7_.refs_3_), channel_id=1, source_target_pairs={{0,2},{2,0},{4,6},{6,4},{1,3},{3,1},{5,7},{7,5},{8,10},{10,8},{12,... | collective-permute-start | bytes 983048 | tf_op jit(solution)/shard_map/ppermute | solution.py:565
  (67 other events, 296.2 us)

commit v3 on v0

--- a/solution.py
+++ b/solution.py
@@ -62,7 +62,7 @@
     return (column <= row) & (column < limit)
 
 
-def split_kernel(core_ref, w_ref, *refs):
+def split_kernel(core_ref, w_ref, token_ref, *refs):
     own_refs, other_refs = refs[:CHUNKS], refs[CHUNKS : 2 * CHUNKS]
     landed, own_sem, other_sem = refs[2 * CHUNKS :]
     cols = own_refs[0].shape[1]
@@ -92,12 +92,12 @@
         own_copy(k).wait()
 
 
-def split(core, w_out):
+def split(core, w_out, token):
     inner, width = w_out.shape
     cols = width // 2 // CHUNKS
     out = pl.pallas_call(
         split_kernel,
-        in_specs=[SMEM, pl.BlockSpec(memory_space=pltpu.HBM)],
+        in_specs=[SMEM, pl.BlockSpec(memory_space=pltpu.HBM), token_spec()],
         out_specs=[VMEM] * (2 * CHUNKS),
         out_shape=[jax.ShapeDtypeStruct((inner, cols), BF16)] * CHUNKS
         + [jax.ShapeDtypeStruct((inner, cols), F32)] * CHUNKS,
@@ -107,20 +107,47 @@
             pltpu.SemaphoreType.DMA((CHUNKS,)),
         ],
         compiler_params=pltpu.CompilerParams(vmem_limit_bytes=LIMIT),
-    )(core, w_out)
+    )(core, w_out, token)
     return out[:CHUNKS], out[CHUNKS:]
 
 
+def norm_kernel(x_ref, gain_ref, bias_ref, out_ref):
+    length, width = x_ref.shape
+    blocks = [slice(i, i + DEPTH) for i in range(0, width, DEPTH)]
+    total = jnp.zeros((length, 1), F32)
+    for block in blocks:
+        total = total + jnp.sum(x_ref[:, block].astype(F32), axis=-1, keepdims=True)
+    mean = total / width
+    total = jnp.zeros((length, 1), F32)
+    for block in blocks:
+        centred = x_ref[:, block].astype(F32) - mean
+        total = total + jnp.sum(centred * centred, axis=-1, keepdims=True)
+    spread = lax.rsqrt(total / width + EPS)
+    for block in blocks:
+        centred = x_ref[:, block].astype(F32) - mean
+        full = centred * spread * gain_ref[:, block] + bias_ref[:, block]
+        out_ref[:, block] = full.astype(BF16)
+
+
+def layer_norm(x, gain, bias):
+    return pl.pallas_call(
+        norm_kernel,
+        in_specs=[VMEM] * 3,
+        out_specs=VMEM,
+        out_shape=jax.ShapeDtypeStruct(x.shape, BF16),
+        compiler_params=pltpu.CompilerParams(vmem_limit_bytes=LIMIT),
+        cost_estimate=STEP_COST,
+    )(x, gain[None], bias[None])
+
+
 def project_kernel(
-    limit_ref, x_ref, wq_ref, wk_ref, wv_ref, gain_ref, bias_ref, aq_ref, av_ref, bq_ref, bv_ref,
+    limit_ref, normed, wq_ref, wk_ref, wv_ref, aq_ref, av_ref, bq_ref, bv_ref,
     soft_ref, key_ref, value_ref, down_q_ref, down_v_ref, mixed_ref,
-    rows_in, normed, wq_in, wk_in, wv_in, rows_sem, weight_sem,
+    wq_in, wk_in, wv_in, weight_sem,
 ):
     length, width = normed.shape
     inner = key_ref.shape[1]
     blocks = [slice(i, i + DEPTH) for i in range(0, width, DEPTH)]
-    rows_copy = pltpu.make_async_copy(x_ref, rows_in, rows_sem)
-    rows_copy.start()
     copies = []
     for i, block in enumerate(blocks):
         for j, (source, target) in enumerate(
@@ -132,20 +159,6 @@
                 )
             )
             copies[-1].start()
-    rows_copy.wait()
-    total = jnp.zeros((length, 1), F32)
-    for block in blocks:
-        total = total + jnp.sum(rows_in[:, block].astype(F32), axis=-1, keepdims=True)
-    mean = total / width
-    total = jnp.zeros((length, 1), F32)
-    for block in blocks:
-        centred = rows_in[:, block].astype(F32) - mean
-        total = total + jnp.sum(centred * centred, axis=-1, keepdims=True)
-    spread = lax.rsqrt(total / width + EPS)
-    for block in blocks:
-        centred = rows_in[:, block].astype(F32) - mean
-        full = centred * spread * gain_ref[:, block] + bias_ref[:, block]
-        normed[:, block] = full.astype(BF16)
     query = jnp.zeros((length, inner), F32)
     key = jnp.zeros((length, inner), F32)
     value = jnp.zeros((length, inner), F32)
@@ -179,15 +192,15 @@
     mixed_ref[length:] = jnp.zeros((8, inner), F32)
 
 
-def project(limit, x, gain, bias, wq, wk, wv, aq, av, bq, bv):
-    length, width = x.shape
+def project(limit, normed, wq, wk, wv, aq, av, bq, bv):
+    length, width = normed.shape
     inner = wq.shape[1]
     rank = aq.shape[1]
     heads = inner // HEAD_DIM
     hbm = pl.BlockSpec(memory_space=pltpu.HBM)
     return pl.pallas_call(
         project_kernel,
-        in_specs=[SMEM] + [hbm] * 4 + [VMEM] * 6,
+        in_specs=[SMEM, VMEM] + [hbm] * 3 + [VMEM] * 4,
         out_specs=[VMEM] * 6,
         out_shape=[
             jax.ShapeDtypeStruct((heads, length, length), F32),
@@ -198,19 +211,16 @@
             jax.ShapeDtypeStruct((length + 8, inner), F32),
         ],
         scratch_shapes=[
-            pltpu.VMEM((length, width), BF16),
-            pltpu.VMEM((length, width), BF16),
             pltpu.VMEM((width, inner), BF16),
             pltpu.VMEM((width, inner), BF16),
             pltpu.VMEM((width, inner), BF16),
-            pltpu.SemaphoreType.DMA,
             pltpu.SemaphoreType.DMA((3 * (width // DEPTH),)),
         ],
         compiler_params=pltpu.CompilerParams(vmem_limit_bytes=STREAM_LIMIT),
         cost_estimate=pl.CostEstimate(
             flops=6 * length * width * inner, bytes_accessed=6 * width * inner, transcendentals=0
         ),
-    )(limit, x, wq, wk, wv, gain[None], bias[None], aq.T, av.T, bq, bv)
+    )(limit, normed, wq, wk, wv, aq.T, av.T, bq, bv)
 
 
 def token_spec():
@@ -523,15 +533,16 @@
         return [part, lax.ppermute(part, "dp", [(d, d ^ step) for d in range(n_dp)])]
 
     where = core.astype(jnp.int32)[None]
-    own_w, other_w = split(where, w_out)
+    normed = layer_norm(inputs, ln_gain, ln_bias)
+    own_w, other_w = split(where, w_out, normed)
     other_w = [swap(part) for part in other_w]
     cols = half // CHUNKS
     gap = lax.dynamic_slice_in_dim(inputs, core * half, half, 1).astype(F32)
     gap = gap - lax.dynamic_slice_in_dim(targets, core * half, half, 1).astype(F32)
 
     soft, key, value, down_q, down_v, mixed = project(
-        lengths, inputs, ln_gain, ln_bias, query_weight, w_key, value_weight, down_query,
-        down_value, query_up_factor, value_up_factor,
+        lengths, normed, query_weight, w_key, value_weight, down_query, down_value,
+        query_up_factor, value_up_factor,
     )
     attention = (soft, key, value, down_q, down_v)
 
@@ -560,50 +571,51 @@
                 own_part[k] = spread(k, length, rows, got_rows, pairs[k], token)
             return own_part[k]
 
-        def finish(k, got):
+        def take_in(k, got):
+            nonlocal parts, scalars
             gap_part = gap[:, k * cols : (k + 1) * cols] if first else None
-            return gather(k, length, ends, got, total[k], pairs[k], parts, lengths, gap_part, token)
+            out = gather(k, length, ends, got, total[k], pairs[k], parts, lengths, gap_part, token)
+            parts = list(out[:2])
+            scalars = out[2] if k == 0 else scalars
+            return parts[0]
 
         if n_chip != 4:
             for k in range(CHUNKS):
                 token = begin(k)
             for k in range(CHUNKS):
                 total[k] = lax.psum(own_part[k], "chip")
-                out = finish(k, total[k])
-                parts, scalars = list(out[:2]), out[2] if k == 0 else scalars
+                token = take_in(k, total[k])
         else:
             for k in [0, 1, 2] if first else [0, *range(2, CHUNKS), 1]:
                 token = begin(k)
             for k in (0, 1):
                 outer[k] = outer_swap(own_part[k])
             for tick in range(CHUNKS + 3):
+                later = tick + 2
+                if tick == CHUNKS - 1:
+                    token = total[tick - 2] = add(own_part[tick - 2], inner[tick - 2], outer[tick])
+                    outer[later - 1] = outer_swap(token)
                 if tick < CHUNKS:
                     own_part[tick] = add(own_part[tick], outer[tick], token)
                     token = own_part[tick]
                     inner[tick] = inner_swap(token)
-                later = tick + 2
                 if tick == CHUNKS:
-                    out = finish(tick - 3, outer[tick])
-                    parts = list(out[:2])
-                    token = parts[0]
-                if 1 <= tick <= CHUNKS:
+                    token = take_in(tick - 3, outer[tick])
+                if tick == 0:
+                    outer[later] = outer_swap(own_part[later])
+                elif tick <= CHUNKS and later != CHUNKS:
                     k = tick - 1
                     if later < CHUNKS:
-                        total[k], sent = add_and_pick(
+                        total[k], token = add_and_pick(
                             own_part[k], inner[k], ends, own_part[later], token
                         )
                     else:
-                        total[k] = sent = add(own_part[k], inner[k], token)
-                    token = sent
-                    outer[later] = outer_swap(sent)
-                elif tick == 0:
-                    outer[later] = outer_swap(own_part[later])
+                        token = total[k] = add(own_part[k], inner[k], token)
+                    outer[later] = outer_swap(token)
                 if tick + 3 < CHUNKS and first:
                     token = begin(tick + 3)
                 if tick >= 3 and tick != CHUNKS:
-                    out = finish(tick - 3, outer[tick])
-                    parts, scalars = list(out[:2]), out[2] if tick == 3 else scalars
-                    token = parts[0]
+                    token = take_in(tick - 3, outer[tick])
         own, other = parts
         share = ADAPTER_SCALE / token_count
         part = cotangent(share, lengths, own, other, swap(other), attention)

time: 304 us -> 314 us (1.033)
  waiting for transfers between devices: 71.8 us -> 93 us
  starting transfers between devices: 173 us -> 155 us
  local copies, waits for them, and re-layouts: 5.26 us -> 12.4 us
    ppermute x36, waiting for transfers between devices: 38.6 us -> 59.8 us  [outer_swap(): return lax.ppermute(part, 'chip', [(0, 1), (1, 0), (2, 3), (3, 2)])]
    ppermute x36, starting transfers between devices: 140 us -> 123 us  [outer_swap(): return lax.ppermute(part, 'chip', [(0, 1), (1, 0), (2, 3), (3, 2)])]
    unnamed x56 -> x62, local copies, waits for them, and re-layouts: 5.14 us -> 12.3 us
    pallas_call x1 -> x2, Pallas kernels: 8.78 us -> 9.58 us  [the longest x1 8.06 us: project(): pl.pallas_call(project_kernel, in_specs=[SMEM, VMEM] + [hbm] * 3 + [VMEM]...]
  transfers between devices with their start and end apart: 82 -> 82, of which waited for: 33 -> 41; matrix products, arithmetic and copies ran while one was open for 0% -> 0% of each run, Pallas kernels for 12% -> 11%
where the time goes in v3:
time: 314 us; the launch traced here: 313 us
  starting transfers between devices  155 us (49%)
  waiting for transfers between devices  93 us (30%)
  Pallas kernels  49.7 us (16%)
  local copies, waits for them, and re-layouts  12.4 us (4%)
    ppermute x36, starting transfers between devices, outer_swap(): return lax.ppermute(part, 'chip', [(0, 1), (1, 0), (2, 3), (3, 2)])  123 us
    ppermute x36, waiting for transfers between devices, outer_swap(): return lax.ppermute(part, 'chip', [(0, 1), (1, 0), (2, 3), (3, 2)])  59.8 us
    pallas_call x96, Pallas kernels, call(): pl.pallas_call(body, in_specs=[SMEM] * len(scalars) + [VMEM] * len(ins) +...  28.4 us
    ppermute x24, starting transfers between devices, inner_swap(): return lax.ppermute(part, 'chip', [(0, 0), (1, 2), (2, 1), (3, 3)])  17.7 us
    unnamed x62, local copies, waits for them, and re-layouts  12.3 us
    ppermute x14, waiting for transfers between devices, swap(): return lax.ppermute(part, 'core', [(0, 1), (1, 0)])  11.2 us
    ppermute x4, waiting for transfers between devices, data_terms(): lax.ppermute(part, 'dp', [(d, d ^ step) for d in range(n_dp)])  11 us
    ppermute x4, waiting for transfers between devices, data_terms(): part = part + lax.ppermute(part, 'dp', [(d, d ^ step) for d in range(n_dp)])  10.9 us
  transfers between devices with their start and end apart: 82, of which 41 were waited for; matrix products, arithmetic and copies ran while one was open for 0% of the time, Pallas kernels for 11%

profile of v3, /device:TPU:0, one launch (start us, length us, event | category | flops | bytes accessed | tf_op | source)
XLA Modules:
  0.0 313.1 jit_solution(13914676707290233363)
XLA Ops:
  7.4 2.5 shard_map.158
  15.4 8.1 %shard_map.157 = (f32[3,128,128]{2,1,0:T(8,128)S(1)}, bf16[128,384]{1,0:T(8,128)(2,1)S(1)}, bf16[128,384]{1,0:T(8,128)(2,1)S(1)}, f32[128,16]{1,0:T(8,128)S(1)},...) custom-call(s32[1]{0:T(128)S(6)} %copy.17.limit_ref.refs_1_.refs_2_.refs_4_.refs_8_, ...), custom_call_target="tpu_custom_call" | custom-call | flops 1811939328 | bytes 14155776 | tf_op jit(solution)/shard_map/pallas_call | solution.py:201
  28.0 3.0 collective-permute-start.6
  35.9 2.6 collective-permute-done.6.refs_1_
  40.0 4.2 %collective-permute-start.11 = (f32[128,512]{1,0:T(8,128)}, f32[128,512]{1,0:T(8,128)S(1)}, u32[]{:S(2)}, u32[]{:S(2)}) collective-permute-start(f32[128,512]{1,0:T(8,128)} %copy-done.17), channel_id=1, source_target_pairs={{0,2},{2,0},{4,6},{6,4},{1,3},{3,1},{5,7},{7,5},{8,10},{10,8},{12,... | collective-permute-start | bytes 786440 | tf_op jit(solution)/shard_map/ppermute | solution.py:552
  60.2 4.0 %collective-permute-start.14 = (f32[128,512]{1,0:T(8,128)S(1)}, f32[128,512]{1,0:T(8,128)S(1)}, u32[]{:S(2)}, u32[]{:S(2)}) collective-permute-start(f32[128,512]{1,0:T(8,128)S(1)} %get-tuple-element.144.refs_6_), channel_id=1, source_target_pairs={{0,2},{2,0},{4,6},{6,4},{1,3},{3,1},{5,7},{7,5},{8,10},{10,8},{12,... | collective-permute-start | bytes 786440 | tf_op jit(solution)/shard_map/ppermute | solution.py:552
  71.9 6.0 %collective-permute-start.21 = (f32[128,512]{1,0:T(8,128)S(1)}, f32[128,512]{1,0:T(8,128)S(1)}, u32[]{:S(2)}, u32[]{:S(2)}) collective-permute-start(f32[128,512]{1,0:T(8,128)S(1)} %shard_map.177.refs_8_.refs_3_), channel_id=1, source_target_pairs={{0,2},{2,0},{4,6},{6,4},{1,3},{3,1},{5,7},{7,5},{8,10},{10,8},{12,... | collective-permute-start | bytes 786440 | tf_op jit(solution)/shard_map/ppermute | solution.py:552
  78.8 2.4 collective-permute-start.20
  81.1 3.7 %collective-permute-done.21.refs_2_ = f32[128,512]{1,0:T(8,128)S(1)} collective-permute-done((f32[128,512]{1,0:T(8,128)S(1)}, f32[128,512]{1,0:T(8,128)S(1)}, u32[]{:S(2)}, u32[]{:S(2)}) %collective-permute-start.21) | collective-permute-done | bytes 262176 | tf_op jit(solution)/shard_map/ppermute | solution.py:552
  85.2 2.6 collective-permute-done.20.refs_2_
  92.9 2.7 collective-permute-done.23
  97.2 2.7 collective-permute-done.24.refs_1_
  106.0 6.0 %collective-permute-done.27.refs_1_ = f32[136,512]{1,0:T(8,128)S(1)} collective-permute-done((f32[136,512]{1,0:T(8,128)S(1)}, f32[136,512]{1,0:T(8,128)S(1)}, u32[]{:S(2)}, u32[]{:S(2)}) %collective-permute-start.27) | collective-permute-done | bytes 278560 | tf_op jit(solution)/shard_map/ppermute | solution.py:552
  112.7 4.3 %collective-permute-start.26 = (f32[128,512]{1,0:T(8,128)S(1)}, f32[128,512]{1,0:T(8,128)S(1)}, u32[]{:S(2)}, u32[]{:S(2)}) collective-permute-start(f32[128,512]{1,0:T(8,128)S(1)} %shard_map.186.refs_3_.refs_0_), channel_id=1, source_target_pairs={{0,2},{2,0},{4,6},{6,4},{1,3},{3,1},{5,7},{7,5},{8,10},{10,8},{12,... | collective-permute-start | bytes 786440 | tf_op jit(solution)/shard_map/ppermute | solution.py:552
  118.4 5.0 %collective-permute-start.31 = (f32[136,512]{1,0:T(8,128)S(1)}, f32[136,512]{1,0:T(8,128)S(1)}, u32[]{:S(2)}, u32[]{:S(2)}) collective-permute-start(f32[136,512]{1,0:T(8,128)S(1)} %get-tuple-element.172.refs_2_), channel_id=1, source_target_pairs={{0,2},{2,0},{4,6},{6,4},{1,3},{3,1},{5,7},{7,5},{8,10},{10,8},{12,... | collective-permute-start | bytes 835592 | tf_op jit(solution)/shard_map/ppermute | solution.py:552
  124.3 5.7 %collective-permute-start.37 = (f32[128,512]{1,0:T(8,128)S(1)}, f32[128,512]{1,0:T(8,128)S(1)}, u32[]{:S(2)}, u32[]{:S(2)}) collective-permute-start(f32[128,512]{1,0:T(8,128)S(1)} %get-tuple-element.173.refs_2_), channel_id=1, source_target_pairs={{0,2},{2,0},{4,6},{6,4},{1,3},{3,1},{5,7},{7,5},{8,10},{10,8},{12,... | collective-permute-start | bytes 786440 | tf_op jit(solution)/shard_map/ppermute | solution.py:552
  130.8 5.2 %collective-permute-start.33 = (f32[128,512]{1,0:T(8,128)S(1)}, f32[128,512]{1,0:T(8,128)S(1)}, u32[]{:S(2)}, u32[]{:S(2)}) collective-permute-start(f32[128,512]{1,0:T(8,128)S(1)} %get-tuple-element.174.refs_5_), channel_id=1, source_target_pairs={{0,2},{2,0},{4,6},{6,4},{1,3},{3,1},{5,7},{7,5},{8,10},{10,8},{12,... | collective-permute-start | bytes 786440 | tf_op jit(solution)/shard_map/ppermute | solution.py:552
  137.6 2.9 collective-permute-done.33.refs_2_.refs_1_
  140.5 2.4 collective-permute-start.36
  143.6 5.0 %collective-permute-start.40 = (f32[128,512]{1,0:T(8,128)S(1)}, f32[128,512]{1,0:T(8,128)S(1)}, u32[]{:S(2)}, u32[]{:S(2)}) collective-permute-start(f32[128,512]{1,0:T(8,128)S(1)} %shard_map.203.refs_7_.refs_3_), channel_id=1, source_target_pairs={{0,2},{2,0},{4,6},{6,4},{1,3},{3,1},{5,7},{7,5},{8,10},{10,8},{12,... | collective-permute-start | bytes 786440 | tf_op jit(solution)/shard_map/ppermute | solution.py:552
  151.9 3.6 %collective-permute-done.40.refs_2_ = f32[128,512]{1,0:T(8,128)S(1)} collective-permute-done((f32[128,512]{1,0:T(8,128)S(1)}, f32[128,512]{1,0:T(8,128)S(1)}, u32[]{:S(2)}, u32[]{:S(2)}) %collective-permute-start.40) | collective-permute-done | bytes 262176 | tf_op jit(solution)/shard_map/ppermute | solution.py:552
  155.9 2.7 collective-permute-done.39.refs_2_
  163.5 2.7 collective-permute-done.42
  167.8 2.7 collective-permute-done.43.refs_1_
  176.8 6.0 %collective-permute-done.46.refs_1_ = f32[136,512]{1,0:T(8,128)S(1)} collective-permute-done((f32[136,512]{1,0:T(8,128)S(1)}, f32[136,512]{1,0:T(8,128)S(1)}, u32[]{:S(2)}, u32[]{:S(2)}) %collective-permute-start.46) | collective-permute-done | bytes 278560 | tf_op jit(solution)/shard_map/ppermute | solution.py:552
  183.4 4.4 %collective-permute-start.45 = (f32[128,512]{1,0:T(8,128)S(1)}, f32[128,512]{1,0:T(8,128)S(1)}, u32[]{:S(2)}, u32[]{:S(2)}) collective-permute-start(f32[128,512]{1,0:T(8,128)S(1)} %shard_map.212.refs_3_.refs_0_), channel_id=1, source_target_pairs={{0,2},{2,0},{4,6},{6,4},{1,3},{3,1},{5,7},{7,5},{8,10},{10,8},{12,... | collective-permute-start | bytes 786440 | tf_op jit(solution)/shard_map/ppermute | solution.py:552
  189.1 5.0 %collective-permute-start.50 = (f32[136,512]{1,0:T(8,128)S(1)}, f32[136,512]{1,0:T(8,128)S(1)}, u32[]{:S(2)}, u32[]{:S(2)}) collective-permute-start(f32[136,512]{1,0:T(8,128)S(1)} %get-tuple-element.193.refs_2_), channel_id=1, source_target_pairs={{0,2},{2,0},{4,6},{6,4},{1,3},{3,1},{5,7},{7,5},{8,10},{10,8},{12,... | collective-permute-start | bytes 835592 | tf_op jit(solution)/shard_map/ppermute | solution.py:552
  195.1 5.8 %collective-permute-start.56 = (f32[128,512]{1,0:T(8,128)S(1)}, f32[128,512]{1,0:T(8,128)S(1)}, u32[]{:S(2)}, u32[]{:S(2)}) collective-permute-start(f32[128,512]{1,0:T(8,128)S(1)} %get-tuple-element.194.refs_2_), channel_id=1, source_target_pairs={{0,2},{2,0},{4,6},{6,4},{1,3},{3,1},{5,7},{7,5},{8,10},{10,8},{12,... | collective-permute-start | bytes 786440 | tf_op jit(solution)/shard_map/ppermute | solution.py:552
  201.6 5.2 %collective-permute-start.52 = (f32[128,512]{1,0:T(8,128)S(1)}, f32[128,512]{1,0:T(8,128)S(1)}, u32[]{:S(2)}, u32[]{:S(2)}) collective-permute-start(f32[128,512]{1,0:T(8,128)S(1)} %get-tuple-element.195.refs_5_), channel_id=1, source_target_pairs={{0,2},{2,0},{4,6},{6,4},{1,3},{3,1},{5,7},{7,5},{8,10},{10,8},{12,... | collective-permute-start | bytes 786440 | tf_op jit(solution)/shard_map/ppermute | solution.py:552
  208.3 2.9 collective-permute-done.52.refs_2_.refs_1_
  211.3 2.4 collective-permute-start.55
  214.6 4.9 %collective-permute-start.59 = (f32[128,512]{1,0:T(8,128)S(1)}, f32[128,512]{1,0:T(8,128)S(1)}, u32[]{:S(2)}, u32[]{:S(2)}) collective-permute-start(f32[128,512]{1,0:T(8,128)S(1)} %shard_map.229.refs_7_.refs_3_), channel_id=1, source_target_pairs={{0,2},{2,0},{4,6},{6,4},{1,3},{3,1},{5,7},{7,5},{8,10},{10,8},{12,... | collective-permute-start | bytes 786440 | tf_op jit(solution)/shard_map/ppermute | solution.py:552
  222.8 3.6 %collective-permute-done.59.refs_2_ = f32[128,512]{1,0:T(8,128)S(1)} collective-permute-done((f32[128,512]{1,0:T(8,128)S(1)}, f32[128,512]{1,0:T(8,128)S(1)}, u32[]{:S(2)}, u32[]{:S(2)}) %collective-permute-start.59) | collective-permute-done | bytes 262176 | tf_op jit(solution)/shard_map/ppermute | solution.py:552
  226.7 2.8 collective-permute-done.58.refs_2_
  234.3 2.8 collective-permute-done.61
  238.7 2.7 collective-permute-done.62.refs_1_
  247.7 6.0 %collective-permute-done.65.refs_1_ = f32[136,512]{1,0:T(8,128)S(1)} collective-permute-done((f32[136,512]{1,0:T(8,128)S(1)}, f32[136,512]{1,0:T(8,128)S(1)}, u32[]{:S(2)}, u32[]{:S(2)}) %collective-permute-start.65) | collective-permute-done | bytes 278560 | tf_op jit(solution)/shard_map/ppermute | solution.py:552
  254.4 4.3 %collective-permute-start.64 = (f32[128,512]{1,0:T(8,128)S(1)}, f32[128,512]{1,0:T(8,128)S(1)}, u32[]{:S(2)}, u32[]{:S(2)}) collective-permute-start(f32[128,512]{1,0:T(8,128)S(1)} %shard_map.238.refs_3_.refs_0_), channel_id=1, source_target_pairs={{0,2},{2,0},{4,6},{6,4},{1,3},{3,1},{5,7},{7,5},{8,10},{10,8},{12,... | collective-permute-start | bytes 786440 | tf_op jit(solution)/shard_map/ppermute | solution.py:552
  260.1 5.0 %collective-permute-start.69 = (f32[136,512]{1,0:T(8,128)S(1)}, f32[136,512]{1,0:T(8,128)S(1)}, u32[]{:S(2)}, u32[]{:S(2)}) collective-permute-start(f32[136,512]{1,0:T(8,128)S(1)} %get-tuple-element.218.refs_2_), channel_id=1, source_target_pairs={{0,2},{2,0},{4,6},{6,4},{1,3},{3,1},{5,7},{7,5},{8,10},{10,8},{12,... | collective-permute-start | bytes 835592 | tf_op jit(solution)/shard_map/ppermute | solution.py:552
  266.1 5.6 %collective-permute-start.75 = (f32[128,512]{1,0:T(8,128)S(1)}, f32[128,512]{1,0:T(8,128)S(1)}, u32[]{:S(2)}, u32[]{:S(2)}) collective-permute-start(f32[128,512]{1,0:T(8,128)S(1)} %get-tuple-element.219.refs_2_), channel_id=1, source_target_pairs={{0,2},{2,0},{4,6},{6,4},{1,3},{3,1},{5,7},{7,5},{8,10},{10,8},{12,... | collective-permute-start | bytes 786440 | tf_op jit(solution)/shard_map/ppermute | solution.py:552
  272.5 5.3 %collective-permute-start.71 = (f32[128,512]{1,0:T(8,128)S(1)}, f32[128,512]{1,0:T(8,128)S(1)}, u32[]{:S(2)}, u32[]{:S(2)}) collective-permute-start(f32[128,512]{1,0:T(8,128)S(1)} %get-tuple-element.220.refs_5_), channel_id=1, source_target_pairs={{0,2},{2,0},{4,6},{6,4},{1,3},{3,1},{5,7},{7,5},{8,10},{10,8},{12,... | collective-permute-start | bytes 786440 | tf_op jit(solution)/shard_map/ppermute | solution.py:552
  279.3 2.9 collective-permute-done.71.refs_2_.refs_1_
  282.3 2.4 collective-permute-start.74
  285.4 5.0 %collective-permute-start.78 = (f32[128,512]{1,0:T(8,128)S(1)}, f32[128,512]{1,0:T(8,128)S(1)}, u32[]{:S(2)}, u32[]{:S(2)}) collective-permute-start(f32[128,512]{1,0:T(8,128)S(1)} %shard_map.255.refs_7_.refs_3_), channel_id=1, source_target_pairs={{0,2},{2,0},{4,6},{6,4},{1,3},{3,1},{5,7},{7,5},{8,10},{10,8},{12,... | collective-permute-start | bytes 786440 | tf_op jit(solution)/shard_map/ppermute | solution.py:552
  293.7 3.6 %collective-permute-done.78.refs_2_ = f32[128,512]{1,0:T(8,128)S(1)} collective-permute-done((f32[128,512]{1,0:T(8,128)S(1)}, f32[128,512]{1,0:T(8,128)S(1)}, u32[]{:S(2)}, u32[]{:S(2)}) %collective-permute-start.78) | collective-permute-done | bytes 262176 | tf_op jit(solution)/shard_map/ppermute | solution.py:552
  297.6 2.7 collective-permute-done.77.refs_2_
  305.4 2.7 collective-permute-done.80
  309.6 2.8 collective-permute-done.81.refs_1_
  (291 shorter events, 121.1 us)
Async XLA Ops:
  13.8 11.5 %collective-permute-start.3 = (f32[384,512]{1,0:T(8,128)}, f32[384,512]{1,0:T(8,128)}, u32[]{:S(2)}, u32[]{:S(2)}) collective-permute-start(f32[384,512]{1,0:T(8,128)} %get-tuple-element.129), channel_id=1, source_target_pairs={{0,1},{1,0},{2,3},{3,2},{4,5},{5,4},{6,7},{7,6},{8,9},{9,8},{10,11... | collective-permute-start | bytes 2359304 | tf_op jit(solution)/shard_map/ppermute | solution.py:526
  14.2 17.0 %collective-permute-start.2 = (f32[384,512]{1,0:T(8,128)}, f32[384,512]{1,0:T(8,128)}, u32[]{:S(2)}, u32[]{:S(2)}) collective-permute-start(f32[384,512]{1,0:T(8,128)} %get-tuple-element.127), channel_id=1, source_target_pairs={{0,1},{1,0},{2,3},{3,2},{4,5},{5,4},{6,7},{7,6},{8,9},{9,8},{10,11... | collective-permute-start | bytes 2359304 | tf_op jit(solution)/shard_map/ppermute | solution.py:526
  14.3 19.4 %collective-permute-start.7 = (f32[384,512]{1,0:T(8,128)S(1)}, f32[384,512]{1,0:T(8,128)S(1)}, u32[]{:S(2)}, u32[]{:S(2)}) collective-permute-start(f32[384,512]{1,0:T(8,128)S(1)} %get-tuple-element.135), channel_id=1, source_target_pairs={{0,1},{1,0},{2,3},{3,2},{4,5},{5,4},{6,7},{7,6},{8,9},{9,8},{10,11... | collective-permute-start | bytes 2359304 | tf_op jit(solution)/shard_map/ppermute | solution.py:526
  23.6 16.4 %collective-permute-start.5 = (f32[384,512]{1,0:T(8,128)}, f32[384,512]{1,0:T(8,128)}, u32[]{:S(2)}, u32[]{:S(2)}) collective-permute-start(f32[384,512]{1,0:T(8,128)} %get-tuple-element.133), channel_id=1, source_target_pairs={{0,1},{1,0},{2,3},{3,2},{4,5},{5,4},{6,7},{7,6},{8,9},{9,8},{10,11... | collective-permute-start | bytes 2359304 | tf_op jit(solution)/shard_map/ppermute | solution.py:526
  25.2 27.8 %collective-permute-start.9 = (f32[384,512]{1,0:T(8,128)}, f32[384,512]{1,0:T(8,128)}, u32[]{:S(2)}, u32[]{:S(2)}) collective-permute-start(f32[384,512]{1,0:T(8,128)} %get-tuple-element.139), channel_id=1, source_target_pairs={{0,1},{1,0},{2,3},{3,2},{4,5},{5,4},{6,7},{7,6},{8,9},{9,8},{10,11... | collective-permute-start | bytes 2359304 | tf_op jit(solution)/shard_map/ppermute | solution.py:526
  28.0 10.5 %collective-permute-start.6 = (f32[136,512]{1,0:T(8,128)S(1)}, f32[136,512]{1,0:T(8,128)S(1)}, u32[]{:S(2)}, u32[]{:S(2)}) collective-permute-start(f32[136,512]{1,0:T(8,128)S(1)} %get-tuple-element.130.refs_4_.refs_0_), channel_id=1, source_target_pairs={{0,2},{2,0},{4,6},{6,4},{1,3},{3,1},{5,7},{7,5},{8,10},{10,8},{12,... | collective-permute-start | bytes 835592 | tf_op jit(solution)/shard_map/ppermute | solution.py:552
  31.3 26.5 %collective-permute-start.1 = (f32[384,512]{1,0:T(8,128)S(1)}, f32[384,512]{1,0:T(8,128)}, u32[]{:S(2)}, u32[]{:S(2)}) collective-permute-start(f32[384,512]{1,0:T(8,128)S(1)} %get-tuple-element.125), channel_id=1, source_target_pairs={{0,1},{1,0},{2,3},{3,2},{4,5},{5,4},{6,7},{7,6},{8,9},{9,8},{10,11... | collective-permute-start | bytes 2359304 | tf_op jit(solution)/shard_map/ppermute | solution.py:526
  33.7 14.1 %collective-permute-start.4 = (f32[128,512]{1,0:T(8,128)}, f32[128,512]{1,0:T(8,128)}, u32[]{:S(2)}, u32[]{:S(2)}) collective-permute-start(f32[128,512]{1,0:T(8,128)} %get-tuple-element.131.refs_4_.refs_0_), channel_id=1, source_target_pairs={{0,2},{2,0},{4,6},{6,4},{1,3},{3,1},{5,7},{7,5},{8,10},{10,8},{12,... | collective-permute-start | bytes 786440 | tf_op jit(solution)/shard_map/ppermute | solution.py:552
  38.5 11.0 %collective-permute-start.10 = (f32[136,512]{1,0:T(8,128)S(1)}, f32[136,512]{1,0:T(8,128)}, u32[]{:S(2)}, u32[]{:S(2)}) collective-permute-start(f32[136,512]{1,0:T(8,128)S(1)} %shard_map.162.refs_4_.refs_1_), channel_id=1, source_target_pairs={{0,0},{2,4},{4,2},{6,6},{1,1},{3,5},{5,3},{7,7},{8,8},{10,12},{12,... | collective-permute-start | bytes 835592 | tf_op jit(solution)/shard_map/ppermute | solution.py:555
  40.0 14.5 %collective-permute-start.11 = (f32[128,512]{1,0:T(8,128)}, f32[128,512]{1,0:T(8,128)S(1)}, u32[]{:S(2)}, u32[]{:S(2)}) collective-permute-start(f32[128,512]{1,0:T(8,128)} %copy-done.17), channel_id=1, source_target_pairs={{0,2},{2,0},{4,6},{6,4},{1,3},{3,1},{5,7},{7,5},{8,10},{10,8},{12,... | collective-permute-start | bytes 786440 | tf_op jit(solution)/shard_map/ppermute | solution.py:552
  50.6 8.7 %collective-permute-start.13 = (f32[136,512]{1,0:T(8,128)S(1)}, f32[136,512]{1,0:T(8,128)S(1)}, u32[]{:S(2)}, u32[]{:S(2)}) collective-permute-start(f32[136,512]{1,0:T(8,128)S(1)} %get-tuple-element.140.refs_4_), channel_id=1, source_target_pairs={{0,2},{2,0},{4,6},{6,4},{1,3},{3,1},{5,7},{7,5},{8,10},{10,8},{12,... | collective-permute-start | bytes 835592 | tf_op jit(solution)/shard_map/ppermute | solution.py:552
  55.4 9.7 %collective-permute-start.18 = (f32[128,512]{1,0:T(8,128)S(1)}, f32[128,512]{1,0:T(8,128)S(1)}, u32[]{:S(2)}, u32[]{:S(2)}) collective-permute-start(f32[128,512]{1,0:T(8,128)S(1)} %get-tuple-element.142.refs_4_), channel_id=1, source_target_pairs={{0,2},{2,0},{4,6},{6,4},{1,3},{3,1},{5,7},{7,5},{8,10},{10,8},{12,... | collective-permute-start | bytes 786440 | tf_op jit(solution)/shard_map/ppermute | solution.py:552
  59.3 9.6 %collective-permute-start.15 = (f32[128,512]{1,0:T(8,128)S(1)}, f32[128,512]{1,0:T(8,128)S(1)}, u32[]{:S(2)}, u32[]{:S(2)}) collective-permute-start(f32[128,512]{1,0:T(8,128)S(1)} %shard_map.170.refs_4_.refs_0_), channel_id=1, source_target_pairs={{0,0},{2,4},{4,2},{6,6},{1,1},{3,5},{5,3},{7,7},{8,8},{10,12},{12,... | collective-permute-start | bytes 786440 | tf_op jit(solution)/shard_map/ppermute | solution.py:555
  60.2 8.7 %collective-permute-start.14 = (f32[128,512]{1,0:T(8,128)S(1)}, f32[128,512]{1,0:T(8,128)S(1)}, u32[]{:S(2)}, u32[]{:S(2)}) collective-permute-start(f32[128,512]{1,0:T(8,128)S(1)} %get-tuple-element.144.refs_6_), channel_id=1, source_target_pairs={{0,2},{2,0},{4,6},{6,4},{1,3},{3,1},{5,7},{7,5},{8,10},{10,8},{12,... | collective-permute-start | bytes 786440 | tf_op jit(solution)/shard_map/ppermute | solution.py:552
  69.0 9.3 %collective-permute-start.17 = (f32[128,512]{1,0:T(8,128)S(1)}, f32[128,512]{1,0:T(8,128)S(1)}, u32[]{:S(2)}, u32[]{:S(2)}) collective-permute-start(f32[128,512]{1,0:T(8,128)S(1)} %shard_map.172.refs_2_.refs_3_), channel_id=1, source_target_pairs={{0,2},{2,0},{4,6},{6,4},{1,3},{3,1},{5,7},{7,5},{8,10},{10,8},{12,... | collective-permute-start | bytes 786440 | tf_op jit(solution)/shard_map/ppermute | solution.py:552
  70.9 7.8 %collective-permute-start.16 = (f32[128,512]{1,0:T(8,128)S(1)}, f32[128,512]{1,0:T(8,128)S(1)}, u32[]{:S(2)}, u32[]{:S(2)}) collective-permute-start(f32[128,512]{1,0:T(8,128)S(1)} %shard_map.173.refs_2_.refs_0_), channel_id=1, source_target_pairs={{0,0},{2,4},{4,2},{6,6},{1,1},{3,5},{5,3},{7,7},{8,8},{10,12},{12,... | collective-permute-start | bytes 786440 | tf_op jit(solution)/shard_map/ppermute | solution.py:555
  71.9 12.9 %collective-permute-start.21 = (f32[128,512]{1,0:T(8,128)S(1)}, f32[128,512]{1,0:T(8,128)S(1)}, u32[]{:S(2)}, u32[]{:S(2)}) collective-permute-start(f32[128,512]{1,0:T(8,128)S(1)} %shard_map.177.refs_8_.refs_3_), channel_id=1, source_target_pairs={{0,2},{2,0},{4,6},{6,4},{1,3},{3,1},{5,7},{7,5},{8,10},{10,8},{12,... | collective-permute-start | bytes 786440 | tf_op jit(solution)/shard_map/ppermute | solution.py:552
  78.8 9.1 %collective-permute-start.20 = (f32[128,512]{1,0:T(8,128)S(1)}, f32[128,512]{1,0:T(8,128)S(1)}, u32[]{:S(2)}, u32[]{:S(2)}) collective-permute-start(f32[128,512]{1,0:T(8,128)S(1)} %shard_map.180.refs_8_.refs_3_), channel_id=1, source_target_pairs={{0,2},{2,0},{4,6},{6,4},{1,3},{3,1},{5,7},{7,5},{8,10},{10,8},{12,... | collective-permute-start | bytes 786440 | tf_op jit(solution)/shard_map/ppermute | solution.py:552
  102.4 9.5 %collective-permute-start.27 = (f32[136,512]{1,0:T(8,128)S(1)}, f32[136,512]{1,0:T(8,128)S(1)}, u32[]{:S(2)}, u32[]{:S(2)}) collective-permute-start(f32[136,512]{1,0:T(8,128)S(1)} %shard_map.185.refs_3_.refs_0_), channel_id=1, source_target_pairs={{0,2},{2,0},{4,6},{6,4},{1,3},{3,1},{5,7},{7,5},{8,10},{10,8},{12,... | collective-permute-start | bytes 835592 | tf_op jit(solution)/shard_map/ppermute | solution.py:552
  105.8 11.7 %collective-permute-start.29 = (f32[128,512]{1,0:T(8,128)S(1)}, f32[128,512]{1,0:T(8,128)S(1)}, u32[]{:S(2)}, u32[]{:S(2)}) collective-permute-start(f32[128,512]{1,0:T(8,128)S(1)} %shard_map.190.refs_2_.refs_0_), channel_id=1, source_target_pairs={{0,2},{2,0},{4,6},{6,4},{1,3},{3,1},{5,7},{7,5},{8,10},{10,8},{12,... | collective-permute-start | bytes 786440 | tf_op jit(solution)/shard_map/ppermute | solution.py:552
  112.7 10.8 %collective-permute-start.26 = (f32[128,512]{1,0:T(8,128)S(1)}, f32[128,512]{1,0:T(8,128)S(1)}, u32[]{:S(2)}, u32[]{:S(2)}) collective-permute-start(f32[128,512]{1,0:T(8,128)S(1)} %shard_map.186.refs_3_.refs_0_), channel_id=1, source_target_pairs={{0,2},{2,0},{4,6},{6,4},{1,3},{3,1},{5,7},{7,5},{8,10},{10,8},{12,... | collective-permute-start | bytes 786440 | tf_op jit(solution)/shard_map/ppermute | solution.py:552
  118.4 11.6 %collective-permute-start.31 = (f32[136,512]{1,0:T(8,128)S(1)}, f32[136,512]{1,0:T(8,128)S(1)}, u32[]{:S(2)}, u32[]{:S(2)}) collective-permute-start(f32[136,512]{1,0:T(8,128)S(1)} %get-tuple-element.172.refs_2_), channel_id=1, source_target_pairs={{0,2},{2,0},{4,6},{6,4},{1,3},{3,1},{5,7},{7,5},{8,10},{10,8},{12,... | collective-permute-start | bytes 835592 | tf_op jit(solution)/shard_map/ppermute | solution.py:552
  124.3 12.2 %collective-permute-start.37 = (f32[128,512]{1,0:T(8,128)S(1)}, f32[128,512]{1,0:T(8,128)S(1)}, u32[]{:S(2)}, u32[]{:S(2)}) collective-permute-start(f32[128,512]{1,0:T(8,128)S(1)} %get-tuple-element.173.refs_2_), channel_id=1, source_target_pairs={{0,2},{2,0},{4,6},{6,4},{1,3},{3,1},{5,7},{7,5},{8,10},{10,8},{12,... | collective-permute-start | bytes 786440 | tf_op jit(solution)/shard_map/ppermute | solution.py:552
  130.0 10.4 %collective-permute-start.34 = (f32[128,512]{1,0:T(8,128)S(1)}, f32[128,512]{1,0:T(8,128)S(1)}, u32[]{:S(2)}, u32[]{:S(2)}) collective-permute-start(f32[128,512]{1,0:T(8,128)S(1)} %shard_map.196.refs_4_.refs_0_), channel_id=1, source_target_pairs={{0,0},{2,4},{4,2},{6,6},{1,1},{3,5},{5,3},{7,7},{8,8},{10,12},{12,... | collective-permute-start | bytes 786440 | tf_op jit(solution)/shard_map/ppermute | solution.py:555
  130.8 9.7 %collective-permute-start.33 = (f32[128,512]{1,0:T(8,128)S(1)}, f32[128,512]{1,0:T(8,128)S(1)}, u32[]{:S(2)}, u32[]{:S(2)}) collective-permute-start(f32[128,512]{1,0:T(8,128)S(1)} %get-tuple-element.174.refs_5_), channel_id=1, source_target_pairs={{0,2},{2,0},{4,6},{6,4},{1,3},{3,1},{5,7},{7,5},{8,10},{10,8},{12,... | collective-permute-start | bytes 786440 | tf_op jit(solution)/shard_map/ppermute | solution.py:552
  140.5 8.8 %collective-permute-start.36 = (f32[128,512]{1,0:T(8,128)S(1)}, f32[128,512]{1,0:T(8,128)S(1)}, u32[]{:S(2)}, u32[]{:S(2)}) collective-permute-start(f32[128,512]{1,0:T(8,128)S(1)} %shard_map.198.refs_2_.refs_3_), channel_id=1, source_target_pairs={{0,2},{2,0},{4,6},{6,4},{1,3},{3,1},{5,7},{7,5},{8,10},{10,8},{12,... | collective-permute-start | bytes 786440 | tf_op jit(solution)/shard_map/ppermute | solution.py:552
  143.6 11.8 %collective-permute-start.40 = (f32[128,512]{1,0:T(8,128)S(1)}, f32[128,512]{1,0:T(8,128)S(1)}, u32[]{:S(2)}, u32[]{:S(2)}) collective-permute-start(f32[128,512]{1,0:T(8,128)S(1)} %shard_map.203.refs_7_.refs_3_), channel_id=1, source_target_pairs={{0,2},{2,0},{4,6},{6,4},{1,3},{3,1},{5,7},{7,5},{8,10},{10,8},{12,... | collective-permute-start | bytes 786440 | tf_op jit(solution)/shard_map/ppermute | solution.py:552
  149.7 8.8 %collective-permute-start.39 = (f32[128,512]{1,0:T(8,128)S(1)}, f32[128,512]{1,0:T(8,128)S(1)}, u32[]{:S(2)}, u32[]{:S(2)}) collective-permute-start(f32[128,512]{1,0:T(8,128)S(1)} %shard_map.206.refs_7_.refs_3_), channel_id=1, source_target_pairs={{0,2},{2,0},{4,6},{6,4},{1,3},{3,1},{5,7},{7,5},{8,10},{10,8},{12,... | collective-permute-start | bytes 786440 | tf_op jit(solution)/shard_map/ppermute | solution.py:552
  173.2 9.5 %collective-permute-start.46 = (f32[136,512]{1,0:T(8,128)S(1)}, f32[136,512]{1,0:T(8,128)S(1)}, u32[]{:S(2)}, u32[]{:S(2)}) collective-permute-start(f32[136,512]{1,0:T(8,128)S(1)} %shard_map.211.refs_3_.refs_0_), channel_id=1, source_target_pairs={{0,2},{2,0},{4,6},{6,4},{1,3},{3,1},{5,7},{7,5},{8,10},{10,8},{12,... | collective-permute-start | bytes 835592 | tf_op jit(solution)/shard_map/ppermute | solution.py:552
  176.7 11.7 %collective-permute-start.48 = (f32[128,512]{1,0:T(8,128)S(1)}, f32[128,512]{1,0:T(8,128)S(1)}, u32[]{:S(2)}, u32[]{:S(2)}) collective-permute-start(f32[128,512]{1,0:T(8,128)S(1)} %shard_map.216.refs_2_.refs_0_), channel_id=1, source_target_pairs={{0,2},{2,0},{4,6},{6,4},{1,3},{3,1},{5,7},{7,5},{8,10},{10,8},{12,... | collective-permute-start | bytes 786440 | tf_op jit(solution)/shard_map/ppermute | solution.py:552
  183.4 10.9 %collective-permute-start.45 = (f32[128,512]{1,0:T(8,128)S(1)}, f32[128,512]{1,0:T(8,128)S(1)}, u32[]{:S(2)}, u32[]{:S(2)}) collective-permute-start(f32[128,512]{1,0:T(8,128)S(1)} %shard_map.212.refs_3_.refs_0_), channel_id=1, source_target_pairs={{0,2},{2,0},{4,6},{6,4},{1,3},{3,1},{5,7},{7,5},{8,10},{10,8},{12,... | collective-permute-start | bytes 786440 | tf_op jit(solution)/shard_map/ppermute | solution.py:552
  189.1 11.7 %collective-permute-start.50 = (f32[136,512]{1,0:T(8,128)S(1)}, f32[136,512]{1,0:T(8,128)S(1)}, u32[]{:S(2)}, u32[]{:S(2)}) collective-permute-start(f32[136,512]{1,0:T(8,128)S(1)} %get-tuple-element.193.refs_2_), channel_id=1, source_target_pairs={{0,2},{2,0},{4,6},{6,4},{1,3},{3,1},{5,7},{7,5},{8,10},{10,8},{12,... | collective-permute-start | bytes 835592 | tf_op jit(solution)/shard_map/ppermute | solution.py:552
  195.1 12.1 %collective-permute-start.56 = (f32[128,512]{1,0:T(8,128)S(1)}, f32[128,512]{1,0:T(8,128)S(1)}, u32[]{:S(2)}, u32[]{:S(2)}) collective-permute-start(f32[128,512]{1,0:T(8,128)S(1)} %get-tuple-element.194.refs_2_), channel_id=1, source_target_pairs={{0,2},{2,0},{4,6},{6,4},{1,3},{3,1},{5,7},{7,5},{8,10},{10,8},{12,... | collective-permute-start | bytes 786440 | tf_op jit(solution)/shard_map/ppermute | solution.py:552
  200.9 10.3 %collective-permute-start.53 = (f32[128,512]{1,0:T(8,128)S(1)}, f32[128,512]{1,0:T(8,128)S(1)}, u32[]{:S(2)}, u32[]{:S(2)}) collective-permute-start(f32[128,512]{1,0:T(8,128)S(1)} %shard_map.222.refs_4_.refs_0_), channel_id=1, source_target_pairs={{0,0},{2,4},{4,2},{6,6},{1,1},{3,5},{5,3},{7,7},{8,8},{10,12},{12,... | collective-permute-start | bytes 786440 | tf_op jit(solution)/shard_map/ppermute | solution.py:555
  201.6 9.6 %collective-permute-start.52 = (f32[128,512]{1,0:T(8,128)S(1)}, f32[128,512]{1,0:T(8,128)S(1)}, u32[]{:S(2)}, u32[]{:S(2)}) collective-permute-start(f32[128,512]{1,0:T(8,128)S(1)} %get-tuple-element.195.refs_5_), channel_id=1, source_target_pairs={{0,2},{2,0},{4,6},{6,4},{1,3},{3,1},{5,7},{7,5},{8,10},{10,8},{12,... | collective-permute-start | bytes 786440 | tf_op jit(solution)/shard_map/ppermute | solution.py:552
  211.3 8.9 %collective-permute-start.55 = (f32[128,512]{1,0:T(8,128)S(1)}, f32[128,512]{1,0:T(8,128)S(1)}, u32[]{:S(2)}, u32[]{:S(2)}) collective-permute-start(f32[128,512]{1,0:T(8,128)S(1)} %shard_map.224.refs_2_.refs_3_), channel_id=1, source_target_pairs={{0,2},{2,0},{4,6},{6,4},{1,3},{3,1},{5,7},{7,5},{8,10},{10,8},{12,... | collective-permute-start | bytes 786440 | tf_op jit(solution)/shard_map/ppermute | solution.py:552
  214.6 11.7 %collective-permute-start.59 = (f32[128,512]{1,0:T(8,128)S(1)}, f32[128,512]{1,0:T(8,128)S(1)}, u32[]{:S(2)}, u32[]{:S(2)}) collective-permute-start(f32[128,512]{1,0:T(8,128)S(1)} %shard_map.229.refs_7_.refs_3_), channel_id=1, source_target_pairs={{0,2},{2,0},{4,6},{6,4},{1,3},{3,1},{5,7},{7,5},{8,10},{10,8},{12,... | collective-permute-start | bytes 786440 | tf_op jit(solution)/shard_map/ppermute | solution.py:552
  220.5 8.9 %collective-permute-start.58 = (f32[128,512]{1,0:T(8,128)S(1)}, f32[128,512]{1,0:T(8,128)S(1)}, u32[]{:S(2)}, u32[]{:S(2)}) collective-permute-start(f32[128,512]{1,0:T(8,128)S(1)} %shard_map.232.refs_7_.refs_3_), channel_id=1, source_target_pairs={{0,2},{2,0},{4,6},{6,4},{1,3},{3,1},{5,7},{7,5},{8,10},{10,8},{12,... | collective-permute-start | bytes 786440 | tf_op jit(solution)/shard_map/ppermute | solution.py:552
  244.1 9.5 %collective-permute-start.65 = (f32[136,512]{1,0:T(8,128)S(1)}, f32[136,512]{1,0:T(8,128)S(1)}, u32[]{:S(2)}, u32[]{:S(2)}) collective-permute-start(f32[136,512]{1,0:T(8,128)S(1)} %shard_map.237.refs_3_.refs_0_), channel_id=1, source_target_pairs={{0,2},{2,0},{4,6},{6,4},{1,3},{3,1},{5,7},{7,5},{8,10},{10,8},{12,... | collective-permute-start | bytes 835592 | tf_op jit(solution)/shard_map/ppermute | solution.py:552
  247.6 11.7 %collective-permute-start.67 = (f32[128,512]{1,0:T(8,128)S(1)}, f32[128,512]{1,0:T(8,128)S(1)}, u32[]{:S(2)}, u32[]{:S(2)}) collective-permute-start(f32[128,512]{1,0:T(8,128)S(1)} %shard_map.242.refs_2_.refs_0_), channel_id=1, source_target_pairs={{0,2},{2,0},{4,6},{6,4},{1,3},{3,1},{5,7},{7,5},{8,10},{10,8},{12,... | collective-permute-start | bytes 786440 | tf_op jit(solution)/shard_map/ppermute | solution.py:552
  254.4 10.9 %collective-permute-start.64 = (f32[128,512]{1,0:T(8,128)S(1)}, f32[128,512]{1,0:T(8,128)S(1)}, u32[]{:S(2)}, u32[]{:S(2)}) collective-permute-start(f32[128,512]{1,0:T(8,128)S(1)} %shard_map.238.refs_3_.refs_0_), channel_id=1, source_target_pairs={{0,2},{2,0},{4,6},{6,4},{1,3},{3,1},{5,7},{7,5},{8,10},{10,8},{12,... | collective-permute-start | bytes 786440 | tf_op jit(solution)/shard_map/ppermute | solution.py:552
  260.1 11.7 %collective-permute-start.69 = (f32[136,512]{1,0:T(8,128)S(1)}, f32[136,512]{1,0:T(8,128)S(1)}, u32[]{:S(2)}, u32[]{:S(2)}) collective-permute-start(f32[136,512]{1,0:T(8,128)S(1)} %get-tuple-element.218.refs_2_), channel_id=1, source_target_pairs={{0,2},{2,0},{4,6},{6,4},{1,3},{3,1},{5,7},{7,5},{8,10},{10,8},{12,... | collective-permute-start | bytes 835592 | tf_op jit(solution)/shard_map/ppermute | solution.py:552
  266.1 12.1 %collective-permute-start.75 = (f32[128,512]{1,0:T(8,128)S(1)}, f32[128,512]{1,0:T(8,128)S(1)}, u32[]{:S(2)}, u32[]{:S(2)}) collective-permute-start(f32[128,512]{1,0:T(8,128)S(1)} %get-tuple-element.219.refs_2_), channel_id=1, source_target_pairs={{0,2},{2,0},{4,6},{6,4},{1,3},{3,1},{5,7},{7,5},{8,10},{10,8},{12,... | collective-permute-start | bytes 786440 | tf_op jit(solution)/shard_map/ppermute | solution.py:552
  271.8 10.5 %collective-permute-start.72 = (f32[128,512]{1,0:T(8,128)S(1)}, f32[128,512]{1,0:T(8,128)S(1)}, u32[]{:S(2)}, u32[]{:S(2)}) collective-permute-start(f32[128,512]{1,0:T(8,128)S(1)} %shard_map.248.refs_4_.refs_0_), channel_id=1, source_target_pairs={{0,0},{2,4},{4,2},{6,6},{1,1},{3,5},{5,3},{7,7},{8,8},{10,12},{12,... | collective-permute-start | bytes 786440 | tf_op jit(solution)/shard_map/ppermute | solution.py:555
  272.5 9.7 %collective-permute-start.71 = (f32[128,512]{1,0:T(8,128)S(1)}, f32[128,512]{1,0:T(8,128)S(1)}, u32[]{:S(2)}, u32[]{:S(2)}) collective-permute-start(f32[128,512]{1,0:T(8,128)S(1)} %get-tuple-element.220.refs_5_), channel_id=1, source_target_pairs={{0,2},{2,0},{4,6},{6,4},{1,3},{3,1},{5,7},{7,5},{8,10},{10,8},{12,... | collective-permute-start | bytes 786440 | tf_op jit(solution)/shard_map/ppermute | solution.py:552
  282.3 8.8 %collective-permute-start.74 = (f32[128,512]{1,0:T(8,128)S(1)}, f32[128,512]{1,0:T(8,128)S(1)}, u32[]{:S(2)}, u32[]{:S(2)}) collective-permute-start(f32[128,512]{1,0:T(8,128)S(1)} %shard_map.250.refs_2_.refs_3_), channel_id=1, source_target_pairs={{0,2},{2,0},{4,6},{6,4},{1,3},{3,1},{5,7},{7,5},{8,10},{10,8},{12,... | collective-permute-start | bytes 786440 | tf_op jit(solution)/shard_map/ppermute | solution.py:552
  285.4 11.8 %collective-permute-start.78 = (f32[128,512]{1,0:T(8,128)S(1)}, f32[128,512]{1,0:T(8,128)S(1)}, u32[]{:S(2)}, u32[]{:S(2)}) collective-permute-start(f32[128,512]{1,0:T(8,128)S(1)} %shard_map.255.refs_7_.refs_3_), channel_id=1, source_target_pairs={{0,2},{2,0},{4,6},{6,4},{1,3},{3,1},{5,7},{7,5},{8,10},{10,8},{12,... | collective-permute-start | bytes 786440 | tf_op jit(solution)/shard_map/ppermute | solution.py:552
  291.5 8.9 %collective-permute-start.77 = (f32[128,512]{1,0:T(8,128)S(1)}, f32[128,512]{1,0:T(8,128)S(1)}, u32[]{:S(2)}, u32[]{:S(2)}) collective-permute-start(f32[128,512]{1,0:T(8,128)S(1)} %shard_map.258.refs_7_.refs_3_), channel_id=1, source_target_pairs={{0,2},{2,0},{4,6},{6,4},{1,3},{3,1},{5,7},{7,5},{8,10},{10,8},{12,... | collective-permute-start | bytes 786440 | tf_op jit(solution)/shard_map/ppermute | solution.py:552
  (65 other events, 271.1 us)

commit v4 on v0

--- a/solution.py
+++ b/solution.py
@@ -25,7 +25,7 @@
 SMEM = pl.BlockSpec(memory_space=pltpu.SMEM)
 LIMIT = 16 * 1024 * 1024
 STEP_COST = pl.CostEstimate(flops=10**9, bytes_accessed=10**7, transcendentals=0)
-STREAM_LIMIT = 50 * 1024 * 1024
+STREAM_LIMIT = 45 * 1024 * 1024
 
 
 def dot32(first, second):
@@ -540,6 +540,9 @@
     def outer_swap(part):
         return lax.ppermute(part, "chip", [(0, 1), (1, 0), (2, 3), (3, 2)])
 
+    def send_back(part):
+        return lax.ppermute(part, "chip", [(1, 0), (2, 3)])
+
     def inner_swap(part):
         return lax.ppermute(part, "chip", [(0, 0), (1, 2), (2, 1), (3, 3)])
 
@@ -595,7 +598,7 @@
                     else:
                         total[k] = sent = add(own_part[k], inner[k], token)
                     token = sent
-                    outer[later] = outer_swap(sent)
+                    outer[later] = send_back(sent) if later == CHUNKS else outer_swap(sent)
                 elif tick == 0:
                     outer[later] = outer_swap(own_part[later])
                 if tick + 3 < CHUNKS and first:

time: 304 us -> 314 us (1.033)
  waiting for transfers between devices: 71.8 us -> 91.2 us
  starting transfers between devices: 173 us -> 155 us
  local copies, waits for them, and re-layouts: 5.26 us -> 15.5 us
    ppermute x36 -> x32, starting transfers between devices: 140 us -> 119 us  [outer_swap(): return lax.ppermute(part, 'chip', [(0, 1), (1, 0), (2, 3), (3, 2)])]
    ppermute x36 -> x32, waiting for transfers between devices: 38.6 us -> 56.8 us  [outer_swap(): return lax.ppermute(part, 'chip', [(0, 1), (1, 0), (2, 3), (3, 2)])]
    unnamed x56 -> x64, local copies, waits for them, and re-layouts: 5.14 us -> 15.3 us
    ppermute x0 -> x4, starting transfers between devices: none -> 5.17 us  [send_back(): return lax.ppermute(part, 'chip', [(1, 0), (2, 3)])]
  transfers between devices with their start and end apart: 82 -> 82, of which waited for: 33 -> 38; matrix products, arithmetic and copies ran while one was open for 0% -> 0% of each run, Pallas kernels for 12% -> 11%
where the time goes in v4:
time: 314 us; the launch traced here: 312 us
  starting transfers between devices  155 us (49%)
  waiting for transfers between devices  91.2 us (29%)
  Pallas kernels  47.8 us (15%)
  local copies, waits for them, and re-layouts  15.5 us (5%)
    ppermute x32, starting transfers between devices, outer_swap(): return lax.ppermute(part, 'chip', [(0, 1), (1, 0), (2, 3), (3, 2)])  119 us
    ppermute x32, waiting for transfers between devices, outer_swap(): return lax.ppermute(part, 'chip', [(0, 1), (1, 0), (2, 3), (3, 2)])  56.8 us
    pallas_call x96, Pallas kernels, call(): pl.pallas_call(body, in_specs=[SMEM] * len(scalars) + [VMEM] * len(ins) +...  28.3 us
    ppermute x24, starting transfers between devices, inner_swap(): return lax.ppermute(part, 'chip', [(0, 0), (1, 2), (2, 1), (3, 3)])  17.7 us
    unnamed x64, local copies, waits for them, and re-layouts  15.3 us
    ppermute x4, waiting for transfers between devices, data_terms(): part = part + lax.ppermute(part, 'dp', [(d, d ^ step) for d in range(n_dp)])  12.3 us
    ppermute x14, waiting for transfers between devices, swap(): return lax.ppermute(part, 'core', [(0, 1), (1, 0)])  11.2 us
    ppermute x4, waiting for transfers between devices, data_terms(): lax.ppermute(part, 'dp', [(d, d ^ step) for d in range(n_dp)])  10.8 us
  transfers between devices with their start and end apart: 82, of which 38 were waited for; matrix products, arithmetic and copies ran while one was open for 0% of the time, Pallas kernels for 11%

profile of v4, /device:TPU:0, one launch (start us, length us, event | category | flops | bytes accessed | tf_op | source)
XLA Modules:
  0.0 312.3 jit_solution(17625620245754478474)
XLA Ops:
  0.6 2.3 copy-done.1
  3.0 2.5 shard_map.157
  17.1 7.7 %shard_map.156 = (f32[3,128,128]{2,1,0:T(8,128)S(1)}, bf16[128,384]{1,0:T(8,128)(2,1)S(1)}, bf16[128,384]{1,0:T(8,128)(2,1)S(1)}, f32[128,16]{1,0:T(8,128)S(1)},...) custom-call(s32[1]{0:T(128)S(6)} %copy.17.limit_ref.refs_1_.refs_2_.refs_4_.refs_8_, bf16[128,6144]{1,0:T(8,128)(2,1)S(1)} %copy-done.2, ...), custom_call_target="tpu_custom_call" | custom-call | flops 1811939328 | bytes 14155776 | tf_op jit(solution)/shard_map/pallas_call | solution.py:188
  29.4 3.0 collective-permute-start.6
  37.3 2.6 collective-permute-done.6.refs_1_
  41.4 4.3 %collective-permute-start.11 = (f32[128,512]{1,0:T(8,128)}, f32[128,512]{1,0:T(8,128)S(1)}, u32[]{:S(2)}, u32[]{:S(2)}) collective-permute-start(f32[128,512]{1,0:T(8,128)} %copy-done.20), channel_id=1, source_target_pairs={{0,2},{2,0},{4,6},{6,4},{1,3},{3,1},{5,7},{7,5},{8,10},{10,8},{12,... | collective-permute-start | bytes 786440 | tf_op jit(solution)/shard_map/ppermute | solution.py:541
  56.7 2.3 collective-permute-start.15
  61.6 4.0 %collective-permute-start.14 = (f32[128,512]{1,0:T(8,128)S(1)}, f32[128,512]{1,0:T(8,128)S(1)}, u32[]{:S(2)}, u32[]{:S(2)}) collective-permute-start(f32[128,512]{1,0:T(8,128)S(1)} %get-tuple-element.144.refs_6_), channel_id=1, source_target_pairs={{0,2},{2,0},{4,6},{6,4},{1,3},{3,1},{5,7},{7,5},{8,10},{10,8},{12,... | collective-permute-start | bytes 786440 | tf_op jit(solution)/shard_map/ppermute | solution.py:541
  71.9 7.6 %collective-permute-start.21 = (f32[128,512]{1,0:T(8,128)S(1)}, f32[128,512]{1,0:T(8,128)S(1)}, u32[]{:S(2)}, u32[]{:S(2)}) collective-permute-start(f32[128,512]{1,0:T(8,128)S(1)} %shard_map.176.refs_8_.refs_3_), channel_id=1, source_target_pairs={{0,2},{2,0},{4,6},{6,4},{1,3},{3,1},{5,7},{7,5},{8,10},{10,8},{12,... | collective-permute-start | bytes 786440 | tf_op jit(solution)/shard_map/ppermute | solution.py:541
  82.5 3.9 %collective-permute-done.21.refs_2_ = f32[128,512]{1,0:T(8,128)S(1)} collective-permute-done((f32[128,512]{1,0:T(8,128)S(1)}, f32[128,512]{1,0:T(8,128)S(1)}, u32[]{:S(2)}, u32[]{:S(2)}) %collective-permute-start.21) | collective-permute-done | bytes 262176 | tf_op jit(solution)/shard_map/ppermute | solution.py:541
  86.7 2.4 collective-permute-done.20.refs_2_
  94.2 2.7 collective-permute-done.23
  98.4 2.7 collective-permute-done.24.refs_1_
  107.2 6.0 %collective-permute-done.27.refs_1_ = f32[136,512]{1,0:T(8,128)S(1)} collective-permute-done((f32[136,512]{1,0:T(8,128)S(1)}, f32[136,512]{1,0:T(8,128)S(1)}, u32[]{:S(2)}, u32[]{:S(2)}) %collective-permute-start.27) | collective-permute-done | bytes 278560 | tf_op jit(solution)/shard_map/ppermute | solution.py:541
  114.0 4.0 %collective-permute-start.26 = (f32[128,512]{1,0:T(8,128)S(1)}, f32[128,512]{1,0:T(8,128)S(1)}, u32[]{:S(2)}, u32[]{:S(2)}) collective-permute-start(f32[128,512]{1,0:T(8,128)S(1)} %shard_map.185.refs_3_.refs_0_), channel_id=1, source_target_pairs={{0,2},{2,0},{4,6},{6,4},{1,3},{3,1},{5,7},{7,5},{8,10},{10,8},{12,... | collective-permute-start | bytes 786440 | tf_op jit(solution)/shard_map/ppermute | solution.py:541
  119.7 4.7 %collective-permute-start.31 = (f32[136,512]{1,0:T(8,128)S(1)}, f32[136,512]{1,0:T(8,128)S(1)}, u32[]{:S(2)}, u32[]{:S(2)}) collective-permute-start(f32[136,512]{1,0:T(8,128)S(1)} %get-tuple-element.172.refs_2_), channel_id=1, source_target_pairs={{0,2},{2,0},{4,6},{6,4},{1,3},{3,1},{5,7},{7,5},{8,10},{10,8},{12,... | collective-permute-start | bytes 835592 | tf_op jit(solution)/shard_map/ppermute | solution.py:541
  125.4 5.6 %collective-permute-start.34 = (f32[128,512]{1,0:T(8,128)S(1)}, f32[128,512]{1,0:T(8,128)S(1)}, u32[]{:S(2)}, u32[]{:S(2)}) collective-permute-start(f32[128,512]{1,0:T(8,128)S(1)} %get-tuple-element.173.refs_2_), channel_id=1, source_target_pairs={{0,2},{2,0},{4,6},{6,4},{1,3},{3,1},{5,7},{7,5},{8,10},{10,8},{12,... | collective-permute-start | bytes 786440 | tf_op jit(solution)/shard_map/ppermute | solution.py:541
  131.8 5.3 %collective-permute-start.33 = (f32[128,512]{1,0:T(8,128)S(1)}, f32[128,512]{1,0:T(8,128)S(1)}, u32[]{:S(2)}, u32[]{:S(2)}) collective-permute-start(f32[128,512]{1,0:T(8,128)S(1)} %get-tuple-element.174.refs_5_), channel_id=1, source_target_pairs={{0,2},{2,0},{4,6},{6,4},{1,3},{3,1},{5,7},{7,5},{8,10},{10,8},{12,... | collective-permute-start | bytes 786440 | tf_op jit(solution)/shard_map/ppermute | solution.py:541
  140.0 2.5 collective-permute-done.33.refs_1_.refs_2_
  143.2 6.5 %collective-permute-start.40 = (f32[128,512]{1,0:T(8,128)S(1)}, f32[128,512]{1,0:T(8,128)S(1)}, u32[]{:S(2)}, u32[]{:S(2)}) collective-permute-start(f32[128,512]{1,0:T(8,128)S(1)} %shard_map.202.refs_7_.refs_3_), channel_id=1, source_target_pairs={{0,2},{2,0},{4,6},{6,4},{1,3},{3,1},{5,7},{7,5},{8,10},{10,8},{12,... | collective-permute-start | bytes 786440 | tf_op jit(solution)/shard_map/ppermute | solution.py:541
  150.6 2.4 collective-permute-start.39
  153.0 3.4 %collective-permute-done.40.refs_2_ = f32[128,512]{1,0:T(8,128)S(1)} collective-permute-done((f32[128,512]{1,0:T(8,128)S(1)}, f32[128,512]{1,0:T(8,128)S(1)}, u32[]{:S(2)}, u32[]{:S(2)}) %collective-permute-start.40) | collective-permute-done | bytes 262176 | tf_op jit(solution)/shard_map/ppermute | solution.py:541
  156.8 2.4 collective-permute-done.39.refs_2_
  164.2 2.7 collective-permute-done.42
  168.5 2.7 collective-permute-done.43.refs_1_
  177.4 6.0 %collective-permute-done.46.refs_1_ = f32[136,512]{1,0:T(8,128)S(1)} collective-permute-done((f32[136,512]{1,0:T(8,128)S(1)}, f32[136,512]{1,0:T(8,128)S(1)}, u32[]{:S(2)}, u32[]{:S(2)}) %collective-permute-start.46) | collective-permute-done | bytes 278560 | tf_op jit(solution)/shard_map/ppermute | solution.py:541
  184.1 4.1 %collective-permute-start.45 = (f32[128,512]{1,0:T(8,128)S(1)}, f32[128,512]{1,0:T(8,128)S(1)}, u32[]{:S(2)}, u32[]{:S(2)}) collective-permute-start(f32[128,512]{1,0:T(8,128)S(1)} %shard_map.211.refs_3_.refs_0_), channel_id=1, source_target_pairs={{0,2},{2,0},{4,6},{6,4},{1,3},{3,1},{5,7},{7,5},{8,10},{10,8},{12,... | collective-permute-start | bytes 786440 | tf_op jit(solution)/shard_map/ppermute | solution.py:541
  189.8 4.7 %collective-permute-start.50 = (f32[136,512]{1,0:T(8,128)S(1)}, f32[136,512]{1,0:T(8,128)S(1)}, u32[]{:S(2)}, u32[]{:S(2)}) collective-permute-start(f32[136,512]{1,0:T(8,128)S(1)} %get-tuple-element.193.refs_2_), channel_id=1, source_target_pairs={{0,2},{2,0},{4,6},{6,4},{1,3},{3,1},{5,7},{7,5},{8,10},{10,8},{12,... | collective-permute-start | bytes 835592 | tf_op jit(solution)/shard_map/ppermute | solution.py:541
  195.3 5.9 %collective-permute-start.53 = (f32[128,512]{1,0:T(8,128)S(1)}, f32[128,512]{1,0:T(8,128)S(1)}, u32[]{:S(2)}, u32[]{:S(2)}) collective-permute-start(f32[128,512]{1,0:T(8,128)S(1)} %get-tuple-element.194.refs_2_), channel_id=1, source_target_pairs={{0,2},{2,0},{4,6},{6,4},{1,3},{3,1},{5,7},{7,5},{8,10},{10,8},{12,... | collective-permute-start | bytes 786440 | tf_op jit(solution)/shard_map/ppermute | solution.py:541
  202.0 5.2 %collective-permute-start.52 = (f32[128,512]{1,0:T(8,128)S(1)}, f32[128,512]{1,0:T(8,128)S(1)}, u32[]{:S(2)}, u32[]{:S(2)}) collective-permute-start(f32[128,512]{1,0:T(8,128)S(1)} %get-tuple-element.195.refs_5_), channel_id=1, source_target_pairs={{0,2},{2,0},{4,6},{6,4},{1,3},{3,1},{5,7},{7,5},{8,10},{10,8},{12,... | collective-permute-start | bytes 786440 | tf_op jit(solution)/shard_map/ppermute | solution.py:541
  210.0 2.5 collective-permute-done.52.refs_1_.refs_2_
  213.5 6.4 %collective-permute-start.59 = (f32[128,512]{1,0:T(8,128)S(1)}, f32[128,512]{1,0:T(8,128)S(1)}, u32[]{:S(2)}, u32[]{:S(2)}) collective-permute-start(f32[128,512]{1,0:T(8,128)S(1)} %shard_map.228.refs_7_.refs_3_), channel_id=1, source_target_pairs={{0,2},{2,0},{4,6},{6,4},{1,3},{3,1},{5,7},{7,5},{8,10},{10,8},{12,... | collective-permute-start | bytes 786440 | tf_op jit(solution)/shard_map/ppermute | solution.py:541
  223.1 3.5 %collective-permute-done.59.refs_2_ = f32[128,512]{1,0:T(8,128)S(1)} collective-permute-done((f32[128,512]{1,0:T(8,128)S(1)}, f32[128,512]{1,0:T(8,128)S(1)}, u32[]{:S(2)}, u32[]{:S(2)}) %collective-permute-start.59) | collective-permute-done | bytes 262176 | tf_op jit(solution)/shard_map/ppermute | solution.py:541
  227.0 2.4 collective-permute-done.58.refs_2_
  233.6 3.5 %collective-permute-done.61 = f32[40,384]{1,0:T(8,128)S(1)} collective-permute-done((f32[40,384]{1,0:T(8,128)S(1)}, f32[40,384]{1,0:T(8,128)S(1)}, u32[]{:S(2)}, u32[]{:S(2)}) %collective-permute-start.61) | collective-permute-done | bytes 61472 | tf_op jit(solution)/shard_map/ppermute | solution.py:521
  238.7 2.7 collective-permute-done.62.refs_1_
  247.6 6.0 %collective-permute-done.65.refs_1_ = f32[136,512]{1,0:T(8,128)S(1)} collective-permute-done((f32[136,512]{1,0:T(8,128)S(1)}, f32[136,512]{1,0:T(8,128)S(1)}, u32[]{:S(2)}, u32[]{:S(2)}) %collective-permute-start.65) | collective-permute-done | bytes 278560 | tf_op jit(solution)/shard_map/ppermute | solution.py:541
  254.4 4.0 %collective-permute-start.64 = (f32[128,512]{1,0:T(8,128)S(1)}, f32[128,512]{1,0:T(8,128)S(1)}, u32[]{:S(2)}, u32[]{:S(2)}) collective-permute-start(f32[128,512]{1,0:T(8,128)S(1)} %shard_map.237.refs_3_.refs_0_), channel_id=1, source_target_pairs={{0,2},{2,0},{4,6},{6,4},{1,3},{3,1},{5,7},{7,5},{8,10},{10,8},{12,... | collective-permute-start | bytes 786440 | tf_op jit(solution)/shard_map/ppermute | solution.py:541
  260.1 4.7 %collective-permute-start.69 = (f32[136,512]{1,0:T(8,128)S(1)}, f32[136,512]{1,0:T(8,128)S(1)}, u32[]{:S(2)}, u32[]{:S(2)}) collective-permute-start(f32[136,512]{1,0:T(8,128)S(1)} %get-tuple-element.218.refs_2_), channel_id=1, source_target_pairs={{0,2},{2,0},{4,6},{6,4},{1,3},{3,1},{5,7},{7,5},{8,10},{10,8},{12,... | collective-permute-start | bytes 835592 | tf_op jit(solution)/shard_map/ppermute | solution.py:541
  265.8 5.6 %collective-permute-start.72 = (f32[128,512]{1,0:T(8,128)S(1)}, f32[128,512]{1,0:T(8,128)S(1)}, u32[]{:S(2)}, u32[]{:S(2)}) collective-permute-start(f32[128,512]{1,0:T(8,128)S(1)} %get-tuple-element.219.refs_2_), channel_id=1, source_target_pairs={{0,2},{2,0},{4,6},{6,4},{1,3},{3,1},{5,7},{7,5},{8,10},{10,8},{12,... | collective-permute-start | bytes 786440 | tf_op jit(solution)/shard_map/ppermute | solution.py:541
  272.2 5.3 %collective-permute-start.71 = (f32[128,512]{1,0:T(8,128)S(1)}, f32[128,512]{1,0:T(8,128)S(1)}, u32[]{:S(2)}, u32[]{:S(2)}) collective-permute-start(f32[128,512]{1,0:T(8,128)S(1)} %get-tuple-element.220.refs_5_), channel_id=1, source_target_pairs={{0,2},{2,0},{4,6},{6,4},{1,3},{3,1},{5,7},{7,5},{8,10},{10,8},{12,... | collective-permute-start | bytes 786440 | tf_op jit(solution)/shard_map/ppermute | solution.py:541
  280.3 2.5 collective-permute-done.71.refs_1_.refs_2_
  283.6 6.5 %collective-permute-start.78 = (f32[128,512]{1,0:T(8,128)S(1)}, f32[128,512]{1,0:T(8,128)S(1)}, u32[]{:S(2)}, u32[]{:S(2)}) collective-permute-start(f32[128,512]{1,0:T(8,128)S(1)} %shard_map.254.refs_7_.refs_3_), channel_id=1, source_target_pairs={{0,2},{2,0},{4,6},{6,4},{1,3},{3,1},{5,7},{7,5},{8,10},{10,8},{12,... | collective-permute-start | bytes 786440 | tf_op jit(solution)/shard_map/ppermute | solution.py:541
  291.0 2.4 collective-permute-start.77
  293.4 3.4 %collective-permute-done.78.refs_2_ = f32[128,512]{1,0:T(8,128)S(1)} collective-permute-done((f32[128,512]{1,0:T(8,128)S(1)}, f32[128,512]{1,0:T(8,128)S(1)}, u32[]{:S(2)}, u32[]{:S(2)}) %collective-permute-start.78) | collective-permute-done | bytes 262176 | tf_op jit(solution)/shard_map/ppermute | solution.py:541
  297.2 2.4 collective-permute-done.77.refs_2_
  303.9 3.4 %collective-permute-done.80 = f32[40,384]{1,0:T(8,128)S(1)} collective-permute-done((f32[40,384]{1,0:T(8,128)S(1)}, f32[40,384]{1,0:T(8,128)S(1)}, u32[]{:S(2)}, u32[]{:S(2)}) %collective-permute-start.80) | collective-permute-done | bytes 61472 | tf_op jit(solution)/shard_map/ppermute | solution.py:521
  308.9 2.7 collective-permute-done.81.refs_1_
  (292 shorter events, 117.4 us)
Async XLA Ops:
  9.3 17.4 %collective-permute-start.3 = (f32[384,512]{1,0:T(8,128)}, f32[384,512]{1,0:T(8,128)}, u32[]{:S(2)}, u32[]{:S(2)}) collective-permute-start(f32[384,512]{1,0:T(8,128)} %get-tuple-element.129), channel_id=1, source_target_pairs={{0,1},{1,0},{2,3},{3,2},{4,5},{5,4},{6,7},{7,6},{8,9},{9,8},{10,11... | collective-permute-start | bytes 2359304 | tf_op jit(solution)/shard_map/ppermute | solution.py:516
  9.7 22.9 %collective-permute-start.2 = (f32[384,512]{1,0:T(8,128)}, f32[384,512]{1,0:T(8,128)}, u32[]{:S(2)}, u32[]{:S(2)}) collective-permute-start(f32[384,512]{1,0:T(8,128)} %get-tuple-element.127), channel_id=1, source_target_pairs={{0,1},{1,0},{2,3},{3,2},{4,5},{5,4},{6,7},{7,6},{8,9},{9,8},{10,11... | collective-permute-start | bytes 2359304 | tf_op jit(solution)/shard_map/ppermute | solution.py:516
  9.8 25.2 %collective-permute-start.7 = (f32[384,512]{1,0:T(8,128)S(1)}, f32[384,512]{1,0:T(8,128)S(1)}, u32[]{:S(2)}, u32[]{:S(2)}) collective-permute-start(f32[384,512]{1,0:T(8,128)S(1)} %get-tuple-element.135), channel_id=1, source_target_pairs={{0,1},{1,0},{2,3},{3,2},{4,5},{5,4},{6,7},{7,6},{8,9},{9,8},{10,11... | collective-permute-start | bytes 2359304 | tf_op jit(solution)/shard_map/ppermute | solution.py:516
  25.0 16.4 %collective-permute-start.5 = (f32[384,512]{1,0:T(8,128)}, f32[384,512]{1,0:T(8,128)}, u32[]{:S(2)}, u32[]{:S(2)}) collective-permute-start(f32[384,512]{1,0:T(8,128)} %get-tuple-element.133), channel_id=1, source_target_pairs={{0,1},{1,0},{2,3},{3,2},{4,5},{5,4},{6,7},{7,6},{8,9},{9,8},{10,11... | collective-permute-start | bytes 2359304 | tf_op jit(solution)/shard_map/ppermute | solution.py:516
  26.5 27.8 %collective-permute-start.9 = (f32[384,512]{1,0:T(8,128)}, f32[384,512]{1,0:T(8,128)}, u32[]{:S(2)}, u32[]{:S(2)}) collective-permute-start(f32[384,512]{1,0:T(8,128)} %get-tuple-element.139), channel_id=1, source_target_pairs={{0,1},{1,0},{2,3},{3,2},{4,5},{5,4},{6,7},{7,6},{8,9},{9,8},{10,11... | collective-permute-start | bytes 2359304 | tf_op jit(solution)/shard_map/ppermute | solution.py:516
  29.4 10.5 %collective-permute-start.6 = (f32[136,512]{1,0:T(8,128)S(1)}, f32[136,512]{1,0:T(8,128)S(1)}, u32[]{:S(2)}, u32[]{:S(2)}) collective-permute-start(f32[136,512]{1,0:T(8,128)S(1)} %get-tuple-element.130.refs_4_.refs_0_), channel_id=1, source_target_pairs={{0,2},{2,0},{4,6},{6,4},{1,3},{3,1},{5,7},{7,5},{8,10},{10,8},{12,... | collective-permute-start | bytes 835592 | tf_op jit(solution)/shard_map/ppermute | solution.py:541
  32.6 26.5 %collective-permute-start.1 = (f32[384,512]{1,0:T(8,128)S(1)}, f32[384,512]{1,0:T(8,128)}, u32[]{:S(2)}, u32[]{:S(2)}) collective-permute-start(f32[384,512]{1,0:T(8,128)S(1)} %get-tuple-element.125), channel_id=1, source_target_pairs={{0,1},{1,0},{2,3},{3,2},{4,5},{5,4},{6,7},{7,6},{8,9},{9,8},{10,11... | collective-permute-start | bytes 2359304 | tf_op jit(solution)/shard_map/ppermute | solution.py:516
  35.0 14.1 %collective-permute-start.4 = (f32[128,512]{1,0:T(8,128)}, f32[128,512]{1,0:T(8,128)}, u32[]{:S(2)}, u32[]{:S(2)}) collective-permute-start(f32[128,512]{1,0:T(8,128)} %get-tuple-element.131.refs_4_.refs_0_), channel_id=1, source_target_pairs={{0,2},{2,0},{4,6},{6,4},{1,3},{3,1},{5,7},{7,5},{8,10},{10,8},{12,... | collective-permute-start | bytes 786440 | tf_op jit(solution)/shard_map/ppermute | solution.py:541
  39.9 11.0 %collective-permute-start.10 = (f32[136,512]{1,0:T(8,128)S(1)}, f32[136,512]{1,0:T(8,128)}, u32[]{:S(2)}, u32[]{:S(2)}) collective-permute-start(f32[136,512]{1,0:T(8,128)S(1)} %shard_map.161.refs_4_.refs_1_), channel_id=1, source_target_pairs={{0,0},{2,4},{4,2},{6,6},{1,1},{3,5},{5,3},{7,7},{8,8},{10,12},{12,... | collective-permute-start | bytes 835592 | tf_op jit(solution)/shard_map/ppermute | solution.py:547
  41.4 14.5 %collective-permute-start.11 = (f32[128,512]{1,0:T(8,128)}, f32[128,512]{1,0:T(8,128)S(1)}, u32[]{:S(2)}, u32[]{:S(2)}) collective-permute-start(f32[128,512]{1,0:T(8,128)} %copy-done.20), channel_id=1, source_target_pairs={{0,2},{2,0},{4,6},{6,4},{1,3},{3,1},{5,7},{7,5},{8,10},{10,8},{12,... | collective-permute-start | bytes 786440 | tf_op jit(solution)/shard_map/ppermute | solution.py:541
  52.0 8.7 %collective-permute-start.13 = (f32[136,512]{1,0:T(8,128)S(1)}, f32[136,512]{1,0:T(8,128)S(1)}, u32[]{:S(2)}, u32[]{:S(2)}) collective-permute-start(f32[136,512]{1,0:T(8,128)S(1)} %get-tuple-element.140.refs_4_), channel_id=1, source_target_pairs={{0,2},{2,0},{4,6},{6,4},{1,3},{3,1},{5,7},{7,5},{8,10},{10,8},{12,... | collective-permute-start | bytes 835592 | tf_op jit(solution)/shard_map/ppermute | solution.py:541
  56.7 9.7 %collective-permute-start.15 = (f32[128,512]{1,0:T(8,128)S(1)}, f32[128,512]{1,0:T(8,128)S(1)}, u32[]{:S(2)}, u32[]{:S(2)}) collective-permute-start(f32[128,512]{1,0:T(8,128)S(1)} %get-tuple-element.142.refs_4_), channel_id=1, source_target_pairs={{0,2},{2,0},{4,6},{6,4},{1,3},{3,1},{5,7},{7,5},{8,10},{10,8},{12,... | collective-permute-start | bytes 786440 | tf_op jit(solution)/shard_map/ppermute | solution.py:541
  61.6 9.2 %collective-permute-start.14 = (f32[128,512]{1,0:T(8,128)S(1)}, f32[128,512]{1,0:T(8,128)S(1)}, u32[]{:S(2)}, u32[]{:S(2)}) collective-permute-start(f32[128,512]{1,0:T(8,128)S(1)} %get-tuple-element.144.refs_6_), channel_id=1, source_target_pairs={{0,2},{2,0},{4,6},{6,4},{1,3},{3,1},{5,7},{7,5},{8,10},{10,8},{12,... | collective-permute-start | bytes 786440 | tf_op jit(solution)/shard_map/ppermute | solution.py:541
  67.3 12.6 %collective-permute-start.18 = (f32[128,512]{1,0:T(8,128)S(1)}, f32[128,512]{1,0:T(8,128)S(1)}, u32[]{:S(2)}, u32[]{:S(2)}) collective-permute-start(f32[128,512]{1,0:T(8,128)S(1)} %shard_map.173.refs_8_.refs_3_), channel_id=1, source_target_pairs={{2,0},{4,6},{3,1},{5,7},{10,8},{12,14},{11,9},{13,15},{18,16},{20,... | collective-permute-start | bytes 786440 | tf_op jit(solution)/shard_map/ppermute | solution.py:544
  70.8 9.5 %collective-permute-start.17 = (f32[128,512]{1,0:T(8,128)S(1)}, f32[128,512]{1,0:T(8,128)S(1)}, u32[]{:S(2)}, u32[]{:S(2)}) collective-permute-start(f32[128,512]{1,0:T(8,128)S(1)} %shard_map.175.refs_2_.refs_0_), channel_id=1, source_target_pairs={{0,0},{2,4},{4,2},{6,6},{1,1},{3,5},{5,3},{7,7},{8,8},{10,12},{12,... | collective-permute-start | bytes 786440 | tf_op jit(solution)/shard_map/ppermute | solution.py:547
  71.9 14.5 %collective-permute-start.21 = (f32[128,512]{1,0:T(8,128)S(1)}, f32[128,512]{1,0:T(8,128)S(1)}, u32[]{:S(2)}, u32[]{:S(2)}) collective-permute-start(f32[128,512]{1,0:T(8,128)S(1)} %shard_map.176.refs_8_.refs_3_), channel_id=1, source_target_pairs={{0,2},{2,0},{4,6},{6,4},{1,3},{3,1},{5,7},{7,5},{8,10},{10,8},{12,... | collective-permute-start | bytes 786440 | tf_op jit(solution)/shard_map/ppermute | solution.py:541
  80.4 8.8 %collective-permute-start.20 = (f32[128,512]{1,0:T(8,128)S(1)}, f32[128,512]{1,0:T(8,128)S(1)}, u32[]{:S(2)}, u32[]{:S(2)}) collective-permute-start(f32[128,512]{1,0:T(8,128)S(1)} %shard_map.179.refs_8_.refs_3_), channel_id=1, source_target_pairs={{0,2},{2,0},{4,6},{6,4},{1,3},{3,1},{5,7},{7,5},{8,10},{10,8},{12,... | collective-permute-start | bytes 786440 | tf_op jit(solution)/shard_map/ppermute | solution.py:541
  103.7 9.6 %collective-permute-start.27 = (f32[136,512]{1,0:T(8,128)S(1)}, f32[136,512]{1,0:T(8,128)S(1)}, u32[]{:S(2)}, u32[]{:S(2)}) collective-permute-start(f32[136,512]{1,0:T(8,128)S(1)} %shard_map.184.refs_3_.refs_0_), channel_id=1, source_target_pairs={{0,2},{2,0},{4,6},{6,4},{1,3},{3,1},{5,7},{7,5},{8,10},{10,8},{12,... | collective-permute-start | bytes 835592 | tf_op jit(solution)/shard_map/ppermute | solution.py:541
  106.9 12.0 %collective-permute-start.29 = (f32[128,512]{1,0:T(8,128)S(1)}, f32[128,512]{1,0:T(8,128)S(1)}, u32[]{:S(2)}, u32[]{:S(2)}) collective-permute-start(f32[128,512]{1,0:T(8,128)S(1)} %shard_map.189.refs_2_.refs_0_), channel_id=1, source_target_pairs={{0,2},{2,0},{4,6},{6,4},{1,3},{3,1},{5,7},{7,5},{8,10},{10,8},{12,... | collective-permute-start | bytes 786440 | tf_op jit(solution)/shard_map/ppermute | solution.py:541
  114.0 10.6 %collective-permute-start.26 = (f32[128,512]{1,0:T(8,128)S(1)}, f32[128,512]{1,0:T(8,128)S(1)}, u32[]{:S(2)}, u32[]{:S(2)}) collective-permute-start(f32[128,512]{1,0:T(8,128)S(1)} %shard_map.185.refs_3_.refs_0_), channel_id=1, source_target_pairs={{0,2},{2,0},{4,6},{6,4},{1,3},{3,1},{5,7},{7,5},{8,10},{10,8},{12,... | collective-permute-start | bytes 786440 | tf_op jit(solution)/shard_map/ppermute | solution.py:541
  119.7 11.3 %collective-permute-start.31 = (f32[136,512]{1,0:T(8,128)S(1)}, f32[136,512]{1,0:T(8,128)S(1)}, u32[]{:S(2)}, u32[]{:S(2)}) collective-permute-start(f32[136,512]{1,0:T(8,128)S(1)} %get-tuple-element.172.refs_2_), channel_id=1, source_target_pairs={{0,2},{2,0},{4,6},{6,4},{1,3},{3,1},{5,7},{7,5},{8,10},{10,8},{12,... | collective-permute-start | bytes 835592 | tf_op jit(solution)/shard_map/ppermute | solution.py:541
  125.4 12.1 %collective-permute-start.34 = (f32[128,512]{1,0:T(8,128)S(1)}, f32[128,512]{1,0:T(8,128)S(1)}, u32[]{:S(2)}, u32[]{:S(2)}) collective-permute-start(f32[128,512]{1,0:T(8,128)S(1)} %get-tuple-element.173.refs_2_), channel_id=1, source_target_pairs={{0,2},{2,0},{4,6},{6,4},{1,3},{3,1},{5,7},{7,5},{8,10},{10,8},{12,... | collective-permute-start | bytes 786440 | tf_op jit(solution)/shard_map/ppermute | solution.py:541
  131.8 10.7 %collective-permute-start.33 = (f32[128,512]{1,0:T(8,128)S(1)}, f32[128,512]{1,0:T(8,128)S(1)}, u32[]{:S(2)}, u32[]{:S(2)}) collective-permute-start(f32[128,512]{1,0:T(8,128)S(1)} %get-tuple-element.174.refs_5_), channel_id=1, source_target_pairs={{0,2},{2,0},{4,6},{6,4},{1,3},{3,1},{5,7},{7,5},{8,10},{10,8},{12,... | collective-permute-start | bytes 786440 | tf_op jit(solution)/shard_map/ppermute | solution.py:541
  138.3 11.9 %collective-permute-start.37 = (f32[128,512]{1,0:T(8,128)S(1)}, f32[128,512]{1,0:T(8,128)S(1)}, u32[]{:S(2)}, u32[]{:S(2)}) collective-permute-start(f32[128,512]{1,0:T(8,128)S(1)} %shard_map.199.refs_7_.refs_3_), channel_id=1, source_target_pairs={{2,0},{4,6},{3,1},{5,7},{10,8},{12,14},{11,9},{13,15},{18,16},{20,... | collective-permute-start | bytes 786440 | tf_op jit(solution)/shard_map/ppermute | solution.py:544
  142.5 8.1 %collective-permute-start.36 = (f32[128,512]{1,0:T(8,128)S(1)}, f32[128,512]{1,0:T(8,128)S(1)}, u32[]{:S(2)}, u32[]{:S(2)}) collective-permute-start(f32[128,512]{1,0:T(8,128)S(1)} %shard_map.201.refs_2_.refs_0_), channel_id=1, source_target_pairs={{0,0},{2,4},{4,2},{6,6},{1,1},{3,5},{5,3},{7,7},{8,8},{10,12},{12,... | collective-permute-start | bytes 786440 | tf_op jit(solution)/shard_map/ppermute | solution.py:547
  143.2 13.2 %collective-permute-start.40 = (f32[128,512]{1,0:T(8,128)S(1)}, f32[128,512]{1,0:T(8,128)S(1)}, u32[]{:S(2)}, u32[]{:S(2)}) collective-permute-start(f32[128,512]{1,0:T(8,128)S(1)} %shard_map.202.refs_7_.refs_3_), channel_id=1, source_target_pairs={{0,2},{2,0},{4,6},{6,4},{1,3},{3,1},{5,7},{7,5},{8,10},{10,8},{12,... | collective-permute-start | bytes 786440 | tf_op jit(solution)/shard_map/ppermute | solution.py:541
  150.6 8.6 %collective-permute-start.39 = (f32[128,512]{1,0:T(8,128)S(1)}, f32[128,512]{1,0:T(8,128)S(1)}, u32[]{:S(2)}, u32[]{:S(2)}) collective-permute-start(f32[128,512]{1,0:T(8,128)S(1)} %shard_map.205.refs_7_.refs_3_), channel_id=1, source_target_pairs={{0,2},{2,0},{4,6},{6,4},{1,3},{3,1},{5,7},{7,5},{8,10},{10,8},{12,... | collective-permute-start | bytes 786440 | tf_op jit(solution)/shard_map/ppermute | solution.py:541
  173.8 9.6 %collective-permute-start.46 = (f32[136,512]{1,0:T(8,128)S(1)}, f32[136,512]{1,0:T(8,128)S(1)}, u32[]{:S(2)}, u32[]{:S(2)}) collective-permute-start(f32[136,512]{1,0:T(8,128)S(1)} %shard_map.210.refs_3_.refs_0_), channel_id=1, source_target_pairs={{0,2},{2,0},{4,6},{6,4},{1,3},{3,1},{5,7},{7,5},{8,10},{10,8},{12,... | collective-permute-start | bytes 835592 | tf_op jit(solution)/shard_map/ppermute | solution.py:541
  177.0 12.0 %collective-permute-start.48 = (f32[128,512]{1,0:T(8,128)S(1)}, f32[128,512]{1,0:T(8,128)S(1)}, u32[]{:S(2)}, u32[]{:S(2)}) collective-permute-start(f32[128,512]{1,0:T(8,128)S(1)} %shard_map.215.refs_2_.refs_0_), channel_id=1, source_target_pairs={{0,2},{2,0},{4,6},{6,4},{1,3},{3,1},{5,7},{7,5},{8,10},{10,8},{12,... | collective-permute-start | bytes 786440 | tf_op jit(solution)/shard_map/ppermute | solution.py:541
  184.1 10.5 %collective-permute-start.45 = (f32[128,512]{1,0:T(8,128)S(1)}, f32[128,512]{1,0:T(8,128)S(1)}, u32[]{:S(2)}, u32[]{:S(2)}) collective-permute-start(f32[128,512]{1,0:T(8,128)S(1)} %shard_map.211.refs_3_.refs_0_), channel_id=1, source_target_pairs={{0,2},{2,0},{4,6},{6,4},{1,3},{3,1},{5,7},{7,5},{8,10},{10,8},{12,... | collective-permute-start | bytes 786440 | tf_op jit(solution)/shard_map/ppermute | solution.py:541
  189.8 11.4 %collective-permute-start.50 = (f32[136,512]{1,0:T(8,128)S(1)}, f32[136,512]{1,0:T(8,128)S(1)}, u32[]{:S(2)}, u32[]{:S(2)}) collective-permute-start(f32[136,512]{1,0:T(8,128)S(1)} %get-tuple-element.193.refs_2_), channel_id=1, source_target_pairs={{0,2},{2,0},{4,6},{6,4},{1,3},{3,1},{5,7},{7,5},{8,10},{10,8},{12,... | collective-permute-start | bytes 835592 | tf_op jit(solution)/shard_map/ppermute | solution.py:541
  194.6 7.4 %collective-permute-start.49 = (f32[128,512]{1,0:T(8,128)S(1)}, f32[128,512]{1,0:T(8,128)S(1)}, u32[]{:S(2)}, u32[]{:S(2)}) collective-permute-start(f32[128,512]{1,0:T(8,128)S(1)} %shard_map.219.refs_4_.refs_1_), channel_id=1, source_target_pairs={{0,0},{2,4},{4,2},{6,6},{1,1},{3,5},{5,3},{7,7},{8,8},{10,12},{12,... | collective-permute-start | bytes 786440 | tf_op jit(solution)/shard_map/ppermute | solution.py:547
  195.3 12.2 %collective-permute-start.53 = (f32[128,512]{1,0:T(8,128)S(1)}, f32[128,512]{1,0:T(8,128)S(1)}, u32[]{:S(2)}, u32[]{:S(2)}) collective-permute-start(f32[128,512]{1,0:T(8,128)S(1)} %get-tuple-element.194.refs_2_), channel_id=1, source_target_pairs={{0,2},{2,0},{4,6},{6,4},{1,3},{3,1},{5,7},{7,5},{8,10},{10,8},{12,... | collective-permute-start | bytes 786440 | tf_op jit(solution)/shard_map/ppermute | solution.py:541
  202.0 10.5 %collective-permute-start.52 = (f32[128,512]{1,0:T(8,128)S(1)}, f32[128,512]{1,0:T(8,128)S(1)}, u32[]{:S(2)}, u32[]{:S(2)}) collective-permute-start(f32[128,512]{1,0:T(8,128)S(1)} %get-tuple-element.195.refs_5_), channel_id=1, source_target_pairs={{0,2},{2,0},{4,6},{6,4},{1,3},{3,1},{5,7},{7,5},{8,10},{10,8},{12,... | collective-permute-start | bytes 786440 | tf_op jit(solution)/shard_map/ppermute | solution.py:541
  208.3 12.0 %collective-permute-start.56 = (f32[128,512]{1,0:T(8,128)S(1)}, f32[128,512]{1,0:T(8,128)S(1)}, u32[]{:S(2)}, u32[]{:S(2)}) collective-permute-start(f32[128,512]{1,0:T(8,128)S(1)} %shard_map.225.refs_7_.refs_3_), channel_id=1, source_target_pairs={{2,0},{4,6},{3,1},{5,7},{10,8},{12,14},{11,9},{13,15},{18,16},{20,... | collective-permute-start | bytes 786440 | tf_op jit(solution)/shard_map/ppermute | solution.py:544
  212.6 8.2 %collective-permute-start.55 = (f32[128,512]{1,0:T(8,128)S(1)}, f32[128,512]{1,0:T(8,128)S(1)}, u32[]{:S(2)}, u32[]{:S(2)}) collective-permute-start(f32[128,512]{1,0:T(8,128)S(1)} %shard_map.227.refs_2_.refs_0_), channel_id=1, source_target_pairs={{0,0},{2,4},{4,2},{6,6},{1,1},{3,5},{5,3},{7,7},{8,8},{10,12},{12,... | collective-permute-start | bytes 786440 | tf_op jit(solution)/shard_map/ppermute | solution.py:547
  213.5 13.1 %collective-permute-start.59 = (f32[128,512]{1,0:T(8,128)S(1)}, f32[128,512]{1,0:T(8,128)S(1)}, u32[]{:S(2)}, u32[]{:S(2)}) collective-permute-start(f32[128,512]{1,0:T(8,128)S(1)} %shard_map.228.refs_7_.refs_3_), channel_id=1, source_target_pairs={{0,2},{2,0},{4,6},{6,4},{1,3},{3,1},{5,7},{7,5},{8,10},{10,8},{12,... | collective-permute-start | bytes 786440 | tf_op jit(solution)/shard_map/ppermute | solution.py:541
  220.8 8.6 %collective-permute-start.58 = (f32[128,512]{1,0:T(8,128)S(1)}, f32[128,512]{1,0:T(8,128)S(1)}, u32[]{:S(2)}, u32[]{:S(2)}) collective-permute-start(f32[128,512]{1,0:T(8,128)S(1)} %shard_map.231.refs_7_.refs_3_), channel_id=1, source_target_pairs={{0,2},{2,0},{4,6},{6,4},{1,3},{3,1},{5,7},{7,5},{8,10},{10,8},{12,... | collective-permute-start | bytes 786440 | tf_op jit(solution)/shard_map/ppermute | solution.py:541
  244.1 9.6 %collective-permute-start.65 = (f32[136,512]{1,0:T(8,128)S(1)}, f32[136,512]{1,0:T(8,128)S(1)}, u32[]{:S(2)}, u32[]{:S(2)}) collective-permute-start(f32[136,512]{1,0:T(8,128)S(1)} %shard_map.236.refs_3_.refs_0_), channel_id=1, source_target_pairs={{0,2},{2,0},{4,6},{6,4},{1,3},{3,1},{5,7},{7,5},{8,10},{10,8},{12,... | collective-permute-start | bytes 835592 | tf_op jit(solution)/shard_map/ppermute | solution.py:541
  247.3 12.0 %collective-permute-start.67 = (f32[128,512]{1,0:T(8,128)S(1)}, f32[128,512]{1,0:T(8,128)S(1)}, u32[]{:S(2)}, u32[]{:S(2)}) collective-permute-start(f32[128,512]{1,0:T(8,128)S(1)} %shard_map.241.refs_2_.refs_0_), channel_id=1, source_target_pairs={{0,2},{2,0},{4,6},{6,4},{1,3},{3,1},{5,7},{7,5},{8,10},{10,8},{12,... | collective-permute-start | bytes 786440 | tf_op jit(solution)/shard_map/ppermute | solution.py:541
  254.4 10.6 %collective-permute-start.64 = (f32[128,512]{1,0:T(8,128)S(1)}, f32[128,512]{1,0:T(8,128)S(1)}, u32[]{:S(2)}, u32[]{:S(2)}) collective-permute-start(f32[128,512]{1,0:T(8,128)S(1)} %shard_map.237.refs_3_.refs_0_), channel_id=1, source_target_pairs={{0,2},{2,0},{4,6},{6,4},{1,3},{3,1},{5,7},{7,5},{8,10},{10,8},{12,... | collective-permute-start | bytes 786440 | tf_op jit(solution)/shard_map/ppermute | solution.py:541
  260.1 11.3 %collective-permute-start.69 = (f32[136,512]{1,0:T(8,128)S(1)}, f32[136,512]{1,0:T(8,128)S(1)}, u32[]{:S(2)}, u32[]{:S(2)}) collective-permute-start(f32[136,512]{1,0:T(8,128)S(1)} %get-tuple-element.218.refs_2_), channel_id=1, source_target_pairs={{0,2},{2,0},{4,6},{6,4},{1,3},{3,1},{5,7},{7,5},{8,10},{10,8},{12,... | collective-permute-start | bytes 835592 | tf_op jit(solution)/shard_map/ppermute | solution.py:541
  265.8 12.1 %collective-permute-start.72 = (f32[128,512]{1,0:T(8,128)S(1)}, f32[128,512]{1,0:T(8,128)S(1)}, u32[]{:S(2)}, u32[]{:S(2)}) collective-permute-start(f32[128,512]{1,0:T(8,128)S(1)} %get-tuple-element.219.refs_2_), channel_id=1, source_target_pairs={{0,2},{2,0},{4,6},{6,4},{1,3},{3,1},{5,7},{7,5},{8,10},{10,8},{12,... | collective-permute-start | bytes 786440 | tf_op jit(solution)/shard_map/ppermute | solution.py:541
  272.2 10.7 %collective-permute-start.71 = (f32[128,512]{1,0:T(8,128)S(1)}, f32[128,512]{1,0:T(8,128)S(1)}, u32[]{:S(2)}, u32[]{:S(2)}) collective-permute-start(f32[128,512]{1,0:T(8,128)S(1)} %get-tuple-element.220.refs_5_), channel_id=1, source_target_pairs={{0,2},{2,0},{4,6},{6,4},{1,3},{3,1},{5,7},{7,5},{8,10},{10,8},{12,... | collective-permute-start | bytes 786440 | tf_op jit(solution)/shard_map/ppermute | solution.py:541
  278.6 11.9 %collective-permute-start.75 = (f32[128,512]{1,0:T(8,128)S(1)}, f32[128,512]{1,0:T(8,128)S(1)}, u32[]{:S(2)}, u32[]{:S(2)}) collective-permute-start(f32[128,512]{1,0:T(8,128)S(1)} %shard_map.251.refs_7_.refs_3_), channel_id=1, source_target_pairs={{2,0},{4,6},{3,1},{5,7},{10,8},{12,14},{11,9},{13,15},{18,16},{20,... | collective-permute-start | bytes 786440 | tf_op jit(solution)/shard_map/ppermute | solution.py:544
  282.9 8.1 %collective-permute-start.74 = (f32[128,512]{1,0:T(8,128)S(1)}, f32[128,512]{1,0:T(8,128)S(1)}, u32[]{:S(2)}, u32[]{:S(2)}) collective-permute-start(f32[128,512]{1,0:T(8,128)S(1)} %shard_map.253.refs_2_.refs_0_), channel_id=1, source_target_pairs={{0,0},{2,4},{4,2},{6,6},{1,1},{3,5},{5,3},{7,7},{8,8},{10,12},{12,... | collective-permute-start | bytes 786440 | tf_op jit(solution)/shard_map/ppermute | solution.py:547
  283.6 13.2 %collective-permute-start.78 = (f32[128,512]{1,0:T(8,128)S(1)}, f32[128,512]{1,0:T(8,128)S(1)}, u32[]{:S(2)}, u32[]{:S(2)}) collective-permute-start(f32[128,512]{1,0:T(8,128)S(1)} %shard_map.254.refs_7_.refs_3_), channel_id=1, source_target_pairs={{0,2},{2,0},{4,6},{6,4},{1,3},{3,1},{5,7},{7,5},{8,10},{10,8},{12,... | collective-permute-start | bytes 786440 | tf_op jit(solution)/shard_map/ppermute | solution.py:541
  291.0 8.6 %collective-permute-start.77 = (f32[128,512]{1,0:T(8,128)S(1)}, f32[128,512]{1,0:T(8,128)S(1)}, u32[]{:S(2)}, u32[]{:S(2)}) collective-permute-start(f32[128,512]{1,0:T(8,128)S(1)} %shard_map.257.refs_7_.refs_3_), channel_id=1, source_target_pairs={{0,2},{2,0},{4,6},{6,4},{1,3},{3,1},{5,7},{7,5},{8,10},{10,8},{12,... | collective-permute-start | bytes 786440 | tf_op jit(solution)/shard_map/ppermute | solution.py:541
  (66 other events, 246.5 us)

commit v5 on v0

--- a/solution.py
+++ b/solution.py
@@ -541,7 +541,8 @@
         return lax.ppermute(part, "chip", [(0, 1), (1, 0), (2, 3), (3, 2)])
 
     def inner_swap(part):
-        return lax.ppermute(part, "chip", [(0, 0), (1, 2), (2, 1), (3, 3)])
+        hops = [(2, 4), (4, 2), (3, 5), (5, 3), (0, 1), (1, 0), (6, 7), (7, 6)]
+        return lax.ppermute(part, ("chip", "core"), hops)
 
     def product(rows, pairs):
         got_rows = swap(rows)

time: 304 us -> 297 us (0.977)
  starting transfers between devices: 173 us -> 121 us
  waiting for transfers between devices: 71.8 us -> 117 us
    ppermute x36, waiting for transfers between devices: 38.6 us -> 83.4 us  [outer_swap(): return lax.ppermute(part, 'chip', [(0, 1), (1, 0), (2, 3), (3, 2)])]
    ppermute x36, starting transfers between devices: 140 us -> 105 us  [outer_swap(): return lax.ppermute(part, 'chip', [(0, 1), (1, 0), (2, 3), (3, 2)])]
    ppermute x24, starting transfers between devices: 18 us -> 1.64 us  [inner_swap(): return lax.ppermute(part, ('chip', 'core'), hops)]
  transfers between devices with their start and end apart: 82 -> 82, of which waited for: 33 -> 51; matrix products, arithmetic and copies ran while one was open for 0% -> 0% of each run, Pallas kernels for 12% -> 12%
where the time goes in v5:
time: 297 us; the launch traced here: 296 us
  starting transfers between devices  121 us (41%)
  waiting for transfers between devices  117 us (39%)
  Pallas kernels  50.2 us (17%)
  local copies, waits for them, and re-layouts  5.26 us (2%)
    ppermute x36, starting transfers between devices, outer_swap(): return lax.ppermute(part, 'chip', [(0, 1), (1, 0), (2, 3), (3, 2)])  105 us
    ppermute x36, waiting for transfers between devices, outer_swap(): return lax.ppermute(part, 'chip', [(0, 1), (1, 0), (2, 3), (3, 2)])  83.4 us
    pallas_call x96, Pallas kernels, call(): pl.pallas_call(body, in_specs=[SMEM] * len(scalars) + [VMEM] * len(ins) +...  29.6 us
    ppermute x14, waiting for transfers between devices, swap(): return lax.ppermute(part, 'core', [(0, 1), (1, 0)])  11.4 us
    ppermute x4, waiting for transfers between devices, data_terms(): part = part + lax.ppermute(part, 'dp', [(d, d ^ step) for d in range(n_dp)])  10.9 us
    ppermute x4, waiting for transfers between devices, data_terms(): lax.ppermute(part, 'dp', [(d, d ^ step) for d in range(n_dp)])  10.9 us
    pallas_call x1, Pallas kernels, project(): pl.pallas_call(project_kernel, in_specs=[SMEM] + [hbm] * 4 + [VMEM] * 6,...  8.78 us
    ppermute x4, starting transfers between devices, data_terms(): lax.ppermute(part, 'dp', [(d, d ^ step) for d in range(n_dp)])  6.28 us
  transfers between devices with their start and end apart: 82, of which 51 were waited for; matrix products, arithmetic and copies ran while one was open for 0% of the time, Pallas kernels for 12%

profile of v5, /device:TPU:0, one launch (start us, length us, event | category | flops | bytes accessed | tf_op | source)
XLA Modules:
  0.0 296.4 jit_solution(182851082196503)
XLA Ops:
  8.1 8.8 %shard_map.156 = (f32[3,128,128]{2,1,0:T(8,128)S(1)}, bf16[128,384]{1,0:T(8,128)(2,1)S(1)}, bf16[128,384]{1,0:T(8,128)(2,1)S(1)}, f32[128,16]{1,0:T(8,128)S(1)},...) custom-call(s32[1]{0:T(128)S(6)} %copy.17.limit_ref.refs_1_.refs_2_.refs_4_.refs_8_, bf16[128,6144]{1,0:T(8,128)(2,1)S(1)} %copy-done.1, ...), custom_call_target="tpu_custom_call" | custom-call | flops 1811939328 | bytes 14155776 | tf_op jit(solution)/shard_map/pallas_call | solution.py:188
  21.7 3.0 %collective-permute-start.6 = (f32[136,512]{1,0:T(8,128)S(1)}, f32[136,512]{1,0:T(8,128)S(1)}, u32[]{:S(2)}, u32[]{:S(2)}) collective-permute-start(f32[136,512]{1,0:T(8,128)S(1)} %get-tuple-element.130.refs_4_.refs_0_), channel_id=1, source_target_pairs={{0,2},{2,0},{4,6},{6,4},{1,3},{3,1},{5,7},{7,5},{8,10},{10,8},{12,... | collective-permute-start | bytes 835592 | tf_op jit(solution)/shard_map/ppermute | solution.py:541
  32.0 3.5 %collective-permute-start.11 = (f32[128,512]{1,0:T(8,128)}, f32[128,512]{1,0:T(8,128)S(1)}, u32[]{:S(2)}, u32[]{:S(2)}) collective-permute-start(f32[128,512]{1,0:T(8,128)} %copy-done.19), channel_id=1, source_target_pairs={{0,2},{2,0},{4,6},{6,4},{1,3},{3,1},{5,7},{7,5},{8,10},{10,8},{12,... | collective-permute-start | bytes 786440 | tf_op jit(solution)/shard_map/ppermute | solution.py:541
  39.9 3.3 %collective-permute-start.13 = (f32[136,512]{1,0:T(8,128)S(1)}, f32[136,512]{1,0:T(8,128)S(1)}, u32[]{:S(2)}, u32[]{:S(2)}) collective-permute-start(f32[136,512]{1,0:T(8,128)S(1)} %get-tuple-element.140.refs_4_), channel_id=1, source_target_pairs={{0,2},{2,0},{4,6},{6,4},{1,3},{3,1},{5,7},{7,5},{8,10},{10,8},{12,... | collective-permute-start | bytes 835592 | tf_op jit(solution)/shard_map/ppermute | solution.py:541
  45.1 3.2 %collective-permute-start.15 = (f32[128,512]{1,0:T(8,128)S(1)}, f32[128,512]{1,0:T(8,128)S(1)}, u32[]{:S(2)}, u32[]{:S(2)}) collective-permute-start(f32[128,512]{1,0:T(8,128)S(1)} %get-tuple-element.142.refs_4_), channel_id=1, source_target_pairs={{0,2},{2,0},{4,6},{6,4},{1,3},{3,1},{5,7},{7,5},{8,10},{10,8},{12,... | collective-permute-start | bytes 786440 | tf_op jit(solution)/shard_map/ppermute | solution.py:541
  50.7 3.7 %collective-permute-start.14 = (f32[128,512]{1,0:T(8,128)S(1)}, f32[128,512]{1,0:T(8,128)S(1)}, u32[]{:S(2)}, u32[]{:S(2)}) collective-permute-start(f32[128,512]{1,0:T(8,128)S(1)} %get-tuple-element.144.refs_6_), channel_id=1, source_target_pairs={{0,2},{2,0},{4,6},{6,4},{1,3},{3,1},{5,7},{7,5},{8,10},{10,8},{12,... | collective-permute-start | bytes 786440 | tf_op jit(solution)/shard_map/ppermute | solution.py:541
  55.6 5.1 %collective-permute-start.18 = (f32[128,512]{1,0:T(8,128)S(1)}, f32[128,512]{1,0:T(8,128)S(1)}, u32[]{:S(2)}, u32[]{:S(2)}) collective-permute-start(f32[128,512]{1,0:T(8,128)S(1)} %shard_map.173.refs_8_.refs_3_), channel_id=1, source_target_pairs={{0,2},{2,0},{4,6},{6,4},{1,3},{3,1},{5,7},{7,5},{8,10},{10,8},{12,... | collective-permute-start | bytes 786440 | tf_op jit(solution)/shard_map/ppermute | solution.py:541
  61.8 4.6 %collective-permute-start.21 = (f32[128,512]{1,0:T(8,128)S(1)}, f32[128,512]{1,0:T(8,128)S(1)}, u32[]{:S(2)}, u32[]{:S(2)}) collective-permute-start(f32[128,512]{1,0:T(8,128)S(1)} %shard_map.176.refs_8_.refs_3_), channel_id=1, source_target_pairs={{0,2},{2,0},{4,6},{6,4},{1,3},{3,1},{5,7},{7,5},{8,10},{10,8},{12,... | collective-permute-start | bytes 786440 | tf_op jit(solution)/shard_map/ppermute | solution.py:541
  68.0 2.9 collective-permute-start.20
  70.9 2.7 collective-permute-done.21.refs_2_
  74.0 3.5 %collective-permute-done.20.refs_2_ = f32[128,512]{1,0:T(8,128)S(1)} collective-permute-done((f32[128,512]{1,0:T(8,128)S(1)}, f32[128,512]{1,0:T(8,128)S(1)}, u32[]{:S(2)}, u32[]{:S(2)}) %collective-permute-start.20) | collective-permute-done | bytes 262176 | tf_op jit(solution)/shard_map/ppermute | solution.py:541
  82.5 2.7 collective-permute-done.23
  87.0 2.7 collective-permute-done.24.refs_1_
  95.8 6.0 %collective-permute-done.27.refs_1_ = f32[136,512]{1,0:T(8,128)S(1)} collective-permute-done((f32[136,512]{1,0:T(8,128)S(1)}, f32[136,512]{1,0:T(8,128)S(1)}, u32[]{:S(2)}, u32[]{:S(2)}) %collective-permute-start.27) | collective-permute-done | bytes 278560 | tf_op jit(solution)/shard_map/ppermute | solution.py:541
  101.9 3.3 %collective-permute-start.26 = (f32[128,512]{1,0:T(8,128)S(1)}, f32[128,512]{1,0:T(8,128)S(1)}, u32[]{:S(2)}, u32[]{:S(2)}) collective-permute-start(f32[128,512]{1,0:T(8,128)S(1)} %shard_map.185.refs_3_.refs_0_), channel_id=1, source_target_pairs={{0,2},{2,0},{4,6},{6,4},{1,3},{3,1},{5,7},{7,5},{8,10},{10,8},{12,... | collective-permute-start | bytes 786440 | tf_op jit(solution)/shard_map/ppermute | solution.py:541
  107.6 3.5 %collective-permute-start.31 = (f32[136,512]{1,0:T(8,128)S(1)}, f32[136,512]{1,0:T(8,128)S(1)}, u32[]{:S(2)}, u32[]{:S(2)}) collective-permute-start(f32[136,512]{1,0:T(8,128)S(1)} %get-tuple-element.172.refs_2_), channel_id=1, source_target_pairs={{0,2},{2,0},{4,6},{6,4},{1,3},{3,1},{5,7},{7,5},{8,10},{10,8},{12,... | collective-permute-start | bytes 835592 | tf_op jit(solution)/shard_map/ppermute | solution.py:541
  113.2 3.5 %collective-permute-start.34 = (f32[128,512]{1,0:T(8,128)S(1)}, f32[128,512]{1,0:T(8,128)S(1)}, u32[]{:S(2)}, u32[]{:S(2)}) collective-permute-start(f32[128,512]{1,0:T(8,128)S(1)} %get-tuple-element.173.refs_2_), channel_id=1, source_target_pairs={{0,2},{2,0},{4,6},{6,4},{1,3},{3,1},{5,7},{7,5},{8,10},{10,8},{12,... | collective-permute-start | bytes 786440 | tf_op jit(solution)/shard_map/ppermute | solution.py:541
  119.2 3.3 %collective-permute-start.33 = (f32[128,512]{1,0:T(8,128)S(1)}, f32[128,512]{1,0:T(8,128)S(1)}, u32[]{:S(2)}, u32[]{:S(2)}) collective-permute-start(f32[128,512]{1,0:T(8,128)S(1)} %get-tuple-element.174.refs_5_), channel_id=1, source_target_pairs={{0,2},{2,0},{4,6},{6,4},{1,3},{3,1},{5,7},{7,5},{8,10},{10,8},{12,... | collective-permute-start | bytes 786440 | tf_op jit(solution)/shard_map/ppermute | solution.py:541
  124.8 3.3 %collective-permute-start.37 = (f32[128,512]{1,0:T(8,128)S(1)}, f32[128,512]{1,0:T(8,128)S(1)}, u32[]{:S(2)}, u32[]{:S(2)}) collective-permute-start(f32[128,512]{1,0:T(8,128)S(1)} %shard_map.199.refs_7_.refs_3_), channel_id=1, source_target_pairs={{0,2},{2,0},{4,6},{6,4},{1,3},{3,1},{5,7},{7,5},{8,10},{10,8},{12,... | collective-permute-start | bytes 786440 | tf_op jit(solution)/shard_map/ppermute | solution.py:541
  130.4 3.3 %collective-permute-start.40 = (f32[128,512]{1,0:T(8,128)S(1)}, f32[128,512]{1,0:T(8,128)S(1)}, u32[]{:S(2)}, u32[]{:S(2)}) collective-permute-start(f32[128,512]{1,0:T(8,128)S(1)} %shard_map.202.refs_7_.refs_3_), channel_id=1, source_target_pairs={{0,2},{2,0},{4,6},{6,4},{1,3},{3,1},{5,7},{7,5},{8,10},{10,8},{12,... | collective-permute-start | bytes 786440 | tf_op jit(solution)/shard_map/ppermute | solution.py:541
  136.3 2.6 collective-permute-start.39
  141.9 4.4 %collective-permute-done.39.refs_2_ = f32[128,512]{1,0:T(8,128)S(1)} collective-permute-done((f32[128,512]{1,0:T(8,128)S(1)}, f32[128,512]{1,0:T(8,128)S(1)}, u32[]{:S(2)}, u32[]{:S(2)}) %collective-permute-start.39) | collective-permute-done | bytes 262176 | tf_op jit(solution)/shard_map/ppermute | solution.py:541
  151.2 2.7 collective-permute-done.42
  155.6 2.7 collective-permute-done.43.refs_1_
  164.4 6.0 %collective-permute-done.46.refs_1_ = f32[136,512]{1,0:T(8,128)S(1)} collective-permute-done((f32[136,512]{1,0:T(8,128)S(1)}, f32[136,512]{1,0:T(8,128)S(1)}, u32[]{:S(2)}, u32[]{:S(2)}) %collective-permute-start.46) | collective-permute-done | bytes 278560 | tf_op jit(solution)/shard_map/ppermute | solution.py:541
  170.6 3.3 %collective-permute-start.45 = (f32[128,512]{1,0:T(8,128)S(1)}, f32[128,512]{1,0:T(8,128)S(1)}, u32[]{:S(2)}, u32[]{:S(2)}) collective-permute-start(f32[128,512]{1,0:T(8,128)S(1)} %shard_map.211.refs_3_.refs_0_), channel_id=1, source_target_pairs={{0,2},{2,0},{4,6},{6,4},{1,3},{3,1},{5,7},{7,5},{8,10},{10,8},{12,... | collective-permute-start | bytes 786440 | tf_op jit(solution)/shard_map/ppermute | solution.py:541
  176.2 3.5 %collective-permute-start.50 = (f32[136,512]{1,0:T(8,128)S(1)}, f32[136,512]{1,0:T(8,128)S(1)}, u32[]{:S(2)}, u32[]{:S(2)}) collective-permute-start(f32[136,512]{1,0:T(8,128)S(1)} %get-tuple-element.193.refs_2_), channel_id=1, source_target_pairs={{0,2},{2,0},{4,6},{6,4},{1,3},{3,1},{5,7},{7,5},{8,10},{10,8},{12,... | collective-permute-start | bytes 835592 | tf_op jit(solution)/shard_map/ppermute | solution.py:541
  181.9 3.5 %collective-permute-start.53 = (f32[128,512]{1,0:T(8,128)S(1)}, f32[128,512]{1,0:T(8,128)S(1)}, u32[]{:S(2)}, u32[]{:S(2)}) collective-permute-start(f32[128,512]{1,0:T(8,128)S(1)} %get-tuple-element.194.refs_2_), channel_id=1, source_target_pairs={{0,2},{2,0},{4,6},{6,4},{1,3},{3,1},{5,7},{7,5},{8,10},{10,8},{12,... | collective-permute-start | bytes 786440 | tf_op jit(solution)/shard_map/ppermute | solution.py:541
  187.8 3.3 %collective-permute-start.52 = (f32[128,512]{1,0:T(8,128)S(1)}, f32[128,512]{1,0:T(8,128)S(1)}, u32[]{:S(2)}, u32[]{:S(2)}) collective-permute-start(f32[128,512]{1,0:T(8,128)S(1)} %get-tuple-element.195.refs_5_), channel_id=1, source_target_pairs={{0,2},{2,0},{4,6},{6,4},{1,3},{3,1},{5,7},{7,5},{8,10},{10,8},{12,... | collective-permute-start | bytes 786440 | tf_op jit(solution)/shard_map/ppermute | solution.py:541
  193.4 3.3 %collective-permute-start.56 = (f32[128,512]{1,0:T(8,128)S(1)}, f32[128,512]{1,0:T(8,128)S(1)}, u32[]{:S(2)}, u32[]{:S(2)}) collective-permute-start(f32[128,512]{1,0:T(8,128)S(1)} %shard_map.225.refs_7_.refs_3_), channel_id=1, source_target_pairs={{0,2},{2,0},{4,6},{6,4},{1,3},{3,1},{5,7},{7,5},{8,10},{10,8},{12,... | collective-permute-start | bytes 786440 | tf_op jit(solution)/shard_map/ppermute | solution.py:541
  199.0 3.3 %collective-permute-start.59 = (f32[128,512]{1,0:T(8,128)S(1)}, f32[128,512]{1,0:T(8,128)S(1)}, u32[]{:S(2)}, u32[]{:S(2)}) collective-permute-start(f32[128,512]{1,0:T(8,128)S(1)} %shard_map.228.refs_7_.refs_3_), channel_id=1, source_target_pairs={{0,2},{2,0},{4,6},{6,4},{1,3},{3,1},{5,7},{7,5},{8,10},{10,8},{12,... | collective-permute-start | bytes 786440 | tf_op jit(solution)/shard_map/ppermute | solution.py:541
  204.9 2.6 collective-permute-start.58
  207.5 2.6 collective-permute-done.59.refs_2_
  210.5 4.4 %collective-permute-done.58.refs_2_ = f32[128,512]{1,0:T(8,128)S(1)} collective-permute-done((f32[128,512]{1,0:T(8,128)S(1)}, f32[128,512]{1,0:T(8,128)S(1)}, u32[]{:S(2)}, u32[]{:S(2)}) %collective-permute-start.58) | collective-permute-done | bytes 262176 | tf_op jit(solution)/shard_map/ppermute | solution.py:541
  219.9 2.7 collective-permute-done.61
  224.2 2.7 collective-permute-done.62.refs_1_
  233.3 5.8 %collective-permute-done.65.refs_1_ = f32[136,512]{1,0:T(8,128)S(1)} collective-permute-done((f32[136,512]{1,0:T(8,128)S(1)}, f32[136,512]{1,0:T(8,128)S(1)}, u32[]{:S(2)}, u32[]{:S(2)}) %collective-permute-start.65) | collective-permute-done | bytes 278560 | tf_op jit(solution)/shard_map/ppermute | solution.py:541
  239.3 3.3 %collective-permute-start.64 = (f32[128,512]{1,0:T(8,128)S(1)}, f32[128,512]{1,0:T(8,128)S(1)}, u32[]{:S(2)}, u32[]{:S(2)}) collective-permute-start(f32[128,512]{1,0:T(8,128)S(1)} %shard_map.237.refs_3_.refs_0_), channel_id=1, source_target_pairs={{0,2},{2,0},{4,6},{6,4},{1,3},{3,1},{5,7},{7,5},{8,10},{10,8},{12,... | collective-permute-start | bytes 786440 | tf_op jit(solution)/shard_map/ppermute | solution.py:541
  245.0 3.5 %collective-permute-start.69 = (f32[136,512]{1,0:T(8,128)S(1)}, f32[136,512]{1,0:T(8,128)S(1)}, u32[]{:S(2)}, u32[]{:S(2)}) collective-permute-start(f32[136,512]{1,0:T(8,128)S(1)} %get-tuple-element.218.refs_2_), channel_id=1, source_target_pairs={{0,2},{2,0},{4,6},{6,4},{1,3},{3,1},{5,7},{7,5},{8,10},{10,8},{12,... | collective-permute-start | bytes 835592 | tf_op jit(solution)/shard_map/ppermute | solution.py:541
  250.6 3.5 %collective-permute-start.72 = (f32[128,512]{1,0:T(8,128)S(1)}, f32[128,512]{1,0:T(8,128)S(1)}, u32[]{:S(2)}, u32[]{:S(2)}) collective-permute-start(f32[128,512]{1,0:T(8,128)S(1)} %get-tuple-element.219.refs_2_), channel_id=1, source_target_pairs={{0,2},{2,0},{4,6},{6,4},{1,3},{3,1},{5,7},{7,5},{8,10},{10,8},{12,... | collective-permute-start | bytes 786440 | tf_op jit(solution)/shard_map/ppermute | solution.py:541
  256.6 3.3 %collective-permute-start.71 = (f32[128,512]{1,0:T(8,128)S(1)}, f32[128,512]{1,0:T(8,128)S(1)}, u32[]{:S(2)}, u32[]{:S(2)}) collective-permute-start(f32[128,512]{1,0:T(8,128)S(1)} %get-tuple-element.220.refs_5_), channel_id=1, source_target_pairs={{0,2},{2,0},{4,6},{6,4},{1,3},{3,1},{5,7},{7,5},{8,10},{10,8},{12,... | collective-permute-start | bytes 786440 | tf_op jit(solution)/shard_map/ppermute | solution.py:541
  262.1 3.3 %collective-permute-start.75 = (f32[128,512]{1,0:T(8,128)S(1)}, f32[128,512]{1,0:T(8,128)S(1)}, u32[]{:S(2)}, u32[]{:S(2)}) collective-permute-start(f32[128,512]{1,0:T(8,128)S(1)} %shard_map.251.refs_7_.refs_3_), channel_id=1, source_target_pairs={{0,2},{2,0},{4,6},{6,4},{1,3},{3,1},{5,7},{7,5},{8,10},{10,8},{12,... | collective-permute-start | bytes 786440 | tf_op jit(solution)/shard_map/ppermute | solution.py:541
  267.8 3.3 %collective-permute-start.78 = (f32[128,512]{1,0:T(8,128)S(1)}, f32[128,512]{1,0:T(8,128)S(1)}, u32[]{:S(2)}, u32[]{:S(2)}) collective-permute-start(f32[128,512]{1,0:T(8,128)S(1)} %shard_map.254.refs_7_.refs_3_), channel_id=1, source_target_pairs={{0,2},{2,0},{4,6},{6,4},{1,3},{3,1},{5,7},{7,5},{8,10},{10,8},{12,... | collective-permute-start | bytes 786440 | tf_op jit(solution)/shard_map/ppermute | solution.py:541
  273.7 2.6 collective-permute-start.77
  276.3 2.6 collective-permute-done.78.refs_2_
  279.2 4.4 %collective-permute-done.77.refs_2_ = f32[128,512]{1,0:T(8,128)S(1)} collective-permute-done((f32[128,512]{1,0:T(8,128)S(1)}, f32[128,512]{1,0:T(8,128)S(1)}, u32[]{:S(2)}, u32[]{:S(2)}) %collective-permute-start.77) | collective-permute-done | bytes 262176 | tf_op jit(solution)/shard_map/ppermute | solution.py:541
  288.6 2.7 collective-permute-done.80
  292.9 2.7 collective-permute-done.81.refs_1_
  (284 shorter events, 122.9 us)
Async XLA Ops:
  6.3 12.6 %collective-permute-start.3 = (f32[384,512]{1,0:T(8,128)}, f32[384,512]{1,0:T(8,128)}, u32[]{:S(2)}, u32[]{:S(2)}) collective-permute-start(f32[384,512]{1,0:T(8,128)} %get-tuple-element.129), channel_id=1, source_target_pairs={{0,1},{1,0},{2,3},{3,2},{4,5},{5,4},{6,7},{7,6},{8,9},{9,8},{10,11... | collective-permute-start | bytes 2359304 | tf_op jit(solution)/shard_map/ppermute | solution.py:516
  6.9 18.1 %collective-permute-start.2 = (f32[384,512]{1,0:T(8,128)}, f32[384,512]{1,0:T(8,128)}, u32[]{:S(2)}, u32[]{:S(2)}) collective-permute-start(f32[384,512]{1,0:T(8,128)} %get-tuple-element.127), channel_id=1, source_target_pairs={{0,1},{1,0},{2,3},{3,2},{4,5},{5,4},{6,7},{7,6},{8,9},{9,8},{10,11... | collective-permute-start | bytes 2359304 | tf_op jit(solution)/shard_map/ppermute | solution.py:516
  6.9 21.3 %collective-permute-start.7 = (f32[384,512]{1,0:T(8,128)}, f32[384,512]{1,0:T(8,128)}, u32[]{:S(2)}, u32[]{:S(2)}) collective-permute-start(f32[384,512]{1,0:T(8,128)} %get-tuple-element.135), channel_id=1, source_target_pairs={{0,1},{1,0},{2,3},{3,2},{4,5},{5,4},{6,7},{7,6},{8,9},{9,8},{10,11... | collective-permute-start | bytes 2359304 | tf_op jit(solution)/shard_map/ppermute | solution.py:516
  17.1 14.9 %collective-permute-start.5 = (f32[384,512]{1,0:T(8,128)}, f32[384,512]{1,0:T(8,128)}, u32[]{:S(2)}, u32[]{:S(2)}) collective-permute-start(f32[384,512]{1,0:T(8,128)} %get-tuple-element.133), channel_id=1, source_target_pairs={{0,1},{1,0},{2,3},{3,2},{4,5},{5,4},{6,7},{7,6},{8,9},{9,8},{10,11... | collective-permute-start | bytes 2359304 | tf_op jit(solution)/shard_map/ppermute | solution.py:516
  18.8 24.4 %collective-permute-start.9 = (f32[384,512]{1,0:T(8,128)}, f32[384,512]{1,0:T(8,128)}, u32[]{:S(2)}, u32[]{:S(2)}) collective-permute-start(f32[384,512]{1,0:T(8,128)} %copy-done.8), channel_id=1, source_target_pairs={{0,1},{1,0},{2,3},{3,2},{4,5},{5,4},{6,7},{7,6},{8,9},{9,8},{10,11... | collective-permute-start | bytes 2359304 | tf_op jit(solution)/shard_map/ppermute | solution.py:516
  21.7 10.0 %collective-permute-start.6 = (f32[136,512]{1,0:T(8,128)S(1)}, f32[136,512]{1,0:T(8,128)S(1)}, u32[]{:S(2)}, u32[]{:S(2)}) collective-permute-start(f32[136,512]{1,0:T(8,128)S(1)} %get-tuple-element.130.refs_4_.refs_0_), channel_id=1, source_target_pairs={{0,2},{2,0},{4,6},{6,4},{1,3},{3,1},{5,7},{7,5},{8,10},{10,8},{12,... | collective-permute-start | bytes 835592 | tf_op jit(solution)/shard_map/ppermute | solution.py:541
  24.9 23.4 %collective-permute-start.1 = (f32[384,512]{1,0:T(8,128)S(1)}, f32[384,512]{1,0:T(8,128)}, u32[]{:S(2)}, u32[]{:S(2)}) collective-permute-start(f32[384,512]{1,0:T(8,128)S(1)} %get-tuple-element.125), channel_id=1, source_target_pairs={{0,1},{1,0},{2,3},{3,2},{4,5},{5,4},{6,7},{7,6},{8,9},{9,8},{10,11... | collective-permute-start | bytes 2359304 | tf_op jit(solution)/shard_map/ppermute | solution.py:516
  28.3 9.4 %collective-permute-start.4 = (f32[128,512]{1,0:T(8,128)}, f32[128,512]{1,0:T(8,128)}, u32[]{:S(2)}, u32[]{:S(2)}) collective-permute-start(f32[128,512]{1,0:T(8,128)} %get-tuple-element.131.refs_4_.refs_0_), channel_id=1, source_target_pairs={{0,2},{2,0},{4,6},{6,4},{1,3},{3,1},{5,7},{7,5},{8,10},{10,8},{12,... | collective-permute-start | bytes 786440 | tf_op jit(solution)/shard_map/ppermute | solution.py:541
  31.9 6.9 %collective-permute-start.10 = (f32[136,512]{1,0:T(8,128)S(1)}, f32[136,512]{1,0:T(8,128)}, u32[]{:S(2)}, u32[]{:S(2)}) collective-permute-start(f32[136,512]{1,0:T(8,128)S(1)} %shard_map.161.refs_4_.refs_1_), channel_id=1, source_target_pairs={{2,4},{4,2},{3,5},{5,3},{0,1},{1,0},{6,7},{7,6},{10,12},{12,10},{1... | collective-permute-start | bytes 835592 | tf_op jit(solution)/shard_map/ppermute | solution.py:545
  32.0 12.8 %collective-permute-start.11 = (f32[128,512]{1,0:T(8,128)}, f32[128,512]{1,0:T(8,128)S(1)}, u32[]{:S(2)}, u32[]{:S(2)}) collective-permute-start(f32[128,512]{1,0:T(8,128)} %copy-done.19), channel_id=1, source_target_pairs={{0,2},{2,0},{4,6},{6,4},{1,3},{3,1},{5,7},{7,5},{8,10},{10,8},{12,... | collective-permute-start | bytes 786440 | tf_op jit(solution)/shard_map/ppermute | solution.py:541
  38.8 6.3 %collective-permute-start.8 = (f32[128,512]{1,0:T(8,128)S(1)}, f32[128,512]{1,0:T(8,128)S(1)}, u32[]{:S(2)}, u32[]{:S(2)}) collective-permute-start(f32[128,512]{1,0:T(8,128)S(1)} %shard_map.163.refs_4_.refs_1_), channel_id=1, source_target_pairs={{2,4},{4,2},{3,5},{5,3},{0,1},{1,0},{6,7},{7,6},{10,12},{12,10},{1... | collective-permute-start | bytes 786440 | tf_op jit(solution)/shard_map/ppermute | solution.py:545
  39.9 10.6 %collective-permute-start.13 = (f32[136,512]{1,0:T(8,128)S(1)}, f32[136,512]{1,0:T(8,128)S(1)}, u32[]{:S(2)}, u32[]{:S(2)}) collective-permute-start(f32[136,512]{1,0:T(8,128)S(1)} %get-tuple-element.140.refs_4_), channel_id=1, source_target_pairs={{0,2},{2,0},{4,6},{6,4},{1,3},{3,1},{5,7},{7,5},{8,10},{10,8},{12,... | collective-permute-start | bytes 835592 | tf_op jit(solution)/shard_map/ppermute | solution.py:541
  45.1 10.3 %collective-permute-start.15 = (f32[128,512]{1,0:T(8,128)S(1)}, f32[128,512]{1,0:T(8,128)S(1)}, u32[]{:S(2)}, u32[]{:S(2)}) collective-permute-start(f32[128,512]{1,0:T(8,128)S(1)} %get-tuple-element.142.refs_4_), channel_id=1, source_target_pairs={{0,2},{2,0},{4,6},{6,4},{1,3},{3,1},{5,7},{7,5},{8,10},{10,8},{12,... | collective-permute-start | bytes 786440 | tf_op jit(solution)/shard_map/ppermute | solution.py:541
  50.7 10.9 %collective-permute-start.14 = (f32[128,512]{1,0:T(8,128)S(1)}, f32[128,512]{1,0:T(8,128)S(1)}, u32[]{:S(2)}, u32[]{:S(2)}) collective-permute-start(f32[128,512]{1,0:T(8,128)S(1)} %get-tuple-element.144.refs_6_), channel_id=1, source_target_pairs={{0,2},{2,0},{4,6},{6,4},{1,3},{3,1},{5,7},{7,5},{8,10},{10,8},{12,... | collective-permute-start | bytes 786440 | tf_op jit(solution)/shard_map/ppermute | solution.py:541
  55.5 6.3 %collective-permute-start.19 = (f32[128,512]{1,0:T(8,128)S(1)}, f32[128,512]{1,0:T(8,128)S(1)}, u32[]{:S(2)}, u32[]{:S(2)}) collective-permute-start(f32[128,512]{1,0:T(8,128)S(1)} %shard_map.172.refs_2_.refs_0_), channel_id=1, source_target_pairs={{2,4},{4,2},{3,5},{5,3},{0,1},{1,0},{6,7},{7,6},{10,12},{12,10},{1... | collective-permute-start | bytes 786440 | tf_op jit(solution)/shard_map/ppermute | solution.py:545
  55.6 11.9 %collective-permute-start.18 = (f32[128,512]{1,0:T(8,128)S(1)}, f32[128,512]{1,0:T(8,128)S(1)}, u32[]{:S(2)}, u32[]{:S(2)}) collective-permute-start(f32[128,512]{1,0:T(8,128)S(1)} %shard_map.173.refs_8_.refs_3_), channel_id=1, source_target_pairs={{0,2},{2,0},{4,6},{6,4},{1,3},{3,1},{5,7},{7,5},{8,10},{10,8},{12,... | collective-permute-start | bytes 786440 | tf_op jit(solution)/shard_map/ppermute | solution.py:541
  61.7 6.2 %collective-permute-start.17 = (f32[128,512]{1,0:T(8,128)S(1)}, f32[128,512]{1,0:T(8,128)S(1)}, u32[]{:S(2)}, u32[]{:S(2)}) collective-permute-start(f32[128,512]{1,0:T(8,128)S(1)} %shard_map.175.refs_2_.refs_0_), channel_id=1, source_target_pairs={{2,4},{4,2},{3,5},{5,3},{0,1},{1,0},{6,7},{7,6},{10,12},{12,10},{1... | collective-permute-start | bytes 786440 | tf_op jit(solution)/shard_map/ppermute | solution.py:545
  61.8 11.8 %collective-permute-start.21 = (f32[128,512]{1,0:T(8,128)S(1)}, f32[128,512]{1,0:T(8,128)S(1)}, u32[]{:S(2)}, u32[]{:S(2)}) collective-permute-start(f32[128,512]{1,0:T(8,128)S(1)} %shard_map.176.refs_8_.refs_3_), channel_id=1, source_target_pairs={{0,2},{2,0},{4,6},{6,4},{1,3},{3,1},{5,7},{7,5},{8,10},{10,8},{12,... | collective-permute-start | bytes 786440 | tf_op jit(solution)/shard_map/ppermute | solution.py:541
  68.0 9.6 %collective-permute-start.20 = (f32[128,512]{1,0:T(8,128)S(1)}, f32[128,512]{1,0:T(8,128)S(1)}, u32[]{:S(2)}, u32[]{:S(2)}) collective-permute-start(f32[128,512]{1,0:T(8,128)S(1)} %shard_map.179.refs_8_.refs_3_), channel_id=1, source_target_pairs={{0,2},{2,0},{4,6},{6,4},{1,3},{3,1},{5,7},{7,5},{8,10},{10,8},{12,... | collective-permute-start | bytes 786440 | tf_op jit(solution)/shard_map/ppermute | solution.py:541
  92.2 9.6 %collective-permute-start.27 = (f32[136,512]{1,0:T(8,128)S(1)}, f32[136,512]{1,0:T(8,128)S(1)}, u32[]{:S(2)}, u32[]{:S(2)}) collective-permute-start(f32[136,512]{1,0:T(8,128)S(1)} %shard_map.184.refs_3_.refs_0_), channel_id=1, source_target_pairs={{0,2},{2,0},{4,6},{6,4},{1,3},{3,1},{5,7},{7,5},{8,10},{10,8},{12,... | collective-permute-start | bytes 835592 | tf_op jit(solution)/shard_map/ppermute | solution.py:541
  95.4 12.0 %collective-permute-start.29 = (f32[128,512]{1,0:T(8,128)S(1)}, f32[128,512]{1,0:T(8,128)S(1)}, u32[]{:S(2)}, u32[]{:S(2)}) collective-permute-start(f32[128,512]{1,0:T(8,128)S(1)} %shard_map.189.refs_2_.refs_0_), channel_id=1, source_target_pairs={{0,2},{2,0},{4,6},{6,4},{1,3},{3,1},{5,7},{7,5},{8,10},{10,8},{12,... | collective-permute-start | bytes 786440 | tf_op jit(solution)/shard_map/ppermute | solution.py:541
  101.9 11.1 %collective-permute-start.26 = (f32[128,512]{1,0:T(8,128)S(1)}, f32[128,512]{1,0:T(8,128)S(1)}, u32[]{:S(2)}, u32[]{:S(2)}) collective-permute-start(f32[128,512]{1,0:T(8,128)S(1)} %shard_map.185.refs_3_.refs_0_), channel_id=1, source_target_pairs={{0,2},{2,0},{4,6},{6,4},{1,3},{3,1},{5,7},{7,5},{8,10},{10,8},{12,... | collective-permute-start | bytes 786440 | tf_op jit(solution)/shard_map/ppermute | solution.py:541
  107.6 11.4 %collective-permute-start.31 = (f32[136,512]{1,0:T(8,128)S(1)}, f32[136,512]{1,0:T(8,128)S(1)}, u32[]{:S(2)}, u32[]{:S(2)}) collective-permute-start(f32[136,512]{1,0:T(8,128)S(1)} %get-tuple-element.172.refs_2_), channel_id=1, source_target_pairs={{0,2},{2,0},{4,6},{6,4},{1,3},{3,1},{5,7},{7,5},{8,10},{10,8},{12,... | collective-permute-start | bytes 835592 | tf_op jit(solution)/shard_map/ppermute | solution.py:541
  113.1 6.1 %collective-permute-start.30 = (f32[128,512]{1,0:T(8,128)S(1)}, f32[128,512]{1,0:T(8,128)S(1)}, u32[]{:S(2)}, u32[]{:S(2)}) collective-permute-start(f32[128,512]{1,0:T(8,128)S(1)} %shard_map.193.refs_4_.refs_1_), channel_id=1, source_target_pairs={{2,4},{4,2},{3,5},{5,3},{0,1},{1,0},{6,7},{7,6},{10,12},{12,10},{1... | collective-permute-start | bytes 786440 | tf_op jit(solution)/shard_map/ppermute | solution.py:545
  113.2 11.4 %collective-permute-start.34 = (f32[128,512]{1,0:T(8,128)S(1)}, f32[128,512]{1,0:T(8,128)S(1)}, u32[]{:S(2)}, u32[]{:S(2)}) collective-permute-start(f32[128,512]{1,0:T(8,128)S(1)} %get-tuple-element.173.refs_2_), channel_id=1, source_target_pairs={{0,2},{2,0},{4,6},{6,4},{1,3},{3,1},{5,7},{7,5},{8,10},{10,8},{12,... | collective-permute-start | bytes 786440 | tf_op jit(solution)/shard_map/ppermute | solution.py:541
  119.2 11.0 %collective-permute-start.33 = (f32[128,512]{1,0:T(8,128)S(1)}, f32[128,512]{1,0:T(8,128)S(1)}, u32[]{:S(2)}, u32[]{:S(2)}) collective-permute-start(f32[128,512]{1,0:T(8,128)S(1)} %get-tuple-element.174.refs_5_), channel_id=1, source_target_pairs={{0,2},{2,0},{4,6},{6,4},{1,3},{3,1},{5,7},{7,5},{8,10},{10,8},{12,... | collective-permute-start | bytes 786440 | tf_op jit(solution)/shard_map/ppermute | solution.py:541
  124.8 11.1 %collective-permute-start.37 = (f32[128,512]{1,0:T(8,128)S(1)}, f32[128,512]{1,0:T(8,128)S(1)}, u32[]{:S(2)}, u32[]{:S(2)}) collective-permute-start(f32[128,512]{1,0:T(8,128)S(1)} %shard_map.199.refs_7_.refs_3_), channel_id=1, source_target_pairs={{0,2},{2,0},{4,6},{6,4},{1,3},{3,1},{5,7},{7,5},{8,10},{10,8},{12,... | collective-permute-start | bytes 786440 | tf_op jit(solution)/shard_map/ppermute | solution.py:541
  130.4 11.1 %collective-permute-start.40 = (f32[128,512]{1,0:T(8,128)S(1)}, f32[128,512]{1,0:T(8,128)S(1)}, u32[]{:S(2)}, u32[]{:S(2)}) collective-permute-start(f32[128,512]{1,0:T(8,128)S(1)} %shard_map.202.refs_7_.refs_3_), channel_id=1, source_target_pairs={{0,2},{2,0},{4,6},{6,4},{1,3},{3,1},{5,7},{7,5},{8,10},{10,8},{12,... | collective-permute-start | bytes 786440 | tf_op jit(solution)/shard_map/ppermute | solution.py:541
  136.3 10.0 %collective-permute-start.39 = (f32[128,512]{1,0:T(8,128)S(1)}, f32[128,512]{1,0:T(8,128)S(1)}, u32[]{:S(2)}, u32[]{:S(2)}) collective-permute-start(f32[128,512]{1,0:T(8,128)S(1)} %shard_map.205.refs_7_.refs_3_), channel_id=1, source_target_pairs={{0,2},{2,0},{4,6},{6,4},{1,3},{3,1},{5,7},{7,5},{8,10},{10,8},{12,... | collective-permute-start | bytes 786440 | tf_op jit(solution)/shard_map/ppermute | solution.py:541
  160.9 9.6 %collective-permute-start.46 = (f32[136,512]{1,0:T(8,128)S(1)}, f32[136,512]{1,0:T(8,128)S(1)}, u32[]{:S(2)}, u32[]{:S(2)}) collective-permute-start(f32[136,512]{1,0:T(8,128)S(1)} %shard_map.210.refs_3_.refs_0_), channel_id=1, source_target_pairs={{0,2},{2,0},{4,6},{6,4},{1,3},{3,1},{5,7},{7,5},{8,10},{10,8},{12,... | collective-permute-start | bytes 835592 | tf_op jit(solution)/shard_map/ppermute | solution.py:541
  164.1 12.0 %collective-permute-start.48 = (f32[128,512]{1,0:T(8,128)S(1)}, f32[128,512]{1,0:T(8,128)S(1)}, u32[]{:S(2)}, u32[]{:S(2)}) collective-permute-start(f32[128,512]{1,0:T(8,128)S(1)} %shard_map.215.refs_2_.refs_0_), channel_id=1, source_target_pairs={{0,2},{2,0},{4,6},{6,4},{1,3},{3,1},{5,7},{7,5},{8,10},{10,8},{12,... | collective-permute-start | bytes 786440 | tf_op jit(solution)/shard_map/ppermute | solution.py:541
  170.6 11.1 %collective-permute-start.45 = (f32[128,512]{1,0:T(8,128)S(1)}, f32[128,512]{1,0:T(8,128)S(1)}, u32[]{:S(2)}, u32[]{:S(2)}) collective-permute-start(f32[128,512]{1,0:T(8,128)S(1)} %shard_map.211.refs_3_.refs_0_), channel_id=1, source_target_pairs={{0,2},{2,0},{4,6},{6,4},{1,3},{3,1},{5,7},{7,5},{8,10},{10,8},{12,... | collective-permute-start | bytes 786440 | tf_op jit(solution)/shard_map/ppermute | solution.py:541
  176.2 11.4 %collective-permute-start.50 = (f32[136,512]{1,0:T(8,128)S(1)}, f32[136,512]{1,0:T(8,128)S(1)}, u32[]{:S(2)}, u32[]{:S(2)}) collective-permute-start(f32[136,512]{1,0:T(8,128)S(1)} %get-tuple-element.193.refs_2_), channel_id=1, source_target_pairs={{0,2},{2,0},{4,6},{6,4},{1,3},{3,1},{5,7},{7,5},{8,10},{10,8},{12,... | collective-permute-start | bytes 835592 | tf_op jit(solution)/shard_map/ppermute | solution.py:541
  181.9 11.4 %collective-permute-start.53 = (f32[128,512]{1,0:T(8,128)S(1)}, f32[128,512]{1,0:T(8,128)S(1)}, u32[]{:S(2)}, u32[]{:S(2)}) collective-permute-start(f32[128,512]{1,0:T(8,128)S(1)} %get-tuple-element.194.refs_2_), channel_id=1, source_target_pairs={{0,2},{2,0},{4,6},{6,4},{1,3},{3,1},{5,7},{7,5},{8,10},{10,8},{12,... | collective-permute-start | bytes 786440 | tf_op jit(solution)/shard_map/ppermute | solution.py:541
  187.8 11.1 %collective-permute-start.52 = (f32[128,512]{1,0:T(8,128)S(1)}, f32[128,512]{1,0:T(8,128)S(1)}, u32[]{:S(2)}, u32[]{:S(2)}) collective-permute-start(f32[128,512]{1,0:T(8,128)S(1)} %get-tuple-element.195.refs_5_), channel_id=1, source_target_pairs={{0,2},{2,0},{4,6},{6,4},{1,3},{3,1},{5,7},{7,5},{8,10},{10,8},{12,... | collective-permute-start | bytes 786440 | tf_op jit(solution)/shard_map/ppermute | solution.py:541
  193.4 11.1 %collective-permute-start.56 = (f32[128,512]{1,0:T(8,128)S(1)}, f32[128,512]{1,0:T(8,128)S(1)}, u32[]{:S(2)}, u32[]{:S(2)}) collective-permute-start(f32[128,512]{1,0:T(8,128)S(1)} %shard_map.225.refs_7_.refs_3_), channel_id=1, source_target_pairs={{0,2},{2,0},{4,6},{6,4},{1,3},{3,1},{5,7},{7,5},{8,10},{10,8},{12,... | collective-permute-start | bytes 786440 | tf_op jit(solution)/shard_map/ppermute | solution.py:541
  199.0 11.1 %collective-permute-start.59 = (f32[128,512]{1,0:T(8,128)S(1)}, f32[128,512]{1,0:T(8,128)S(1)}, u32[]{:S(2)}, u32[]{:S(2)}) collective-permute-start(f32[128,512]{1,0:T(8,128)S(1)} %shard_map.228.refs_7_.refs_3_), channel_id=1, source_target_pairs={{0,2},{2,0},{4,6},{6,4},{1,3},{3,1},{5,7},{7,5},{8,10},{10,8},{12,... | collective-permute-start | bytes 786440 | tf_op jit(solution)/shard_map/ppermute | solution.py:541
  204.9 10.0 %collective-permute-start.58 = (f32[128,512]{1,0:T(8,128)S(1)}, f32[128,512]{1,0:T(8,128)S(1)}, u32[]{:S(2)}, u32[]{:S(2)}) collective-permute-start(f32[128,512]{1,0:T(8,128)S(1)} %shard_map.231.refs_7_.refs_3_), channel_id=1, source_target_pairs={{0,2},{2,0},{4,6},{6,4},{1,3},{3,1},{5,7},{7,5},{8,10},{10,8},{12,... | collective-permute-start | bytes 786440 | tf_op jit(solution)/shard_map/ppermute | solution.py:541
  229.6 9.6 %collective-permute-start.65 = (f32[136,512]{1,0:T(8,128)S(1)}, f32[136,512]{1,0:T(8,128)S(1)}, u32[]{:S(2)}, u32[]{:S(2)}) collective-permute-start(f32[136,512]{1,0:T(8,128)S(1)} %shard_map.236.refs_3_.refs_0_), channel_id=1, source_target_pairs={{0,2},{2,0},{4,6},{6,4},{1,3},{3,1},{5,7},{7,5},{8,10},{10,8},{12,... | collective-permute-start | bytes 835592 | tf_op jit(solution)/shard_map/ppermute | solution.py:541
  233.0 11.8 %collective-permute-start.67 = (f32[128,512]{1,0:T(8,128)S(1)}, f32[128,512]{1,0:T(8,128)S(1)}, u32[]{:S(2)}, u32[]{:S(2)}) collective-permute-start(f32[128,512]{1,0:T(8,128)S(1)} %shard_map.241.refs_2_.refs_0_), channel_id=1, source_target_pairs={{0,2},{2,0},{4,6},{6,4},{1,3},{3,1},{5,7},{7,5},{8,10},{10,8},{12,... | collective-permute-start | bytes 786440 | tf_op jit(solution)/shard_map/ppermute | solution.py:541
  239.3 11.1 %collective-permute-start.64 = (f32[128,512]{1,0:T(8,128)S(1)}, f32[128,512]{1,0:T(8,128)S(1)}, u32[]{:S(2)}, u32[]{:S(2)}) collective-permute-start(f32[128,512]{1,0:T(8,128)S(1)} %shard_map.237.refs_3_.refs_0_), channel_id=1, source_target_pairs={{0,2},{2,0},{4,6},{6,4},{1,3},{3,1},{5,7},{7,5},{8,10},{10,8},{12,... | collective-permute-start | bytes 786440 | tf_op jit(solution)/shard_map/ppermute | solution.py:541
  245.0 11.4 %collective-permute-start.69 = (f32[136,512]{1,0:T(8,128)S(1)}, f32[136,512]{1,0:T(8,128)S(1)}, u32[]{:S(2)}, u32[]{:S(2)}) collective-permute-start(f32[136,512]{1,0:T(8,128)S(1)} %get-tuple-element.218.refs_2_), channel_id=1, source_target_pairs={{0,2},{2,0},{4,6},{6,4},{1,3},{3,1},{5,7},{7,5},{8,10},{10,8},{12,... | collective-permute-start | bytes 835592 | tf_op jit(solution)/shard_map/ppermute | solution.py:541
  250.4 6.1 %collective-permute-start.68 = (f32[128,512]{1,0:T(8,128)S(1)}, f32[128,512]{1,0:T(8,128)S(1)}, u32[]{:S(2)}, u32[]{:S(2)}) collective-permute-start(f32[128,512]{1,0:T(8,128)S(1)} %shard_map.245.refs_4_.refs_1_), channel_id=1, source_target_pairs={{2,4},{4,2},{3,5},{5,3},{0,1},{1,0},{6,7},{7,6},{10,12},{12,10},{1... | collective-permute-start | bytes 786440 | tf_op jit(solution)/shard_map/ppermute | solution.py:545
  250.6 11.4 %collective-permute-start.72 = (f32[128,512]{1,0:T(8,128)S(1)}, f32[128,512]{1,0:T(8,128)S(1)}, u32[]{:S(2)}, u32[]{:S(2)}) collective-permute-start(f32[128,512]{1,0:T(8,128)S(1)} %get-tuple-element.219.refs_2_), channel_id=1, source_target_pairs={{0,2},{2,0},{4,6},{6,4},{1,3},{3,1},{5,7},{7,5},{8,10},{10,8},{12,... | collective-permute-start | bytes 786440 | tf_op jit(solution)/shard_map/ppermute | solution.py:541
  256.6 11.0 %collective-permute-start.71 = (f32[128,512]{1,0:T(8,128)S(1)}, f32[128,512]{1,0:T(8,128)S(1)}, u32[]{:S(2)}, u32[]{:S(2)}) collective-permute-start(f32[128,512]{1,0:T(8,128)S(1)} %get-tuple-element.220.refs_5_), channel_id=1, source_target_pairs={{0,2},{2,0},{4,6},{6,4},{1,3},{3,1},{5,7},{7,5},{8,10},{10,8},{12,... | collective-permute-start | bytes 786440 | tf_op jit(solution)/shard_map/ppermute | solution.py:541
  262.1 11.1 %collective-permute-start.75 = (f32[128,512]{1,0:T(8,128)S(1)}, f32[128,512]{1,0:T(8,128)S(1)}, u32[]{:S(2)}, u32[]{:S(2)}) collective-permute-start(f32[128,512]{1,0:T(8,128)S(1)} %shard_map.251.refs_7_.refs_3_), channel_id=1, source_target_pairs={{0,2},{2,0},{4,6},{6,4},{1,3},{3,1},{5,7},{7,5},{8,10},{10,8},{12,... | collective-permute-start | bytes 786440 | tf_op jit(solution)/shard_map/ppermute | solution.py:541
  267.8 11.1 %collective-permute-start.78 = (f32[128,512]{1,0:T(8,128)S(1)}, f32[128,512]{1,0:T(8,128)S(1)}, u32[]{:S(2)}, u32[]{:S(2)}) collective-permute-start(f32[128,512]{1,0:T(8,128)S(1)} %shard_map.254.refs_7_.refs_3_), channel_id=1, source_target_pairs={{0,2},{2,0},{4,6},{6,4},{1,3},{3,1},{5,7},{7,5},{8,10},{10,8},{12,... | collective-permute-start | bytes 786440 | tf_op jit(solution)/shard_map/ppermute | solution.py:541
  273.7 10.0 %collective-permute-start.77 = (f32[128,512]{1,0:T(8,128)S(1)}, f32[128,512]{1,0:T(8,128)S(1)}, u32[]{:S(2)}, u32[]{:S(2)}) collective-permute-start(f32[128,512]{1,0:T(8,128)S(1)} %shard_map.257.refs_7_.refs_3_), channel_id=1, source_target_pairs={{0,2},{2,0},{4,6},{6,4},{1,3},{3,1},{5,7},{7,5},{8,10},{10,8},{12,... | collective-permute-start | bytes 786440 | tf_op jit(solution)/shard_map/ppermute | solution.py:541
  (62 other events, 283.1 us)

commit v6 on v5

--- a/solution.py
+++ b/solution.py
@@ -25,7 +25,7 @@
 SMEM = pl.BlockSpec(memory_space=pltpu.SMEM)
 LIMIT = 16 * 1024 * 1024
 STEP_COST = pl.CostEstimate(flops=10**9, bytes_accessed=10**7, transcendentals=0)
-STREAM_LIMIT = 50 * 1024 * 1024
+STREAM_LIMIT = 54 * 1024 * 1024
 
 
 def dot32(first, second):
@@ -62,53 +62,56 @@
     return (column <= row) & (column < limit)
 
 
-def split_kernel(core_ref, w_ref, *refs):
-    own_refs, other_refs = refs[:CHUNKS], refs[CHUNKS : 2 * CHUNKS]
-    landed, own_sem, other_sem = refs[2 * CHUNKS :]
+def split_kernel(chunks, half, core_ref, w_ref, token_ref, *refs):
+    count = len(chunks)
+    own_refs, other_refs = refs[:count], refs[count : 2 * count]
+    landed, own_sem, other_sem = refs[2 * count :]
     cols = own_refs[0].shape[1]
-    half = CHUNKS * cols
     core = core_ref[0]
 
-    def own_copy(k):
-        start = pl.multiple_of(core * half + k * cols, HEAD_DIM)
+    def own_copy(i):
+        start = pl.multiple_of(core * half + chunks[i] * cols, HEAD_DIM)
         return pltpu.make_async_copy(
-            w_ref.at[:, pl.ds(start, cols)], own_refs[k], own_sem.at[k]
+            w_ref.at[:, pl.ds(start, cols)], own_refs[i], own_sem.at[i]
         )
 
-    def other_copy(k):
-        start = pl.multiple_of((1 - core) * half + k * cols, HEAD_DIM)
+    def other_copy(i):
+        start = pl.multiple_of((1 - core) * half + chunks[i] * cols, HEAD_DIM)
         return pltpu.make_async_copy(
-            w_ref.at[:, pl.ds(start, cols)], landed.at[k], other_sem.at[k]
+            w_ref.at[:, pl.ds(start, cols)], landed.at[i], other_sem.at[i]
         )
 
-    for k in range(CHUNKS):
-        other_copy(k).start()
-    for k in range(CHUNKS):
-        own_copy(k).start()
-    for k in range(CHUNKS):
-        other_copy(k).wait()
-        other_refs[k][...] = landed[k].astype(F32)
-    for k in range(CHUNKS):
-        own_copy(k).wait()
-
-
-def split(core, w_out):
+    for i in range(count):
+        other_copy(i).start()
+    for i in range(count):
+        own_copy(i).start()
+    for i in range(count):
+        other_copy(i).wait()
+        other_refs[i][...] = landed[i].astype(F32)
+    for i in range(count):
+        own_copy(i).wait()
+
+
+def split(core, w_out, chunks, token):
     inner, width = w_out.shape
-    cols = width // 2 // CHUNKS
+    half = width // 2
+    cols = half // CHUNKS
+    count = len(chunks)
     out = pl.pallas_call(
-        split_kernel,
-        in_specs=[SMEM, pl.BlockSpec(memory_space=pltpu.HBM)],
-        out_specs=[VMEM] * (2 * CHUNKS),
-        out_shape=[jax.ShapeDtypeStruct((inner, cols), BF16)] * CHUNKS
-        + [jax.ShapeDtypeStruct((inner, cols), F32)] * CHUNKS,
+        functools.partial(split_kernel, tuple(chunks), half),
+        in_specs=[SMEM, pl.BlockSpec(memory_space=pltpu.HBM), token_spec()],
+        out_specs=[VMEM] * (2 * count),
+        out_shape=[jax.ShapeDtypeStruct((inner, cols), BF16)] * count
+        + [jax.ShapeDtypeStruct((inner, cols), F32)] * count,
         scratch_shapes=[
-            pltpu.VMEM((CHUNKS, inner, cols), BF16),
-            pltpu.SemaphoreType.DMA((CHUNKS,)),
-            pltpu.SemaphoreType.DMA((CHUNKS,)),
+            pltpu.VMEM((count, inner, cols), BF16),
+            pltpu.SemaphoreType.DMA((count,)),
+            pltpu.SemaphoreType.DMA((count,)),
         ],
         compiler_params=pltpu.CompilerParams(vmem_limit_bytes=LIMIT),
-    )(core, w_out)
-    return out[:CHUNKS], out[CHUNKS:]
+        cost_estimate=STEP_COST,
+    )(core, w_out, token)
+    return out[:count], out[count:]
 
 
 def project_kernel(
@@ -146,6 +149,8 @@
         centred = rows_in[:, block].astype(F32) - mean
         full = centred * spread * gain_ref[:, block] + bias_ref[:, block]
         normed[:, block] = full.astype(BF16)
+    down_q = dot_nt(normed[...], aq_ref[...])
+    down_v = dot_nt(normed[...], av_ref[...])
     query = jnp.zeros((length, inner), F32)
     key = jnp.zeros((length, inner), F32)
     value = jnp.zeros((length, inner), F32)
@@ -156,8 +161,6 @@
         query = query + dot32(part, wq_in[block])
         key = key + dot32(part, wk_in[block])
         value = value + dot32(part, wv_in[block])
-    down_q = dot_nt(normed[...], aq_ref[...])
-    down_v = dot_nt(normed[...], av_ref[...])
     down_q_ref[...] = down_q
     down_v_ref[...] = down_v
     limit = limit_ref[0]
@@ -523,8 +526,6 @@
         return [part, lax.ppermute(part, "dp", [(d, d ^ step) for d in range(n_dp)])]
 
     where = core.astype(jnp.int32)[None]
-    own_w, other_w = split(where, w_out)
-    other_w = [swap(part) for part in other_w]
     cols = half // CHUNKS
     gap = lax.dynamic_slice_in_dim(inputs, core * half, half, 1).astype(F32)
     gap = gap - lax.dynamic_slice_in_dim(targets, core * half, half, 1).astype(F32)
@@ -534,6 +535,8 @@
         down_value, query_up_factor, value_up_factor,
     )
     attention = (soft, key, value, down_q, down_v)
+    own_first, other_first = split(where, w_out, [0], mixed)
+    own_w, other_w = list(own_first), [swap(part) for part in other_first]
 
     ends = ((chip == 0) | (chip == n_chip - 1)).astype(jnp.int32)[None]
 
@@ -557,6 +560,10 @@
                 own_part[k], pairs[k] = first_spread(
                     k, length, rows, got_rows, own_w[k], other_w[k], token
                 )
+                if k == 0:
+                    own, other = split(where, w_out, range(1, CHUNKS), own_part[k])
+                    own_w.extend(own)
+                    other_w.extend([swap(part) for part in other])
             else:
                 own_part[k] = spread(k, length, rows, got_rows, pairs[k], token)
             return own_part[k]

time: 297 us -> 302 us (1.017)
  starting transfers between devices: 121 us -> 110 us
  waiting for transfers between devices: 117 us -> 127 us
    ppermute x36, starting transfers between devices: 105 us -> 93.9 us  [outer_swap(): return lax.ppermute(part, 'chip', [(0, 1), (1, 0), (2, 3), (3, 2)])]
    ppermute x36, waiting for transfers between devices: 83.4 us -> 93.4 us  [outer_swap(): return lax.ppermute(part, 'chip', [(0, 1), (1, 0), (2, 3), (3, 2)])]
    pallas_call x1, Pallas kernels: 8.78 us -> 13.9 us  [project(): pl.pallas_call(project_kernel, in_specs=[SMEM] + [hbm] * 4 + [VMEM] * 6,...]
  transfers between devices with their start and end apart: 82 -> 82, of which waited for: 51 -> 49; matrix products, arithmetic and copies ran while one was open for 0% -> 1% of each run, Pallas kernels for 12% -> 8%
where the time goes in v6:
time: 302 us; the launch traced here: 301 us
  waiting for transfers between devices  127 us (42%)
  starting transfers between devices  110 us (36%)
  Pallas kernels  53.1 us (18%)
  local copies, waits for them, and re-layouts  6.58 us (2%)
    ppermute x36, starting transfers between devices, outer_swap(): return lax.ppermute(part, 'chip', [(0, 1), (1, 0), (2, 3), (3, 2)])  93.9 us
    ppermute x36, waiting for transfers between devices, outer_swap(): return lax.ppermute(part, 'chip', [(0, 1), (1, 0), (2, 3), (3, 2)])  93.4 us
    pallas_call x96, Pallas kernels, call(): pl.pallas_call(body, in_specs=[SMEM] * len(scalars) + [VMEM] * len(ins) +...  27.6 us
    pallas_call x1, Pallas kernels, project(): pl.pallas_call(project_kernel, in_specs=[SMEM] + [hbm] * 4 + [VMEM] * 6,...  13.9 us
    ppermute x14, waiting for transfers between devices, swap(): return lax.ppermute(part, 'core', [(0, 1), (1, 0)])  12.3 us
    ppermute x4, waiting for transfers between devices, data_terms(): part = part + lax.ppermute(part, 'dp', [(d, d ^ step) for d in range(n_dp)])  10.8 us
    ppermute x4, waiting for transfers between devices, data_terms(): lax.ppermute(part, 'dp', [(d, d ^ step) for d in range(n_dp)])  10.7 us
    unnamed x56, local copies, waits for them, and re-layouts  6.46 us
  transfers between devices with their start and end apart: 82, of which 49 were waited for; matrix products, arithmetic and copies ran while one was open for 1% of the time, Pallas kernels for 8%

profile of v6, /device:TPU:0, one launch (start us, length us, event | category | flops | bytes accessed | tf_op | source)
XLA Modules:
  0.0 301.5 jit_solution(6936743986223957973)
XLA Ops:
  1.3 13.9 %shard_map.156 = (f32[3,128,128]{2,1,0:T(8,128)}, bf16[128,384]{1,0:T(8,128)(2,1)}, bf16[128,384]{1,0:T(8,128)(2,1)}, f32[128,16]{1,0:T(8,128)}, f32[128,16]{1,0:T(8,128)}, /*index=5*/f32[136,384]{1,0:T(8,128)}) custom-call(s32[1]{0:T(128)S(6)} %copy.17.limit_ref.refs_1_.refs_2_.refs_4_.refs_8_, bf16[128,6144]{1,0:T(8,128)(2,1)} %x_ref.1, ...), custom_call_target="tpu_custom_call" | custom-call | flops 1811939328 | bytes 14155776 | tf_op jit(solution)/shard_map/pallas_call | solution.py:191
  25.4 2.9 collective-permute-start.6
  36.3 3.4 %collective-permute-start.11 = (f32[128,512]{1,0:T(8,128)}, f32[128,512]{1,0:T(8,128)S(1)}, u32[]{:S(2)}, u32[]{:S(2)}) collective-permute-start(f32[128,512]{1,0:T(8,128)} %copy-done.16), channel_id=1, source_target_pairs={{0,2},{2,0},{4,6},{6,4},{1,3},{3,1},{5,7},{7,5},{8,10},{10,8},{12,... | collective-permute-start | bytes 786440 | tf_op jit(solution)/shard_map/ppermute | solution.py:544
  49.4 4.5 %collective-permute-start.15 = (f32[128,512]{1,0:T(8,128)S(1)}, f32[128,512]{1,0:T(8,128)S(1)}, u32[]{:S(2)}, u32[]{:S(2)}) collective-permute-start(f32[128,512]{1,0:T(8,128)S(1)} %get-tuple-element.142.refs_4_), channel_id=1, source_target_pairs={{0,2},{2,0},{4,6},{6,4},{1,3},{3,1},{5,7},{7,5},{8,10},{10,8},{12,... | collective-permute-start | bytes 786440 | tf_op jit(solution)/shard_map/ppermute | solution.py:544
  55.6 4.0 %collective-permute-start.14 = (f32[128,512]{1,0:T(8,128)S(1)}, f32[128,512]{1,0:T(8,128)S(1)}, u32[]{:S(2)}, u32[]{:S(2)}) collective-permute-start(f32[128,512]{1,0:T(8,128)S(1)} %get-tuple-element.144.refs_6_), channel_id=1, source_target_pairs={{0,2},{2,0},{4,6},{6,4},{1,3},{3,1},{5,7},{7,5},{8,10},{10,8},{12,... | collective-permute-start | bytes 786440 | tf_op jit(solution)/shard_map/ppermute | solution.py:544
  61.3 4.2 %collective-permute-start.18 = (f32[128,512]{1,0:T(8,128)S(1)}, f32[128,512]{1,0:T(8,128)S(1)}, u32[]{:S(2)}, u32[]{:S(2)}) collective-permute-start(f32[128,512]{1,0:T(8,128)S(1)} %shard_map.174.refs_8_.refs_3_), channel_id=1, source_target_pairs={{0,2},{2,0},{4,6},{6,4},{1,3},{3,1},{5,7},{7,5},{8,10},{10,8},{12,... | collective-permute-start | bytes 786440 | tf_op jit(solution)/shard_map/ppermute | solution.py:544
  66.9 4.2 %collective-permute-start.21 = (f32[128,512]{1,0:T(8,128)S(1)}, f32[128,512]{1,0:T(8,128)S(1)}, u32[]{:S(2)}, u32[]{:S(2)}) collective-permute-start(f32[128,512]{1,0:T(8,128)S(1)} %shard_map.177.refs_8_.refs_3_), channel_id=1, source_target_pairs={{0,2},{2,0},{4,6},{6,4},{1,3},{3,1},{5,7},{7,5},{8,10},{10,8},{12,... | collective-permute-start | bytes 786440 | tf_op jit(solution)/shard_map/ppermute | solution.py:544
  72.9 2.7 collective-permute-start.20
  75.5 2.8 collective-permute-done.21.refs_2_
  78.8 3.7 %collective-permute-done.20.refs_2_ = f32[128,512]{1,0:T(8,128)S(1)} collective-permute-done((f32[128,512]{1,0:T(8,128)S(1)}, f32[128,512]{1,0:T(8,128)S(1)}, u32[]{:S(2)}, u32[]{:S(2)}) %collective-permute-start.20) | collective-permute-done | bytes 262176 | tf_op jit(solution)/shard_map/ppermute | solution.py:544
  87.6 2.7 collective-permute-done.23
  91.9 2.7 collective-permute-done.24.refs_1_
  100.7 6.0 %collective-permute-done.27.refs_1_ = f32[136,512]{1,0:T(8,128)S(1)} collective-permute-done((f32[136,512]{1,0:T(8,128)S(1)}, f32[136,512]{1,0:T(8,128)S(1)}, u32[]{:S(2)}, u32[]{:S(2)}) %collective-permute-start.27) | collective-permute-done | bytes 278560 | tf_op jit(solution)/shard_map/ppermute | solution.py:544
  109.1 3.2 %collective-permute-done.29.refs_1_ = f32[128,512]{1,0:T(8,128)S(1)} collective-permute-done((f32[128,512]{1,0:T(8,128)S(1)}, f32[128,512]{1,0:T(8,128)S(1)}, u32[]{:S(2)}, u32[]{:S(2)}) %collective-permute-start.29) | collective-permute-done | bytes 262176 | tf_op jit(solution)/shard_map/ppermute | solution.py:544
  112.5 3.4 %collective-permute-start.31 = (f32[136,512]{1,0:T(8,128)S(1)}, f32[136,512]{1,0:T(8,128)S(1)}, u32[]{:S(2)}, u32[]{:S(2)}) collective-permute-start(f32[136,512]{1,0:T(8,128)S(1)} %get-tuple-element.172.refs_2_), channel_id=1, source_target_pairs={{0,2},{2,0},{4,6},{6,4},{1,3},{3,1},{5,7},{7,5},{8,10},{10,8},{12,... | collective-permute-start | bytes 835592 | tf_op jit(solution)/shard_map/ppermute | solution.py:544
  118.1 3.4 %collective-permute-start.34 = (f32[128,512]{1,0:T(8,128)S(1)}, f32[128,512]{1,0:T(8,128)S(1)}, u32[]{:S(2)}, u32[]{:S(2)}) collective-permute-start(f32[128,512]{1,0:T(8,128)S(1)} %get-tuple-element.173.refs_2_), channel_id=1, source_target_pairs={{0,2},{2,0},{4,6},{6,4},{1,3},{3,1},{5,7},{7,5},{8,10},{10,8},{12,... | collective-permute-start | bytes 786440 | tf_op jit(solution)/shard_map/ppermute | solution.py:544
  124.1 2.7 collective-permute-start.33
  129.7 2.7 collective-permute-start.37
  135.3 2.7 collective-permute-start.40
  141.2 2.5 collective-permute-start.39
  143.6 2.7 collective-permute-done.40.refs_2_
  146.7 4.4 %collective-permute-done.39.refs_2_ = f32[128,512]{1,0:T(8,128)S(1)} collective-permute-done((f32[128,512]{1,0:T(8,128)S(1)}, f32[128,512]{1,0:T(8,128)S(1)}, u32[]{:S(2)}, u32[]{:S(2)}) %collective-permute-start.39) | collective-permute-done | bytes 262176 | tf_op jit(solution)/shard_map/ppermute | solution.py:544
  156.2 2.7 collective-permute-done.42
  160.5 2.7 collective-permute-done.43.refs_1_
  169.5 6.0 %collective-permute-done.46.refs_1_ = f32[136,512]{1,0:T(8,128)S(1)} collective-permute-done((f32[136,512]{1,0:T(8,128)S(1)}, f32[136,512]{1,0:T(8,128)S(1)}, u32[]{:S(2)}, u32[]{:S(2)}) %collective-permute-start.46) | collective-permute-done | bytes 278560 | tf_op jit(solution)/shard_map/ppermute | solution.py:544
  178.0 3.2 %collective-permute-done.48.refs_1_ = f32[128,512]{1,0:T(8,128)S(1)} collective-permute-done((f32[128,512]{1,0:T(8,128)S(1)}, f32[128,512]{1,0:T(8,128)S(1)}, u32[]{:S(2)}, u32[]{:S(2)}) %collective-permute-start.48) | collective-permute-done | bytes 262176 | tf_op jit(solution)/shard_map/ppermute | solution.py:544
  181.4 3.4 %collective-permute-start.50 = (f32[136,512]{1,0:T(8,128)S(1)}, f32[136,512]{1,0:T(8,128)S(1)}, u32[]{:S(2)}, u32[]{:S(2)}) collective-permute-start(f32[136,512]{1,0:T(8,128)S(1)} %get-tuple-element.193.refs_2_), channel_id=1, source_target_pairs={{0,2},{2,0},{4,6},{6,4},{1,3},{3,1},{5,7},{7,5},{8,10},{10,8},{12,... | collective-permute-start | bytes 835592 | tf_op jit(solution)/shard_map/ppermute | solution.py:544
  187.0 3.4 %collective-permute-start.53 = (f32[128,512]{1,0:T(8,128)S(1)}, f32[128,512]{1,0:T(8,128)S(1)}, u32[]{:S(2)}, u32[]{:S(2)}) collective-permute-start(f32[128,512]{1,0:T(8,128)S(1)} %get-tuple-element.194.refs_2_), channel_id=1, source_target_pairs={{0,2},{2,0},{4,6},{6,4},{1,3},{3,1},{5,7},{7,5},{8,10},{10,8},{12,... | collective-permute-start | bytes 786440 | tf_op jit(solution)/shard_map/ppermute | solution.py:544
  192.9 2.7 collective-permute-start.52
  198.5 2.7 collective-permute-start.56
  204.2 2.7 collective-permute-start.59
  210.0 2.5 collective-permute-start.58
  212.5 2.7 collective-permute-done.59.refs_2_
  215.6 4.4 %collective-permute-done.58.refs_2_ = f32[128,512]{1,0:T(8,128)S(1)} collective-permute-done((f32[128,512]{1,0:T(8,128)S(1)}, f32[128,512]{1,0:T(8,128)S(1)}, u32[]{:S(2)}, u32[]{:S(2)}) %collective-permute-start.58) | collective-permute-done | bytes 262176 | tf_op jit(solution)/shard_map/ppermute | solution.py:544
  225.0 2.7 collective-permute-done.61
  229.3 2.7 collective-permute-done.62.refs_1_
  238.2 6.0 %collective-permute-done.65.refs_1_ = f32[136,512]{1,0:T(8,128)S(1)} collective-permute-done((f32[136,512]{1,0:T(8,128)S(1)}, f32[136,512]{1,0:T(8,128)S(1)}, u32[]{:S(2)}, u32[]{:S(2)}) %collective-permute-start.65) | collective-permute-done | bytes 278560 | tf_op jit(solution)/shard_map/ppermute | solution.py:544
  246.7 3.2 %collective-permute-done.67.refs_1_ = f32[128,512]{1,0:T(8,128)S(1)} collective-permute-done((f32[128,512]{1,0:T(8,128)S(1)}, f32[128,512]{1,0:T(8,128)S(1)}, u32[]{:S(2)}, u32[]{:S(2)}) %collective-permute-start.67) | collective-permute-done | bytes 262176 | tf_op jit(solution)/shard_map/ppermute | solution.py:544
  250.1 3.4 %collective-permute-start.69 = (f32[136,512]{1,0:T(8,128)S(1)}, f32[136,512]{1,0:T(8,128)S(1)}, u32[]{:S(2)}, u32[]{:S(2)}) collective-permute-start(f32[136,512]{1,0:T(8,128)S(1)} %get-tuple-element.218.refs_2_), channel_id=1, source_target_pairs={{0,2},{2,0},{4,6},{6,4},{1,3},{3,1},{5,7},{7,5},{8,10},{10,8},{12,... | collective-permute-start | bytes 835592 | tf_op jit(solution)/shard_map/ppermute | solution.py:544
  255.7 3.4 %collective-permute-start.72 = (f32[128,512]{1,0:T(8,128)S(1)}, f32[128,512]{1,0:T(8,128)S(1)}, u32[]{:S(2)}, u32[]{:S(2)}) collective-permute-start(f32[128,512]{1,0:T(8,128)S(1)} %get-tuple-element.219.refs_2_), channel_id=1, source_target_pairs={{0,2},{2,0},{4,6},{6,4},{1,3},{3,1},{5,7},{7,5},{8,10},{10,8},{12,... | collective-permute-start | bytes 786440 | tf_op jit(solution)/shard_map/ppermute | solution.py:544
  261.7 2.7 collective-permute-start.71
  267.2 2.7 collective-permute-start.75
  272.9 2.7 collective-permute-start.78
  278.8 2.5 collective-permute-start.77
  281.2 2.7 collective-permute-done.78.refs_2_
  284.3 4.4 %collective-permute-done.77.refs_2_ = f32[128,512]{1,0:T(8,128)S(1)} collective-permute-done((f32[128,512]{1,0:T(8,128)S(1)}, f32[128,512]{1,0:T(8,128)S(1)}, u32[]{:S(2)}, u32[]{:S(2)}) %collective-permute-start.77) | collective-permute-done | bytes 262176 | tf_op jit(solution)/shard_map/ppermute | solution.py:544
  293.7 2.7 collective-permute-done.80
  298.1 2.7 collective-permute-done.81.refs_1_
  (285 shorter events, 130.0 us)
Async XLA Ops:
  25.3 7.5 %collective-permute-start.7 = (f32[384,512]{1,0:T(8,128)S(1)}, f32[384,512]{1,0:T(8,128)}, u32[]{:S(2)}, u32[]{:S(2)}) collective-permute-start(f32[384,512]{1,0:T(8,128)S(1)} %get-tuple-element.135), channel_id=1, source_target_pairs={{0,1},{1,0},{2,3},{3,2},{4,5},{5,4},{6,7},{7,6},{8,9},{9,8},{10,11... | collective-permute-start | bytes 2359304 | tf_op jit(solution)/shard_map/ppermute | solution.py:519
  25.4 9.9 %collective-permute-start.6 = (f32[136,512]{1,0:T(8,128)S(1)}, f32[136,512]{1,0:T(8,128)S(1)}, u32[]{:S(2)}, u32[]{:S(2)}) collective-permute-start(f32[136,512]{1,0:T(8,128)S(1)} %get-tuple-element.126.token_ref.refs_4_.refs_0_), channel_id=1, source_target_pairs={{0,2},{2,0},{4,6},{6,4},{1,3},{3,1},{5,7},{7,5},{8,10},{10,8},{12,... | collective-permute-start | bytes 835592 | tf_op jit(solution)/shard_map/ppermute | solution.py:544
  28.4 7.9 %collective-permute-start.5 = (f32[384,512]{1,0:T(8,128)}, f32[384,512]{1,0:T(8,128)}, u32[]{:S(2)}, u32[]{:S(2)}) collective-permute-start(f32[384,512]{1,0:T(8,128)} %get-tuple-element.133), channel_id=1, source_target_pairs={{0,1},{1,0},{2,3},{3,2},{4,5},{5,4},{6,7},{7,6},{8,9},{9,8},{10,11... | collective-permute-start | bytes 2359304 | tf_op jit(solution)/shard_map/ppermute | solution.py:519
  30.0 17.7 %collective-permute-start.9 = (f32[384,512]{1,0:T(8,128)S(1)}, f32[384,512]{1,0:T(8,128)}, u32[]{:S(2)}, u32[]{:S(2)}) collective-permute-start(f32[384,512]{1,0:T(8,128)S(1)} %get-tuple-element.139), channel_id=1, source_target_pairs={{0,1},{1,0},{2,3},{3,2},{4,5},{5,4},{6,7},{7,6},{8,9},{9,8},{10,11... | collective-permute-start | bytes 2359304 | tf_op jit(solution)/shard_map/ppermute | solution.py:519
  30.5 23.4 %collective-permute-start.2 = (f32[384,512]{1,0:T(8,128)S(1)}, f32[384,512]{1,0:T(8,128)}, u32[]{:S(2)}, u32[]{:S(2)}) collective-permute-start(f32[384,512]{1,0:T(8,128)S(1)} %get-tuple-element.128), channel_id=1, source_target_pairs={{0,1},{1,0},{2,3},{3,2},{4,5},{5,4},{6,7},{7,6},{8,9},{9,8},{10,11... | collective-permute-start | bytes 2359304 | tf_op jit(solution)/shard_map/ppermute | solution.py:519
  32.8 10.2 %collective-permute-start.4 = (f32[128,512]{1,0:T(8,128)}, f32[128,512]{1,0:T(8,128)}, u32[]{:S(2)}, u32[]{:S(2)}) collective-permute-start(f32[128,512]{1,0:T(8,128)} %get-tuple-element.131.refs_4_.refs_0_), channel_id=1, source_target_pairs={{0,2},{2,0},{4,6},{6,4},{1,3},{3,1},{5,7},{7,5},{8,10},{10,8},{12,... | collective-permute-start | bytes 786440 | tf_op jit(solution)/shard_map/ppermute | solution.py:544
  36.1 8.0 %collective-permute-start.10 = (f32[136,512]{1,0:T(8,128)}, f32[136,512]{1,0:T(8,128)}, u32[]{:S(2)}, u32[]{:S(2)}) collective-permute-start(f32[136,512]{1,0:T(8,128)} %shard_map.162.refs_4_.refs_1_), channel_id=1, source_target_pairs={{2,4},{4,2},{3,5},{5,3},{0,1},{1,0},{6,7},{7,6},{10,12},{12,10},{1... | collective-permute-start | bytes 835592 | tf_op jit(solution)/shard_map/ppermute | solution.py:548
  36.3 13.0 %collective-permute-start.11 = (f32[128,512]{1,0:T(8,128)}, f32[128,512]{1,0:T(8,128)S(1)}, u32[]{:S(2)}, u32[]{:S(2)}) collective-permute-start(f32[128,512]{1,0:T(8,128)} %copy-done.16), channel_id=1, source_target_pairs={{0,2},{2,0},{4,6},{6,4},{1,3},{3,1},{5,7},{7,5},{8,10},{10,8},{12,... | collective-permute-start | bytes 786440 | tf_op jit(solution)/shard_map/ppermute | solution.py:544
  45.3 10.1 %collective-permute-start.13 = (f32[136,512]{1,0:T(8,128)S(1)}, f32[136,512]{1,0:T(8,128)S(1)}, u32[]{:S(2)}, u32[]{:S(2)}) collective-permute-start(f32[136,512]{1,0:T(8,128)S(1)} %get-tuple-element.140.refs_4_), channel_id=1, source_target_pairs={{0,2},{2,0},{4,6},{6,4},{1,3},{3,1},{5,7},{7,5},{8,10},{10,8},{12,... | collective-permute-start | bytes 835592 | tf_op jit(solution)/shard_map/ppermute | solution.py:544
  49.3 6.2 %collective-permute-start.12 = (f32[128,512]{1,0:T(8,128)S(1)}, f32[128,512]{1,0:T(8,128)S(1)}, u32[]{:S(2)}, u32[]{:S(2)}) collective-permute-start(f32[128,512]{1,0:T(8,128)S(1)} %shard_map.167.refs_4_.refs_1_), channel_id=1, source_target_pairs={{2,4},{4,2},{3,5},{5,3},{0,1},{1,0},{6,7},{7,6},{10,12},{12,10},{1... | collective-permute-start | bytes 786440 | tf_op jit(solution)/shard_map/ppermute | solution.py:548
  49.4 11.7 %collective-permute-start.15 = (f32[128,512]{1,0:T(8,128)S(1)}, f32[128,512]{1,0:T(8,128)S(1)}, u32[]{:S(2)}, u32[]{:S(2)}) collective-permute-start(f32[128,512]{1,0:T(8,128)S(1)} %get-tuple-element.142.refs_4_), channel_id=1, source_target_pairs={{0,2},{2,0},{4,6},{6,4},{1,3},{3,1},{5,7},{7,5},{8,10},{10,8},{12,... | collective-permute-start | bytes 786440 | tf_op jit(solution)/shard_map/ppermute | solution.py:544
  55.6 11.2 %collective-permute-start.14 = (f32[128,512]{1,0:T(8,128)S(1)}, f32[128,512]{1,0:T(8,128)S(1)}, u32[]{:S(2)}, u32[]{:S(2)}) collective-permute-start(f32[128,512]{1,0:T(8,128)S(1)} %get-tuple-element.144.refs_6_), channel_id=1, source_target_pairs={{0,2},{2,0},{4,6},{6,4},{1,3},{3,1},{5,7},{7,5},{8,10},{10,8},{12,... | collective-permute-start | bytes 786440 | tf_op jit(solution)/shard_map/ppermute | solution.py:544
  61.3 11.1 %collective-permute-start.18 = (f32[128,512]{1,0:T(8,128)S(1)}, f32[128,512]{1,0:T(8,128)S(1)}, u32[]{:S(2)}, u32[]{:S(2)}) collective-permute-start(f32[128,512]{1,0:T(8,128)S(1)} %shard_map.174.refs_8_.refs_3_), channel_id=1, source_target_pairs={{0,2},{2,0},{4,6},{6,4},{1,3},{3,1},{5,7},{7,5},{8,10},{10,8},{12,... | collective-permute-start | bytes 786440 | tf_op jit(solution)/shard_map/ppermute | solution.py:544
  66.8 6.0 %collective-permute-start.17 = (f32[128,512]{1,0:T(8,128)S(1)}, f32[128,512]{1,0:T(8,128)S(1)}, u32[]{:S(2)}, u32[]{:S(2)}) collective-permute-start(f32[128,512]{1,0:T(8,128)S(1)} %shard_map.176.refs_2_.refs_0_), channel_id=1, source_target_pairs={{2,4},{4,2},{3,5},{5,3},{0,1},{1,0},{6,7},{7,6},{10,12},{12,10},{1... | collective-permute-start | bytes 786440 | tf_op jit(solution)/shard_map/ppermute | solution.py:548
  66.9 11.4 %collective-permute-start.21 = (f32[128,512]{1,0:T(8,128)S(1)}, f32[128,512]{1,0:T(8,128)S(1)}, u32[]{:S(2)}, u32[]{:S(2)}) collective-permute-start(f32[128,512]{1,0:T(8,128)S(1)} %shard_map.177.refs_8_.refs_3_), channel_id=1, source_target_pairs={{0,2},{2,0},{4,6},{6,4},{1,3},{3,1},{5,7},{7,5},{8,10},{10,8},{12,... | collective-permute-start | bytes 786440 | tf_op jit(solution)/shard_map/ppermute | solution.py:544
  72.9 9.7 %collective-permute-start.20 = (f32[128,512]{1,0:T(8,128)S(1)}, f32[128,512]{1,0:T(8,128)S(1)}, u32[]{:S(2)}, u32[]{:S(2)}) collective-permute-start(f32[128,512]{1,0:T(8,128)S(1)} %shard_map.180.refs_8_.refs_3_), channel_id=1, source_target_pairs={{0,2},{2,0},{4,6},{6,4},{1,3},{3,1},{5,7},{7,5},{8,10},{10,8},{12,... | collective-permute-start | bytes 786440 | tf_op jit(solution)/shard_map/ppermute | solution.py:544
  97.1 9.6 %collective-permute-start.27 = (f32[136,512]{1,0:T(8,128)S(1)}, f32[136,512]{1,0:T(8,128)S(1)}, u32[]{:S(2)}, u32[]{:S(2)}) collective-permute-start(f32[136,512]{1,0:T(8,128)S(1)} %shard_map.185.refs_3_.refs_0_), channel_id=1, source_target_pairs={{0,2},{2,0},{4,6},{6,4},{1,3},{3,1},{5,7},{7,5},{8,10},{10,8},{12,... | collective-permute-start | bytes 835592 | tf_op jit(solution)/shard_map/ppermute | solution.py:544
  100.2 12.1 %collective-permute-start.29 = (f32[128,512]{1,0:T(8,128)S(1)}, f32[128,512]{1,0:T(8,128)S(1)}, u32[]{:S(2)}, u32[]{:S(2)}) collective-permute-start(f32[128,512]{1,0:T(8,128)S(1)} %shard_map.190.refs_2_.refs_0_), channel_id=1, source_target_pairs={{0,2},{2,0},{4,6},{6,4},{1,3},{3,1},{5,7},{7,5},{8,10},{10,8},{12,... | collective-permute-start | bytes 786440 | tf_op jit(solution)/shard_map/ppermute | solution.py:544
  106.8 11.1 %collective-permute-start.26 = (f32[128,512]{1,0:T(8,128)S(1)}, f32[128,512]{1,0:T(8,128)S(1)}, u32[]{:S(2)}, u32[]{:S(2)}) collective-permute-start(f32[128,512]{1,0:T(8,128)S(1)} %shard_map.186.refs_3_.refs_0_), channel_id=1, source_target_pairs={{0,2},{2,0},{4,6},{6,4},{1,3},{3,1},{5,7},{7,5},{8,10},{10,8},{12,... | collective-permute-start | bytes 786440 | tf_op jit(solution)/shard_map/ppermute | solution.py:544
  112.5 11.4 %collective-permute-start.31 = (f32[136,512]{1,0:T(8,128)S(1)}, f32[136,512]{1,0:T(8,128)S(1)}, u32[]{:S(2)}, u32[]{:S(2)}) collective-permute-start(f32[136,512]{1,0:T(8,128)S(1)} %get-tuple-element.172.refs_2_), channel_id=1, source_target_pairs={{0,2},{2,0},{4,6},{6,4},{1,3},{3,1},{5,7},{7,5},{8,10},{10,8},{12,... | collective-permute-start | bytes 835592 | tf_op jit(solution)/shard_map/ppermute | solution.py:544
  118.0 6.0 %collective-permute-start.30 = (f32[128,512]{1,0:T(8,128)S(1)}, f32[128,512]{1,0:T(8,128)S(1)}, u32[]{:S(2)}, u32[]{:S(2)}) collective-permute-start(f32[128,512]{1,0:T(8,128)S(1)} %shard_map.194.refs_4_.refs_1_), channel_id=1, source_target_pairs={{2,4},{4,2},{3,5},{5,3},{0,1},{1,0},{6,7},{7,6},{10,12},{12,10},{1... | collective-permute-start | bytes 786440 | tf_op jit(solution)/shard_map/ppermute | solution.py:548
  118.1 11.4 %collective-permute-start.34 = (f32[128,512]{1,0:T(8,128)S(1)}, f32[128,512]{1,0:T(8,128)S(1)}, u32[]{:S(2)}, u32[]{:S(2)}) collective-permute-start(f32[128,512]{1,0:T(8,128)S(1)} %get-tuple-element.173.refs_2_), channel_id=1, source_target_pairs={{0,2},{2,0},{4,6},{6,4},{1,3},{3,1},{5,7},{7,5},{8,10},{10,8},{12,... | collective-permute-start | bytes 786440 | tf_op jit(solution)/shard_map/ppermute | solution.py:544
  124.1 11.1 %collective-permute-start.33 = (f32[128,512]{1,0:T(8,128)S(1)}, f32[128,512]{1,0:T(8,128)S(1)}, u32[]{:S(2)}, u32[]{:S(2)}) collective-permute-start(f32[128,512]{1,0:T(8,128)S(1)} %get-tuple-element.174.refs_5_), channel_id=1, source_target_pairs={{0,2},{2,0},{4,6},{6,4},{1,3},{3,1},{5,7},{7,5},{8,10},{10,8},{12,... | collective-permute-start | bytes 786440 | tf_op jit(solution)/shard_map/ppermute | solution.py:544
  129.7 11.1 %collective-permute-start.37 = (f32[128,512]{1,0:T(8,128)S(1)}, f32[128,512]{1,0:T(8,128)S(1)}, u32[]{:S(2)}, u32[]{:S(2)}) collective-permute-start(f32[128,512]{1,0:T(8,128)S(1)} %shard_map.200.refs_7_.refs_3_), channel_id=1, source_target_pairs={{0,2},{2,0},{4,6},{6,4},{1,3},{3,1},{5,7},{7,5},{8,10},{10,8},{12,... | collective-permute-start | bytes 786440 | tf_op jit(solution)/shard_map/ppermute | solution.py:544
  135.2 6.0 %collective-permute-start.36 = (f32[128,512]{1,0:T(8,128)S(1)}, f32[128,512]{1,0:T(8,128)S(1)}, u32[]{:S(2)}, u32[]{:S(2)}) collective-permute-start(f32[128,512]{1,0:T(8,128)S(1)} %shard_map.202.refs_2_.refs_0_), channel_id=1, source_target_pairs={{2,4},{4,2},{3,5},{5,3},{0,1},{1,0},{6,7},{7,6},{10,12},{12,10},{1... | collective-permute-start | bytes 786440 | tf_op jit(solution)/shard_map/ppermute | solution.py:548
  135.3 11.1 %collective-permute-start.40 = (f32[128,512]{1,0:T(8,128)S(1)}, f32[128,512]{1,0:T(8,128)S(1)}, u32[]{:S(2)}, u32[]{:S(2)}) collective-permute-start(f32[128,512]{1,0:T(8,128)S(1)} %shard_map.203.refs_7_.refs_3_), channel_id=1, source_target_pairs={{0,2},{2,0},{4,6},{6,4},{1,3},{3,1},{5,7},{7,5},{8,10},{10,8},{12,... | collective-permute-start | bytes 786440 | tf_op jit(solution)/shard_map/ppermute | solution.py:544
  141.2 10.0 %collective-permute-start.39 = (f32[128,512]{1,0:T(8,128)S(1)}, f32[128,512]{1,0:T(8,128)S(1)}, u32[]{:S(2)}, u32[]{:S(2)}) collective-permute-start(f32[128,512]{1,0:T(8,128)S(1)} %shard_map.206.refs_7_.refs_3_), channel_id=1, source_target_pairs={{0,2},{2,0},{4,6},{6,4},{1,3},{3,1},{5,7},{7,5},{8,10},{10,8},{12,... | collective-permute-start | bytes 786440 | tf_op jit(solution)/shard_map/ppermute | solution.py:544
  166.0 9.6 %collective-permute-start.46 = (f32[136,512]{1,0:T(8,128)S(1)}, f32[136,512]{1,0:T(8,128)S(1)}, u32[]{:S(2)}, u32[]{:S(2)}) collective-permute-start(f32[136,512]{1,0:T(8,128)S(1)} %shard_map.211.refs_3_.refs_0_), channel_id=1, source_target_pairs={{0,2},{2,0},{4,6},{6,4},{1,3},{3,1},{5,7},{7,5},{8,10},{10,8},{12,... | collective-permute-start | bytes 835592 | tf_op jit(solution)/shard_map/ppermute | solution.py:544
  169.0 12.1 %collective-permute-start.48 = (f32[128,512]{1,0:T(8,128)S(1)}, f32[128,512]{1,0:T(8,128)S(1)}, u32[]{:S(2)}, u32[]{:S(2)}) collective-permute-start(f32[128,512]{1,0:T(8,128)S(1)} %shard_map.216.refs_2_.refs_0_), channel_id=1, source_target_pairs={{0,2},{2,0},{4,6},{6,4},{1,3},{3,1},{5,7},{7,5},{8,10},{10,8},{12,... | collective-permute-start | bytes 786440 | tf_op jit(solution)/shard_map/ppermute | solution.py:544
  175.7 11.1 %collective-permute-start.45 = (f32[128,512]{1,0:T(8,128)S(1)}, f32[128,512]{1,0:T(8,128)S(1)}, u32[]{:S(2)}, u32[]{:S(2)}) collective-permute-start(f32[128,512]{1,0:T(8,128)S(1)} %shard_map.212.refs_3_.refs_0_), channel_id=1, source_target_pairs={{0,2},{2,0},{4,6},{6,4},{1,3},{3,1},{5,7},{7,5},{8,10},{10,8},{12,... | collective-permute-start | bytes 786440 | tf_op jit(solution)/shard_map/ppermute | solution.py:544
  181.4 11.4 %collective-permute-start.50 = (f32[136,512]{1,0:T(8,128)S(1)}, f32[136,512]{1,0:T(8,128)S(1)}, u32[]{:S(2)}, u32[]{:S(2)}) collective-permute-start(f32[136,512]{1,0:T(8,128)S(1)} %get-tuple-element.193.refs_2_), channel_id=1, source_target_pairs={{0,2},{2,0},{4,6},{6,4},{1,3},{3,1},{5,7},{7,5},{8,10},{10,8},{12,... | collective-permute-start | bytes 835592 | tf_op jit(solution)/shard_map/ppermute | solution.py:544
  186.8 6.1 %collective-permute-start.49 = (f32[128,512]{1,0:T(8,128)S(1)}, f32[128,512]{1,0:T(8,128)S(1)}, u32[]{:S(2)}, u32[]{:S(2)}) collective-permute-start(f32[128,512]{1,0:T(8,128)S(1)} %shard_map.220.refs_4_.refs_1_), channel_id=1, source_target_pairs={{2,4},{4,2},{3,5},{5,3},{0,1},{1,0},{6,7},{7,6},{10,12},{12,10},{1... | collective-permute-start | bytes 786440 | tf_op jit(solution)/shard_map/ppermute | solution.py:548
  187.0 11.4 %collective-permute-start.53 = (f32[128,512]{1,0:T(8,128)S(1)}, f32[128,512]{1,0:T(8,128)S(1)}, u32[]{:S(2)}, u32[]{:S(2)}) collective-permute-start(f32[128,512]{1,0:T(8,128)S(1)} %get-tuple-element.194.refs_2_), channel_id=1, source_target_pairs={{0,2},{2,0},{4,6},{6,4},{1,3},{3,1},{5,7},{7,5},{8,10},{10,8},{12,... | collective-permute-start | bytes 786440 | tf_op jit(solution)/shard_map/ppermute | solution.py:544
  192.9 11.0 %collective-permute-start.52 = (f32[128,512]{1,0:T(8,128)S(1)}, f32[128,512]{1,0:T(8,128)S(1)}, u32[]{:S(2)}, u32[]{:S(2)}) collective-permute-start(f32[128,512]{1,0:T(8,128)S(1)} %get-tuple-element.195.refs_5_), channel_id=1, source_target_pairs={{0,2},{2,0},{4,6},{6,4},{1,3},{3,1},{5,7},{7,5},{8,10},{10,8},{12,... | collective-permute-start | bytes 786440 | tf_op jit(solution)/shard_map/ppermute | solution.py:544
  198.5 11.1 %collective-permute-start.56 = (f32[128,512]{1,0:T(8,128)S(1)}, f32[128,512]{1,0:T(8,128)S(1)}, u32[]{:S(2)}, u32[]{:S(2)}) collective-permute-start(f32[128,512]{1,0:T(8,128)S(1)} %shard_map.226.refs_7_.refs_3_), channel_id=1, source_target_pairs={{0,2},{2,0},{4,6},{6,4},{1,3},{3,1},{5,7},{7,5},{8,10},{10,8},{12,... | collective-permute-start | bytes 786440 | tf_op jit(solution)/shard_map/ppermute | solution.py:544
  204.0 6.0 %collective-permute-start.55 = (f32[128,512]{1,0:T(8,128)S(1)}, f32[128,512]{1,0:T(8,128)S(1)}, u32[]{:S(2)}, u32[]{:S(2)}) collective-permute-start(f32[128,512]{1,0:T(8,128)S(1)} %shard_map.228.refs_2_.refs_0_), channel_id=1, source_target_pairs={{2,4},{4,2},{3,5},{5,3},{0,1},{1,0},{6,7},{7,6},{10,12},{12,10},{1... | collective-permute-start | bytes 786440 | tf_op jit(solution)/shard_map/ppermute | solution.py:548
  204.2 11.1 %collective-permute-start.59 = (f32[128,512]{1,0:T(8,128)S(1)}, f32[128,512]{1,0:T(8,128)S(1)}, u32[]{:S(2)}, u32[]{:S(2)}) collective-permute-start(f32[128,512]{1,0:T(8,128)S(1)} %shard_map.229.refs_7_.refs_3_), channel_id=1, source_target_pairs={{0,2},{2,0},{4,6},{6,4},{1,3},{3,1},{5,7},{7,5},{8,10},{10,8},{12,... | collective-permute-start | bytes 786440 | tf_op jit(solution)/shard_map/ppermute | solution.py:544
  210.0 10.0 %collective-permute-start.58 = (f32[128,512]{1,0:T(8,128)S(1)}, f32[128,512]{1,0:T(8,128)S(1)}, u32[]{:S(2)}, u32[]{:S(2)}) collective-permute-start(f32[128,512]{1,0:T(8,128)S(1)} %shard_map.232.refs_7_.refs_3_), channel_id=1, source_target_pairs={{0,2},{2,0},{4,6},{6,4},{1,3},{3,1},{5,7},{7,5},{8,10},{10,8},{12,... | collective-permute-start | bytes 786440 | tf_op jit(solution)/shard_map/ppermute | solution.py:544
  234.7 9.6 %collective-permute-start.65 = (f32[136,512]{1,0:T(8,128)S(1)}, f32[136,512]{1,0:T(8,128)S(1)}, u32[]{:S(2)}, u32[]{:S(2)}) collective-permute-start(f32[136,512]{1,0:T(8,128)S(1)} %shard_map.237.refs_3_.refs_0_), channel_id=1, source_target_pairs={{0,2},{2,0},{4,6},{6,4},{1,3},{3,1},{5,7},{7,5},{8,10},{10,8},{12,... | collective-permute-start | bytes 835592 | tf_op jit(solution)/shard_map/ppermute | solution.py:544
  237.7 12.1 %collective-permute-start.67 = (f32[128,512]{1,0:T(8,128)S(1)}, f32[128,512]{1,0:T(8,128)S(1)}, u32[]{:S(2)}, u32[]{:S(2)}) collective-permute-start(f32[128,512]{1,0:T(8,128)S(1)} %shard_map.242.refs_2_.refs_0_), channel_id=1, source_target_pairs={{0,2},{2,0},{4,6},{6,4},{1,3},{3,1},{5,7},{7,5},{8,10},{10,8},{12,... | collective-permute-start | bytes 786440 | tf_op jit(solution)/shard_map/ppermute | solution.py:544
  244.4 11.1 %collective-permute-start.64 = (f32[128,512]{1,0:T(8,128)S(1)}, f32[128,512]{1,0:T(8,128)S(1)}, u32[]{:S(2)}, u32[]{:S(2)}) collective-permute-start(f32[128,512]{1,0:T(8,128)S(1)} %shard_map.238.refs_3_.refs_0_), channel_id=1, source_target_pairs={{0,2},{2,0},{4,6},{6,4},{1,3},{3,1},{5,7},{7,5},{8,10},{10,8},{12,... | collective-permute-start | bytes 786440 | tf_op jit(solution)/shard_map/ppermute | solution.py:544
  250.1 11.4 %collective-permute-start.69 = (f32[136,512]{1,0:T(8,128)S(1)}, f32[136,512]{1,0:T(8,128)S(1)}, u32[]{:S(2)}, u32[]{:S(2)}) collective-permute-start(f32[136,512]{1,0:T(8,128)S(1)} %get-tuple-element.218.refs_2_), channel_id=1, source_target_pairs={{0,2},{2,0},{4,6},{6,4},{1,3},{3,1},{5,7},{7,5},{8,10},{10,8},{12,... | collective-permute-start | bytes 835592 | tf_op jit(solution)/shard_map/ppermute | solution.py:544
  255.5 6.1 %collective-permute-start.68 = (f32[128,512]{1,0:T(8,128)S(1)}, f32[128,512]{1,0:T(8,128)S(1)}, u32[]{:S(2)}, u32[]{:S(2)}) collective-permute-start(f32[128,512]{1,0:T(8,128)S(1)} %shard_map.246.refs_4_.refs_1_), channel_id=1, source_target_pairs={{2,4},{4,2},{3,5},{5,3},{0,1},{1,0},{6,7},{7,6},{10,12},{12,10},{1... | collective-permute-start | bytes 786440 | tf_op jit(solution)/shard_map/ppermute | solution.py:548
  255.7 11.4 %collective-permute-start.72 = (f32[128,512]{1,0:T(8,128)S(1)}, f32[128,512]{1,0:T(8,128)S(1)}, u32[]{:S(2)}, u32[]{:S(2)}) collective-permute-start(f32[128,512]{1,0:T(8,128)S(1)} %get-tuple-element.219.refs_2_), channel_id=1, source_target_pairs={{0,2},{2,0},{4,6},{6,4},{1,3},{3,1},{5,7},{7,5},{8,10},{10,8},{12,... | collective-permute-start | bytes 786440 | tf_op jit(solution)/shard_map/ppermute | solution.py:544
  261.7 11.0 %collective-permute-start.71 = (f32[128,512]{1,0:T(8,128)S(1)}, f32[128,512]{1,0:T(8,128)S(1)}, u32[]{:S(2)}, u32[]{:S(2)}) collective-permute-start(f32[128,512]{1,0:T(8,128)S(1)} %get-tuple-element.220.refs_5_), channel_id=1, source_target_pairs={{0,2},{2,0},{4,6},{6,4},{1,3},{3,1},{5,7},{7,5},{8,10},{10,8},{12,... | collective-permute-start | bytes 786440 | tf_op jit(solution)/shard_map/ppermute | solution.py:544
  267.2 11.1 %collective-permute-start.75 = (f32[128,512]{1,0:T(8,128)S(1)}, f32[128,512]{1,0:T(8,128)S(1)}, u32[]{:S(2)}, u32[]{:S(2)}) collective-permute-start(f32[128,512]{1,0:T(8,128)S(1)} %shard_map.252.refs_7_.refs_3_), channel_id=1, source_target_pairs={{0,2},{2,0},{4,6},{6,4},{1,3},{3,1},{5,7},{7,5},{8,10},{10,8},{12,... | collective-permute-start | bytes 786440 | tf_op jit(solution)/shard_map/ppermute | solution.py:544
  272.9 11.1 %collective-permute-start.78 = (f32[128,512]{1,0:T(8,128)S(1)}, f32[128,512]{1,0:T(8,128)S(1)}, u32[]{:S(2)}, u32[]{:S(2)}) collective-permute-start(f32[128,512]{1,0:T(8,128)S(1)} %shard_map.255.refs_7_.refs_3_), channel_id=1, source_target_pairs={{0,2},{2,0},{4,6},{6,4},{1,3},{3,1},{5,7},{7,5},{8,10},{10,8},{12,... | collective-permute-start | bytes 786440 | tf_op jit(solution)/shard_map/ppermute | solution.py:544
  278.8 10.0 %collective-permute-start.77 = (f32[128,512]{1,0:T(8,128)S(1)}, f32[128,512]{1,0:T(8,128)S(1)}, u32[]{:S(2)}, u32[]{:S(2)}) collective-permute-start(f32[128,512]{1,0:T(8,128)S(1)} %shard_map.258.refs_7_.refs_3_), channel_id=1, source_target_pairs={{0,2},{2,0},{4,6},{6,4},{1,3},{3,1},{5,7},{7,5},{8,10},{10,8},{12,... | collective-permute-start | bytes 786440 | tf_op jit(solution)/shard_map/ppermute | solution.py:544
  (62 other events, 216.7 us)

commit v7 on v5

--- a/solution.py
+++ b/solution.py
@@ -146,6 +146,8 @@
         centred = rows_in[:, block].astype(F32) - mean
         full = centred * spread * gain_ref[:, block] + bias_ref[:, block]
         normed[:, block] = full.astype(BF16)
+    down_q = dot_nt(normed[...], aq_ref[...])
+    down_v = dot_nt(normed[...], av_ref[...])
     query = jnp.zeros((length, inner), F32)
     key = jnp.zeros((length, inner), F32)
     value = jnp.zeros((length, inner), F32)
@@ -156,8 +158,6 @@
         query = query + dot32(part, wq_in[block])
         key = key + dot32(part, wk_in[block])
         value = value + dot32(part, wv_in[block])
-    down_q = dot_nt(normed[...], aq_ref[...])
-    down_v = dot_nt(normed[...], av_ref[...])
     down_q_ref[...] = down_q
     down_v_ref[...] = down_v
     limit = limit_ref[0]
@@ -335,22 +335,24 @@
     live = live_pairs(limit_ref[0], length)
     pulled = (own_ref[...] + got_ref[:length]).astype(BF16)
     out_ref[2 * rank :] = other_ref[length:] + got_ref[length:]
+    queries, values = [], []
     for h in range(inner // HEAD_DIM):
         soft = soft_ref[h]
         rows = pulled[:, head(h)]
         d_probs = dot_nt(rows, value_ref[:, head(h)]).astype(BF16).astype(F32)
-        d_value = dot_tn(soft.astype(BF16), rows).astype(BF16).astype(F32)
+        values.append(dot_tn(soft.astype(BF16), rows).astype(BF16).astype(F32))
         d_scores = soft * (d_probs - jnp.sum(soft * d_probs, axis=-1, keepdims=True))
         d_scores = jnp.where(live, d_scores, 0.0) * SCALE
-        d_query = dot32(d_scores.astype(BF16), key_ref[:, head(h)]).astype(BF16).astype(F32)
-        out_ref[:rank, head(h)] = share * lax.dot_general(
-            down_q_ref[...], d_query, (((0,), (0,)), ((), ())), precision=HIGH,
-            preferred_element_type=F32,
-        )
-        out_ref[rank : 2 * rank, head(h)] = share * lax.dot_general(
-            down_v_ref[...], d_value, (((0,), (0,)), ((), ())), precision=HIGH,
-            preferred_element_type=F32,
-        )
+        d_query = dot32(d_scores.astype(BF16), key_ref[:, head(h)])
+        queries.append(d_query.astype(BF16).astype(F32))
+    out_ref[:rank] = share * lax.dot_general(
+        down_q_ref[...], jnp.concatenate(queries, axis=1), (((0,), (0,)), ((), ())),
+        precision=HIGH, preferred_element_type=F32,
+    )
+    out_ref[rank : 2 * rank] = share * lax.dot_general(
+        down_v_ref[...], jnp.concatenate(values, axis=1), (((0,), (0,)), ((), ())),
+        precision=HIGH, preferred_element_type=F32,
+    )
 
 
 def cotangent(share, limit, own, other, got, attention):
@@ -516,11 +518,11 @@
         return lax.ppermute(part, "core", [(0, 1), (1, 0)])
 
     def data_terms(part):
-        step = 1
-        while 2 * step < n_dp:
-            part = part + lax.ppermute(part, "dp", [(d, d ^ step) for d in range(n_dp)])
-            step *= 2
-        return [part, lax.ppermute(part, "dp", [(d, d ^ step) for d in range(n_dp)])]
+        sent = [
+            lax.ppermute(part, "dp", [(d, d ^ step) for d in range(n_dp)])
+            for step in range(1, n_dp)
+        ]
+        return [part, *sent]
 
     where = core.astype(jnp.int32)[None]
     own_w, other_w = split(where, w_out)

time: 297 us -> 287 us (0.966)
  waiting for transfers between devices: 117 us -> 110 us
  Pallas kernels: 50.2 us -> 46.1 us
    ppermute x4 -> x0, waiting for transfers between devices: 10.9 us -> none  [data_terms(): part = part + lax.ppermute(part, 'dp', [(d, d ^ step) for d in range(n_dp)])]
    ppermute x4 -> x12, starting transfers between devices: 6.28 us -> 14 us  [data_terms(): lax.ppermute(part, 'dp', [(d, d ^ step) for d in range(n_dp)])]
    ppermute x4 -> x0, starting transfers between devices: 6.01 us -> none  [data_terms(): part = part + lax.ppermute(part, 'dp', [(d, d ^ step) for d in range(n_dp)])]
    ppermute x4 -> x12, waiting for transfers between devices: 10.9 us -> 14.6 us  [data_terms(): lax.ppermute(part, 'dp', [(d, d ^ step) for d in range(n_dp)])]
    pallas_call x4, Pallas kernels: 6.12 us -> 3.07 us  [cotangent(): pl.pallas_call(functools.partial(cotangent_kernel, share), in_specs=[SMEM...]
  transfers between devices with their start and end apart: 82 -> 86, of which waited for: 51 -> 55; matrix products, arithmetic and copies ran while one was open for 0% -> 0% of each run, Pallas kernels for 12% -> 12%
where the time goes in v7:
time: 287 us
  starting transfers between devices  123 us (43%)
  waiting for transfers between devices  110 us (38%)
  Pallas kernels  46.1 us (16%)
  local copies, waits for them, and re-layouts  5.24 us (2%)
    ppermute x36, starting transfers between devices, outer_swap(): return lax.ppermute(part, 'chip', [(0, 1), (1, 0), (2, 3), (3, 2)])  105 us
    ppermute x36, waiting for transfers between devices, outer_swap(): return lax.ppermute(part, 'chip', [(0, 1), (1, 0), (2, 3), (3, 2)])  83.6 us
    pallas_call x96, Pallas kernels, call(): pl.pallas_call(body, in_specs=[SMEM] * len(scalars) + [VMEM] * len(ins) +...  29.4 us
    ppermute x12, waiting for transfers between devices, data_terms(): lax.ppermute(part, 'dp', [(d, d ^ step) for d in range(n_dp)])  14.6 us
    ppermute x12, starting transfers between devices, data_terms(): lax.ppermute(part, 'dp', [(d, d ^ step) for d in range(n_dp)])  14 us
    ppermute x14, waiting for transfers between devices, swap(): return lax.ppermute(part, 'core', [(0, 1), (1, 0)])  11.4 us
    pallas_call x1, Pallas kernels, project(): pl.pallas_call(project_kernel, in_specs=[SMEM] + [hbm] * 4 + [VMEM] * 6,...  7.81 us
  transfers between devices with their start and end apart: 86, of which 55 were waited for; matrix products, arithmetic and copies ran while one was open for 0% of the time, Pallas kernels for 12%

profile of v7, /device:TPU:0, one launch (start us, length us, event | category | flops | bytes accessed | tf_op | source)
XLA Modules:
  0.0 286.8 jit_solution(10781075460794215775)
XLA Ops:
  0.6 2.3 copy-done
  3.0 2.5 shard_map.157
  8.1 7.8 %shard_map.156 = (f32[3,128,128]{2,1,0:T(8,128)S(1)}, bf16[128,384]{1,0:T(8,128)(2,1)S(1)}, bf16[128,384]{1,0:T(8,128)(2,1)S(1)}, f32[128,16]{1,0:T(8,128)S(1)},...) custom-call(s32[1]{0:T(128)S(6)} %copy.17.limit_ref.refs_1_.refs_4_.refs_6_.refs_10_, bf16[128,6144]{1,0:T(8,128)(2,1)S(1)} %copy-done.1, ...), custom_call_target="tpu_custom_call" | custom-call | flops 1811939328 | bytes 14155776 | tf_op jit(solution)/shard_map/pallas_call | solution.py:188
  20.7 3.0 %collective-permute-start.6 = (f32[136,512]{1,0:T(8,128)S(1)}, f32[136,512]{1,0:T(8,128)S(1)}, u32[]{:S(2)}, u32[]{:S(2)}) collective-permute-start(f32[136,512]{1,0:T(8,128)S(1)} %get-tuple-element.130.refs_4_.refs_0_), channel_id=1, source_target_pairs={{0,2},{2,0},{4,6},{6,4},{1,3},{3,1},{5,7},{7,5},{8,10},{10,8},{12,... | collective-permute-start | bytes 835592 | tf_op jit(solution)/shard_map/ppermute | solution.py:543
  24.0 2.4 shard_map.159
  31.1 3.5 %collective-permute-start.11 = (f32[128,512]{1,0:T(8,128)}, f32[128,512]{1,0:T(8,128)S(1)}, u32[]{:S(2)}, u32[]{:S(2)}) collective-permute-start(f32[128,512]{1,0:T(8,128)} %copy-done.19), channel_id=1, source_target_pairs={{0,2},{2,0},{4,6},{6,4},{1,3},{3,1},{5,7},{7,5},{8,10},{10,8},{12,... | collective-permute-start | bytes 786440 | tf_op jit(solution)/shard_map/ppermute | solution.py:543
  38.9 3.3 %collective-permute-start.13 = (f32[136,512]{1,0:T(8,128)S(1)}, f32[136,512]{1,0:T(8,128)S(1)}, u32[]{:S(2)}, u32[]{:S(2)}) collective-permute-start(f32[136,512]{1,0:T(8,128)S(1)} %get-tuple-element.140.refs_4_), channel_id=1, source_target_pairs={{0,2},{2,0},{4,6},{6,4},{1,3},{3,1},{5,7},{7,5},{8,10},{10,8},{12,... | collective-permute-start | bytes 835592 | tf_op jit(solution)/shard_map/ppermute | solution.py:543
  44.1 3.2 %collective-permute-start.15 = (f32[128,512]{1,0:T(8,128)S(1)}, f32[128,512]{1,0:T(8,128)S(1)}, u32[]{:S(2)}, u32[]{:S(2)}) collective-permute-start(f32[128,512]{1,0:T(8,128)S(1)} %get-tuple-element.142.refs_4_), channel_id=1, source_target_pairs={{0,2},{2,0},{4,6},{6,4},{1,3},{3,1},{5,7},{7,5},{8,10},{10,8},{12,... | collective-permute-start | bytes 786440 | tf_op jit(solution)/shard_map/ppermute | solution.py:543
  49.7 3.7 %collective-permute-start.14 = (f32[128,512]{1,0:T(8,128)S(1)}, f32[128,512]{1,0:T(8,128)S(1)}, u32[]{:S(2)}, u32[]{:S(2)}) collective-permute-start(f32[128,512]{1,0:T(8,128)S(1)} %get-tuple-element.144.refs_6_), channel_id=1, source_target_pairs={{0,2},{2,0},{4,6},{6,4},{1,3},{3,1},{5,7},{7,5},{8,10},{10,8},{12,... | collective-permute-start | bytes 786440 | tf_op jit(solution)/shard_map/ppermute | solution.py:543
  54.6 5.1 %collective-permute-start.18 = (f32[128,512]{1,0:T(8,128)S(1)}, f32[128,512]{1,0:T(8,128)S(1)}, u32[]{:S(2)}, u32[]{:S(2)}) collective-permute-start(f32[128,512]{1,0:T(8,128)S(1)} %shard_map.173.refs_8_.refs_3_), channel_id=1, source_target_pairs={{0,2},{2,0},{4,6},{6,4},{1,3},{3,1},{5,7},{7,5},{8,10},{10,8},{12,... | collective-permute-start | bytes 786440 | tf_op jit(solution)/shard_map/ppermute | solution.py:543
  60.8 4.6 %collective-permute-start.21 = (f32[128,512]{1,0:T(8,128)S(1)}, f32[128,512]{1,0:T(8,128)S(1)}, u32[]{:S(2)}, u32[]{:S(2)}) collective-permute-start(f32[128,512]{1,0:T(8,128)S(1)} %shard_map.176.refs_8_.refs_3_), channel_id=1, source_target_pairs={{0,2},{2,0},{4,6},{6,4},{1,3},{3,1},{5,7},{7,5},{8,10},{10,8},{12,... | collective-permute-start | bytes 786440 | tf_op jit(solution)/shard_map/ppermute | solution.py:543
  67.0 2.9 %collective-permute-start.20 = (f32[128,512]{1,0:T(8,128)S(1)}, f32[128,512]{1,0:T(8,128)S(1)}, u32[]{:S(2)}, u32[]{:S(2)}) collective-permute-start(f32[128,512]{1,0:T(8,128)S(1)} %shard_map.179.refs_8_.refs_3_), channel_id=1, source_target_pairs={{0,2},{2,0},{4,6},{6,4},{1,3},{3,1},{5,7},{7,5},{8,10},{10,8},{12,... | collective-permute-start | bytes 786440 | tf_op jit(solution)/shard_map/ppermute | solution.py:543
  69.9 2.7 collective-permute-done.21.refs_2_
  73.0 3.5 %collective-permute-done.20.refs_2_ = f32[128,512]{1,0:T(8,128)S(1)} collective-permute-done((f32[128,512]{1,0:T(8,128)S(1)}, f32[128,512]{1,0:T(8,128)S(1)}, u32[]{:S(2)}, u32[]{:S(2)}) %collective-permute-start.20) | collective-permute-done | bytes 262176 | tf_op jit(solution)/shard_map/ppermute | solution.py:543
  84.9 2.4 collective-permute-done.25.refs_3_
  93.6 6.0 %collective-permute-done.28.refs_1_ = f32[136,512]{1,0:T(8,128)S(1)} collective-permute-done((f32[136,512]{1,0:T(8,128)S(1)}, f32[136,512]{1,0:T(8,128)S(1)}, u32[]{:S(2)}, u32[]{:S(2)}) %collective-permute-start.28) | collective-permute-done | bytes 278560 | tf_op jit(solution)/shard_map/ppermute | solution.py:543
  99.8 3.3 %collective-permute-start.27 = (f32[128,512]{1,0:T(8,128)S(1)}, f32[128,512]{1,0:T(8,128)S(1)}, u32[]{:S(2)}, u32[]{:S(2)}) collective-permute-start(f32[128,512]{1,0:T(8,128)S(1)} %shard_map.185.refs_3_.refs_0_), channel_id=1, source_target_pairs={{0,2},{2,0},{4,6},{6,4},{1,3},{3,1},{5,7},{7,5},{8,10},{10,8},{12,... | collective-permute-start | bytes 786440 | tf_op jit(solution)/shard_map/ppermute | solution.py:543
  105.5 3.5 %collective-permute-start.32 = (f32[136,512]{1,0:T(8,128)S(1)}, f32[136,512]{1,0:T(8,128)S(1)}, u32[]{:S(2)}, u32[]{:S(2)}) collective-permute-start(f32[136,512]{1,0:T(8,128)S(1)} %get-tuple-element.172.refs_2_), channel_id=1, source_target_pairs={{0,2},{2,0},{4,6},{6,4},{1,3},{3,1},{5,7},{7,5},{8,10},{10,8},{12,... | collective-permute-start | bytes 835592 | tf_op jit(solution)/shard_map/ppermute | solution.py:543
  111.1 3.5 %collective-permute-start.35 = (f32[128,512]{1,0:T(8,128)S(1)}, f32[128,512]{1,0:T(8,128)S(1)}, u32[]{:S(2)}, u32[]{:S(2)}) collective-permute-start(f32[128,512]{1,0:T(8,128)S(1)} %get-tuple-element.173.refs_2_), channel_id=1, source_target_pairs={{0,2},{2,0},{4,6},{6,4},{1,3},{3,1},{5,7},{7,5},{8,10},{10,8},{12,... | collective-permute-start | bytes 786440 | tf_op jit(solution)/shard_map/ppermute | solution.py:543
  117.0 3.3 %collective-permute-start.34 = (f32[128,512]{1,0:T(8,128)S(1)}, f32[128,512]{1,0:T(8,128)S(1)}, u32[]{:S(2)}, u32[]{:S(2)}) collective-permute-start(f32[128,512]{1,0:T(8,128)S(1)} %get-tuple-element.174.refs_5_), channel_id=1, source_target_pairs={{0,2},{2,0},{4,6},{6,4},{1,3},{3,1},{5,7},{7,5},{8,10},{10,8},{12,... | collective-permute-start | bytes 786440 | tf_op jit(solution)/shard_map/ppermute | solution.py:543
  122.6 3.3 %collective-permute-start.38 = (f32[128,512]{1,0:T(8,128)S(1)}, f32[128,512]{1,0:T(8,128)S(1)}, u32[]{:S(2)}, u32[]{:S(2)}) collective-permute-start(f32[128,512]{1,0:T(8,128)S(1)} %shard_map.199.refs_7_.refs_3_), channel_id=1, source_target_pairs={{0,2},{2,0},{4,6},{6,4},{1,3},{3,1},{5,7},{7,5},{8,10},{10,8},{12,... | collective-permute-start | bytes 786440 | tf_op jit(solution)/shard_map/ppermute | solution.py:543
  128.3 3.3 %collective-permute-start.41 = (f32[128,512]{1,0:T(8,128)S(1)}, f32[128,512]{1,0:T(8,128)S(1)}, u32[]{:S(2)}, u32[]{:S(2)}) collective-permute-start(f32[128,512]{1,0:T(8,128)S(1)} %shard_map.202.refs_7_.refs_3_), channel_id=1, source_target_pairs={{0,2},{2,0},{4,6},{6,4},{1,3},{3,1},{5,7},{7,5},{8,10},{10,8},{12,... | collective-permute-start | bytes 786440 | tf_op jit(solution)/shard_map/ppermute | solution.py:543
  134.2 2.6 collective-permute-start.40
  136.8 2.6 collective-permute-done.41.refs_2_
  139.7 4.4 %collective-permute-done.40.refs_2_ = f32[128,512]{1,0:T(8,128)S(1)} collective-permute-done((f32[128,512]{1,0:T(8,128)S(1)}, f32[128,512]{1,0:T(8,128)S(1)}, u32[]{:S(2)}, u32[]{:S(2)}) %collective-permute-start.40) | collective-permute-done | bytes 262176 | tf_op jit(solution)/shard_map/ppermute | solution.py:543
  147.9 2.5 collective-permute-start.45
  159.2 6.0 %collective-permute-done.48.refs_1_ = f32[136,512]{1,0:T(8,128)S(1)} collective-permute-done((f32[136,512]{1,0:T(8,128)S(1)}, f32[136,512]{1,0:T(8,128)S(1)}, u32[]{:S(2)}, u32[]{:S(2)}) %collective-permute-start.48) | collective-permute-done | bytes 278560 | tf_op jit(solution)/shard_map/ppermute | solution.py:543
  165.3 3.3 %collective-permute-start.47 = (f32[128,512]{1,0:T(8,128)S(1)}, f32[128,512]{1,0:T(8,128)S(1)}, u32[]{:S(2)}, u32[]{:S(2)}) collective-permute-start(f32[128,512]{1,0:T(8,128)S(1)} %shard_map.211.refs_3_.refs_0_), channel_id=1, source_target_pairs={{0,2},{2,0},{4,6},{6,4},{1,3},{3,1},{5,7},{7,5},{8,10},{10,8},{12,... | collective-permute-start | bytes 786440 | tf_op jit(solution)/shard_map/ppermute | solution.py:543
  171.0 3.5 %collective-permute-start.52 = (f32[136,512]{1,0:T(8,128)S(1)}, f32[136,512]{1,0:T(8,128)S(1)}, u32[]{:S(2)}, u32[]{:S(2)}) collective-permute-start(f32[136,512]{1,0:T(8,128)S(1)} %get-tuple-element.193.refs_2_), channel_id=1, source_target_pairs={{0,2},{2,0},{4,6},{6,4},{1,3},{3,1},{5,7},{7,5},{8,10},{10,8},{12,... | collective-permute-start | bytes 835592 | tf_op jit(solution)/shard_map/ppermute | solution.py:543
  176.6 3.5 %collective-permute-start.55 = (f32[128,512]{1,0:T(8,128)S(1)}, f32[128,512]{1,0:T(8,128)S(1)}, u32[]{:S(2)}, u32[]{:S(2)}) collective-permute-start(f32[128,512]{1,0:T(8,128)S(1)} %get-tuple-element.194.refs_2_), channel_id=1, source_target_pairs={{0,2},{2,0},{4,6},{6,4},{1,3},{3,1},{5,7},{7,5},{8,10},{10,8},{12,... | collective-permute-start | bytes 786440 | tf_op jit(solution)/shard_map/ppermute | solution.py:543
  182.6 3.3 %collective-permute-start.54 = (f32[128,512]{1,0:T(8,128)S(1)}, f32[128,512]{1,0:T(8,128)S(1)}, u32[]{:S(2)}, u32[]{:S(2)}) collective-permute-start(f32[128,512]{1,0:T(8,128)S(1)} %get-tuple-element.195.refs_5_), channel_id=1, source_target_pairs={{0,2},{2,0},{4,6},{6,4},{1,3},{3,1},{5,7},{7,5},{8,10},{10,8},{12,... | collective-permute-start | bytes 786440 | tf_op jit(solution)/shard_map/ppermute | solution.py:543
  188.2 3.3 %collective-permute-start.58 = (f32[128,512]{1,0:T(8,128)S(1)}, f32[128,512]{1,0:T(8,128)S(1)}, u32[]{:S(2)}, u32[]{:S(2)}) collective-permute-start(f32[128,512]{1,0:T(8,128)S(1)} %shard_map.225.refs_7_.refs_3_), channel_id=1, source_target_pairs={{0,2},{2,0},{4,6},{6,4},{1,3},{3,1},{5,7},{7,5},{8,10},{10,8},{12,... | collective-permute-start | bytes 786440 | tf_op jit(solution)/shard_map/ppermute | solution.py:543
  193.8 3.3 %collective-permute-start.61 = (f32[128,512]{1,0:T(8,128)S(1)}, f32[128,512]{1,0:T(8,128)S(1)}, u32[]{:S(2)}, u32[]{:S(2)}) collective-permute-start(f32[128,512]{1,0:T(8,128)S(1)} %shard_map.228.refs_7_.refs_3_), channel_id=1, source_target_pairs={{0,2},{2,0},{4,6},{6,4},{1,3},{3,1},{5,7},{7,5},{8,10},{10,8},{12,... | collective-permute-start | bytes 786440 | tf_op jit(solution)/shard_map/ppermute | solution.py:543
  199.7 2.6 collective-permute-start.60
  202.3 2.6 collective-permute-done.61.refs_2_
  205.2 4.4 %collective-permute-done.60.refs_2_ = f32[128,512]{1,0:T(8,128)S(1)} collective-permute-done((f32[128,512]{1,0:T(8,128)S(1)}, f32[128,512]{1,0:T(8,128)S(1)}, u32[]{:S(2)}, u32[]{:S(2)}) %collective-permute-start.60) | collective-permute-done | bytes 262176 | tf_op jit(solution)/shard_map/ppermute | solution.py:543
  218.1 2.4 collective-permute-done.65.refs_3_
  226.7 6.0 %collective-permute-done.68.refs_1_ = f32[136,512]{1,0:T(8,128)S(1)} collective-permute-done((f32[136,512]{1,0:T(8,128)S(1)}, f32[136,512]{1,0:T(8,128)S(1)}, u32[]{:S(2)}, u32[]{:S(2)}) %collective-permute-start.68) | collective-permute-done | bytes 278560 | tf_op jit(solution)/shard_map/ppermute | solution.py:543
  232.9 3.3 %collective-permute-start.67 = (f32[128,512]{1,0:T(8,128)S(1)}, f32[128,512]{1,0:T(8,128)S(1)}, u32[]{:S(2)}, u32[]{:S(2)}) collective-permute-start(f32[128,512]{1,0:T(8,128)S(1)} %shard_map.237.refs_3_.refs_0_), channel_id=1, source_target_pairs={{0,2},{2,0},{4,6},{6,4},{1,3},{3,1},{5,7},{7,5},{8,10},{10,8},{12,... | collective-permute-start | bytes 786440 | tf_op jit(solution)/shard_map/ppermute | solution.py:543
  238.5 3.5 %collective-permute-start.72 = (f32[136,512]{1,0:T(8,128)S(1)}, f32[136,512]{1,0:T(8,128)S(1)}, u32[]{:S(2)}, u32[]{:S(2)}) collective-permute-start(f32[136,512]{1,0:T(8,128)S(1)} %get-tuple-element.218.refs_2_), channel_id=1, source_target_pairs={{0,2},{2,0},{4,6},{6,4},{1,3},{3,1},{5,7},{7,5},{8,10},{10,8},{12,... | collective-permute-start | bytes 835592 | tf_op jit(solution)/shard_map/ppermute | solution.py:543
  244.2 3.5 %collective-permute-start.75 = (f32[128,512]{1,0:T(8,128)S(1)}, f32[128,512]{1,0:T(8,128)S(1)}, u32[]{:S(2)}, u32[]{:S(2)}) collective-permute-start(f32[128,512]{1,0:T(8,128)S(1)} %get-tuple-element.219.refs_2_), channel_id=1, source_target_pairs={{0,2},{2,0},{4,6},{6,4},{1,3},{3,1},{5,7},{7,5},{8,10},{10,8},{12,... | collective-permute-start | bytes 786440 | tf_op jit(solution)/shard_map/ppermute | solution.py:543
  250.1 3.3 %collective-permute-start.74 = (f32[128,512]{1,0:T(8,128)S(1)}, f32[128,512]{1,0:T(8,128)S(1)}, u32[]{:S(2)}, u32[]{:S(2)}) collective-permute-start(f32[128,512]{1,0:T(8,128)S(1)} %get-tuple-element.220.refs_5_), channel_id=1, source_target_pairs={{0,2},{2,0},{4,6},{6,4},{1,3},{3,1},{5,7},{7,5},{8,10},{10,8},{12,... | collective-permute-start | bytes 786440 | tf_op jit(solution)/shard_map/ppermute | solution.py:543
  255.7 3.3 %collective-permute-start.78 = (f32[128,512]{1,0:T(8,128)S(1)}, f32[128,512]{1,0:T(8,128)S(1)}, u32[]{:S(2)}, u32[]{:S(2)}) collective-permute-start(f32[128,512]{1,0:T(8,128)S(1)} %shard_map.251.refs_7_.refs_3_), channel_id=1, source_target_pairs={{0,2},{2,0},{4,6},{6,4},{1,3},{3,1},{5,7},{7,5},{8,10},{10,8},{12,... | collective-permute-start | bytes 786440 | tf_op jit(solution)/shard_map/ppermute | solution.py:543
  261.3 3.3 %collective-permute-start.81 = (f32[128,512]{1,0:T(8,128)S(1)}, f32[128,512]{1,0:T(8,128)S(1)}, u32[]{:S(2)}, u32[]{:S(2)}) collective-permute-start(f32[128,512]{1,0:T(8,128)S(1)} %shard_map.254.refs_7_.refs_3_), channel_id=1, source_target_pairs={{0,2},{2,0},{4,6},{6,4},{1,3},{3,1},{5,7},{7,5},{8,10},{10,8},{12,... | collective-permute-start | bytes 786440 | tf_op jit(solution)/shard_map/ppermute | solution.py:543
  267.2 2.6 collective-permute-start.80
  269.8 2.6 collective-permute-done.81.refs_2_
  272.8 4.4 %collective-permute-done.80.refs_2_ = f32[128,512]{1,0:T(8,128)S(1)} collective-permute-done((f32[128,512]{1,0:T(8,128)S(1)}, f32[128,512]{1,0:T(8,128)S(1)}, u32[]{:S(2)}, u32[]{:S(2)}) %collective-permute-start.80) | collective-permute-done | bytes 262176 | tf_op jit(solution)/shard_map/ppermute | solution.py:543
  281.0 2.5 collective-permute-start.85
  (288 shorter events, 116.5 us)
Async XLA Ops:
  6.3 11.6 %collective-permute-start.3 = (f32[384,512]{1,0:T(8,128)}, f32[384,512]{1,0:T(8,128)}, u32[]{:S(2)}, u32[]{:S(2)}) collective-permute-start(f32[384,512]{1,0:T(8,128)} %get-tuple-element.129), channel_id=1, source_target_pairs={{0,1},{1,0},{2,3},{3,2},{4,5},{5,4},{6,7},{7,6},{8,9},{9,8},{10,11... | collective-permute-start | bytes 2359304 | tf_op jit(solution)/shard_map/ppermute | solution.py:518
  6.8 17.1 %collective-permute-start.2 = (f32[384,512]{1,0:T(8,128)}, f32[384,512]{1,0:T(8,128)}, u32[]{:S(2)}, u32[]{:S(2)}) collective-permute-start(f32[384,512]{1,0:T(8,128)} %get-tuple-element.127), channel_id=1, source_target_pairs={{0,1},{1,0},{2,3},{3,2},{4,5},{5,4},{6,7},{7,6},{8,9},{9,8},{10,11... | collective-permute-start | bytes 2359304 | tf_op jit(solution)/shard_map/ppermute | solution.py:518
  6.9 20.4 %collective-permute-start.7 = (f32[384,512]{1,0:T(8,128)}, f32[384,512]{1,0:T(8,128)}, u32[]{:S(2)}, u32[]{:S(2)}) collective-permute-start(f32[384,512]{1,0:T(8,128)} %get-tuple-element.135), channel_id=1, source_target_pairs={{0,1},{1,0},{2,3},{3,2},{4,5},{5,4},{6,7},{7,6},{8,9},{9,8},{10,11... | collective-permute-start | bytes 2359304 | tf_op jit(solution)/shard_map/ppermute | solution.py:518
  16.1 14.9 %collective-permute-start.5 = (f32[384,512]{1,0:T(8,128)}, f32[384,512]{1,0:T(8,128)}, u32[]{:S(2)}, u32[]{:S(2)}) collective-permute-start(f32[384,512]{1,0:T(8,128)} %get-tuple-element.133), channel_id=1, source_target_pairs={{0,1},{1,0},{2,3},{3,2},{4,5},{5,4},{6,7},{7,6},{8,9},{9,8},{10,11... | collective-permute-start | bytes 2359304 | tf_op jit(solution)/shard_map/ppermute | solution.py:518
  17.8 24.4 %collective-permute-start.9 = (f32[384,512]{1,0:T(8,128)}, f32[384,512]{1,0:T(8,128)}, u32[]{:S(2)}, u32[]{:S(2)}) collective-permute-start(f32[384,512]{1,0:T(8,128)} %copy-done.8), channel_id=1, source_target_pairs={{0,1},{1,0},{2,3},{3,2},{4,5},{5,4},{6,7},{7,6},{8,9},{9,8},{10,11... | collective-permute-start | bytes 2359304 | tf_op jit(solution)/shard_map/ppermute | solution.py:518
  20.7 10.0 %collective-permute-start.6 = (f32[136,512]{1,0:T(8,128)S(1)}, f32[136,512]{1,0:T(8,128)S(1)}, u32[]{:S(2)}, u32[]{:S(2)}) collective-permute-start(f32[136,512]{1,0:T(8,128)S(1)} %get-tuple-element.130.refs_4_.refs_0_), channel_id=1, source_target_pairs={{0,2},{2,0},{4,6},{6,4},{1,3},{3,1},{5,7},{7,5},{8,10},{10,8},{12,... | collective-permute-start | bytes 835592 | tf_op jit(solution)/shard_map/ppermute | solution.py:543
  24.0 23.4 %collective-permute-start.1 = (f32[384,512]{1,0:T(8,128)S(1)}, f32[384,512]{1,0:T(8,128)}, u32[]{:S(2)}, u32[]{:S(2)}) collective-permute-start(f32[384,512]{1,0:T(8,128)S(1)} %get-tuple-element.125), channel_id=1, source_target_pairs={{0,1},{1,0},{2,3},{3,2},{4,5},{5,4},{6,7},{7,6},{8,9},{9,8},{10,11... | collective-permute-start | bytes 2359304 | tf_op jit(solution)/shard_map/ppermute | solution.py:518
  27.3 9.4 %collective-permute-start.4 = (f32[128,512]{1,0:T(8,128)}, f32[128,512]{1,0:T(8,128)}, u32[]{:S(2)}, u32[]{:S(2)}) collective-permute-start(f32[128,512]{1,0:T(8,128)} %get-tuple-element.131.refs_4_.refs_0_), channel_id=1, source_target_pairs={{0,2},{2,0},{4,6},{6,4},{1,3},{3,1},{5,7},{7,5},{8,10},{10,8},{12,... | collective-permute-start | bytes 786440 | tf_op jit(solution)/shard_map/ppermute | solution.py:543
  30.9 6.9 %collective-permute-start.10 = (f32[136,512]{1,0:T(8,128)S(1)}, f32[136,512]{1,0:T(8,128)}, u32[]{:S(2)}, u32[]{:S(2)}) collective-permute-start(f32[136,512]{1,0:T(8,128)S(1)} %shard_map.161.refs_4_.refs_1_), channel_id=1, source_target_pairs={{2,4},{4,2},{3,5},{5,3},{0,1},{1,0},{6,7},{7,6},{10,12},{12,10},{1... | collective-permute-start | bytes 835592 | tf_op jit(solution)/shard_map/ppermute | solution.py:547
  31.1 12.9 %collective-permute-start.11 = (f32[128,512]{1,0:T(8,128)}, f32[128,512]{1,0:T(8,128)S(1)}, u32[]{:S(2)}, u32[]{:S(2)}) collective-permute-start(f32[128,512]{1,0:T(8,128)} %copy-done.19), channel_id=1, source_target_pairs={{0,2},{2,0},{4,6},{6,4},{1,3},{3,1},{5,7},{7,5},{8,10},{10,8},{12,... | collective-permute-start | bytes 786440 | tf_op jit(solution)/shard_map/ppermute | solution.py:543
  37.8 6.3 %collective-permute-start.8 = (f32[128,512]{1,0:T(8,128)S(1)}, f32[128,512]{1,0:T(8,128)S(1)}, u32[]{:S(2)}, u32[]{:S(2)}) collective-permute-start(f32[128,512]{1,0:T(8,128)S(1)} %shard_map.163.refs_4_.refs_1_), channel_id=1, source_target_pairs={{2,4},{4,2},{3,5},{5,3},{0,1},{1,0},{6,7},{7,6},{10,12},{12,10},{1... | collective-permute-start | bytes 786440 | tf_op jit(solution)/shard_map/ppermute | solution.py:547
  38.9 10.6 %collective-permute-start.13 = (f32[136,512]{1,0:T(8,128)S(1)}, f32[136,512]{1,0:T(8,128)S(1)}, u32[]{:S(2)}, u32[]{:S(2)}) collective-permute-start(f32[136,512]{1,0:T(8,128)S(1)} %get-tuple-element.140.refs_4_), channel_id=1, source_target_pairs={{0,2},{2,0},{4,6},{6,4},{1,3},{3,1},{5,7},{7,5},{8,10},{10,8},{12,... | collective-permute-start | bytes 835592 | tf_op jit(solution)/shard_map/ppermute | solution.py:543
  44.1 10.3 %collective-permute-start.15 = (f32[128,512]{1,0:T(8,128)S(1)}, f32[128,512]{1,0:T(8,128)S(1)}, u32[]{:S(2)}, u32[]{:S(2)}) collective-permute-start(f32[128,512]{1,0:T(8,128)S(1)} %get-tuple-element.142.refs_4_), channel_id=1, source_target_pairs={{0,2},{2,0},{4,6},{6,4},{1,3},{3,1},{5,7},{7,5},{8,10},{10,8},{12,... | collective-permute-start | bytes 786440 | tf_op jit(solution)/shard_map/ppermute | solution.py:543
  49.7 10.9 %collective-permute-start.14 = (f32[128,512]{1,0:T(8,128)S(1)}, f32[128,512]{1,0:T(8,128)S(1)}, u32[]{:S(2)}, u32[]{:S(2)}) collective-permute-start(f32[128,512]{1,0:T(8,128)S(1)} %get-tuple-element.144.refs_6_), channel_id=1, source_target_pairs={{0,2},{2,0},{4,6},{6,4},{1,3},{3,1},{5,7},{7,5},{8,10},{10,8},{12,... | collective-permute-start | bytes 786440 | tf_op jit(solution)/shard_map/ppermute | solution.py:543
  54.5 6.3 %collective-permute-start.19 = (f32[128,512]{1,0:T(8,128)S(1)}, f32[128,512]{1,0:T(8,128)S(1)}, u32[]{:S(2)}, u32[]{:S(2)}) collective-permute-start(f32[128,512]{1,0:T(8,128)S(1)} %shard_map.172.refs_2_.refs_0_), channel_id=1, source_target_pairs={{2,4},{4,2},{3,5},{5,3},{0,1},{1,0},{6,7},{7,6},{10,12},{12,10},{1... | collective-permute-start | bytes 786440 | tf_op jit(solution)/shard_map/ppermute | solution.py:547
  54.6 11.9 %collective-permute-start.18 = (f32[128,512]{1,0:T(8,128)S(1)}, f32[128,512]{1,0:T(8,128)S(1)}, u32[]{:S(2)}, u32[]{:S(2)}) collective-permute-start(f32[128,512]{1,0:T(8,128)S(1)} %shard_map.173.refs_8_.refs_3_), channel_id=1, source_target_pairs={{0,2},{2,0},{4,6},{6,4},{1,3},{3,1},{5,7},{7,5},{8,10},{10,8},{12,... | collective-permute-start | bytes 786440 | tf_op jit(solution)/shard_map/ppermute | solution.py:543
  60.7 6.2 %collective-permute-start.17 = (f32[128,512]{1,0:T(8,128)S(1)}, f32[128,512]{1,0:T(8,128)S(1)}, u32[]{:S(2)}, u32[]{:S(2)}) collective-permute-start(f32[128,512]{1,0:T(8,128)S(1)} %shard_map.175.refs_2_.refs_0_), channel_id=1, source_target_pairs={{2,4},{4,2},{3,5},{5,3},{0,1},{1,0},{6,7},{7,6},{10,12},{12,10},{1... | collective-permute-start | bytes 786440 | tf_op jit(solution)/shard_map/ppermute | solution.py:547
  60.8 11.8 %collective-permute-start.21 = (f32[128,512]{1,0:T(8,128)S(1)}, f32[128,512]{1,0:T(8,128)S(1)}, u32[]{:S(2)}, u32[]{:S(2)}) collective-permute-start(f32[128,512]{1,0:T(8,128)S(1)} %shard_map.176.refs_8_.refs_3_), channel_id=1, source_target_pairs={{0,2},{2,0},{4,6},{6,4},{1,3},{3,1},{5,7},{7,5},{8,10},{10,8},{12,... | collective-permute-start | bytes 786440 | tf_op jit(solution)/shard_map/ppermute | solution.py:543
  67.0 9.5 %collective-permute-start.20 = (f32[128,512]{1,0:T(8,128)S(1)}, f32[128,512]{1,0:T(8,128)S(1)}, u32[]{:S(2)}, u32[]{:S(2)}) collective-permute-start(f32[128,512]{1,0:T(8,128)S(1)} %shard_map.179.refs_8_.refs_3_), channel_id=1, source_target_pairs={{0,2},{2,0},{4,6},{6,4},{1,3},{3,1},{5,7},{7,5},{8,10},{10,8},{12,... | collective-permute-start | bytes 786440 | tf_op jit(solution)/shard_map/ppermute | solution.py:543
  90.1 9.6 %collective-permute-start.28 = (f32[136,512]{1,0:T(8,128)S(1)}, f32[136,512]{1,0:T(8,128)S(1)}, u32[]{:S(2)}, u32[]{:S(2)}) collective-permute-start(f32[136,512]{1,0:T(8,128)S(1)} %shard_map.184.refs_3_.refs_0_), channel_id=1, source_target_pairs={{0,2},{2,0},{4,6},{6,4},{1,3},{3,1},{5,7},{7,5},{8,10},{10,8},{12,... | collective-permute-start | bytes 835592 | tf_op jit(solution)/shard_map/ppermute | solution.py:543
  93.3 12.0 %collective-permute-start.30 = (f32[128,512]{1,0:T(8,128)S(1)}, f32[128,512]{1,0:T(8,128)S(1)}, u32[]{:S(2)}, u32[]{:S(2)}) collective-permute-start(f32[128,512]{1,0:T(8,128)S(1)} %shard_map.189.refs_2_.refs_0_), channel_id=1, source_target_pairs={{0,2},{2,0},{4,6},{6,4},{1,3},{3,1},{5,7},{7,5},{8,10},{10,8},{12,... | collective-permute-start | bytes 786440 | tf_op jit(solution)/shard_map/ppermute | solution.py:543
  99.8 11.1 %collective-permute-start.27 = (f32[128,512]{1,0:T(8,128)S(1)}, f32[128,512]{1,0:T(8,128)S(1)}, u32[]{:S(2)}, u32[]{:S(2)}) collective-permute-start(f32[128,512]{1,0:T(8,128)S(1)} %shard_map.185.refs_3_.refs_0_), channel_id=1, source_target_pairs={{0,2},{2,0},{4,6},{6,4},{1,3},{3,1},{5,7},{7,5},{8,10},{10,8},{12,... | collective-permute-start | bytes 786440 | tf_op jit(solution)/shard_map/ppermute | solution.py:543
  105.5 11.4 %collective-permute-start.32 = (f32[136,512]{1,0:T(8,128)S(1)}, f32[136,512]{1,0:T(8,128)S(1)}, u32[]{:S(2)}, u32[]{:S(2)}) collective-permute-start(f32[136,512]{1,0:T(8,128)S(1)} %get-tuple-element.172.refs_2_), channel_id=1, source_target_pairs={{0,2},{2,0},{4,6},{6,4},{1,3},{3,1},{5,7},{7,5},{8,10},{10,8},{12,... | collective-permute-start | bytes 835592 | tf_op jit(solution)/shard_map/ppermute | solution.py:543
  110.9 6.1 %collective-permute-start.31 = (f32[128,512]{1,0:T(8,128)S(1)}, f32[128,512]{1,0:T(8,128)S(1)}, u32[]{:S(2)}, u32[]{:S(2)}) collective-permute-start(f32[128,512]{1,0:T(8,128)S(1)} %shard_map.193.refs_4_.refs_1_), channel_id=1, source_target_pairs={{2,4},{4,2},{3,5},{5,3},{0,1},{1,0},{6,7},{7,6},{10,12},{12,10},{1... | collective-permute-start | bytes 786440 | tf_op jit(solution)/shard_map/ppermute | solution.py:547
  111.1 11.4 %collective-permute-start.35 = (f32[128,512]{1,0:T(8,128)S(1)}, f32[128,512]{1,0:T(8,128)S(1)}, u32[]{:S(2)}, u32[]{:S(2)}) collective-permute-start(f32[128,512]{1,0:T(8,128)S(1)} %get-tuple-element.173.refs_2_), channel_id=1, source_target_pairs={{0,2},{2,0},{4,6},{6,4},{1,3},{3,1},{5,7},{7,5},{8,10},{10,8},{12,... | collective-permute-start | bytes 786440 | tf_op jit(solution)/shard_map/ppermute | solution.py:543
  117.0 11.0 %collective-permute-start.34 = (f32[128,512]{1,0:T(8,128)S(1)}, f32[128,512]{1,0:T(8,128)S(1)}, u32[]{:S(2)}, u32[]{:S(2)}) collective-permute-start(f32[128,512]{1,0:T(8,128)S(1)} %get-tuple-element.174.refs_5_), channel_id=1, source_target_pairs={{0,2},{2,0},{4,6},{6,4},{1,3},{3,1},{5,7},{7,5},{8,10},{10,8},{12,... | collective-permute-start | bytes 786440 | tf_op jit(solution)/shard_map/ppermute | solution.py:543
  122.6 11.1 %collective-permute-start.38 = (f32[128,512]{1,0:T(8,128)S(1)}, f32[128,512]{1,0:T(8,128)S(1)}, u32[]{:S(2)}, u32[]{:S(2)}) collective-permute-start(f32[128,512]{1,0:T(8,128)S(1)} %shard_map.199.refs_7_.refs_3_), channel_id=1, source_target_pairs={{0,2},{2,0},{4,6},{6,4},{1,3},{3,1},{5,7},{7,5},{8,10},{10,8},{12,... | collective-permute-start | bytes 786440 | tf_op jit(solution)/shard_map/ppermute | solution.py:543
  128.3 11.1 %collective-permute-start.41 = (f32[128,512]{1,0:T(8,128)S(1)}, f32[128,512]{1,0:T(8,128)S(1)}, u32[]{:S(2)}, u32[]{:S(2)}) collective-permute-start(f32[128,512]{1,0:T(8,128)S(1)} %shard_map.202.refs_7_.refs_3_), channel_id=1, source_target_pairs={{0,2},{2,0},{4,6},{6,4},{1,3},{3,1},{5,7},{7,5},{8,10},{10,8},{12,... | collective-permute-start | bytes 786440 | tf_op jit(solution)/shard_map/ppermute | solution.py:543
  134.2 10.0 %collective-permute-start.40 = (f32[128,512]{1,0:T(8,128)S(1)}, f32[128,512]{1,0:T(8,128)S(1)}, u32[]{:S(2)}, u32[]{:S(2)}) collective-permute-start(f32[128,512]{1,0:T(8,128)S(1)} %shard_map.205.refs_7_.refs_3_), channel_id=1, source_target_pairs={{0,2},{2,0},{4,6},{6,4},{1,3},{3,1},{5,7},{7,5},{8,10},{10,8},{12,... | collective-permute-start | bytes 786440 | tf_op jit(solution)/shard_map/ppermute | solution.py:543
  155.6 9.6 %collective-permute-start.48 = (f32[136,512]{1,0:T(8,128)S(1)}, f32[136,512]{1,0:T(8,128)S(1)}, u32[]{:S(2)}, u32[]{:S(2)}) collective-permute-start(f32[136,512]{1,0:T(8,128)S(1)} %shard_map.210.refs_3_.refs_0_), channel_id=1, source_target_pairs={{0,2},{2,0},{4,6},{6,4},{1,3},{3,1},{5,7},{7,5},{8,10},{10,8},{12,... | collective-permute-start | bytes 835592 | tf_op jit(solution)/shard_map/ppermute | solution.py:543
  158.8 12.0 %collective-permute-start.50 = (f32[128,512]{1,0:T(8,128)S(1)}, f32[128,512]{1,0:T(8,128)S(1)}, u32[]{:S(2)}, u32[]{:S(2)}) collective-permute-start(f32[128,512]{1,0:T(8,128)S(1)} %shard_map.215.refs_2_.refs_0_), channel_id=1, source_target_pairs={{0,2},{2,0},{4,6},{6,4},{1,3},{3,1},{5,7},{7,5},{8,10},{10,8},{12,... | collective-permute-start | bytes 786440 | tf_op jit(solution)/shard_map/ppermute | solution.py:543
  165.3 11.1 %collective-permute-start.47 = (f32[128,512]{1,0:T(8,128)S(1)}, f32[128,512]{1,0:T(8,128)S(1)}, u32[]{:S(2)}, u32[]{:S(2)}) collective-permute-start(f32[128,512]{1,0:T(8,128)S(1)} %shard_map.211.refs_3_.refs_0_), channel_id=1, source_target_pairs={{0,2},{2,0},{4,6},{6,4},{1,3},{3,1},{5,7},{7,5},{8,10},{10,8},{12,... | collective-permute-start | bytes 786440 | tf_op jit(solution)/shard_map/ppermute | solution.py:543
  171.0 11.4 %collective-permute-start.52 = (f32[136,512]{1,0:T(8,128)S(1)}, f32[136,512]{1,0:T(8,128)S(1)}, u32[]{:S(2)}, u32[]{:S(2)}) collective-permute-start(f32[136,512]{1,0:T(8,128)S(1)} %get-tuple-element.193.refs_2_), channel_id=1, source_target_pairs={{0,2},{2,0},{4,6},{6,4},{1,3},{3,1},{5,7},{7,5},{8,10},{10,8},{12,... | collective-permute-start | bytes 835592 | tf_op jit(solution)/shard_map/ppermute | solution.py:543
  176.6 11.4 %collective-permute-start.55 = (f32[128,512]{1,0:T(8,128)S(1)}, f32[128,512]{1,0:T(8,128)S(1)}, u32[]{:S(2)}, u32[]{:S(2)}) collective-permute-start(f32[128,512]{1,0:T(8,128)S(1)} %get-tuple-element.194.refs_2_), channel_id=1, source_target_pairs={{0,2},{2,0},{4,6},{6,4},{1,3},{3,1},{5,7},{7,5},{8,10},{10,8},{12,... | collective-permute-start | bytes 786440 | tf_op jit(solution)/shard_map/ppermute | solution.py:543
  182.6 11.1 %collective-permute-start.54 = (f32[128,512]{1,0:T(8,128)S(1)}, f32[128,512]{1,0:T(8,128)S(1)}, u32[]{:S(2)}, u32[]{:S(2)}) collective-permute-start(f32[128,512]{1,0:T(8,128)S(1)} %get-tuple-element.195.refs_5_), channel_id=1, source_target_pairs={{0,2},{2,0},{4,6},{6,4},{1,3},{3,1},{5,7},{7,5},{8,10},{10,8},{12,... | collective-permute-start | bytes 786440 | tf_op jit(solution)/shard_map/ppermute | solution.py:543
  188.2 11.1 %collective-permute-start.58 = (f32[128,512]{1,0:T(8,128)S(1)}, f32[128,512]{1,0:T(8,128)S(1)}, u32[]{:S(2)}, u32[]{:S(2)}) collective-permute-start(f32[128,512]{1,0:T(8,128)S(1)} %shard_map.225.refs_7_.refs_3_), channel_id=1, source_target_pairs={{0,2},{2,0},{4,6},{6,4},{1,3},{3,1},{5,7},{7,5},{8,10},{10,8},{12,... | collective-permute-start | bytes 786440 | tf_op jit(solution)/shard_map/ppermute | solution.py:543
  193.8 11.1 %collective-permute-start.61 = (f32[128,512]{1,0:T(8,128)S(1)}, f32[128,512]{1,0:T(8,128)S(1)}, u32[]{:S(2)}, u32[]{:S(2)}) collective-permute-start(f32[128,512]{1,0:T(8,128)S(1)} %shard_map.228.refs_7_.refs_3_), channel_id=1, source_target_pairs={{0,2},{2,0},{4,6},{6,4},{1,3},{3,1},{5,7},{7,5},{8,10},{10,8},{12,... | collective-permute-start | bytes 786440 | tf_op jit(solution)/shard_map/ppermute | solution.py:543
  199.7 10.0 %collective-permute-start.60 = (f32[128,512]{1,0:T(8,128)S(1)}, f32[128,512]{1,0:T(8,128)S(1)}, u32[]{:S(2)}, u32[]{:S(2)}) collective-permute-start(f32[128,512]{1,0:T(8,128)S(1)} %shard_map.231.refs_7_.refs_3_), channel_id=1, source_target_pairs={{0,2},{2,0},{4,6},{6,4},{1,3},{3,1},{5,7},{7,5},{8,10},{10,8},{12,... | collective-permute-start | bytes 786440 | tf_op jit(solution)/shard_map/ppermute | solution.py:543
  223.2 9.6 %collective-permute-start.68 = (f32[136,512]{1,0:T(8,128)S(1)}, f32[136,512]{1,0:T(8,128)S(1)}, u32[]{:S(2)}, u32[]{:S(2)}) collective-permute-start(f32[136,512]{1,0:T(8,128)S(1)} %shard_map.236.refs_3_.refs_0_), channel_id=1, source_target_pairs={{0,2},{2,0},{4,6},{6,4},{1,3},{3,1},{5,7},{7,5},{8,10},{10,8},{12,... | collective-permute-start | bytes 835592 | tf_op jit(solution)/shard_map/ppermute | solution.py:543
  226.4 12.0 %collective-permute-start.70 = (f32[128,512]{1,0:T(8,128)S(1)}, f32[128,512]{1,0:T(8,128)S(1)}, u32[]{:S(2)}, u32[]{:S(2)}) collective-permute-start(f32[128,512]{1,0:T(8,128)S(1)} %shard_map.241.refs_2_.refs_0_), channel_id=1, source_target_pairs={{0,2},{2,0},{4,6},{6,4},{1,3},{3,1},{5,7},{7,5},{8,10},{10,8},{12,... | collective-permute-start | bytes 786440 | tf_op jit(solution)/shard_map/ppermute | solution.py:543
  232.9 11.1 %collective-permute-start.67 = (f32[128,512]{1,0:T(8,128)S(1)}, f32[128,512]{1,0:T(8,128)S(1)}, u32[]{:S(2)}, u32[]{:S(2)}) collective-permute-start(f32[128,512]{1,0:T(8,128)S(1)} %shard_map.237.refs_3_.refs_0_), channel_id=1, source_target_pairs={{0,2},{2,0},{4,6},{6,4},{1,3},{3,1},{5,7},{7,5},{8,10},{10,8},{12,... | collective-permute-start | bytes 786440 | tf_op jit(solution)/shard_map/ppermute | solution.py:543
  238.5 11.4 %collective-permute-start.72 = (f32[136,512]{1,0:T(8,128)S(1)}, f32[136,512]{1,0:T(8,128)S(1)}, u32[]{:S(2)}, u32[]{:S(2)}) collective-permute-start(f32[136,512]{1,0:T(8,128)S(1)} %get-tuple-element.218.refs_2_), channel_id=1, source_target_pairs={{0,2},{2,0},{4,6},{6,4},{1,3},{3,1},{5,7},{7,5},{8,10},{10,8},{12,... | collective-permute-start | bytes 835592 | tf_op jit(solution)/shard_map/ppermute | solution.py:543
  244.0 6.1 %collective-permute-start.71 = (f32[128,512]{1,0:T(8,128)S(1)}, f32[128,512]{1,0:T(8,128)S(1)}, u32[]{:S(2)}, u32[]{:S(2)}) collective-permute-start(f32[128,512]{1,0:T(8,128)S(1)} %shard_map.245.refs_4_.refs_1_), channel_id=1, source_target_pairs={{2,4},{4,2},{3,5},{5,3},{0,1},{1,0},{6,7},{7,6},{10,12},{12,10},{1... | collective-permute-start | bytes 786440 | tf_op jit(solution)/shard_map/ppermute | solution.py:547
  244.2 11.4 %collective-permute-start.75 = (f32[128,512]{1,0:T(8,128)S(1)}, f32[128,512]{1,0:T(8,128)S(1)}, u32[]{:S(2)}, u32[]{:S(2)}) collective-permute-start(f32[128,512]{1,0:T(8,128)S(1)} %get-tuple-element.219.refs_2_), channel_id=1, source_target_pairs={{0,2},{2,0},{4,6},{6,4},{1,3},{3,1},{5,7},{7,5},{8,10},{10,8},{12,... | collective-permute-start | bytes 786440 | tf_op jit(solution)/shard_map/ppermute | solution.py:543
  250.1 11.0 %collective-permute-start.74 = (f32[128,512]{1,0:T(8,128)S(1)}, f32[128,512]{1,0:T(8,128)S(1)}, u32[]{:S(2)}, u32[]{:S(2)}) collective-permute-start(f32[128,512]{1,0:T(8,128)S(1)} %get-tuple-element.220.refs_5_), channel_id=1, source_target_pairs={{0,2},{2,0},{4,6},{6,4},{1,3},{3,1},{5,7},{7,5},{8,10},{10,8},{12,... | collective-permute-start | bytes 786440 | tf_op jit(solution)/shard_map/ppermute | solution.py:543
  255.7 11.1 %collective-permute-start.78 = (f32[128,512]{1,0:T(8,128)S(1)}, f32[128,512]{1,0:T(8,128)S(1)}, u32[]{:S(2)}, u32[]{:S(2)}) collective-permute-start(f32[128,512]{1,0:T(8,128)S(1)} %shard_map.251.refs_7_.refs_3_), channel_id=1, source_target_pairs={{0,2},{2,0},{4,6},{6,4},{1,3},{3,1},{5,7},{7,5},{8,10},{10,8},{12,... | collective-permute-start | bytes 786440 | tf_op jit(solution)/shard_map/ppermute | solution.py:543
  261.3 11.1 %collective-permute-start.81 = (f32[128,512]{1,0:T(8,128)S(1)}, f32[128,512]{1,0:T(8,128)S(1)}, u32[]{:S(2)}, u32[]{:S(2)}) collective-permute-start(f32[128,512]{1,0:T(8,128)S(1)} %shard_map.254.refs_7_.refs_3_), channel_id=1, source_target_pairs={{0,2},{2,0},{4,6},{6,4},{1,3},{3,1},{5,7},{7,5},{8,10},{10,8},{12,... | collective-permute-start | bytes 786440 | tf_op jit(solution)/shard_map/ppermute | solution.py:543
  267.2 10.0 %collective-permute-start.80 = (f32[128,512]{1,0:T(8,128)S(1)}, f32[128,512]{1,0:T(8,128)S(1)}, u32[]{:S(2)}, u32[]{:S(2)}) collective-permute-start(f32[128,512]{1,0:T(8,128)S(1)} %shard_map.257.refs_7_.refs_3_), channel_id=1, source_target_pairs={{0,2},{2,0},{4,6},{6,4},{1,3},{3,1},{5,7},{7,5},{8,10},{10,8},{12,... | collective-permute-start | bytes 786440 | tf_op jit(solution)/shard_map/ppermute | solution.py:543
  (66 other events, 300.0 us)

commit v8 on v7

--- a/solution.py
+++ b/solution.py
@@ -542,6 +542,12 @@
     def outer_swap(part):
         return lax.ppermute(part, "chip", [(0, 1), (1, 0), (2, 3), (3, 2)])
 
+    def send_in(part):
+        return lax.ppermute(part, "chip", [(0, 1), (3, 2)])
+
+    def send_back(part):
+        return lax.ppermute(part, "chip", [(1, 0), (2, 3)])
+
     def inner_swap(part):
         hops = [(2, 4), (4, 2), (3, 5), (5, 3), (0, 1), (1, 0), (6, 7), (7, 6)]
         return lax.ppermute(part, ("chip", "core"), hops)
@@ -598,9 +604,9 @@
                     else:
                         total[k] = sent = add(own_part[k], inner[k], token)
                     token = sent
-                    outer[later] = outer_swap(sent)
+                    outer[later] = send_back(sent) if later == CHUNKS else outer_swap(sent)
                 elif tick == 0:
-                    outer[later] = outer_swap(own_part[later])
+                    outer[later] = send_in(own_part[later])
                 if tick + 3 < CHUNKS and first:
                     token = begin(tick + 3)
                 if tick >= 3 and tick != CHUNKS:

time: 287 us -> 285 us (level)
  starting transfers between devices: 123 us -> 119 us
    ppermute x36 -> x28, starting transfers between devices: 105 us -> 80.6 us  [outer_swap(): return lax.ppermute(part, 'chip', [(0, 1), (1, 0), (2, 3), (3, 2)])]
    ppermute x0 -> x8, starting transfers between devices: none -> 20.8 us  [the longest x4 15.1 us: send_in(): return lax.ppermute(part, 'chip', [(0, 1), (3, 2)])]
    ppermute x0 -> x8, waiting for transfers between devices: none -> 15.9 us  [the longest x4 9.95 us: send_back(): return lax.ppermute(part, 'chip', [(1, 0), (2, 3)])]
    ppermute x36 -> x28, waiting for transfers between devices: 83.6 us -> 69.1 us  [outer_swap(): return lax.ppermute(part, 'chip', [(0, 1), (1, 0), (2, 3), (3, 2)])]
  transfers between devices with their start and end apart: 86 -> 86, of which waited for: 55 -> 54; matrix products, arithmetic and copies ran while one was open for 0% -> 0% of each run, Pallas kernels for 12% -> 12%
where the time goes in v8:
time: 285 us
  starting transfers between devices  119 us (42%)
  waiting for transfers between devices  111 us (39%)
  Pallas kernels  46 us (16%)
  local copies, waits for them, and re-layouts  5.24 us (2%)
    ppermute x28, starting transfers between devices, outer_swap(): return lax.ppermute(part, 'chip', [(0, 1), (1, 0), (2, 3), (3, 2)])  80.6 us
    ppermute x28, waiting for transfers between devices, outer_swap(): return lax.ppermute(part, 'chip', [(0, 1), (1, 0), (2, 3), (3, 2)])  69.1 us
    pallas_call x96, Pallas kernels, call(): pl.pallas_call(body, in_specs=[SMEM] * len(scalars) + [VMEM] * len(ins) +...  29.4 us
    ppermute x4, starting transfers between devices, send_in(): return lax.ppermute(part, 'chip', [(0, 1), (3, 2)])  15.1 us
    ppermute x12, waiting for transfers between devices, data_terms(): lax.ppermute(part, 'dp', [(d, d ^ step) for d in range(n_dp)])  14.8 us
    ppermute x12, starting transfers between devices, data_terms(): lax.ppermute(part, 'dp', [(d, d ^ step) for d in range(n_dp)])  14 us
    ppermute x14, waiting for transfers between devices, swap(): return lax.ppermute(part, 'core', [(0, 1), (1, 0)])  11.4 us
    ppermute x4, waiting for transfers between devices, send_back(): return lax.ppermute(part, 'chip', [(1, 0), (2, 3)])  9.95 us
  transfers between devices with their start and end apart: 86, of which 54 were waited for; matrix products, arithmetic and copies ran while one was open for 0% of the time, Pallas kernels for 12%

profile of v8, /device:TPU:0, one launch (start us, length us, event | category | flops | bytes accessed | tf_op | source)
XLA Modules:
  0.0 284.8 jit_solution(2174400264346188340)
XLA Ops:
  0.6 2.3 copy-done
  3.0 2.5 shard_map.157
  8.1 7.8 %shard_map.156 = (f32[3,128,128]{2,1,0:T(8,128)S(1)}, bf16[128,384]{1,0:T(8,128)(2,1)S(1)}, bf16[128,384]{1,0:T(8,128)(2,1)S(1)}, f32[128,16]{1,0:T(8,128)S(1)},...) custom-call(s32[1]{0:T(128)S(6)} %copy.17.limit_ref.refs_1_.refs_4_.refs_6_.refs_10_, bf16[128,6144]{1,0:T(8,128)(2,1)S(1)} %copy-done.1, ...), custom_call_target="tpu_custom_call" | custom-call | flops 1811939328 | bytes 14155776 | tf_op jit(solution)/shard_map/pallas_call | solution.py:188
  20.7 3.0 %collective-permute-start.6 = (f32[136,512]{1,0:T(8,128)S(1)}, f32[136,512]{1,0:T(8,128)S(1)}, u32[]{:S(2)}, u32[]{:S(2)}) collective-permute-start(f32[136,512]{1,0:T(8,128)S(1)} %get-tuple-element.130.refs_4_.refs_0_), channel_id=1, source_target_pairs={{0,2},{2,0},{4,6},{6,4},{1,3},{3,1},{5,7},{7,5},{8,10},{10,8},{12,... | collective-permute-start | bytes 835592 | tf_op jit(solution)/shard_map/ppermute | solution.py:543
  24.0 2.4 shard_map.159
  31.1 5.4 %collective-permute-start.11 = (f32[128,512]{1,0:T(8,128)}, f32[128,512]{1,0:T(8,128)S(1)}, u32[]{:S(2)}, u32[]{:S(2)}) collective-permute-start(f32[128,512]{1,0:T(8,128)} %copy-done.19), channel_id=1, source_target_pairs={{0,2},{6,4},{1,3},{7,5},{8,10},{14,12},{9,11},{15,13},{16,18},{22,... | collective-permute-start | bytes 786440 | tf_op jit(solution)/shard_map/ppermute | solution.py:546
  44.0 3.5 %collective-permute-start.15 = (f32[128,512]{1,0:T(8,128)S(1)}, f32[128,512]{1,0:T(8,128)S(1)}, u32[]{:S(2)}, u32[]{:S(2)}) collective-permute-start(f32[128,512]{1,0:T(8,128)S(1)} %get-tuple-element.142.refs_4_), channel_id=1, source_target_pairs={{0,2},{2,0},{4,6},{6,4},{1,3},{3,1},{5,7},{7,5},{8,10},{10,8},{12,... | collective-permute-start | bytes 786440 | tf_op jit(solution)/shard_map/ppermute | solution.py:543
  50.1 3.5 %collective-permute-start.14 = (f32[128,512]{1,0:T(8,128)S(1)}, f32[128,512]{1,0:T(8,128)S(1)}, u32[]{:S(2)}, u32[]{:S(2)}) collective-permute-start(f32[128,512]{1,0:T(8,128)S(1)} %get-tuple-element.144.refs_6_), channel_id=1, source_target_pairs={{0,2},{2,0},{4,6},{6,4},{1,3},{3,1},{5,7},{7,5},{8,10},{10,8},{12,... | collective-permute-start | bytes 786440 | tf_op jit(solution)/shard_map/ppermute | solution.py:543
  57.7 3.0 %collective-permute-done.14.refs_1_.refs_2_ = f32[128,512]{1,0:T(8,128)S(1)} collective-permute-done((f32[128,512]{1,0:T(8,128)S(1)}, f32[128,512]{1,0:T(8,128)S(1)}, u32[]{:S(2)}, u32[]{:S(2)}) %collective-permute-start.14) | collective-permute-done | bytes 262176 | tf_op jit(solution)/shard_map/ppermute | solution.py:543
  60.9 4.2 %collective-permute-start.21 = (f32[128,512]{1,0:T(8,128)S(1)}, f32[128,512]{1,0:T(8,128)S(1)}, u32[]{:S(2)}, u32[]{:S(2)}) collective-permute-start(f32[128,512]{1,0:T(8,128)S(1)} %shard_map.176.refs_8_.refs_3_), channel_id=1, source_target_pairs={{0,2},{2,0},{4,6},{6,4},{1,3},{3,1},{5,7},{7,5},{8,10},{10,8},{12,... | collective-permute-start | bytes 786440 | tf_op jit(solution)/shard_map/ppermute | solution.py:543
  65.5 2.7 collective-permute-done.18.refs_2_
  69.8 4.0 %collective-permute-done.21.refs_2_ = f32[128,512]{1,0:T(8,128)S(1)} collective-permute-done((f32[128,512]{1,0:T(8,128)S(1)}, f32[128,512]{1,0:T(8,128)S(1)}, u32[]{:S(2)}, u32[]{:S(2)}) %collective-permute-start.21) | collective-permute-done | bytes 262176 | tf_op jit(solution)/shard_map/ppermute | solution.py:543
  74.1 3.4 %collective-permute-done.20.refs_2_ = f32[128,512]{1,0:T(8,128)S(1)} collective-permute-done((f32[128,512]{1,0:T(8,128)S(1)}, f32[128,512]{1,0:T(8,128)S(1)}, u32[]{:S(2)}, u32[]{:S(2)}) %collective-permute-start.20) | collective-permute-done | bytes 262176 | tf_op jit(solution)/shard_map/ppermute | solution.py:543
  85.9 2.4 collective-permute-done.25.refs_3_
  92.4 2.1 collective-permute-start.30
  94.5 6.0 %collective-permute-done.28.refs_1_ = f32[136,512]{1,0:T(8,128)S(1)} collective-permute-done((f32[136,512]{1,0:T(8,128)S(1)}, f32[136,512]{1,0:T(8,128)S(1)}, u32[]{:S(2)}, u32[]{:S(2)}) %collective-permute-start.28) | collective-permute-done | bytes 278560 | tf_op jit(solution)/shard_map/ppermute | solution.py:543
  100.6 3.3 %collective-permute-start.27 = (f32[128,512]{1,0:T(8,128)S(1)}, f32[128,512]{1,0:T(8,128)S(1)}, u32[]{:S(2)}, u32[]{:S(2)}) collective-permute-start(f32[128,512]{1,0:T(8,128)S(1)} %shard_map.185.refs_3_.refs_0_), channel_id=1, source_target_pairs={{0,2},{6,4},{1,3},{7,5},{8,10},{14,12},{9,11},{15,13},{16,18},{22,... | collective-permute-start | bytes 786440 | tf_op jit(solution)/shard_map/ppermute | solution.py:546
  105.5 3.2 %collective-permute-start.32 = (f32[136,512]{1,0:T(8,128)S(1)}, f32[136,512]{1,0:T(8,128)S(1)}, u32[]{:S(2)}, u32[]{:S(2)}) collective-permute-start(f32[136,512]{1,0:T(8,128)S(1)} %get-tuple-element.172.refs_2_), channel_id=1, source_target_pairs={{0,2},{2,0},{4,6},{6,4},{1,3},{3,1},{5,7},{7,5},{8,10},{10,8},{12,... | collective-permute-start | bytes 835592 | tf_op jit(solution)/shard_map/ppermute | solution.py:543
  110.9 4.2 %collective-permute-start.35 = (f32[128,512]{1,0:T(8,128)S(1)}, f32[128,512]{1,0:T(8,128)S(1)}, u32[]{:S(2)}, u32[]{:S(2)}) collective-permute-start(f32[128,512]{1,0:T(8,128)S(1)} %get-tuple-element.173.refs_2_), channel_id=1, source_target_pairs={{0,2},{2,0},{4,6},{6,4},{1,3},{3,1},{5,7},{7,5},{8,10},{10,8},{12,... | collective-permute-start | bytes 786440 | tf_op jit(solution)/shard_map/ppermute | solution.py:543
  116.6 4.1 %collective-permute-start.34 = (f32[128,512]{1,0:T(8,128)S(1)}, f32[128,512]{1,0:T(8,128)S(1)}, u32[]{:S(2)}, u32[]{:S(2)}) collective-permute-start(f32[128,512]{1,0:T(8,128)S(1)} %get-tuple-element.174.refs_5_), channel_id=1, source_target_pairs={{0,2},{2,0},{4,6},{6,4},{1,3},{3,1},{5,7},{7,5},{8,10},{10,8},{12,... | collective-permute-start | bytes 786440 | tf_op jit(solution)/shard_map/ppermute | solution.py:543
  123.8 2.1 collective-permute-done.34.refs_1_.refs_2_
  126.1 6.1 %collective-permute-start.41 = (f32[128,512]{1,0:T(8,128)S(1)}, f32[128,512]{1,0:T(8,128)S(1)}, u32[]{:S(2)}, u32[]{:S(2)}) collective-permute-start(f32[128,512]{1,0:T(8,128)S(1)} %shard_map.202.refs_7_.refs_3_), channel_id=1, source_target_pairs={{0,2},{2,0},{4,6},{6,4},{1,3},{3,1},{5,7},{7,5},{8,10},{10,8},{12,... | collective-permute-start | bytes 786440 | tf_op jit(solution)/shard_map/ppermute | solution.py:543
  132.6 2.4 collective-permute-done.38.refs_2_
  136.7 3.5 %collective-permute-done.41.refs_2_ = f32[128,512]{1,0:T(8,128)S(1)} collective-permute-done((f32[128,512]{1,0:T(8,128)S(1)}, f32[128,512]{1,0:T(8,128)S(1)}, u32[]{:S(2)}, u32[]{:S(2)}) %collective-permute-start.41) | collective-permute-done | bytes 262176 | tf_op jit(solution)/shard_map/ppermute | solution.py:543
  140.6 3.4 %collective-permute-done.40.refs_2_ = f32[128,512]{1,0:T(8,128)S(1)} collective-permute-done((f32[128,512]{1,0:T(8,128)S(1)}, f32[128,512]{1,0:T(8,128)S(1)}, u32[]{:S(2)}, u32[]{:S(2)}) %collective-permute-start.40) | collective-permute-done | bytes 262176 | tf_op jit(solution)/shard_map/ppermute | solution.py:543
  147.7 2.4 collective-permute-start.45
  159.0 6.0 %collective-permute-done.48.refs_1_ = f32[136,512]{1,0:T(8,128)S(1)} collective-permute-done((f32[136,512]{1,0:T(8,128)S(1)}, f32[136,512]{1,0:T(8,128)S(1)}, u32[]{:S(2)}, u32[]{:S(2)}) %collective-permute-start.48) | collective-permute-done | bytes 278560 | tf_op jit(solution)/shard_map/ppermute | solution.py:543
  165.1 2.9 %collective-permute-start.47 = (f32[128,512]{1,0:T(8,128)S(1)}, f32[128,512]{1,0:T(8,128)S(1)}, u32[]{:S(2)}, u32[]{:S(2)}) collective-permute-start(f32[128,512]{1,0:T(8,128)S(1)} %shard_map.211.refs_3_.refs_0_), channel_id=1, source_target_pairs={{0,2},{6,4},{1,3},{7,5},{8,10},{14,12},{9,11},{15,13},{16,18},{22,... | collective-permute-start | bytes 786440 | tf_op jit(solution)/shard_map/ppermute | solution.py:546
  170.0 2.8 %collective-permute-start.52 = (f32[136,512]{1,0:T(8,128)S(1)}, f32[136,512]{1,0:T(8,128)S(1)}, u32[]{:S(2)}, u32[]{:S(2)}) collective-permute-start(f32[136,512]{1,0:T(8,128)S(1)} %get-tuple-element.193.refs_2_), channel_id=1, source_target_pairs={{0,2},{2,0},{4,6},{6,4},{1,3},{3,1},{5,7},{7,5},{8,10},{10,8},{12,... | collective-permute-start | bytes 835592 | tf_op jit(solution)/shard_map/ppermute | solution.py:543
  175.0 4.2 %collective-permute-start.55 = (f32[128,512]{1,0:T(8,128)S(1)}, f32[128,512]{1,0:T(8,128)S(1)}, u32[]{:S(2)}, u32[]{:S(2)}) collective-permute-start(f32[128,512]{1,0:T(8,128)S(1)} %get-tuple-element.194.refs_2_), channel_id=1, source_target_pairs={{0,2},{2,0},{4,6},{6,4},{1,3},{3,1},{5,7},{7,5},{8,10},{10,8},{12,... | collective-permute-start | bytes 786440 | tf_op jit(solution)/shard_map/ppermute | solution.py:543
  180.9 3.8 %collective-permute-start.54 = (f32[128,512]{1,0:T(8,128)S(1)}, f32[128,512]{1,0:T(8,128)S(1)}, u32[]{:S(2)}, u32[]{:S(2)}) collective-permute-start(f32[128,512]{1,0:T(8,128)S(1)} %get-tuple-element.195.refs_5_), channel_id=1, source_target_pairs={{0,2},{2,0},{4,6},{6,4},{1,3},{3,1},{5,7},{7,5},{8,10},{10,8},{12,... | collective-permute-start | bytes 786440 | tf_op jit(solution)/shard_map/ppermute | solution.py:543
  190.6 5.8 %collective-permute-start.61 = (f32[128,512]{1,0:T(8,128)S(1)}, f32[128,512]{1,0:T(8,128)S(1)}, u32[]{:S(2)}, u32[]{:S(2)}) collective-permute-start(f32[128,512]{1,0:T(8,128)S(1)} %shard_map.228.refs_7_.refs_3_), channel_id=1, source_target_pairs={{0,2},{2,0},{4,6},{6,4},{1,3},{3,1},{5,7},{7,5},{8,10},{10,8},{12,... | collective-permute-start | bytes 786440 | tf_op jit(solution)/shard_map/ppermute | solution.py:543
  196.8 2.4 collective-permute-done.58.refs_2_
  201.0 3.7 %collective-permute-done.61.refs_2_ = f32[128,512]{1,0:T(8,128)S(1)} collective-permute-done((f32[128,512]{1,0:T(8,128)S(1)}, f32[128,512]{1,0:T(8,128)S(1)}, u32[]{:S(2)}, u32[]{:S(2)}) %collective-permute-start.61) | collective-permute-done | bytes 262176 | tf_op jit(solution)/shard_map/ppermute | solution.py:543
  205.1 3.2 %collective-permute-done.60.refs_2_ = f32[128,512]{1,0:T(8,128)S(1)} collective-permute-done((f32[128,512]{1,0:T(8,128)S(1)}, f32[128,512]{1,0:T(8,128)S(1)}, u32[]{:S(2)}, u32[]{:S(2)}) %collective-permute-start.60) | collective-permute-done | bytes 262176 | tf_op jit(solution)/shard_map/ppermute | solution.py:543
  216.7 2.4 collective-permute-done.65.refs_3_
  223.3 2.1 collective-permute-start.70
  225.4 6.0 %collective-permute-done.68.refs_1_ = f32[136,512]{1,0:T(8,128)S(1)} collective-permute-done((f32[136,512]{1,0:T(8,128)S(1)}, f32[136,512]{1,0:T(8,128)S(1)}, u32[]{:S(2)}, u32[]{:S(2)}) %collective-permute-start.68) | collective-permute-done | bytes 278560 | tf_op jit(solution)/shard_map/ppermute | solution.py:543
  231.5 3.5 %collective-permute-start.67 = (f32[128,512]{1,0:T(8,128)S(1)}, f32[128,512]{1,0:T(8,128)S(1)}, u32[]{:S(2)}, u32[]{:S(2)}) collective-permute-start(f32[128,512]{1,0:T(8,128)S(1)} %shard_map.237.refs_3_.refs_0_), channel_id=1, source_target_pairs={{0,2},{6,4},{1,3},{7,5},{8,10},{14,12},{9,11},{15,13},{16,18},{22,... | collective-permute-start | bytes 786440 | tf_op jit(solution)/shard_map/ppermute | solution.py:546
  236.4 3.2 %collective-permute-start.72 = (f32[136,512]{1,0:T(8,128)S(1)}, f32[136,512]{1,0:T(8,128)S(1)}, u32[]{:S(2)}, u32[]{:S(2)}) collective-permute-start(f32[136,512]{1,0:T(8,128)S(1)} %get-tuple-element.218.refs_2_), channel_id=1, source_target_pairs={{0,2},{2,0},{4,6},{6,4},{1,3},{3,1},{5,7},{7,5},{8,10},{10,8},{12,... | collective-permute-start | bytes 835592 | tf_op jit(solution)/shard_map/ppermute | solution.py:543
  239.5 2.0 collective-permute-done.67.refs_1_
  241.8 4.5 %collective-permute-start.75 = (f32[128,512]{1,0:T(8,128)S(1)}, f32[128,512]{1,0:T(8,128)S(1)}, u32[]{:S(2)}, u32[]{:S(2)}) collective-permute-start(f32[128,512]{1,0:T(8,128)S(1)} %get-tuple-element.219.refs_2_), channel_id=1, source_target_pairs={{0,2},{2,0},{4,6},{6,4},{1,3},{3,1},{5,7},{7,5},{8,10},{10,8},{12,... | collective-permute-start | bytes 786440 | tf_op jit(solution)/shard_map/ppermute | solution.py:543
  247.5 4.3 %collective-permute-start.74 = (f32[128,512]{1,0:T(8,128)S(1)}, f32[128,512]{1,0:T(8,128)S(1)}, u32[]{:S(2)}, u32[]{:S(2)}) collective-permute-start(f32[128,512]{1,0:T(8,128)S(1)} %get-tuple-element.220.refs_5_), channel_id=1, source_target_pairs={{0,2},{2,0},{4,6},{6,4},{1,3},{3,1},{5,7},{7,5},{8,10},{10,8},{12,... | collective-permute-start | bytes 786440 | tf_op jit(solution)/shard_map/ppermute | solution.py:543
  257.0 6.4 %collective-permute-start.81 = (f32[128,512]{1,0:T(8,128)S(1)}, f32[128,512]{1,0:T(8,128)S(1)}, u32[]{:S(2)}, u32[]{:S(2)}) collective-permute-start(f32[128,512]{1,0:T(8,128)S(1)} %shard_map.254.refs_7_.refs_3_), channel_id=1, source_target_pairs={{0,2},{2,0},{4,6},{6,4},{1,3},{3,1},{5,7},{7,5},{8,10},{10,8},{12,... | collective-permute-start | bytes 786440 | tf_op jit(solution)/shard_map/ppermute | solution.py:543
  263.8 2.4 collective-permute-done.78.refs_2_
  267.6 3.7 %collective-permute-done.81.refs_2_ = f32[128,512]{1,0:T(8,128)S(1)} collective-permute-done((f32[128,512]{1,0:T(8,128)S(1)}, f32[128,512]{1,0:T(8,128)S(1)}, u32[]{:S(2)}, u32[]{:S(2)}) %collective-permute-start.81) | collective-permute-done | bytes 262176 | tf_op jit(solution)/shard_map/ppermute | solution.py:543
  271.7 3.2 %collective-permute-done.80.refs_2_ = f32[128,512]{1,0:T(8,128)S(1)} collective-permute-done((f32[128,512]{1,0:T(8,128)S(1)}, f32[128,512]{1,0:T(8,128)S(1)}, u32[]{:S(2)}, u32[]{:S(2)}) %collective-permute-start.80) | collective-permute-done | bytes 262176 | tf_op jit(solution)/shard_map/ppermute | solution.py:543
  278.9 2.2 collective-permute-start.85
  (288 shorter events, 108.3 us)
Async XLA Ops:
  6.3 11.6 %collective-permute-start.3 = (f32[384,512]{1,0:T(8,128)}, f32[384,512]{1,0:T(8,128)}, u32[]{:S(2)}, u32[]{:S(2)}) collective-permute-start(f32[384,512]{1,0:T(8,128)} %get-tuple-element.129), channel_id=1, source_target_pairs={{0,1},{1,0},{2,3},{3,2},{4,5},{5,4},{6,7},{7,6},{8,9},{9,8},{10,11... | collective-permute-start | bytes 2359304 | tf_op jit(solution)/shard_map/ppermute | solution.py:518
  6.8 17.1 %collective-permute-start.2 = (f32[384,512]{1,0:T(8,128)}, f32[384,512]{1,0:T(8,128)}, u32[]{:S(2)}, u32[]{:S(2)}) collective-permute-start(f32[384,512]{1,0:T(8,128)} %get-tuple-element.127), channel_id=1, source_target_pairs={{0,1},{1,0},{2,3},{3,2},{4,5},{5,4},{6,7},{7,6},{8,9},{9,8},{10,11... | collective-permute-start | bytes 2359304 | tf_op jit(solution)/shard_map/ppermute | solution.py:518
  6.9 20.4 %collective-permute-start.7 = (f32[384,512]{1,0:T(8,128)}, f32[384,512]{1,0:T(8,128)}, u32[]{:S(2)}, u32[]{:S(2)}) collective-permute-start(f32[384,512]{1,0:T(8,128)} %get-tuple-element.135), channel_id=1, source_target_pairs={{0,1},{1,0},{2,3},{3,2},{4,5},{5,4},{6,7},{7,6},{8,9},{9,8},{10,11... | collective-permute-start | bytes 2359304 | tf_op jit(solution)/shard_map/ppermute | solution.py:518
  16.1 14.9 %collective-permute-start.5 = (f32[384,512]{1,0:T(8,128)}, f32[384,512]{1,0:T(8,128)}, u32[]{:S(2)}, u32[]{:S(2)}) collective-permute-start(f32[384,512]{1,0:T(8,128)} %get-tuple-element.133), channel_id=1, source_target_pairs={{0,1},{1,0},{2,3},{3,2},{4,5},{5,4},{6,7},{7,6},{8,9},{9,8},{10,11... | collective-permute-start | bytes 2359304 | tf_op jit(solution)/shard_map/ppermute | solution.py:518
  17.8 24.2 %collective-permute-start.9 = (f32[384,512]{1,0:T(8,128)}, f32[384,512]{1,0:T(8,128)}, u32[]{:S(2)}, u32[]{:S(2)}) collective-permute-start(f32[384,512]{1,0:T(8,128)} %copy-done.8), channel_id=1, source_target_pairs={{0,1},{1,0},{2,3},{3,2},{4,5},{5,4},{6,7},{7,6},{8,9},{9,8},{10,11... | collective-permute-start | bytes 2359304 | tf_op jit(solution)/shard_map/ppermute | solution.py:518
  20.7 10.0 %collective-permute-start.6 = (f32[136,512]{1,0:T(8,128)S(1)}, f32[136,512]{1,0:T(8,128)S(1)}, u32[]{:S(2)}, u32[]{:S(2)}) collective-permute-start(f32[136,512]{1,0:T(8,128)S(1)} %get-tuple-element.130.refs_4_.refs_0_), channel_id=1, source_target_pairs={{0,2},{2,0},{4,6},{6,4},{1,3},{3,1},{5,7},{7,5},{8,10},{10,8},{12,... | collective-permute-start | bytes 835592 | tf_op jit(solution)/shard_map/ppermute | solution.py:543
  24.0 23.5 %collective-permute-start.1 = (f32[384,512]{1,0:T(8,128)S(1)}, f32[384,512]{1,0:T(8,128)}, u32[]{:S(2)}, u32[]{:S(2)}) collective-permute-start(f32[384,512]{1,0:T(8,128)S(1)} %get-tuple-element.125), channel_id=1, source_target_pairs={{0,1},{1,0},{2,3},{3,2},{4,5},{5,4},{6,7},{7,6},{8,9},{9,8},{10,11... | collective-permute-start | bytes 2359304 | tf_op jit(solution)/shard_map/ppermute | solution.py:518
  27.3 10.8 %collective-permute-start.4 = (f32[128,512]{1,0:T(8,128)}, f32[128,512]{1,0:T(8,128)}, u32[]{:S(2)}, u32[]{:S(2)}) collective-permute-start(f32[128,512]{1,0:T(8,128)} %get-tuple-element.131.refs_4_.refs_0_), channel_id=1, source_target_pairs={{0,2},{2,0},{4,6},{6,4},{1,3},{3,1},{5,7},{7,5},{8,10},{10,8},{12,... | collective-permute-start | bytes 786440 | tf_op jit(solution)/shard_map/ppermute | solution.py:543
  30.9 8.3 %collective-permute-start.10 = (f32[136,512]{1,0:T(8,128)S(1)}, f32[136,512]{1,0:T(8,128)}, u32[]{:S(2)}, u32[]{:S(2)}) collective-permute-start(f32[136,512]{1,0:T(8,128)S(1)} %shard_map.161.refs_4_.refs_1_), channel_id=1, source_target_pairs={{2,4},{4,2},{3,5},{5,3},{0,1},{1,0},{6,7},{7,6},{10,12},{12,10},{1... | collective-permute-start | bytes 835592 | tf_op jit(solution)/shard_map/ppermute | solution.py:553
  31.1 12.7 %collective-permute-start.11 = (f32[128,512]{1,0:T(8,128)}, f32[128,512]{1,0:T(8,128)S(1)}, u32[]{:S(2)}, u32[]{:S(2)}) collective-permute-start(f32[128,512]{1,0:T(8,128)} %copy-done.19), channel_id=1, source_target_pairs={{0,2},{6,4},{1,3},{7,5},{8,10},{14,12},{9,11},{15,13},{16,18},{22,... | collective-permute-start | bytes 786440 | tf_op jit(solution)/shard_map/ppermute | solution.py:546
  40.3 9.5 %collective-permute-start.13 = (f32[136,512]{1,0:T(8,128)S(1)}, f32[136,512]{1,0:T(8,128)S(1)}, u32[]{:S(2)}, u32[]{:S(2)}) collective-permute-start(f32[136,512]{1,0:T(8,128)S(1)} %get-tuple-element.140.refs_4_), channel_id=1, source_target_pairs={{0,2},{2,0},{4,6},{6,4},{1,3},{3,1},{5,7},{7,5},{8,10},{10,8},{12,... | collective-permute-start | bytes 835592 | tf_op jit(solution)/shard_map/ppermute | solution.py:543
  43.8 6.2 %collective-permute-start.12 = (f32[128,512]{1,0:T(8,128)S(1)}, f32[128,512]{1,0:T(8,128)S(1)}, u32[]{:S(2)}, u32[]{:S(2)}) collective-permute-start(f32[128,512]{1,0:T(8,128)S(1)} %shard_map.166.refs_4_.refs_1_), channel_id=1, source_target_pairs={{2,4},{4,2},{3,5},{5,3},{0,1},{1,0},{6,7},{7,6},{10,12},{12,10},{1... | collective-permute-start | bytes 786440 | tf_op jit(solution)/shard_map/ppermute | solution.py:553
  44.0 11.5 %collective-permute-start.15 = (f32[128,512]{1,0:T(8,128)S(1)}, f32[128,512]{1,0:T(8,128)S(1)}, u32[]{:S(2)}, u32[]{:S(2)}) collective-permute-start(f32[128,512]{1,0:T(8,128)S(1)} %get-tuple-element.142.refs_4_), channel_id=1, source_target_pairs={{0,2},{2,0},{4,6},{6,4},{1,3},{3,1},{5,7},{7,5},{8,10},{10,8},{12,... | collective-permute-start | bytes 786440 | tf_op jit(solution)/shard_map/ppermute | solution.py:543
  50.1 10.6 %collective-permute-start.14 = (f32[128,512]{1,0:T(8,128)S(1)}, f32[128,512]{1,0:T(8,128)S(1)}, u32[]{:S(2)}, u32[]{:S(2)}) collective-permute-start(f32[128,512]{1,0:T(8,128)S(1)} %get-tuple-element.144.refs_6_), channel_id=1, source_target_pairs={{0,2},{2,0},{4,6},{6,4},{1,3},{3,1},{5,7},{7,5},{8,10},{10,8},{12,... | collective-permute-start | bytes 786440 | tf_op jit(solution)/shard_map/ppermute | solution.py:543
  55.6 12.5 %collective-permute-start.18 = (f32[128,512]{1,0:T(8,128)S(1)}, f32[128,512]{1,0:T(8,128)S(1)}, u32[]{:S(2)}, u32[]{:S(2)}) collective-permute-start(f32[128,512]{1,0:T(8,128)S(1)} %shard_map.173.refs_8_.refs_3_), channel_id=1, source_target_pairs={{2,0},{4,6},{3,1},{5,7},{10,8},{12,14},{11,9},{13,15},{18,16},{20,... | collective-permute-start | bytes 786440 | tf_op jit(solution)/shard_map/ppermute | solution.py:549
  60.7 7.8 %collective-permute-start.17 = (f32[128,512]{1,0:T(8,128)S(1)}, f32[128,512]{1,0:T(8,128)S(1)}, u32[]{:S(2)}, u32[]{:S(2)}) collective-permute-start(f32[128,512]{1,0:T(8,128)S(1)} %shard_map.175.refs_2_.refs_0_), channel_id=1, source_target_pairs={{2,4},{4,2},{3,5},{5,3},{0,1},{1,0},{6,7},{7,6},{10,12},{12,10},{1... | collective-permute-start | bytes 786440 | tf_op jit(solution)/shard_map/ppermute | solution.py:553
  60.9 12.9 %collective-permute-start.21 = (f32[128,512]{1,0:T(8,128)S(1)}, f32[128,512]{1,0:T(8,128)S(1)}, u32[]{:S(2)}, u32[]{:S(2)}) collective-permute-start(f32[128,512]{1,0:T(8,128)S(1)} %shard_map.176.refs_8_.refs_3_), channel_id=1, source_target_pairs={{0,2},{2,0},{4,6},{6,4},{1,3},{3,1},{5,7},{7,5},{8,10},{10,8},{12,... | collective-permute-start | bytes 786440 | tf_op jit(solution)/shard_map/ppermute | solution.py:543
  68.6 9.0 %collective-permute-start.20 = (f32[128,512]{1,0:T(8,128)S(1)}, f32[128,512]{1,0:T(8,128)S(1)}, u32[]{:S(2)}, u32[]{:S(2)}) collective-permute-start(f32[128,512]{1,0:T(8,128)S(1)} %shard_map.179.refs_8_.refs_3_), channel_id=1, source_target_pairs={{0,2},{2,0},{4,6},{6,4},{1,3},{3,1},{5,7},{7,5},{8,10},{10,8},{12,... | collective-permute-start | bytes 786440 | tf_op jit(solution)/shard_map/ppermute | solution.py:543
  90.9 9.6 %collective-permute-start.28 = (f32[136,512]{1,0:T(8,128)S(1)}, f32[136,512]{1,0:T(8,128)S(1)}, u32[]{:S(2)}, u32[]{:S(2)}) collective-permute-start(f32[136,512]{1,0:T(8,128)S(1)} %shard_map.184.refs_3_.refs_0_), channel_id=1, source_target_pairs={{0,2},{2,0},{4,6},{6,4},{1,3},{3,1},{5,7},{7,5},{8,10},{10,8},{12,... | collective-permute-start | bytes 835592 | tf_op jit(solution)/shard_map/ppermute | solution.py:543
  92.4 12.9 %collective-permute-start.30 = (f32[128,512]{1,0:T(8,128)S(1)}, f32[128,512]{1,0:T(8,128)S(1)}, u32[]{:S(2)}, u32[]{:S(2)}) collective-permute-start(f32[128,512]{1,0:T(8,128)S(1)} %shard_map.189.refs_2_.refs_0_), channel_id=1, source_target_pairs={{0,2},{2,0},{4,6},{6,4},{1,3},{3,1},{5,7},{7,5},{8,10},{10,8},{12,... | collective-permute-start | bytes 786440 | tf_op jit(solution)/shard_map/ppermute | solution.py:543
  100.6 10.1 %collective-permute-start.27 = (f32[128,512]{1,0:T(8,128)S(1)}, f32[128,512]{1,0:T(8,128)S(1)}, u32[]{:S(2)}, u32[]{:S(2)}) collective-permute-start(f32[128,512]{1,0:T(8,128)S(1)} %shard_map.185.refs_3_.refs_0_), channel_id=1, source_target_pairs={{0,2},{6,4},{1,3},{7,5},{8,10},{14,12},{9,11},{15,13},{16,18},{22,... | collective-permute-start | bytes 786440 | tf_op jit(solution)/shard_map/ppermute | solution.py:546
  105.5 10.9 %collective-permute-start.32 = (f32[136,512]{1,0:T(8,128)S(1)}, f32[136,512]{1,0:T(8,128)S(1)}, u32[]{:S(2)}, u32[]{:S(2)}) collective-permute-start(f32[136,512]{1,0:T(8,128)S(1)} %get-tuple-element.172.refs_2_), channel_id=1, source_target_pairs={{0,2},{2,0},{4,6},{6,4},{1,3},{3,1},{5,7},{7,5},{8,10},{10,8},{12,... | collective-permute-start | bytes 835592 | tf_op jit(solution)/shard_map/ppermute | solution.py:543
  110.9 11.1 %collective-permute-start.35 = (f32[128,512]{1,0:T(8,128)S(1)}, f32[128,512]{1,0:T(8,128)S(1)}, u32[]{:S(2)}, u32[]{:S(2)}) collective-permute-start(f32[128,512]{1,0:T(8,128)S(1)} %get-tuple-element.173.refs_2_), channel_id=1, source_target_pairs={{0,2},{2,0},{4,6},{6,4},{1,3},{3,1},{5,7},{7,5},{8,10},{10,8},{12,... | collective-permute-start | bytes 786440 | tf_op jit(solution)/shard_map/ppermute | solution.py:543
  116.6 9.4 %collective-permute-start.34 = (f32[128,512]{1,0:T(8,128)S(1)}, f32[128,512]{1,0:T(8,128)S(1)}, u32[]{:S(2)}, u32[]{:S(2)}) collective-permute-start(f32[128,512]{1,0:T(8,128)S(1)} %get-tuple-element.174.refs_5_), channel_id=1, source_target_pairs={{0,2},{2,0},{4,6},{6,4},{1,3},{3,1},{5,7},{7,5},{8,10},{10,8},{12,... | collective-permute-start | bytes 786440 | tf_op jit(solution)/shard_map/ppermute | solution.py:543
  122.1 12.9 %collective-permute-start.38 = (f32[128,512]{1,0:T(8,128)S(1)}, f32[128,512]{1,0:T(8,128)S(1)}, u32[]{:S(2)}, u32[]{:S(2)}) collective-permute-start(f32[128,512]{1,0:T(8,128)S(1)} %shard_map.199.refs_7_.refs_3_), channel_id=1, source_target_pairs={{2,0},{4,6},{3,1},{5,7},{10,8},{12,14},{11,9},{13,15},{18,16},{20,... | collective-permute-start | bytes 786440 | tf_op jit(solution)/shard_map/ppermute | solution.py:549
  126.0 9.4 %collective-permute-start.37 = (f32[128,512]{1,0:T(8,128)S(1)}, f32[128,512]{1,0:T(8,128)S(1)}, u32[]{:S(2)}, u32[]{:S(2)}) collective-permute-start(f32[128,512]{1,0:T(8,128)S(1)} %shard_map.201.refs_2_.refs_0_), channel_id=1, source_target_pairs={{2,4},{4,2},{3,5},{5,3},{0,1},{1,0},{6,7},{7,6},{10,12},{12,10},{1... | collective-permute-start | bytes 786440 | tf_op jit(solution)/shard_map/ppermute | solution.py:553
  126.1 14.1 %collective-permute-start.41 = (f32[128,512]{1,0:T(8,128)S(1)}, f32[128,512]{1,0:T(8,128)S(1)}, u32[]{:S(2)}, u32[]{:S(2)}) collective-permute-start(f32[128,512]{1,0:T(8,128)S(1)} %shard_map.202.refs_7_.refs_3_), channel_id=1, source_target_pairs={{0,2},{2,0},{4,6},{6,4},{1,3},{3,1},{5,7},{7,5},{8,10},{10,8},{12,... | collective-permute-start | bytes 786440 | tf_op jit(solution)/shard_map/ppermute | solution.py:543
  135.5 8.5 %collective-permute-start.40 = (f32[128,512]{1,0:T(8,128)S(1)}, f32[128,512]{1,0:T(8,128)S(1)}, u32[]{:S(2)}, u32[]{:S(2)}) collective-permute-start(f32[128,512]{1,0:T(8,128)S(1)} %shard_map.205.refs_7_.refs_3_), channel_id=1, source_target_pairs={{0,2},{2,0},{4,6},{6,4},{1,3},{3,1},{5,7},{7,5},{8,10},{10,8},{12,... | collective-permute-start | bytes 786440 | tf_op jit(solution)/shard_map/ppermute | solution.py:543
  155.4 9.6 %collective-permute-start.48 = (f32[136,512]{1,0:T(8,128)S(1)}, f32[136,512]{1,0:T(8,128)S(1)}, u32[]{:S(2)}, u32[]{:S(2)}) collective-permute-start(f32[136,512]{1,0:T(8,128)S(1)} %shard_map.210.refs_3_.refs_0_), channel_id=1, source_target_pairs={{0,2},{2,0},{4,6},{6,4},{1,3},{3,1},{5,7},{7,5},{8,10},{10,8},{12,... | collective-permute-start | bytes 835592 | tf_op jit(solution)/shard_map/ppermute | solution.py:543
  157.2 12.6 %collective-permute-start.50 = (f32[128,512]{1,0:T(8,128)S(1)}, f32[128,512]{1,0:T(8,128)S(1)}, u32[]{:S(2)}, u32[]{:S(2)}) collective-permute-start(f32[128,512]{1,0:T(8,128)S(1)} %shard_map.215.refs_2_.refs_0_), channel_id=1, source_target_pairs={{0,2},{2,0},{4,6},{6,4},{1,3},{3,1},{5,7},{7,5},{8,10},{10,8},{12,... | collective-permute-start | bytes 786440 | tf_op jit(solution)/shard_map/ppermute | solution.py:543
  165.1 9.7 %collective-permute-start.47 = (f32[128,512]{1,0:T(8,128)S(1)}, f32[128,512]{1,0:T(8,128)S(1)}, u32[]{:S(2)}, u32[]{:S(2)}) collective-permute-start(f32[128,512]{1,0:T(8,128)S(1)} %shard_map.211.refs_3_.refs_0_), channel_id=1, source_target_pairs={{0,2},{6,4},{1,3},{7,5},{8,10},{14,12},{9,11},{15,13},{16,18},{22,... | collective-permute-start | bytes 786440 | tf_op jit(solution)/shard_map/ppermute | solution.py:546
  170.0 10.7 %collective-permute-start.52 = (f32[136,512]{1,0:T(8,128)S(1)}, f32[136,512]{1,0:T(8,128)S(1)}, u32[]{:S(2)}, u32[]{:S(2)}) collective-permute-start(f32[136,512]{1,0:T(8,128)S(1)} %get-tuple-element.193.refs_2_), channel_id=1, source_target_pairs={{0,2},{2,0},{4,6},{6,4},{1,3},{3,1},{5,7},{7,5},{8,10},{10,8},{12,... | collective-permute-start | bytes 835592 | tf_op jit(solution)/shard_map/ppermute | solution.py:543
  175.0 11.4 %collective-permute-start.55 = (f32[128,512]{1,0:T(8,128)S(1)}, f32[128,512]{1,0:T(8,128)S(1)}, u32[]{:S(2)}, u32[]{:S(2)}) collective-permute-start(f32[128,512]{1,0:T(8,128)S(1)} %get-tuple-element.194.refs_2_), channel_id=1, source_target_pairs={{0,2},{2,0},{4,6},{6,4},{1,3},{3,1},{5,7},{7,5},{8,10},{10,8},{12,... | collective-permute-start | bytes 786440 | tf_op jit(solution)/shard_map/ppermute | solution.py:543
  180.9 9.5 %collective-permute-start.54 = (f32[128,512]{1,0:T(8,128)S(1)}, f32[128,512]{1,0:T(8,128)S(1)}, u32[]{:S(2)}, u32[]{:S(2)}) collective-permute-start(f32[128,512]{1,0:T(8,128)S(1)} %get-tuple-element.195.refs_5_), channel_id=1, source_target_pairs={{0,2},{2,0},{4,6},{6,4},{1,3},{3,1},{5,7},{7,5},{8,10},{10,8},{12,... | collective-permute-start | bytes 786440 | tf_op jit(solution)/shard_map/ppermute | solution.py:543
  186.5 12.7 %collective-permute-start.58 = (f32[128,512]{1,0:T(8,128)S(1)}, f32[128,512]{1,0:T(8,128)S(1)}, u32[]{:S(2)}, u32[]{:S(2)}) collective-permute-start(f32[128,512]{1,0:T(8,128)S(1)} %shard_map.225.refs_7_.refs_3_), channel_id=1, source_target_pairs={{2,0},{4,6},{3,1},{5,7},{10,8},{12,14},{11,9},{13,15},{18,16},{20,... | collective-permute-start | bytes 786440 | tf_op jit(solution)/shard_map/ppermute | solution.py:549
  190.5 9.2 %collective-permute-start.57 = (f32[128,512]{1,0:T(8,128)S(1)}, f32[128,512]{1,0:T(8,128)S(1)}, u32[]{:S(2)}, u32[]{:S(2)}) collective-permute-start(f32[128,512]{1,0:T(8,128)S(1)} %shard_map.227.refs_2_.refs_0_), channel_id=1, source_target_pairs={{2,4},{4,2},{3,5},{5,3},{0,1},{1,0},{6,7},{7,6},{10,12},{12,10},{1... | collective-permute-start | bytes 786440 | tf_op jit(solution)/shard_map/ppermute | solution.py:553
  190.6 14.1 %collective-permute-start.61 = (f32[128,512]{1,0:T(8,128)S(1)}, f32[128,512]{1,0:T(8,128)S(1)}, u32[]{:S(2)}, u32[]{:S(2)}) collective-permute-start(f32[128,512]{1,0:T(8,128)S(1)} %shard_map.228.refs_7_.refs_3_), channel_id=1, source_target_pairs={{0,2},{2,0},{4,6},{6,4},{1,3},{3,1},{5,7},{7,5},{8,10},{10,8},{12,... | collective-permute-start | bytes 786440 | tf_op jit(solution)/shard_map/ppermute | solution.py:543
  199.7 8.7 %collective-permute-start.60 = (f32[128,512]{1,0:T(8,128)S(1)}, f32[128,512]{1,0:T(8,128)S(1)}, u32[]{:S(2)}, u32[]{:S(2)}) collective-permute-start(f32[128,512]{1,0:T(8,128)S(1)} %shard_map.231.refs_7_.refs_3_), channel_id=1, source_target_pairs={{0,2},{2,0},{4,6},{6,4},{1,3},{3,1},{5,7},{7,5},{8,10},{10,8},{12,... | collective-permute-start | bytes 786440 | tf_op jit(solution)/shard_map/ppermute | solution.py:543
  221.8 9.6 %collective-permute-start.68 = (f32[136,512]{1,0:T(8,128)S(1)}, f32[136,512]{1,0:T(8,128)S(1)}, u32[]{:S(2)}, u32[]{:S(2)}) collective-permute-start(f32[136,512]{1,0:T(8,128)S(1)} %shard_map.236.refs_3_.refs_0_), channel_id=1, source_target_pairs={{0,2},{2,0},{4,6},{6,4},{1,3},{3,1},{5,7},{7,5},{8,10},{10,8},{12,... | collective-permute-start | bytes 835592 | tf_op jit(solution)/shard_map/ppermute | solution.py:543
  223.3 12.9 %collective-permute-start.70 = (f32[128,512]{1,0:T(8,128)S(1)}, f32[128,512]{1,0:T(8,128)S(1)}, u32[]{:S(2)}, u32[]{:S(2)}) collective-permute-start(f32[128,512]{1,0:T(8,128)S(1)} %shard_map.241.refs_2_.refs_0_), channel_id=1, source_target_pairs={{0,2},{2,0},{4,6},{6,4},{1,3},{3,1},{5,7},{7,5},{8,10},{10,8},{12,... | collective-permute-start | bytes 786440 | tf_op jit(solution)/shard_map/ppermute | solution.py:543
  231.5 10.1 %collective-permute-start.67 = (f32[128,512]{1,0:T(8,128)S(1)}, f32[128,512]{1,0:T(8,128)S(1)}, u32[]{:S(2)}, u32[]{:S(2)}) collective-permute-start(f32[128,512]{1,0:T(8,128)S(1)} %shard_map.237.refs_3_.refs_0_), channel_id=1, source_target_pairs={{0,2},{6,4},{1,3},{7,5},{8,10},{14,12},{9,11},{15,13},{16,18},{22,... | collective-permute-start | bytes 786440 | tf_op jit(solution)/shard_map/ppermute | solution.py:546
  236.4 11.0 %collective-permute-start.72 = (f32[136,512]{1,0:T(8,128)S(1)}, f32[136,512]{1,0:T(8,128)S(1)}, u32[]{:S(2)}, u32[]{:S(2)}) collective-permute-start(f32[136,512]{1,0:T(8,128)S(1)} %get-tuple-element.218.refs_2_), channel_id=1, source_target_pairs={{0,2},{2,0},{4,6},{6,4},{1,3},{3,1},{5,7},{7,5},{8,10},{10,8},{12,... | collective-permute-start | bytes 835592 | tf_op jit(solution)/shard_map/ppermute | solution.py:543
  241.8 11.2 %collective-permute-start.75 = (f32[128,512]{1,0:T(8,128)S(1)}, f32[128,512]{1,0:T(8,128)S(1)}, u32[]{:S(2)}, u32[]{:S(2)}) collective-permute-start(f32[128,512]{1,0:T(8,128)S(1)} %get-tuple-element.219.refs_2_), channel_id=1, source_target_pairs={{0,2},{2,0},{4,6},{6,4},{1,3},{3,1},{5,7},{7,5},{8,10},{10,8},{12,... | collective-permute-start | bytes 786440 | tf_op jit(solution)/shard_map/ppermute | solution.py:543
  247.5 9.3 %collective-permute-start.74 = (f32[128,512]{1,0:T(8,128)S(1)}, f32[128,512]{1,0:T(8,128)S(1)}, u32[]{:S(2)}, u32[]{:S(2)}) collective-permute-start(f32[128,512]{1,0:T(8,128)S(1)} %get-tuple-element.220.refs_5_), channel_id=1, source_target_pairs={{0,2},{2,0},{4,6},{6,4},{1,3},{3,1},{5,7},{7,5},{8,10},{10,8},{12,... | collective-permute-start | bytes 786440 | tf_op jit(solution)/shard_map/ppermute | solution.py:543
  253.1 13.1 %collective-permute-start.78 = (f32[128,512]{1,0:T(8,128)S(1)}, f32[128,512]{1,0:T(8,128)S(1)}, u32[]{:S(2)}, u32[]{:S(2)}) collective-permute-start(f32[128,512]{1,0:T(8,128)S(1)} %shard_map.251.refs_7_.refs_3_), channel_id=1, source_target_pairs={{2,0},{4,6},{3,1},{5,7},{10,8},{12,14},{11,9},{13,15},{18,16},{20,... | collective-permute-start | bytes 786440 | tf_op jit(solution)/shard_map/ppermute | solution.py:549
  256.9 9.7 %collective-permute-start.77 = (f32[128,512]{1,0:T(8,128)S(1)}, f32[128,512]{1,0:T(8,128)S(1)}, u32[]{:S(2)}, u32[]{:S(2)}) collective-permute-start(f32[128,512]{1,0:T(8,128)S(1)} %shard_map.253.refs_2_.refs_0_), channel_id=1, source_target_pairs={{2,4},{4,2},{3,5},{5,3},{0,1},{1,0},{6,7},{7,6},{10,12},{12,10},{1... | collective-permute-start | bytes 786440 | tf_op jit(solution)/shard_map/ppermute | solution.py:553
  257.0 14.4 %collective-permute-start.81 = (f32[128,512]{1,0:T(8,128)S(1)}, f32[128,512]{1,0:T(8,128)S(1)}, u32[]{:S(2)}, u32[]{:S(2)}) collective-permute-start(f32[128,512]{1,0:T(8,128)S(1)} %shard_map.254.refs_7_.refs_3_), channel_id=1, source_target_pairs={{0,2},{2,0},{4,6},{6,4},{1,3},{3,1},{5,7},{7,5},{8,10},{10,8},{12,... | collective-permute-start | bytes 786440 | tf_op jit(solution)/shard_map/ppermute | solution.py:543
  266.6 8.3 %collective-permute-start.80 = (f32[128,512]{1,0:T(8,128)S(1)}, f32[128,512]{1,0:T(8,128)S(1)}, u32[]{:S(2)}, u32[]{:S(2)}) collective-permute-start(f32[128,512]{1,0:T(8,128)S(1)} %shard_map.257.refs_7_.refs_3_), channel_id=1, source_target_pairs={{0,2},{2,0},{4,6},{6,4},{1,3},{3,1},{5,7},{7,5},{8,10},{10,8},{12,... | collective-permute-start | bytes 786440 | tf_op jit(solution)/shard_map/ppermute | solution.py:543
  (66 other events, 286.7 us)

commit v9 on v8

--- a/solution.py
+++ b/solution.py
@@ -25,7 +25,7 @@
 SMEM = pl.BlockSpec(memory_space=pltpu.SMEM)
 LIMIT = 16 * 1024 * 1024
 STEP_COST = pl.CostEstimate(flops=10**9, bytes_accessed=10**7, transcendentals=0)
-STREAM_LIMIT = 50 * 1024 * 1024
+STREAM_LIMIT = 48 * 1024 * 1024
 
 
 def dot32(first, second):

time: 285 us -> 285 us (level)
  no operation moved by 1% of the time
where the time goes in v9:
time: 285 us
  starting transfers between devices  119 us (42%)
  waiting for transfers between devices  111 us (39%)
  Pallas kernels  46 us (16%)
  local copies, waits for them, and re-layouts  5.24 us (2%)
    ppermute x28, starting transfers between devices, outer_swap(): return lax.ppermute(part, 'chip', [(0, 1), (1, 0), (2, 3), (3, 2)])  80.6 us
    ppermute x28, waiting for transfers between devices, outer_swap(): return lax.ppermute(part, 'chip', [(0, 1), (1, 0), (2, 3), (3, 2)])  69.1 us
    pallas_call x96, Pallas kernels, call(): pl.pallas_call(body, in_specs=[SMEM] * len(scalars) + [VMEM] * len(ins) +...  29.4 us
    ppermute x4, starting transfers between devices, send_in(): return lax.ppermute(part, 'chip', [(0, 1), (3, 2)])  15.1 us
    ppermute x12, waiting for transfers between devices, data_terms(): lax.ppermute(part, 'dp', [(d, d ^ step) for d in range(n_dp)])  14.8 us
    ppermute x12, starting transfers between devices, data_terms(): lax.ppermute(part, 'dp', [(d, d ^ step) for d in range(n_dp)])  14 us
    ppermute x14, waiting for transfers between devices, swap(): return lax.ppermute(part, 'core', [(0, 1), (1, 0)])  11.4 us
    ppermute x4, waiting for transfers between devices, send_back(): return lax.ppermute(part, 'chip', [(1, 0), (2, 3)])  9.95 us
  transfers between devices with their start and end apart: 86, of which 54 were waited for; matrix products, arithmetic and copies ran while one was open for 0% of the time, Pallas kernels for 12%

profile of v9, /device:TPU:0, one launch (start us, length us, event | category | flops | bytes accessed | tf_op | source)
XLA Modules:
  0.0 284.8 jit_solution(3142070231864387789)
XLA Ops:
  0.6 2.3 copy-done
  3.0 2.5 shard_map.157
  8.1 7.8 %shard_map.156 = (f32[3,128,128]{2,1,0:T(8,128)S(1)}, bf16[128,384]{1,0:T(8,128)(2,1)S(1)}, bf16[128,384]{1,0:T(8,128)(2,1)S(1)}, f32[128,16]{1,0:T(8,128)S(1)},...) custom-call(s32[1]{0:T(128)S(6)} %copy.17.limit_ref.refs_1_.refs_4_.refs_6_.refs_10_, bf16[128,6144]{1,0:T(8,128)(2,1)S(1)} %copy-done.1, ...), custom_call_target="tpu_custom_call" | custom-call | flops 1811939328 | bytes 14155776 | tf_op jit(solution)/shard_map/pallas_call | solution.py:188
  20.7 3.0 %collective-permute-start.6 = (f32[136,512]{1,0:T(8,128)S(1)}, f32[136,512]{1,0:T(8,128)S(1)}, u32[]{:S(2)}, u32[]{:S(2)}) collective-permute-start(f32[136,512]{1,0:T(8,128)S(1)} %get-tuple-element.130.refs_4_.refs_0_), channel_id=1, source_target_pairs={{0,2},{2,0},{4,6},{6,4},{1,3},{3,1},{5,7},{7,5},{8,10},{10,8},{12,... | collective-permute-start | bytes 835592 | tf_op jit(solution)/shard_map/ppermute | solution.py:543
  24.0 2.4 shard_map.159
  31.1 5.4 %collective-permute-start.11 = (f32[128,512]{1,0:T(8,128)}, f32[128,512]{1,0:T(8,128)S(1)}, u32[]{:S(2)}, u32[]{:S(2)}) collective-permute-start(f32[128,512]{1,0:T(8,128)} %copy-done.19), channel_id=1, source_target_pairs={{0,2},{6,4},{1,3},{7,5},{8,10},{14,12},{9,11},{15,13},{16,18},{22,... | collective-permute-start | bytes 786440 | tf_op jit(solution)/shard_map/ppermute | solution.py:546
  44.0 3.5 %collective-permute-start.15 = (f32[128,512]{1,0:T(8,128)S(1)}, f32[128,512]{1,0:T(8,128)S(1)}, u32[]{:S(2)}, u32[]{:S(2)}) collective-permute-start(f32[128,512]{1,0:T(8,128)S(1)} %get-tuple-element.142.refs_4_), channel_id=1, source_target_pairs={{0,2},{2,0},{4,6},{6,4},{1,3},{3,1},{5,7},{7,5},{8,10},{10,8},{12,... | collective-permute-start | bytes 786440 | tf_op jit(solution)/shard_map/ppermute | solution.py:543
  50.1 3.5 %collective-permute-start.14 = (f32[128,512]{1,0:T(8,128)S(1)}, f32[128,512]{1,0:T(8,128)S(1)}, u32[]{:S(2)}, u32[]{:S(2)}) collective-permute-start(f32[128,512]{1,0:T(8,128)S(1)} %get-tuple-element.144.refs_6_), channel_id=1, source_target_pairs={{0,2},{2,0},{4,6},{6,4},{1,3},{3,1},{5,7},{7,5},{8,10},{10,8},{12,... | collective-permute-start | bytes 786440 | tf_op jit(solution)/shard_map/ppermute | solution.py:543
  57.7 3.0 %collective-permute-done.14.refs_1_.refs_2_ = f32[128,512]{1,0:T(8,128)S(1)} collective-permute-done((f32[128,512]{1,0:T(8,128)S(1)}, f32[128,512]{1,0:T(8,128)S(1)}, u32[]{:S(2)}, u32[]{:S(2)}) %collective-permute-start.14) | collective-permute-done | bytes 262176 | tf_op jit(solution)/shard_map/ppermute | solution.py:543
  60.9 4.2 %collective-permute-start.21 = (f32[128,512]{1,0:T(8,128)S(1)}, f32[128,512]{1,0:T(8,128)S(1)}, u32[]{:S(2)}, u32[]{:S(2)}) collective-permute-start(f32[128,512]{1,0:T(8,128)S(1)} %shard_map.176.refs_8_.refs_3_), channel_id=1, source_target_pairs={{0,2},{2,0},{4,6},{6,4},{1,3},{3,1},{5,7},{7,5},{8,10},{10,8},{12,... | collective-permute-start | bytes 786440 | tf_op jit(solution)/shard_map/ppermute | solution.py:543
  65.5 2.7 collective-permute-done.18.refs_2_
  69.8 4.0 %collective-permute-done.21.refs_2_ = f32[128,512]{1,0:T(8,128)S(1)} collective-permute-done((f32[128,512]{1,0:T(8,128)S(1)}, f32[128,512]{1,0:T(8,128)S(1)}, u32[]{:S(2)}, u32[]{:S(2)}) %collective-permute-start.21) | collective-permute-done | bytes 262176 | tf_op jit(solution)/shard_map/ppermute | solution.py:543
  74.1 3.4 %collective-permute-done.20.refs_2_ = f32[128,512]{1,0:T(8,128)S(1)} collective-permute-done((f32[128,512]{1,0:T(8,128)S(1)}, f32[128,512]{1,0:T(8,128)S(1)}, u32[]{:S(2)}, u32[]{:S(2)}) %collective-permute-start.20) | collective-permute-done | bytes 262176 | tf_op jit(solution)/shard_map/ppermute | solution.py:543
  85.9 2.4 collective-permute-done.25.refs_3_
  92.4 2.1 collective-permute-start.30
  94.5 6.0 %collective-permute-done.28.refs_1_ = f32[136,512]{1,0:T(8,128)S(1)} collective-permute-done((f32[136,512]{1,0:T(8,128)S(1)}, f32[136,512]{1,0:T(8,128)S(1)}, u32[]{:S(2)}, u32[]{:S(2)}) %collective-permute-start.28) | collective-permute-done | bytes 278560 | tf_op jit(solution)/shard_map/ppermute | solution.py:543
  100.6 3.3 %collective-permute-start.27 = (f32[128,512]{1,0:T(8,128)S(1)}, f32[128,512]{1,0:T(8,128)S(1)}, u32[]{:S(2)}, u32[]{:S(2)}) collective-permute-start(f32[128,512]{1,0:T(8,128)S(1)} %shard_map.185.refs_3_.refs_0_), channel_id=1, source_target_pairs={{0,2},{6,4},{1,3},{7,5},{8,10},{14,12},{9,11},{15,13},{16,18},{22,... | collective-permute-start | bytes 786440 | tf_op jit(solution)/shard_map/ppermute | solution.py:546
  105.5 3.2 %collective-permute-start.32 = (f32[136,512]{1,0:T(8,128)S(1)}, f32[136,512]{1,0:T(8,128)S(1)}, u32[]{:S(2)}, u32[]{:S(2)}) collective-permute-start(f32[136,512]{1,0:T(8,128)S(1)} %get-tuple-element.172.refs_2_), channel_id=1, source_target_pairs={{0,2},{2,0},{4,6},{6,4},{1,3},{3,1},{5,7},{7,5},{8,10},{10,8},{12,... | collective-permute-start | bytes 835592 | tf_op jit(solution)/shard_map/ppermute | solution.py:543
  110.9 4.2 %collective-permute-start.35 = (f32[128,512]{1,0:T(8,128)S(1)}, f32[128,512]{1,0:T(8,128)S(1)}, u32[]{:S(2)}, u32[]{:S(2)}) collective-permute-start(f32[128,512]{1,0:T(8,128)S(1)} %get-tuple-element.173.refs_2_), channel_id=1, source_target_pairs={{0,2},{2,0},{4,6},{6,4},{1,3},{3,1},{5,7},{7,5},{8,10},{10,8},{12,... | collective-permute-start | bytes 786440 | tf_op jit(solution)/shard_map/ppermute | solution.py:543
  116.6 4.1 %collective-permute-start.34 = (f32[128,512]{1,0:T(8,128)S(1)}, f32[128,512]{1,0:T(8,128)S(1)}, u32[]{:S(2)}, u32[]{:S(2)}) collective-permute-start(f32[128,512]{1,0:T(8,128)S(1)} %get-tuple-element.174.refs_5_), channel_id=1, source_target_pairs={{0,2},{2,0},{4,6},{6,4},{1,3},{3,1},{5,7},{7,5},{8,10},{10,8},{12,... | collective-permute-start | bytes 786440 | tf_op jit(solution)/shard_map/ppermute | solution.py:543
  123.8 2.1 collective-permute-done.34.refs_1_.refs_2_
  126.1 6.1 %collective-permute-start.41 = (f32[128,512]{1,0:T(8,128)S(1)}, f32[128,512]{1,0:T(8,128)S(1)}, u32[]{:S(2)}, u32[]{:S(2)}) collective-permute-start(f32[128,512]{1,0:T(8,128)S(1)} %shard_map.202.refs_7_.refs_3_), channel_id=1, source_target_pairs={{0,2},{2,0},{4,6},{6,4},{1,3},{3,1},{5,7},{7,5},{8,10},{10,8},{12,... | collective-permute-start | bytes 786440 | tf_op jit(solution)/shard_map/ppermute | solution.py:543
  132.6 2.4 collective-permute-done.38.refs_2_
  136.7 3.5 %collective-permute-done.41.refs_2_ = f32[128,512]{1,0:T(8,128)S(1)} collective-permute-done((f32[128,512]{1,0:T(8,128)S(1)}, f32[128,512]{1,0:T(8,128)S(1)}, u32[]{:S(2)}, u32[]{:S(2)}) %collective-permute-start.41) | collective-permute-done | bytes 262176 | tf_op jit(solution)/shard_map/ppermute | solution.py:543
  140.6 3.4 %collective-permute-done.40.refs_2_ = f32[128,512]{1,0:T(8,128)S(1)} collective-permute-done((f32[128,512]{1,0:T(8,128)S(1)}, f32[128,512]{1,0:T(8,128)S(1)}, u32[]{:S(2)}, u32[]{:S(2)}) %collective-permute-start.40) | collective-permute-done | bytes 262176 | tf_op jit(solution)/shard_map/ppermute | solution.py:543
  147.7 2.4 collective-permute-start.45
  159.0 6.0 %collective-permute-done.48.refs_1_ = f32[136,512]{1,0:T(8,128)S(1)} collective-permute-done((f32[136,512]{1,0:T(8,128)S(1)}, f32[136,512]{1,0:T(8,128)S(1)}, u32[]{:S(2)}, u32[]{:S(2)}) %collective-permute-start.48) | collective-permute-done | bytes 278560 | tf_op jit(solution)/shard_map/ppermute | solution.py:543
  165.1 2.9 %collective-permute-start.47 = (f32[128,512]{1,0:T(8,128)S(1)}, f32[128,512]{1,0:T(8,128)S(1)}, u32[]{:S(2)}, u32[]{:S(2)}) collective-permute-start(f32[128,512]{1,0:T(8,128)S(1)} %shard_map.211.refs_3_.refs_0_), channel_id=1, source_target_pairs={{0,2},{6,4},{1,3},{7,5},{8,10},{14,12},{9,11},{15,13},{16,18},{22,... | collective-permute-start | bytes 786440 | tf_op jit(solution)/shard_map/ppermute | solution.py:546
  170.0 2.8 %collective-permute-start.52 = (f32[136,512]{1,0:T(8,128)S(1)}, f32[136,512]{1,0:T(8,128)S(1)}, u32[]{:S(2)}, u32[]{:S(2)}) collective-permute-start(f32[136,512]{1,0:T(8,128)S(1)} %get-tuple-element.193.refs_2_), channel_id=1, source_target_pairs={{0,2},{2,0},{4,6},{6,4},{1,3},{3,1},{5,7},{7,5},{8,10},{10,8},{12,... | collective-permute-start | bytes 835592 | tf_op jit(solution)/shard_map/ppermute | solution.py:543
  175.0 4.2 %collective-permute-start.55 = (f32[128,512]{1,0:T(8,128)S(1)}, f32[128,512]{1,0:T(8,128)S(1)}, u32[]{:S(2)}, u32[]{:S(2)}) collective-permute-start(f32[128,512]{1,0:T(8,128)S(1)} %get-tuple-element.194.refs_2_), channel_id=1, source_target_pairs={{0,2},{2,0},{4,6},{6,4},{1,3},{3,1},{5,7},{7,5},{8,10},{10,8},{12,... | collective-permute-start | bytes 786440 | tf_op jit(solution)/shard_map/ppermute | solution.py:543
  180.9 3.8 %collective-permute-start.54 = (f32[128,512]{1,0:T(8,128)S(1)}, f32[128,512]{1,0:T(8,128)S(1)}, u32[]{:S(2)}, u32[]{:S(2)}) collective-permute-start(f32[128,512]{1,0:T(8,128)S(1)} %get-tuple-element.195.refs_5_), channel_id=1, source_target_pairs={{0,2},{2,0},{4,6},{6,4},{1,3},{3,1},{5,7},{7,5},{8,10},{10,8},{12,... | collective-permute-start | bytes 786440 | tf_op jit(solution)/shard_map/ppermute | solution.py:543
  190.6 5.8 %collective-permute-start.61 = (f32[128,512]{1,0:T(8,128)S(1)}, f32[128,512]{1,0:T(8,128)S(1)}, u32[]{:S(2)}, u32[]{:S(2)}) collective-permute-start(f32[128,512]{1,0:T(8,128)S(1)} %shard_map.228.refs_7_.refs_3_), channel_id=1, source_target_pairs={{0,2},{2,0},{4,6},{6,4},{1,3},{3,1},{5,7},{7,5},{8,10},{10,8},{12,... | collective-permute-start | bytes 786440 | tf_op jit(solution)/shard_map/ppermute | solution.py:543
  196.8 2.4 collective-permute-done.58.refs_2_
  201.0 3.7 %collective-permute-done.61.refs_2_ = f32[128,512]{1,0:T(8,128)S(1)} collective-permute-done((f32[128,512]{1,0:T(8,128)S(1)}, f32[128,512]{1,0:T(8,128)S(1)}, u32[]{:S(2)}, u32[]{:S(2)}) %collective-permute-start.61) | collective-permute-done | bytes 262176 | tf_op jit(solution)/shard_map/ppermute | solution.py:543
  205.1 3.2 %collective-permute-done.60.refs_2_ = f32[128,512]{1,0:T(8,128)S(1)} collective-permute-done((f32[128,512]{1,0:T(8,128)S(1)}, f32[128,512]{1,0:T(8,128)S(1)}, u32[]{:S(2)}, u32[]{:S(2)}) %collective-permute-start.60) | collective-permute-done | bytes 262176 | tf_op jit(solution)/shard_map/ppermute | solution.py:543
  216.7 2.4 collective-permute-done.65.refs_3_
  223.3 2.1 collective-permute-start.70
  225.4 6.0 %collective-permute-done.68.refs_1_ = f32[136,512]{1,0:T(8,128)S(1)} collective-permute-done((f32[136,512]{1,0:T(8,128)S(1)}, f32[136,512]{1,0:T(8,128)S(1)}, u32[]{:S(2)}, u32[]{:S(2)}) %collective-permute-start.68) | collective-permute-done | bytes 278560 | tf_op jit(solution)/shard_map/ppermute | solution.py:543
  231.5 3.5 %collective-permute-start.67 = (f32[128,512]{1,0:T(8,128)S(1)}, f32[128,512]{1,0:T(8,128)S(1)}, u32[]{:S(2)}, u32[]{:S(2)}) collective-permute-start(f32[128,512]{1,0:T(8,128)S(1)} %shard_map.237.refs_3_.refs_0_), channel_id=1, source_target_pairs={{0,2},{6,4},{1,3},{7,5},{8,10},{14,12},{9,11},{15,13},{16,18},{22,... | collective-permute-start | bytes 786440 | tf_op jit(solution)/shard_map/ppermute | solution.py:546
  236.4 3.2 %collective-permute-start.72 = (f32[136,512]{1,0:T(8,128)S(1)}, f32[136,512]{1,0:T(8,128)S(1)}, u32[]{:S(2)}, u32[]{:S(2)}) collective-permute-start(f32[136,512]{1,0:T(8,128)S(1)} %get-tuple-element.218.refs_2_), channel_id=1, source_target_pairs={{0,2},{2,0},{4,6},{6,4},{1,3},{3,1},{5,7},{7,5},{8,10},{10,8},{12,... | collective-permute-start | bytes 835592 | tf_op jit(solution)/shard_map/ppermute | solution.py:543
  239.5 2.0 collective-permute-done.67.refs_1_
  241.8 4.5 %collective-permute-start.75 = (f32[128,512]{1,0:T(8,128)S(1)}, f32[128,512]{1,0:T(8,128)S(1)}, u32[]{:S(2)}, u32[]{:S(2)}) collective-permute-start(f32[128,512]{1,0:T(8,128)S(1)} %get-tuple-element.219.refs_2_), channel_id=1, source_target_pairs={{0,2},{2,0},{4,6},{6,4},{1,3},{3,1},{5,7},{7,5},{8,10},{10,8},{12,... | collective-permute-start | bytes 786440 | tf_op jit(solution)/shard_map/ppermute | solution.py:543
  247.5 4.3 %collective-permute-start.74 = (f32[128,512]{1,0:T(8,128)S(1)}, f32[128,512]{1,0:T(8,128)S(1)}, u32[]{:S(2)}, u32[]{:S(2)}) collective-permute-start(f32[128,512]{1,0:T(8,128)S(1)} %get-tuple-element.220.refs_5_), channel_id=1, source_target_pairs={{0,2},{2,0},{4,6},{6,4},{1,3},{3,1},{5,7},{7,5},{8,10},{10,8},{12,... | collective-permute-start | bytes 786440 | tf_op jit(solution)/shard_map/ppermute | solution.py:543
  257.0 6.4 %collective-permute-start.81 = (f32[128,512]{1,0:T(8,128)S(1)}, f32[128,512]{1,0:T(8,128)S(1)}, u32[]{:S(2)}, u32[]{:S(2)}) collective-permute-start(f32[128,512]{1,0:T(8,128)S(1)} %shard_map.254.refs_7_.refs_3_), channel_id=1, source_target_pairs={{0,2},{2,0},{4,6},{6,4},{1,3},{3,1},{5,7},{7,5},{8,10},{10,8},{12,... | collective-permute-start | bytes 786440 | tf_op jit(solution)/shard_map/ppermute | solution.py:543
  263.8 2.4 collective-permute-done.78.refs_2_
  267.6 3.7 %collective-permute-done.81.refs_2_ = f32[128,512]{1,0:T(8,128)S(1)} collective-permute-done((f32[128,512]{1,0:T(8,128)S(1)}, f32[128,512]{1,0:T(8,128)S(1)}, u32[]{:S(2)}, u32[]{:S(2)}) %collective-permute-start.81) | collective-permute-done | bytes 262176 | tf_op jit(solution)/shard_map/ppermute | solution.py:543
  271.7 3.2 %collective-permute-done.80.refs_2_ = f32[128,512]{1,0:T(8,128)S(1)} collective-permute-done((f32[128,512]{1,0:T(8,128)S(1)}, f32[128,512]{1,0:T(8,128)S(1)}, u32[]{:S(2)}, u32[]{:S(2)}) %collective-permute-start.80) | collective-permute-done | bytes 262176 | tf_op jit(solution)/shard_map/ppermute | solution.py:543
  278.9 2.2 collective-permute-start.85
  (288 shorter events, 108.3 us)
Async XLA Ops:
  6.3 11.6 %collective-permute-start.3 = (f32[384,512]{1,0:T(8,128)}, f32[384,512]{1,0:T(8,128)}, u32[]{:S(2)}, u32[]{:S(2)}) collective-permute-start(f32[384,512]{1,0:T(8,128)} %get-tuple-element.129), channel_id=1, source_target_pairs={{0,1},{1,0},{2,3},{3,2},{4,5},{5,4},{6,7},{7,6},{8,9},{9,8},{10,11... | collective-permute-start | bytes 2359304 | tf_op jit(solution)/shard_map/ppermute | solution.py:518
  6.8 17.1 %collective-permute-start.2 = (f32[384,512]{1,0:T(8,128)}, f32[384,512]{1,0:T(8,128)}, u32[]{:S(2)}, u32[]{:S(2)}) collective-permute-start(f32[384,512]{1,0:T(8,128)} %get-tuple-element.127), channel_id=1, source_target_pairs={{0,1},{1,0},{2,3},{3,2},{4,5},{5,4},{6,7},{7,6},{8,9},{9,8},{10,11... | collective-permute-start | bytes 2359304 | tf_op jit(solution)/shard_map/ppermute | solution.py:518
  6.9 20.4 %collective-permute-start.7 = (f32[384,512]{1,0:T(8,128)}, f32[384,512]{1,0:T(8,128)}, u32[]{:S(2)}, u32[]{:S(2)}) collective-permute-start(f32[384,512]{1,0:T(8,128)} %get-tuple-element.135), channel_id=1, source_target_pairs={{0,1},{1,0},{2,3},{3,2},{4,5},{5,4},{6,7},{7,6},{8,9},{9,8},{10,11... | collective-permute-start | bytes 2359304 | tf_op jit(solution)/shard_map/ppermute | solution.py:518
  16.1 14.9 %collective-permute-start.5 = (f32[384,512]{1,0:T(8,128)}, f32[384,512]{1,0:T(8,128)}, u32[]{:S(2)}, u32[]{:S(2)}) collective-permute-start(f32[384,512]{1,0:T(8,128)} %get-tuple-element.133), channel_id=1, source_target_pairs={{0,1},{1,0},{2,3},{3,2},{4,5},{5,4},{6,7},{7,6},{8,9},{9,8},{10,11... | collective-permute-start | bytes 2359304 | tf_op jit(solution)/shard_map/ppermute | solution.py:518
  17.8 24.2 %collective-permute-start.9 = (f32[384,512]{1,0:T(8,128)}, f32[384,512]{1,0:T(8,128)}, u32[]{:S(2)}, u32[]{:S(2)}) collective-permute-start(f32[384,512]{1,0:T(8,128)} %copy-done.8), channel_id=1, source_target_pairs={{0,1},{1,0},{2,3},{3,2},{4,5},{5,4},{6,7},{7,6},{8,9},{9,8},{10,11... | collective-permute-start | bytes 2359304 | tf_op jit(solution)/shard_map/ppermute | solution.py:518
  20.7 10.0 %collective-permute-start.6 = (f32[136,512]{1,0:T(8,128)S(1)}, f32[136,512]{1,0:T(8,128)S(1)}, u32[]{:S(2)}, u32[]{:S(2)}) collective-permute-start(f32[136,512]{1,0:T(8,128)S(1)} %get-tuple-element.130.refs_4_.refs_0_), channel_id=1, source_target_pairs={{0,2},{2,0},{4,6},{6,4},{1,3},{3,1},{5,7},{7,5},{8,10},{10,8},{12,... | collective-permute-start | bytes 835592 | tf_op jit(solution)/shard_map/ppermute | solution.py:543
  24.0 23.5 %collective-permute-start.1 = (f32[384,512]{1,0:T(8,128)S(1)}, f32[384,512]{1,0:T(8,128)}, u32[]{:S(2)}, u32[]{:S(2)}) collective-permute-start(f32[384,512]{1,0:T(8,128)S(1)} %get-tuple-element.125), channel_id=1, source_target_pairs={{0,1},{1,0},{2,3},{3,2},{4,5},{5,4},{6,7},{7,6},{8,9},{9,8},{10,11... | collective-permute-start | bytes 2359304 | tf_op jit(solution)/shard_map/ppermute | solution.py:518
  27.3 10.8 %collective-permute-start.4 = (f32[128,512]{1,0:T(8,128)}, f32[128,512]{1,0:T(8,128)}, u32[]{:S(2)}, u32[]{:S(2)}) collective-permute-start(f32[128,512]{1,0:T(8,128)} %get-tuple-element.131.refs_4_.refs_0_), channel_id=1, source_target_pairs={{0,2},{2,0},{4,6},{6,4},{1,3},{3,1},{5,7},{7,5},{8,10},{10,8},{12,... | collective-permute-start | bytes 786440 | tf_op jit(solution)/shard_map/ppermute | solution.py:543
  30.9 8.3 %collective-permute-start.10 = (f32[136,512]{1,0:T(8,128)S(1)}, f32[136,512]{1,0:T(8,128)}, u32[]{:S(2)}, u32[]{:S(2)}) collective-permute-start(f32[136,512]{1,0:T(8,128)S(1)} %shard_map.161.refs_4_.refs_1_), channel_id=1, source_target_pairs={{2,4},{4,2},{3,5},{5,3},{0,1},{1,0},{6,7},{7,6},{10,12},{12,10},{1... | collective-permute-start | bytes 835592 | tf_op jit(solution)/shard_map/ppermute | solution.py:553
  31.1 12.7 %collective-permute-start.11 = (f32[128,512]{1,0:T(8,128)}, f32[128,512]{1,0:T(8,128)S(1)}, u32[]{:S(2)}, u32[]{:S(2)}) collective-permute-start(f32[128,512]{1,0:T(8,128)} %copy-done.19), channel_id=1, source_target_pairs={{0,2},{6,4},{1,3},{7,5},{8,10},{14,12},{9,11},{15,13},{16,18},{22,... | collective-permute-start | bytes 786440 | tf_op jit(solution)/shard_map/ppermute | solution.py:546
  40.3 9.5 %collective-permute-start.13 = (f32[136,512]{1,0:T(8,128)S(1)}, f32[136,512]{1,0:T(8,128)S(1)}, u32[]{:S(2)}, u32[]{:S(2)}) collective-permute-start(f32[136,512]{1,0:T(8,128)S(1)} %get-tuple-element.140.refs_4_), channel_id=1, source_target_pairs={{0,2},{2,0},{4,6},{6,4},{1,3},{3,1},{5,7},{7,5},{8,10},{10,8},{12,... | collective-permute-start | bytes 835592 | tf_op jit(solution)/shard_map/ppermute | solution.py:543
  43.8 6.2 %collective-permute-start.12 = (f32[128,512]{1,0:T(8,128)S(1)}, f32[128,512]{1,0:T(8,128)S(1)}, u32[]{:S(2)}, u32[]{:S(2)}) collective-permute-start(f32[128,512]{1,0:T(8,128)S(1)} %shard_map.166.refs_4_.refs_1_), channel_id=1, source_target_pairs={{2,4},{4,2},{3,5},{5,3},{0,1},{1,0},{6,7},{7,6},{10,12},{12,10},{1... | collective-permute-start | bytes 786440 | tf_op jit(solution)/shard_map/ppermute | solution.py:553
  44.0 11.5 %collective-permute-start.15 = (f32[128,512]{1,0:T(8,128)S(1)}, f32[128,512]{1,0:T(8,128)S(1)}, u32[]{:S(2)}, u32[]{:S(2)}) collective-permute-start(f32[128,512]{1,0:T(8,128)S(1)} %get-tuple-element.142.refs_4_), channel_id=1, source_target_pairs={{0,2},{2,0},{4,6},{6,4},{1,3},{3,1},{5,7},{7,5},{8,10},{10,8},{12,... | collective-permute-start | bytes 786440 | tf_op jit(solution)/shard_map/ppermute | solution.py:543
  50.1 10.6 %collective-permute-start.14 = (f32[128,512]{1,0:T(8,128)S(1)}, f32[128,512]{1,0:T(8,128)S(1)}, u32[]{:S(2)}, u32[]{:S(2)}) collective-permute-start(f32[128,512]{1,0:T(8,128)S(1)} %get-tuple-element.144.refs_6_), channel_id=1, source_target_pairs={{0,2},{2,0},{4,6},{6,4},{1,3},{3,1},{5,7},{7,5},{8,10},{10,8},{12,... | collective-permute-start | bytes 786440 | tf_op jit(solution)/shard_map/ppermute | solution.py:543
  55.6 12.5 %collective-permute-start.18 = (f32[128,512]{1,0:T(8,128)S(1)}, f32[128,512]{1,0:T(8,128)S(1)}, u32[]{:S(2)}, u32[]{:S(2)}) collective-permute-start(f32[128,512]{1,0:T(8,128)S(1)} %shard_map.173.refs_8_.refs_3_), channel_id=1, source_target_pairs={{2,0},{4,6},{3,1},{5,7},{10,8},{12,14},{11,9},{13,15},{18,16},{20,... | collective-permute-start | bytes 786440 | tf_op jit(solution)/shard_map/ppermute | solution.py:549
  60.7 7.8 %collective-permute-start.17 = (f32[128,512]{1,0:T(8,128)S(1)}, f32[128,512]{1,0:T(8,128)S(1)}, u32[]{:S(2)}, u32[]{:S(2)}) collective-permute-start(f32[128,512]{1,0:T(8,128)S(1)} %shard_map.175.refs_2_.refs_0_), channel_id=1, source_target_pairs={{2,4},{4,2},{3,5},{5,3},{0,1},{1,0},{6,7},{7,6},{10,12},{12,10},{1... | collective-permute-start | bytes 786440 | tf_op jit(solution)/shard_map/ppermute | solution.py:553
  60.9 12.9 %collective-permute-start.21 = (f32[128,512]{1,0:T(8,128)S(1)}, f32[128,512]{1,0:T(8,128)S(1)}, u32[]{:S(2)}, u32[]{:S(2)}) collective-permute-start(f32[128,512]{1,0:T(8,128)S(1)} %shard_map.176.refs_8_.refs_3_), channel_id=1, source_target_pairs={{0,2},{2,0},{4,6},{6,4},{1,3},{3,1},{5,7},{7,5},{8,10},{10,8},{12,... | collective-permute-start | bytes 786440 | tf_op jit(solution)/shard_map/ppermute | solution.py:543
  68.6 9.0 %collective-permute-start.20 = (f32[128,512]{1,0:T(8,128)S(1)}, f32[128,512]{1,0:T(8,128)S(1)}, u32[]{:S(2)}, u32[]{:S(2)}) collective-permute-start(f32[128,512]{1,0:T(8,128)S(1)} %shard_map.179.refs_8_.refs_3_), channel_id=1, source_target_pairs={{0,2},{2,0},{4,6},{6,4},{1,3},{3,1},{5,7},{7,5},{8,10},{10,8},{12,... | collective-permute-start | bytes 786440 | tf_op jit(solution)/shard_map/ppermute | solution.py:543
  90.9 9.6 %collective-permute-start.28 = (f32[136,512]{1,0:T(8,128)S(1)}, f32[136,512]{1,0:T(8,128)S(1)}, u32[]{:S(2)}, u32[]{:S(2)}) collective-permute-start(f32[136,512]{1,0:T(8,128)S(1)} %shard_map.184.refs_3_.refs_0_), channel_id=1, source_target_pairs={{0,2},{2,0},{4,6},{6,4},{1,3},{3,1},{5,7},{7,5},{8,10},{10,8},{12,... | collective-permute-start | bytes 835592 | tf_op jit(solution)/shard_map/ppermute | solution.py:543
  92.4 12.9 %collective-permute-start.30 = (f32[128,512]{1,0:T(8,128)S(1)}, f32[128,512]{1,0:T(8,128)S(1)}, u32[]{:S(2)}, u32[]{:S(2)}) collective-permute-start(f32[128,512]{1,0:T(8,128)S(1)} %shard_map.189.refs_2_.refs_0_), channel_id=1, source_target_pairs={{0,2},{2,0},{4,6},{6,4},{1,3},{3,1},{5,7},{7,5},{8,10},{10,8},{12,... | collective-permute-start | bytes 786440 | tf_op jit(solution)/shard_map/ppermute | solution.py:543
  100.6 10.1 %collective-permute-start.27 = (f32[128,512]{1,0:T(8,128)S(1)}, f32[128,512]{1,0:T(8,128)S(1)}, u32[]{:S(2)}, u32[]{:S(2)}) collective-permute-start(f32[128,512]{1,0:T(8,128)S(1)} %shard_map.185.refs_3_.refs_0_), channel_id=1, source_target_pairs={{0,2},{6,4},{1,3},{7,5},{8,10},{14,12},{9,11},{15,13},{16,18},{22,... | collective-permute-start | bytes 786440 | tf_op jit(solution)/shard_map/ppermute | solution.py:546
  105.5 10.9 %collective-permute-start.32 = (f32[136,512]{1,0:T(8,128)S(1)}, f32[136,512]{1,0:T(8,128)S(1)}, u32[]{:S(2)}, u32[]{:S(2)}) collective-permute-start(f32[136,512]{1,0:T(8,128)S(1)} %get-tuple-element.172.refs_2_), channel_id=1, source_target_pairs={{0,2},{2,0},{4,6},{6,4},{1,3},{3,1},{5,7},{7,5},{8,10},{10,8},{12,... | collective-permute-start | bytes 835592 | tf_op jit(solution)/shard_map/ppermute | solution.py:543
  110.9 11.1 %collective-permute-start.35 = (f32[128,512]{1,0:T(8,128)S(1)}, f32[128,512]{1,0:T(8,128)S(1)}, u32[]{:S(2)}, u32[]{:S(2)}) collective-permute-start(f32[128,512]{1,0:T(8,128)S(1)} %get-tuple-element.173.refs_2_), channel_id=1, source_target_pairs={{0,2},{2,0},{4,6},{6,4},{1,3},{3,1},{5,7},{7,5},{8,10},{10,8},{12,... | collective-permute-start | bytes 786440 | tf_op jit(solution)/shard_map/ppermute | solution.py:543
  116.6 9.4 %collective-permute-start.34 = (f32[128,512]{1,0:T(8,128)S(1)}, f32[128,512]{1,0:T(8,128)S(1)}, u32[]{:S(2)}, u32[]{:S(2)}) collective-permute-start(f32[128,512]{1,0:T(8,128)S(1)} %get-tuple-element.174.refs_5_), channel_id=1, source_target_pairs={{0,2},{2,0},{4,6},{6,4},{1,3},{3,1},{5,7},{7,5},{8,10},{10,8},{12,... | collective-permute-start | bytes 786440 | tf_op jit(solution)/shard_map/ppermute | solution.py:543
  122.1 12.9 %collective-permute-start.38 = (f32[128,512]{1,0:T(8,128)S(1)}, f32[128,512]{1,0:T(8,128)S(1)}, u32[]{:S(2)}, u32[]{:S(2)}) collective-permute-start(f32[128,512]{1,0:T(8,128)S(1)} %shard_map.199.refs_7_.refs_3_), channel_id=1, source_target_pairs={{2,0},{4,6},{3,1},{5,7},{10,8},{12,14},{11,9},{13,15},{18,16},{20,... | collective-permute-start | bytes 786440 | tf_op jit(solution)/shard_map/ppermute | solution.py:549
  126.0 9.4 %collective-permute-start.37 = (f32[128,512]{1,0:T(8,128)S(1)}, f32[128,512]{1,0:T(8,128)S(1)}, u32[]{:S(2)}, u32[]{:S(2)}) collective-permute-start(f32[128,512]{1,0:T(8,128)S(1)} %shard_map.201.refs_2_.refs_0_), channel_id=1, source_target_pairs={{2,4},{4,2},{3,5},{5,3},{0,1},{1,0},{6,7},{7,6},{10,12},{12,10},{1... | collective-permute-start | bytes 786440 | tf_op jit(solution)/shard_map/ppermute | solution.py:553
  126.1 14.1 %collective-permute-start.41 = (f32[128,512]{1,0:T(8,128)S(1)}, f32[128,512]{1,0:T(8,128)S(1)}, u32[]{:S(2)}, u32[]{:S(2)}) collective-permute-start(f32[128,512]{1,0:T(8,128)S(1)} %shard_map.202.refs_7_.refs_3_), channel_id=1, source_target_pairs={{0,2},{2,0},{4,6},{6,4},{1,3},{3,1},{5,7},{7,5},{8,10},{10,8},{12,... | collective-permute-start | bytes 786440 | tf_op jit(solution)/shard_map/ppermute | solution.py:543
  135.5 8.5 %collective-permute-start.40 = (f32[128,512]{1,0:T(8,128)S(1)}, f32[128,512]{1,0:T(8,128)S(1)}, u32[]{:S(2)}, u32[]{:S(2)}) collective-permute-start(f32[128,512]{1,0:T(8,128)S(1)} %shard_map.205.refs_7_.refs_3_), channel_id=1, source_target_pairs={{0,2},{2,0},{4,6},{6,4},{1,3},{3,1},{5,7},{7,5},{8,10},{10,8},{12,... | collective-permute-start | bytes 786440 | tf_op jit(solution)/shard_map/ppermute | solution.py:543
  155.4 9.6 %collective-permute-start.48 = (f32[136,512]{1,0:T(8,128)S(1)}, f32[136,512]{1,0:T(8,128)S(1)}, u32[]{:S(2)}, u32[]{:S(2)}) collective-permute-start(f32[136,512]{1,0:T(8,128)S(1)} %shard_map.210.refs_3_.refs_0_), channel_id=1, source_target_pairs={{0,2},{2,0},{4,6},{6,4},{1,3},{3,1},{5,7},{7,5},{8,10},{10,8},{12,... | collective-permute-start | bytes 835592 | tf_op jit(solution)/shard_map/ppermute | solution.py:543
  157.2 12.6 %collective-permute-start.50 = (f32[128,512]{1,0:T(8,128)S(1)}, f32[128,512]{1,0:T(8,128)S(1)}, u32[]{:S(2)}, u32[]{:S(2)}) collective-permute-start(f32[128,512]{1,0:T(8,128)S(1)} %shard_map.215.refs_2_.refs_0_), channel_id=1, source_target_pairs={{0,2},{2,0},{4,6},{6,4},{1,3},{3,1},{5,7},{7,5},{8,10},{10,8},{12,... | collective-permute-start | bytes 786440 | tf_op jit(solution)/shard_map/ppermute | solution.py:543
  165.1 9.7 %collective-permute-start.47 = (f32[128,512]{1,0:T(8,128)S(1)}, f32[128,512]{1,0:T(8,128)S(1)}, u32[]{:S(2)}, u32[]{:S(2)}) collective-permute-start(f32[128,512]{1,0:T(8,128)S(1)} %shard_map.211.refs_3_.refs_0_), channel_id=1, source_target_pairs={{0,2},{6,4},{1,3},{7,5},{8,10},{14,12},{9,11},{15,13},{16,18},{22,... | collective-permute-start | bytes 786440 | tf_op jit(solution)/shard_map/ppermute | solution.py:546
  170.0 10.7 %collective-permute-start.52 = (f32[136,512]{1,0:T(8,128)S(1)}, f32[136,512]{1,0:T(8,128)S(1)}, u32[]{:S(2)}, u32[]{:S(2)}) collective-permute-start(f32[136,512]{1,0:T(8,128)S(1)} %get-tuple-element.193.refs_2_), channel_id=1, source_target_pairs={{0,2},{2,0},{4,6},{6,4},{1,3},{3,1},{5,7},{7,5},{8,10},{10,8},{12,... | collective-permute-start | bytes 835592 | tf_op jit(solution)/shard_map/ppermute | solution.py:543
  175.0 11.4 %collective-permute-start.55 = (f32[128,512]{1,0:T(8,128)S(1)}, f32[128,512]{1,0:T(8,128)S(1)}, u32[]{:S(2)}, u32[]{:S(2)}) collective-permute-start(f32[128,512]{1,0:T(8,128)S(1)} %get-tuple-element.194.refs_2_), channel_id=1, source_target_pairs={{0,2},{2,0},{4,6},{6,4},{1,3},{3,1},{5,7},{7,5},{8,10},{10,8},{12,... | collective-permute-start | bytes 786440 | tf_op jit(solution)/shard_map/ppermute | solution.py:543
  180.9 9.5 %collective-permute-start.54 = (f32[128,512]{1,0:T(8,128)S(1)}, f32[128,512]{1,0:T(8,128)S(1)}, u32[]{:S(2)}, u32[]{:S(2)}) collective-permute-start(f32[128,512]{1,0:T(8,128)S(1)} %get-tuple-element.195.refs_5_), channel_id=1, source_target_pairs={{0,2},{2,0},{4,6},{6,4},{1,3},{3,1},{5,7},{7,5},{8,10},{10,8},{12,... | collective-permute-start | bytes 786440 | tf_op jit(solution)/shard_map/ppermute | solution.py:543
  186.5 12.7 %collective-permute-start.58 = (f32[128,512]{1,0:T(8,128)S(1)}, f32[128,512]{1,0:T(8,128)S(1)}, u32[]{:S(2)}, u32[]{:S(2)}) collective-permute-start(f32[128,512]{1,0:T(8,128)S(1)} %shard_map.225.refs_7_.refs_3_), channel_id=1, source_target_pairs={{2,0},{4,6},{3,1},{5,7},{10,8},{12,14},{11,9},{13,15},{18,16},{20,... | collective-permute-start | bytes 786440 | tf_op jit(solution)/shard_map/ppermute | solution.py:549
  190.5 9.2 %collective-permute-start.57 = (f32[128,512]{1,0:T(8,128)S(1)}, f32[128,512]{1,0:T(8,128)S(1)}, u32[]{:S(2)}, u32[]{:S(2)}) collective-permute-start(f32[128,512]{1,0:T(8,128)S(1)} %shard_map.227.refs_2_.refs_0_), channel_id=1, source_target_pairs={{2,4},{4,2},{3,5},{5,3},{0,1},{1,0},{6,7},{7,6},{10,12},{12,10},{1... | collective-permute-start | bytes 786440 | tf_op jit(solution)/shard_map/ppermute | solution.py:553
  190.6 14.1 %collective-permute-start.61 = (f32[128,512]{1,0:T(8,128)S(1)}, f32[128,512]{1,0:T(8,128)S(1)}, u32[]{:S(2)}, u32[]{:S(2)}) collective-permute-start(f32[128,512]{1,0:T(8,128)S(1)} %shard_map.228.refs_7_.refs_3_), channel_id=1, source_target_pairs={{0,2},{2,0},{4,6},{6,4},{1,3},{3,1},{5,7},{7,5},{8,10},{10,8},{12,... | collective-permute-start | bytes 786440 | tf_op jit(solution)/shard_map/ppermute | solution.py:543
  199.7 8.7 %collective-permute-start.60 = (f32[128,512]{1,0:T(8,128)S(1)}, f32[128,512]{1,0:T(8,128)S(1)}, u32[]{:S(2)}, u32[]{:S(2)}) collective-permute-start(f32[128,512]{1,0:T(8,128)S(1)} %shard_map.231.refs_7_.refs_3_), channel_id=1, source_target_pairs={{0,2},{2,0},{4,6},{6,4},{1,3},{3,1},{5,7},{7,5},{8,10},{10,8},{12,... | collective-permute-start | bytes 786440 | tf_op jit(solution)/shard_map/ppermute | solution.py:543
  221.8 9.6 %collective-permute-start.68 = (f32[136,512]{1,0:T(8,128)S(1)}, f32[136,512]{1,0:T(8,128)S(1)}, u32[]{:S(2)}, u32[]{:S(2)}) collective-permute-start(f32[136,512]{1,0:T(8,128)S(1)} %shard_map.236.refs_3_.refs_0_), channel_id=1, source_target_pairs={{0,2},{2,0},{4,6},{6,4},{1,3},{3,1},{5,7},{7,5},{8,10},{10,8},{12,... | collective-permute-start | bytes 835592 | tf_op jit(solution)/shard_map/ppermute | solution.py:543
  223.3 12.9 %collective-permute-start.70 = (f32[128,512]{1,0:T(8,128)S(1)}, f32[128,512]{1,0:T(8,128)S(1)}, u32[]{:S(2)}, u32[]{:S(2)}) collective-permute-start(f32[128,512]{1,0:T(8,128)S(1)} %shard_map.241.refs_2_.refs_0_), channel_id=1, source_target_pairs={{0,2},{2,0},{4,6},{6,4},{1,3},{3,1},{5,7},{7,5},{8,10},{10,8},{12,... | collective-permute-start | bytes 786440 | tf_op jit(solution)/shard_map/ppermute | solution.py:543
  231.5 10.1 %collective-permute-start.67 = (f32[128,512]{1,0:T(8,128)S(1)}, f32[128,512]{1,0:T(8,128)S(1)}, u32[]{:S(2)}, u32[]{:S(2)}) collective-permute-start(f32[128,512]{1,0:T(8,128)S(1)} %shard_map.237.refs_3_.refs_0_), channel_id=1, source_target_pairs={{0,2},{6,4},{1,3},{7,5},{8,10},{14,12},{9,11},{15,13},{16,18},{22,... | collective-permute-start | bytes 786440 | tf_op jit(solution)/shard_map/ppermute | solution.py:546
  236.4 11.0 %collective-permute-start.72 = (f32[136,512]{1,0:T(8,128)S(1)}, f32[136,512]{1,0:T(8,128)S(1)}, u32[]{:S(2)}, u32[]{:S(2)}) collective-permute-start(f32[136,512]{1,0:T(8,128)S(1)} %get-tuple-element.218.refs_2_), channel_id=1, source_target_pairs={{0,2},{2,0},{4,6},{6,4},{1,3},{3,1},{5,7},{7,5},{8,10},{10,8},{12,... | collective-permute-start | bytes 835592 | tf_op jit(solution)/shard_map/ppermute | solution.py:543
  241.8 11.2 %collective-permute-start.75 = (f32[128,512]{1,0:T(8,128)S(1)}, f32[128,512]{1,0:T(8,128)S(1)}, u32[]{:S(2)}, u32[]{:S(2)}) collective-permute-start(f32[128,512]{1,0:T(8,128)S(1)} %get-tuple-element.219.refs_2_), channel_id=1, source_target_pairs={{0,2},{2,0},{4,6},{6,4},{1,3},{3,1},{5,7},{7,5},{8,10},{10,8},{12,... | collective-permute-start | bytes 786440 | tf_op jit(solution)/shard_map/ppermute | solution.py:543
  247.5 9.3 %collective-permute-start.74 = (f32[128,512]{1,0:T(8,128)S(1)}, f32[128,512]{1,0:T(8,128)S(1)}, u32[]{:S(2)}, u32[]{:S(2)}) collective-permute-start(f32[128,512]{1,0:T(8,128)S(1)} %get-tuple-element.220.refs_5_), channel_id=1, source_target_pairs={{0,2},{2,0},{4,6},{6,4},{1,3},{3,1},{5,7},{7,5},{8,10},{10,8},{12,... | collective-permute-start | bytes 786440 | tf_op jit(solution)/shard_map/ppermute | solution.py:543
  253.1 13.1 %collective-permute-start.78 = (f32[128,512]{1,0:T(8,128)S(1)}, f32[128,512]{1,0:T(8,128)S(1)}, u32[]{:S(2)}, u32[]{:S(2)}) collective-permute-start(f32[128,512]{1,0:T(8,128)S(1)} %shard_map.251.refs_7_.refs_3_), channel_id=1, source_target_pairs={{2,0},{4,6},{3,1},{5,7},{10,8},{12,14},{11,9},{13,15},{18,16},{20,... | collective-permute-start | bytes 786440 | tf_op jit(solution)/shard_map/ppermute | solution.py:549
  256.9 9.7 %collective-permute-start.77 = (f32[128,512]{1,0:T(8,128)S(1)}, f32[128,512]{1,0:T(8,128)S(1)}, u32[]{:S(2)}, u32[]{:S(2)}) collective-permute-start(f32[128,512]{1,0:T(8,128)S(1)} %shard_map.253.refs_2_.refs_0_), channel_id=1, source_target_pairs={{2,4},{4,2},{3,5},{5,3},{0,1},{1,0},{6,7},{7,6},{10,12},{12,10},{1... | collective-permute-start | bytes 786440 | tf_op jit(solution)/shard_map/ppermute | solution.py:553
  257.0 14.4 %collective-permute-start.81 = (f32[128,512]{1,0:T(8,128)S(1)}, f32[128,512]{1,0:T(8,128)S(1)}, u32[]{:S(2)}, u32[]{:S(2)}) collective-permute-start(f32[128,512]{1,0:T(8,128)S(1)} %shard_map.254.refs_7_.refs_3_), channel_id=1, source_target_pairs={{0,2},{2,0},{4,6},{6,4},{1,3},{3,1},{5,7},{7,5},{8,10},{10,8},{12,... | collective-permute-start | bytes 786440 | tf_op jit(solution)/shard_map/ppermute | solution.py:543
  266.6 8.3 %collective-permute-start.80 = (f32[128,512]{1,0:T(8,128)S(1)}, f32[128,512]{1,0:T(8,128)S(1)}, u32[]{:S(2)}, u32[]{:S(2)}) collective-permute-start(f32[128,512]{1,0:T(8,128)S(1)} %shard_map.257.refs_7_.refs_3_), channel_id=1, source_target_pairs={{0,2},{2,0},{4,6},{6,4},{1,3},{3,1},{5,7},{7,5},{8,10},{10,8},{12,... | collective-permute-start | bytes 786440 | tf_op jit(solution)/shard_map/ppermute | solution.py:543
  (66 other events, 286.7 us)

commit v10 on v9

--- a/solution.py
+++ b/solution.py
@@ -262,13 +262,19 @@
 
 def spread(index, length, own, got, pair, token):
     height = length + (8 if index == 0 else 0)
-
-    def kernel(own_ref, got_ref, pair_ref, out_ref):
+    last = index == CHUNKS - 1
+
+    def kernel(own_ref, got_ref, pair_ref, out_ref, *meet_ref):
         out_ref[:length] = dot32(rows_of(own_ref, got_ref, length), pair_ref[...])
         if index == 0:
             put_tail(out_ref, own_ref, got_ref, length)
-
-    return call(kernel, [own, got, pair], [((height, pair.shape[1]), F32)], token)[0]
+        if last:
+            meet_ref[0][...] = own_ref[length:, :HEAD_DIM]
+
+    outs = [((height, pair.shape[1]), F32)]
+    if last:
+        outs.append(((8, HEAD_DIM), F32))
+    return call(kernel, [own, got, pair], outs, token)
 
 
 def add(first, second, token):
@@ -566,7 +572,9 @@
                     k, length, rows, got_rows, own_w[k], other_w[k], token
                 )
             else:
-                own_part[k] = spread(k, length, rows, got_rows, pairs[k], token)
+                own_part[k], *meet = spread(k, length, rows, got_rows, pairs[k], token)
+                if meet:
+                    return swap(meet[0])
             return own_part[k]
 
         def finish(k, got):

time: 285 us -> 285 us (level)
    ppermute x28, waiting for transfers between devices: 69.1 us -> 65.4 us  [outer_swap(): return lax.ppermute(part, 'chip', [(0, 1), (1, 0), (2, 3), (3, 2)])]
    ppermute x14 -> x17, waiting for transfers between devices: 11.4 us -> 14.6 us  [swap(): return lax.ppermute(part, 'core', [(0, 1), (1, 0)])]
  transfers between devices with their start and end apart: 86 -> 89, of which waited for: 54 -> 57; matrix products, arithmetic and copies ran while one was open for 0% -> 0% of each run, Pallas kernels for 12% -> 12%
where the time goes in v10:
time: 285 us
  starting transfers between devices  120 us (42%)
  waiting for transfers between devices  111 us (39%)
  Pallas kernels  45.9 us (16%)
  local copies, waits for them, and re-layouts  5.24 us (2%)
    ppermute x28, starting transfers between devices, outer_swap(): return lax.ppermute(part, 'chip', [(0, 1), (1, 0), (2, 3), (3, 2)])  80.7 us
    ppermute x28, waiting for transfers between devices, outer_swap(): return lax.ppermute(part, 'chip', [(0, 1), (1, 0), (2, 3), (3, 2)])  65.4 us
    pallas_call x96, Pallas kernels, call(): pl.pallas_call(body, in_specs=[SMEM] * len(scalars) + [VMEM] * len(ins) +...  29.3 us
    ppermute x4, starting transfers between devices, send_in(): return lax.ppermute(part, 'chip', [(0, 1), (3, 2)])  15.2 us
    ppermute x12, waiting for transfers between devices, data_terms(): lax.ppermute(part, 'dp', [(d, d ^ step) for d in range(n_dp)])  14.8 us
    ppermute x17, waiting for transfers between devices, swap(): return lax.ppermute(part, 'core', [(0, 1), (1, 0)])  14.6 us
    ppermute x12, starting transfers between devices, data_terms(): lax.ppermute(part, 'dp', [(d, d ^ step) for d in range(n_dp)])  14 us
    ppermute x4, waiting for transfers between devices, send_back(): return lax.ppermute(part, 'chip', [(1, 0), (2, 3)])  9.94 us
  transfers between devices with their start and end apart: 89, of which 57 were waited for; matrix products, arithmetic and copies ran while one was open for 0% of the time, Pallas kernels for 12%

profile of v10, /device:TPU:0, one launch (start us, length us, event | category | flops | bytes accessed | tf_op | source)
XLA Modules:
  0.0 284.8 jit_solution(858072669210582710)
XLA Ops:
  0.6 2.3 copy-done
  3.0 2.5 shard_map.157
  8.1 7.8 %shard_map.156 = (f32[3,128,128]{2,1,0:T(8,128)S(1)}, bf16[128,384]{1,0:T(8,128)(2,1)S(1)}, bf16[128,384]{1,0:T(8,128)(2,1)S(1)}, f32[128,16]{1,0:T(8,128)S(1)},...) custom-call(s32[1]{0:T(128)S(6)} %copy.17.limit_ref.refs_1_.refs_4_.refs_6_.refs_10_, bf16[128,6144]{1,0:T(8,128)(2,1)S(1)} %copy-done.1, ...), custom_call_target="tpu_custom_call" | custom-call | flops 1811939328 | bytes 14155776 | tf_op jit(solution)/shard_map/pallas_call | solution.py:188
  20.7 3.0 %collective-permute-start.6 = (f32[136,512]{1,0:T(8,128)S(1)}, f32[136,512]{1,0:T(8,128)S(1)}, u32[]{:S(2)}, u32[]{:S(2)}) collective-permute-start(f32[136,512]{1,0:T(8,128)S(1)} %get-tuple-element.136.refs_4_.refs_0_), channel_id=1, source_target_pairs={{0,2},{2,0},{4,6},{6,4},{1,3},{3,1},{5,7},{7,5},{8,10},{10,8},{12,... | collective-permute-start | bytes 835592 | tf_op jit(solution)/shard_map/ppermute | solution.py:549
  24.0 2.4 shard_map.159
  31.1 5.4 %collective-permute-start.11 = (f32[128,512]{1,0:T(8,128)}, f32[128,512]{1,0:T(8,128)S(1)}, u32[]{:S(2)}, u32[]{:S(2)}) collective-permute-start(f32[128,512]{1,0:T(8,128)} %copy-done.19), channel_id=1, source_target_pairs={{0,2},{6,4},{1,3},{7,5},{8,10},{14,12},{9,11},{15,13},{16,18},{22,... | collective-permute-start | bytes 786440 | tf_op jit(solution)/shard_map/ppermute | solution.py:552
  44.0 3.5 %collective-permute-start.15 = (f32[128,512]{1,0:T(8,128)S(1)}, f32[128,512]{1,0:T(8,128)S(1)}, u32[]{:S(2)}, u32[]{:S(2)}) collective-permute-start(f32[128,512]{1,0:T(8,128)S(1)} %get-tuple-element.148.refs_4_), channel_id=1, source_target_pairs={{0,2},{2,0},{4,6},{6,4},{1,3},{3,1},{5,7},{7,5},{8,10},{10,8},{12,... | collective-permute-start | bytes 786440 | tf_op jit(solution)/shard_map/ppermute | solution.py:549
  50.1 3.5 %collective-permute-start.14 = (f32[128,512]{1,0:T(8,128)S(1)}, f32[128,512]{1,0:T(8,128)S(1)}, u32[]{:S(2)}, u32[]{:S(2)}) collective-permute-start(f32[128,512]{1,0:T(8,128)S(1)} %get-tuple-element.150.refs_6_), channel_id=1, source_target_pairs={{0,2},{2,0},{4,6},{6,4},{1,3},{3,1},{5,7},{7,5},{8,10},{10,8},{12,... | collective-permute-start | bytes 786440 | tf_op jit(solution)/shard_map/ppermute | solution.py:549
  57.7 3.0 %collective-permute-done.14.refs_1_.refs_2_ = f32[128,512]{1,0:T(8,128)S(1)} collective-permute-done((f32[128,512]{1,0:T(8,128)S(1)}, f32[128,512]{1,0:T(8,128)S(1)}, u32[]{:S(2)}, u32[]{:S(2)}) %collective-permute-start.14) | collective-permute-done | bytes 262176 | tf_op jit(solution)/shard_map/ppermute | solution.py:549
  60.9 4.2 %collective-permute-start.21 = (f32[128,512]{1,0:T(8,128)S(1)}, f32[128,512]{1,0:T(8,128)S(1)}, u32[]{:S(2)}, u32[]{:S(2)}) collective-permute-start(f32[128,512]{1,0:T(8,128)S(1)} %shard_map.176.refs_8_.refs_3_), channel_id=1, source_target_pairs={{0,2},{2,0},{4,6},{6,4},{1,3},{3,1},{5,7},{7,5},{8,10},{10,8},{12,... | collective-permute-start | bytes 786440 | tf_op jit(solution)/shard_map/ppermute | solution.py:549
  65.5 2.7 collective-permute-done.18.refs_2_
  69.8 3.9 %collective-permute-done.21.refs_2_ = f32[128,512]{1,0:T(8,128)S(1)} collective-permute-done((f32[128,512]{1,0:T(8,128)S(1)}, f32[128,512]{1,0:T(8,128)S(1)}, u32[]{:S(2)}, u32[]{:S(2)}) %collective-permute-start.21) | collective-permute-done | bytes 262176 | tf_op jit(solution)/shard_map/ppermute | solution.py:549
  74.1 3.4 %collective-permute-done.20.refs_2_ = f32[128,512]{1,0:T(8,128)S(1)} collective-permute-done((f32[128,512]{1,0:T(8,128)S(1)}, f32[128,512]{1,0:T(8,128)S(1)}, u32[]{:S(2)}, u32[]{:S(2)}) %collective-permute-start.20) | collective-permute-done | bytes 262176 | tf_op jit(solution)/shard_map/ppermute | solution.py:549
  85.9 2.4 collective-permute-done.25.refs_3_
  93.6 2.1 collective-permute-start.31
  95.7 4.8 %collective-permute-done.28.refs_1_ = f32[136,512]{1,0:T(8,128)S(1)} collective-permute-done((f32[136,512]{1,0:T(8,128)S(1)}, f32[136,512]{1,0:T(8,128)S(1)}, u32[]{:S(2)}, u32[]{:S(2)}) %collective-permute-start.28) | collective-permute-done | bytes 278560 | tf_op jit(solution)/shard_map/ppermute | solution.py:549
  100.6 3.4 %collective-permute-start.27 = (f32[128,512]{1,0:T(8,128)S(1)}, f32[128,512]{1,0:T(8,128)S(1)}, u32[]{:S(2)}, u32[]{:S(2)}) collective-permute-start(f32[128,512]{1,0:T(8,128)S(1)} %shard_map.185.refs_3_.refs_0_), channel_id=1, source_target_pairs={{0,2},{6,4},{1,3},{7,5},{8,10},{14,12},{9,11},{15,13},{16,18},{22,... | collective-permute-start | bytes 786440 | tf_op jit(solution)/shard_map/ppermute | solution.py:552
  105.5 3.2 %collective-permute-start.33 = (f32[136,512]{1,0:T(8,128)S(1)}, f32[136,512]{1,0:T(8,128)S(1)}, u32[]{:S(2)}, u32[]{:S(2)}) collective-permute-start(f32[136,512]{1,0:T(8,128)S(1)} %get-tuple-element.180.refs_2_), channel_id=1, source_target_pairs={{0,2},{2,0},{4,6},{6,4},{1,3},{3,1},{5,7},{7,5},{8,10},{10,8},{12,... | collective-permute-start | bytes 835592 | tf_op jit(solution)/shard_map/ppermute | solution.py:549
  110.9 4.2 %collective-permute-start.36 = (f32[128,512]{1,0:T(8,128)S(1)}, f32[128,512]{1,0:T(8,128)S(1)}, u32[]{:S(2)}, u32[]{:S(2)}) collective-permute-start(f32[128,512]{1,0:T(8,128)S(1)} %get-tuple-element.181.refs_2_), channel_id=1, source_target_pairs={{0,2},{2,0},{4,6},{6,4},{1,3},{3,1},{5,7},{7,5},{8,10},{10,8},{12,... | collective-permute-start | bytes 786440 | tf_op jit(solution)/shard_map/ppermute | solution.py:549
  116.5 4.1 %collective-permute-start.35 = (f32[128,512]{1,0:T(8,128)S(1)}, f32[128,512]{1,0:T(8,128)S(1)}, u32[]{:S(2)}, u32[]{:S(2)}) collective-permute-start(f32[128,512]{1,0:T(8,128)S(1)} %get-tuple-element.182.refs_5_), channel_id=1, source_target_pairs={{0,2},{2,0},{4,6},{6,4},{1,3},{3,1},{5,7},{7,5},{8,10},{10,8},{12,... | collective-permute-start | bytes 786440 | tf_op jit(solution)/shard_map/ppermute | solution.py:549
  123.8 2.1 collective-permute-done.35.refs_1_.refs_2_
  126.1 6.0 %collective-permute-start.42 = (f32[128,512]{1,0:T(8,128)S(1)}, f32[128,512]{1,0:T(8,128)S(1)}, u32[]{:S(2)}, u32[]{:S(2)}) collective-permute-start(f32[128,512]{1,0:T(8,128)S(1)} %shard_map.202.refs_7_.refs_3_), channel_id=1, source_target_pairs={{0,2},{2,0},{4,6},{6,4},{1,3},{3,1},{5,7},{7,5},{8,10},{10,8},{12,... | collective-permute-start | bytes 786440 | tf_op jit(solution)/shard_map/ppermute | solution.py:549
  132.5 2.4 collective-permute-done.39.refs_2_
  136.6 3.6 %collective-permute-done.42.refs_2_ = f32[128,512]{1,0:T(8,128)S(1)} collective-permute-done((f32[128,512]{1,0:T(8,128)S(1)}, f32[128,512]{1,0:T(8,128)S(1)}, u32[]{:S(2)}, u32[]{:S(2)}) %collective-permute-start.42) | collective-permute-done | bytes 262176 | tf_op jit(solution)/shard_map/ppermute | solution.py:549
  140.6 3.3 %collective-permute-done.41.refs_2_ = f32[128,512]{1,0:T(8,128)S(1)} collective-permute-done((f32[128,512]{1,0:T(8,128)S(1)}, f32[128,512]{1,0:T(8,128)S(1)}, u32[]{:S(2)}, u32[]{:S(2)}) %collective-permute-start.41) | collective-permute-done | bytes 262176 | tf_op jit(solution)/shard_map/ppermute | solution.py:549
  147.7 2.4 collective-permute-start.46
  160.2 4.8 %collective-permute-done.49.refs_1_ = f32[136,512]{1,0:T(8,128)S(1)} collective-permute-done((f32[136,512]{1,0:T(8,128)S(1)}, f32[136,512]{1,0:T(8,128)S(1)}, u32[]{:S(2)}, u32[]{:S(2)}) %collective-permute-start.49) | collective-permute-done | bytes 278560 | tf_op jit(solution)/shard_map/ppermute | solution.py:549
  165.1 2.9 %collective-permute-start.48 = (f32[128,512]{1,0:T(8,128)S(1)}, f32[128,512]{1,0:T(8,128)S(1)}, u32[]{:S(2)}, u32[]{:S(2)}) collective-permute-start(f32[128,512]{1,0:T(8,128)S(1)} %shard_map.211.refs_3_.refs_0_), channel_id=1, source_target_pairs={{0,2},{6,4},{1,3},{7,5},{8,10},{14,12},{9,11},{15,13},{16,18},{22,... | collective-permute-start | bytes 786440 | tf_op jit(solution)/shard_map/ppermute | solution.py:552
  170.0 2.9 %collective-permute-start.54 = (f32[136,512]{1,0:T(8,128)S(1)}, f32[136,512]{1,0:T(8,128)S(1)}, u32[]{:S(2)}, u32[]{:S(2)}) collective-permute-start(f32[136,512]{1,0:T(8,128)S(1)} %get-tuple-element.203.refs_2_), channel_id=1, source_target_pairs={{0,2},{2,0},{4,6},{6,4},{1,3},{3,1},{5,7},{7,5},{8,10},{10,8},{12,... | collective-permute-start | bytes 835592 | tf_op jit(solution)/shard_map/ppermute | solution.py:549
  175.0 4.2 %collective-permute-start.57 = (f32[128,512]{1,0:T(8,128)S(1)}, f32[128,512]{1,0:T(8,128)S(1)}, u32[]{:S(2)}, u32[]{:S(2)}) collective-permute-start(f32[128,512]{1,0:T(8,128)S(1)} %get-tuple-element.204.refs_2_), channel_id=1, source_target_pairs={{0,2},{2,0},{4,6},{6,4},{1,3},{3,1},{5,7},{7,5},{8,10},{10,8},{12,... | collective-permute-start | bytes 786440 | tf_op jit(solution)/shard_map/ppermute | solution.py:549
  180.9 3.8 %collective-permute-start.56 = (f32[128,512]{1,0:T(8,128)S(1)}, f32[128,512]{1,0:T(8,128)S(1)}, u32[]{:S(2)}, u32[]{:S(2)}) collective-permute-start(f32[128,512]{1,0:T(8,128)S(1)} %get-tuple-element.205.refs_5_), channel_id=1, source_target_pairs={{0,2},{2,0},{4,6},{6,4},{1,3},{3,1},{5,7},{7,5},{8,10},{10,8},{12,... | collective-permute-start | bytes 786440 | tf_op jit(solution)/shard_map/ppermute | solution.py:549
  190.6 5.8 %collective-permute-start.63 = (f32[128,512]{1,0:T(8,128)S(1)}, f32[128,512]{1,0:T(8,128)S(1)}, u32[]{:S(2)}, u32[]{:S(2)}) collective-permute-start(f32[128,512]{1,0:T(8,128)S(1)} %shard_map.228.refs_7_.refs_3_), channel_id=1, source_target_pairs={{0,2},{2,0},{4,6},{6,4},{1,3},{3,1},{5,7},{7,5},{8,10},{10,8},{12,... | collective-permute-start | bytes 786440 | tf_op jit(solution)/shard_map/ppermute | solution.py:549
  196.8 2.4 collective-permute-done.60.refs_2_
  201.0 3.7 %collective-permute-done.63.refs_2_ = f32[128,512]{1,0:T(8,128)S(1)} collective-permute-done((f32[128,512]{1,0:T(8,128)S(1)}, f32[128,512]{1,0:T(8,128)S(1)}, u32[]{:S(2)}, u32[]{:S(2)}) %collective-permute-start.63) | collective-permute-done | bytes 262176 | tf_op jit(solution)/shard_map/ppermute | solution.py:549
  205.1 3.2 %collective-permute-done.62.refs_2_ = f32[128,512]{1,0:T(8,128)S(1)} collective-permute-done((f32[128,512]{1,0:T(8,128)S(1)}, f32[128,512]{1,0:T(8,128)S(1)}, u32[]{:S(2)}, u32[]{:S(2)}) %collective-permute-start.62) | collective-permute-done | bytes 262176 | tf_op jit(solution)/shard_map/ppermute | solution.py:549
  216.7 2.4 collective-permute-done.67.refs_3_
  224.5 2.1 collective-permute-start.73
  226.5 4.8 %collective-permute-done.70.refs_1_ = f32[136,512]{1,0:T(8,128)S(1)} collective-permute-done((f32[136,512]{1,0:T(8,128)S(1)}, f32[136,512]{1,0:T(8,128)S(1)}, u32[]{:S(2)}, u32[]{:S(2)}) %collective-permute-start.70) | collective-permute-done | bytes 278560 | tf_op jit(solution)/shard_map/ppermute | solution.py:549
  231.5 3.5 %collective-permute-start.69 = (f32[128,512]{1,0:T(8,128)S(1)}, f32[128,512]{1,0:T(8,128)S(1)}, u32[]{:S(2)}, u32[]{:S(2)}) collective-permute-start(f32[128,512]{1,0:T(8,128)S(1)} %shard_map.237.refs_3_.refs_0_), channel_id=1, source_target_pairs={{0,2},{6,4},{1,3},{7,5},{8,10},{14,12},{9,11},{15,13},{16,18},{22,... | collective-permute-start | bytes 786440 | tf_op jit(solution)/shard_map/ppermute | solution.py:552
  236.4 3.1 %collective-permute-start.75 = (f32[136,512]{1,0:T(8,128)S(1)}, f32[136,512]{1,0:T(8,128)S(1)}, u32[]{:S(2)}, u32[]{:S(2)}) collective-permute-start(f32[136,512]{1,0:T(8,128)S(1)} %get-tuple-element.230.refs_2_), channel_id=1, source_target_pairs={{0,2},{2,0},{4,6},{6,4},{1,3},{3,1},{5,7},{7,5},{8,10},{10,8},{12,... | collective-permute-start | bytes 835592 | tf_op jit(solution)/shard_map/ppermute | solution.py:549
  239.5 2.1 collective-permute-done.69.refs_1_
  241.8 4.4 %collective-permute-start.78 = (f32[128,512]{1,0:T(8,128)S(1)}, f32[128,512]{1,0:T(8,128)S(1)}, u32[]{:S(2)}, u32[]{:S(2)}) collective-permute-start(f32[128,512]{1,0:T(8,128)S(1)} %get-tuple-element.231.refs_2_), channel_id=1, source_target_pairs={{0,2},{2,0},{4,6},{6,4},{1,3},{3,1},{5,7},{7,5},{8,10},{10,8},{12,... | collective-permute-start | bytes 786440 | tf_op jit(solution)/shard_map/ppermute | solution.py:549
  247.6 4.4 %collective-permute-start.77 = (f32[128,512]{1,0:T(8,128)S(1)}, f32[128,512]{1,0:T(8,128)S(1)}, u32[]{:S(2)}, u32[]{:S(2)}) collective-permute-start(f32[128,512]{1,0:T(8,128)S(1)} %get-tuple-element.232.refs_5_), channel_id=1, source_target_pairs={{0,2},{2,0},{4,6},{6,4},{1,3},{3,1},{5,7},{7,5},{8,10},{10,8},{12,... | collective-permute-start | bytes 786440 | tf_op jit(solution)/shard_map/ppermute | solution.py:549
  256.9 6.5 %collective-permute-start.84 = (f32[128,512]{1,0:T(8,128)S(1)}, f32[128,512]{1,0:T(8,128)S(1)}, u32[]{:S(2)}, u32[]{:S(2)}) collective-permute-start(f32[128,512]{1,0:T(8,128)S(1)} %shard_map.254.refs_7_.refs_3_), channel_id=1, source_target_pairs={{0,2},{2,0},{4,6},{6,4},{1,3},{3,1},{5,7},{7,5},{8,10},{10,8},{12,... | collective-permute-start | bytes 786440 | tf_op jit(solution)/shard_map/ppermute | solution.py:549
  263.8 2.4 collective-permute-done.81.refs_2_
  267.7 3.8 %collective-permute-done.84.refs_2_ = f32[128,512]{1,0:T(8,128)S(1)} collective-permute-done((f32[128,512]{1,0:T(8,128)S(1)}, f32[128,512]{1,0:T(8,128)S(1)}, u32[]{:S(2)}, u32[]{:S(2)}) %collective-permute-start.84) | collective-permute-done | bytes 262176 | tf_op jit(solution)/shard_map/ppermute | solution.py:549
  271.8 3.1 %collective-permute-done.83.refs_2_ = f32[128,512]{1,0:T(8,128)S(1)} collective-permute-done((f32[128,512]{1,0:T(8,128)S(1)}, f32[128,512]{1,0:T(8,128)S(1)}, u32[]{:S(2)}, u32[]{:S(2)}) %collective-permute-start.83) | collective-permute-done | bytes 262176 | tf_op jit(solution)/shard_map/ppermute | solution.py:549
  278.9 2.2 collective-permute-start.88
  (294 shorter events, 111.9 us)
Async XLA Ops:
  6.3 11.6 %collective-permute-start.3 = (f32[384,512]{1,0:T(8,128)}, f32[384,512]{1,0:T(8,128)}, u32[]{:S(2)}, u32[]{:S(2)}) collective-permute-start(f32[384,512]{1,0:T(8,128)} %get-tuple-element.135), channel_id=1, source_target_pairs={{0,1},{1,0},{2,3},{3,2},{4,5},{5,4},{6,7},{7,6},{8,9},{9,8},{10,11... | collective-permute-start | bytes 2359304 | tf_op jit(solution)/shard_map/ppermute | solution.py:524
  6.8 17.1 %collective-permute-start.2 = (f32[384,512]{1,0:T(8,128)}, f32[384,512]{1,0:T(8,128)}, u32[]{:S(2)}, u32[]{:S(2)}) collective-permute-start(f32[384,512]{1,0:T(8,128)} %get-tuple-element.133), channel_id=1, source_target_pairs={{0,1},{1,0},{2,3},{3,2},{4,5},{5,4},{6,7},{7,6},{8,9},{9,8},{10,11... | collective-permute-start | bytes 2359304 | tf_op jit(solution)/shard_map/ppermute | solution.py:524
  6.9 20.4 %collective-permute-start.7 = (f32[384,512]{1,0:T(8,128)}, f32[384,512]{1,0:T(8,128)}, u32[]{:S(2)}, u32[]{:S(2)}) collective-permute-start(f32[384,512]{1,0:T(8,128)} %get-tuple-element.141), channel_id=1, source_target_pairs={{0,1},{1,0},{2,3},{3,2},{4,5},{5,4},{6,7},{7,6},{8,9},{9,8},{10,11... | collective-permute-start | bytes 2359304 | tf_op jit(solution)/shard_map/ppermute | solution.py:524
  16.1 14.9 %collective-permute-start.5 = (f32[384,512]{1,0:T(8,128)}, f32[384,512]{1,0:T(8,128)}, u32[]{:S(2)}, u32[]{:S(2)}) collective-permute-start(f32[384,512]{1,0:T(8,128)} %get-tuple-element.139), channel_id=1, source_target_pairs={{0,1},{1,0},{2,3},{3,2},{4,5},{5,4},{6,7},{7,6},{8,9},{9,8},{10,11... | collective-permute-start | bytes 2359304 | tf_op jit(solution)/shard_map/ppermute | solution.py:524
  17.8 24.2 %collective-permute-start.9 = (f32[384,512]{1,0:T(8,128)}, f32[384,512]{1,0:T(8,128)}, u32[]{:S(2)}, u32[]{:S(2)}) collective-permute-start(f32[384,512]{1,0:T(8,128)} %copy-done.8), channel_id=1, source_target_pairs={{0,1},{1,0},{2,3},{3,2},{4,5},{5,4},{6,7},{7,6},{8,9},{9,8},{10,11... | collective-permute-start | bytes 2359304 | tf_op jit(solution)/shard_map/ppermute | solution.py:524
  20.7 10.0 %collective-permute-start.6 = (f32[136,512]{1,0:T(8,128)S(1)}, f32[136,512]{1,0:T(8,128)S(1)}, u32[]{:S(2)}, u32[]{:S(2)}) collective-permute-start(f32[136,512]{1,0:T(8,128)S(1)} %get-tuple-element.136.refs_4_.refs_0_), channel_id=1, source_target_pairs={{0,2},{2,0},{4,6},{6,4},{1,3},{3,1},{5,7},{7,5},{8,10},{10,8},{12,... | collective-permute-start | bytes 835592 | tf_op jit(solution)/shard_map/ppermute | solution.py:549
  24.0 23.5 %collective-permute-start.1 = (f32[384,512]{1,0:T(8,128)S(1)}, f32[384,512]{1,0:T(8,128)}, u32[]{:S(2)}, u32[]{:S(2)}) collective-permute-start(f32[384,512]{1,0:T(8,128)S(1)} %get-tuple-element.131), channel_id=1, source_target_pairs={{0,1},{1,0},{2,3},{3,2},{4,5},{5,4},{6,7},{7,6},{8,9},{9,8},{10,11... | collective-permute-start | bytes 2359304 | tf_op jit(solution)/shard_map/ppermute | solution.py:524
  27.3 10.8 %collective-permute-start.4 = (f32[128,512]{1,0:T(8,128)}, f32[128,512]{1,0:T(8,128)}, u32[]{:S(2)}, u32[]{:S(2)}) collective-permute-start(f32[128,512]{1,0:T(8,128)} %get-tuple-element.137.refs_4_.refs_0_), channel_id=1, source_target_pairs={{0,2},{2,0},{4,6},{6,4},{1,3},{3,1},{5,7},{7,5},{8,10},{10,8},{12,... | collective-permute-start | bytes 786440 | tf_op jit(solution)/shard_map/ppermute | solution.py:549
  30.9 8.4 %collective-permute-start.10 = (f32[136,512]{1,0:T(8,128)S(1)}, f32[136,512]{1,0:T(8,128)}, u32[]{:S(2)}, u32[]{:S(2)}) collective-permute-start(f32[136,512]{1,0:T(8,128)S(1)} %shard_map.161.refs_4_.refs_1_), channel_id=1, source_target_pairs={{2,4},{4,2},{3,5},{5,3},{0,1},{1,0},{6,7},{7,6},{10,12},{12,10},{1... | collective-permute-start | bytes 835592 | tf_op jit(solution)/shard_map/ppermute | solution.py:559
  31.1 12.7 %collective-permute-start.11 = (f32[128,512]{1,0:T(8,128)}, f32[128,512]{1,0:T(8,128)S(1)}, u32[]{:S(2)}, u32[]{:S(2)}) collective-permute-start(f32[128,512]{1,0:T(8,128)} %copy-done.19), channel_id=1, source_target_pairs={{0,2},{6,4},{1,3},{7,5},{8,10},{14,12},{9,11},{15,13},{16,18},{22,... | collective-permute-start | bytes 786440 | tf_op jit(solution)/shard_map/ppermute | solution.py:552
  40.3 9.5 %collective-permute-start.13 = (f32[136,512]{1,0:T(8,128)S(1)}, f32[136,512]{1,0:T(8,128)S(1)}, u32[]{:S(2)}, u32[]{:S(2)}) collective-permute-start(f32[136,512]{1,0:T(8,128)S(1)} %get-tuple-element.146.refs_4_), channel_id=1, source_target_pairs={{0,2},{2,0},{4,6},{6,4},{1,3},{3,1},{5,7},{7,5},{8,10},{10,8},{12,... | collective-permute-start | bytes 835592 | tf_op jit(solution)/shard_map/ppermute | solution.py:549
  43.8 6.2 %collective-permute-start.12 = (f32[128,512]{1,0:T(8,128)S(1)}, f32[128,512]{1,0:T(8,128)S(1)}, u32[]{:S(2)}, u32[]{:S(2)}) collective-permute-start(f32[128,512]{1,0:T(8,128)S(1)} %shard_map.166.refs_4_.refs_1_), channel_id=1, source_target_pairs={{2,4},{4,2},{3,5},{5,3},{0,1},{1,0},{6,7},{7,6},{10,12},{12,10},{1... | collective-permute-start | bytes 786440 | tf_op jit(solution)/shard_map/ppermute | solution.py:559
  44.0 11.5 %collective-permute-start.15 = (f32[128,512]{1,0:T(8,128)S(1)}, f32[128,512]{1,0:T(8,128)S(1)}, u32[]{:S(2)}, u32[]{:S(2)}) collective-permute-start(f32[128,512]{1,0:T(8,128)S(1)} %get-tuple-element.148.refs_4_), channel_id=1, source_target_pairs={{0,2},{2,0},{4,6},{6,4},{1,3},{3,1},{5,7},{7,5},{8,10},{10,8},{12,... | collective-permute-start | bytes 786440 | tf_op jit(solution)/shard_map/ppermute | solution.py:549
  50.1 10.6 %collective-permute-start.14 = (f32[128,512]{1,0:T(8,128)S(1)}, f32[128,512]{1,0:T(8,128)S(1)}, u32[]{:S(2)}, u32[]{:S(2)}) collective-permute-start(f32[128,512]{1,0:T(8,128)S(1)} %get-tuple-element.150.refs_6_), channel_id=1, source_target_pairs={{0,2},{2,0},{4,6},{6,4},{1,3},{3,1},{5,7},{7,5},{8,10},{10,8},{12,... | collective-permute-start | bytes 786440 | tf_op jit(solution)/shard_map/ppermute | solution.py:549
  55.6 12.5 %collective-permute-start.18 = (f32[128,512]{1,0:T(8,128)S(1)}, f32[128,512]{1,0:T(8,128)S(1)}, u32[]{:S(2)}, u32[]{:S(2)}) collective-permute-start(f32[128,512]{1,0:T(8,128)S(1)} %shard_map.173.refs_8_.refs_3_), channel_id=1, source_target_pairs={{2,0},{4,6},{3,1},{5,7},{10,8},{12,14},{11,9},{13,15},{18,16},{20,... | collective-permute-start | bytes 786440 | tf_op jit(solution)/shard_map/ppermute | solution.py:555
  60.7 7.8 %collective-permute-start.17 = (f32[128,512]{1,0:T(8,128)S(1)}, f32[128,512]{1,0:T(8,128)S(1)}, u32[]{:S(2)}, u32[]{:S(2)}) collective-permute-start(f32[128,512]{1,0:T(8,128)S(1)} %shard_map.175.refs_2_.refs_0_), channel_id=1, source_target_pairs={{2,4},{4,2},{3,5},{5,3},{0,1},{1,0},{6,7},{7,6},{10,12},{12,10},{1... | collective-permute-start | bytes 786440 | tf_op jit(solution)/shard_map/ppermute | solution.py:559
  60.9 12.9 %collective-permute-start.21 = (f32[128,512]{1,0:T(8,128)S(1)}, f32[128,512]{1,0:T(8,128)S(1)}, u32[]{:S(2)}, u32[]{:S(2)}) collective-permute-start(f32[128,512]{1,0:T(8,128)S(1)} %shard_map.176.refs_8_.refs_3_), channel_id=1, source_target_pairs={{0,2},{2,0},{4,6},{6,4},{1,3},{3,1},{5,7},{7,5},{8,10},{10,8},{12,... | collective-permute-start | bytes 786440 | tf_op jit(solution)/shard_map/ppermute | solution.py:549
  68.6 9.0 %collective-permute-start.20 = (f32[128,512]{1,0:T(8,128)S(1)}, f32[128,512]{1,0:T(8,128)S(1)}, u32[]{:S(2)}, u32[]{:S(2)}) collective-permute-start(f32[128,512]{1,0:T(8,128)S(1)} %shard_map.179.refs_8_.refs_3_), channel_id=1, source_target_pairs={{0,2},{2,0},{4,6},{6,4},{1,3},{3,1},{5,7},{7,5},{8,10},{10,8},{12,... | collective-permute-start | bytes 786440 | tf_op jit(solution)/shard_map/ppermute | solution.py:549
  90.9 9.6 %collective-permute-start.28 = (f32[136,512]{1,0:T(8,128)S(1)}, f32[136,512]{1,0:T(8,128)S(1)}, u32[]{:S(2)}, u32[]{:S(2)}) collective-permute-start(f32[136,512]{1,0:T(8,128)S(1)} %shard_map.184.refs_3_.refs_0_), channel_id=1, source_target_pairs={{0,2},{2,0},{4,6},{6,4},{1,3},{3,1},{5,7},{7,5},{8,10},{10,8},{12,... | collective-permute-start | bytes 835592 | tf_op jit(solution)/shard_map/ppermute | solution.py:549
  93.6 11.7 %collective-permute-start.31 = (f32[128,512]{1,0:T(8,128)S(1)}, f32[128,512]{1,0:T(8,128)S(1)}, u32[]{:S(2)}, u32[]{:S(2)}) collective-permute-start(f32[128,512]{1,0:T(8,128)S(1)} %shard_map.189.refs_2_.refs_0_), channel_id=1, source_target_pairs={{0,2},{2,0},{4,6},{6,4},{1,3},{3,1},{5,7},{7,5},{8,10},{10,8},{12,... | collective-permute-start | bytes 786440 | tf_op jit(solution)/shard_map/ppermute | solution.py:549
  100.6 10.1 %collective-permute-start.27 = (f32[128,512]{1,0:T(8,128)S(1)}, f32[128,512]{1,0:T(8,128)S(1)}, u32[]{:S(2)}, u32[]{:S(2)}) collective-permute-start(f32[128,512]{1,0:T(8,128)S(1)} %shard_map.185.refs_3_.refs_0_), channel_id=1, source_target_pairs={{0,2},{6,4},{1,3},{7,5},{8,10},{14,12},{9,11},{15,13},{16,18},{22,... | collective-permute-start | bytes 786440 | tf_op jit(solution)/shard_map/ppermute | solution.py:552
  105.5 10.9 %collective-permute-start.33 = (f32[136,512]{1,0:T(8,128)S(1)}, f32[136,512]{1,0:T(8,128)S(1)}, u32[]{:S(2)}, u32[]{:S(2)}) collective-permute-start(f32[136,512]{1,0:T(8,128)S(1)} %get-tuple-element.180.refs_2_), channel_id=1, source_target_pairs={{0,2},{2,0},{4,6},{6,4},{1,3},{3,1},{5,7},{7,5},{8,10},{10,8},{12,... | collective-permute-start | bytes 835592 | tf_op jit(solution)/shard_map/ppermute | solution.py:549
  110.9 11.1 %collective-permute-start.36 = (f32[128,512]{1,0:T(8,128)S(1)}, f32[128,512]{1,0:T(8,128)S(1)}, u32[]{:S(2)}, u32[]{:S(2)}) collective-permute-start(f32[128,512]{1,0:T(8,128)S(1)} %get-tuple-element.181.refs_2_), channel_id=1, source_target_pairs={{0,2},{2,0},{4,6},{6,4},{1,3},{3,1},{5,7},{7,5},{8,10},{10,8},{12,... | collective-permute-start | bytes 786440 | tf_op jit(solution)/shard_map/ppermute | solution.py:549
  116.5 9.4 %collective-permute-start.35 = (f32[128,512]{1,0:T(8,128)S(1)}, f32[128,512]{1,0:T(8,128)S(1)}, u32[]{:S(2)}, u32[]{:S(2)}) collective-permute-start(f32[128,512]{1,0:T(8,128)S(1)} %get-tuple-element.182.refs_5_), channel_id=1, source_target_pairs={{0,2},{2,0},{4,6},{6,4},{1,3},{3,1},{5,7},{7,5},{8,10},{10,8},{12,... | collective-permute-start | bytes 786440 | tf_op jit(solution)/shard_map/ppermute | solution.py:549
  122.1 12.8 %collective-permute-start.39 = (f32[128,512]{1,0:T(8,128)S(1)}, f32[128,512]{1,0:T(8,128)S(1)}, u32[]{:S(2)}, u32[]{:S(2)}) collective-permute-start(f32[128,512]{1,0:T(8,128)S(1)} %shard_map.199.refs_7_.refs_3_), channel_id=1, source_target_pairs={{2,0},{4,6},{3,1},{5,7},{10,8},{12,14},{11,9},{13,15},{18,16},{20,... | collective-permute-start | bytes 786440 | tf_op jit(solution)/shard_map/ppermute | solution.py:555
  126.0 9.4 %collective-permute-start.38 = (f32[128,512]{1,0:T(8,128)S(1)}, f32[128,512]{1,0:T(8,128)S(1)}, u32[]{:S(2)}, u32[]{:S(2)}) collective-permute-start(f32[128,512]{1,0:T(8,128)S(1)} %shard_map.201.refs_2_.refs_0_), channel_id=1, source_target_pairs={{2,4},{4,2},{3,5},{5,3},{0,1},{1,0},{6,7},{7,6},{10,12},{12,10},{1... | collective-permute-start | bytes 786440 | tf_op jit(solution)/shard_map/ppermute | solution.py:559
  126.1 14.1 %collective-permute-start.42 = (f32[128,512]{1,0:T(8,128)S(1)}, f32[128,512]{1,0:T(8,128)S(1)}, u32[]{:S(2)}, u32[]{:S(2)}) collective-permute-start(f32[128,512]{1,0:T(8,128)S(1)} %shard_map.202.refs_7_.refs_3_), channel_id=1, source_target_pairs={{0,2},{2,0},{4,6},{6,4},{1,3},{3,1},{5,7},{7,5},{8,10},{10,8},{12,... | collective-permute-start | bytes 786440 | tf_op jit(solution)/shard_map/ppermute | solution.py:549
  135.4 8.6 %collective-permute-start.41 = (f32[128,512]{1,0:T(8,128)S(1)}, f32[128,512]{1,0:T(8,128)S(1)}, u32[]{:S(2)}, u32[]{:S(2)}) collective-permute-start(f32[128,512]{1,0:T(8,128)S(1)} %shard_map.205.refs_7_.refs_3_), channel_id=1, source_target_pairs={{0,2},{2,0},{4,6},{6,4},{1,3},{3,1},{5,7},{7,5},{8,10},{10,8},{12,... | collective-permute-start | bytes 786440 | tf_op jit(solution)/shard_map/ppermute | solution.py:549
  155.4 9.6 %collective-permute-start.49 = (f32[136,512]{1,0:T(8,128)S(1)}, f32[136,512]{1,0:T(8,128)S(1)}, u32[]{:S(2)}, u32[]{:S(2)}) collective-permute-start(f32[136,512]{1,0:T(8,128)S(1)} %shard_map.210.refs_3_.refs_0_), channel_id=1, source_target_pairs={{0,2},{2,0},{4,6},{6,4},{1,3},{3,1},{5,7},{7,5},{8,10},{10,8},{12,... | collective-permute-start | bytes 835592 | tf_op jit(solution)/shard_map/ppermute | solution.py:549
  158.4 11.4 %collective-permute-start.52 = (f32[128,512]{1,0:T(8,128)S(1)}, f32[128,512]{1,0:T(8,128)S(1)}, u32[]{:S(2)}, u32[]{:S(2)}) collective-permute-start(f32[128,512]{1,0:T(8,128)S(1)} %shard_map.215.refs_2_.refs_0_), channel_id=1, source_target_pairs={{0,2},{2,0},{4,6},{6,4},{1,3},{3,1},{5,7},{7,5},{8,10},{10,8},{12,... | collective-permute-start | bytes 786440 | tf_op jit(solution)/shard_map/ppermute | solution.py:549
  165.1 9.7 %collective-permute-start.48 = (f32[128,512]{1,0:T(8,128)S(1)}, f32[128,512]{1,0:T(8,128)S(1)}, u32[]{:S(2)}, u32[]{:S(2)}) collective-permute-start(f32[128,512]{1,0:T(8,128)S(1)} %shard_map.211.refs_3_.refs_0_), channel_id=1, source_target_pairs={{0,2},{6,4},{1,3},{7,5},{8,10},{14,12},{9,11},{15,13},{16,18},{22,... | collective-permute-start | bytes 786440 | tf_op jit(solution)/shard_map/ppermute | solution.py:552
  170.0 10.7 %collective-permute-start.54 = (f32[136,512]{1,0:T(8,128)S(1)}, f32[136,512]{1,0:T(8,128)S(1)}, u32[]{:S(2)}, u32[]{:S(2)}) collective-permute-start(f32[136,512]{1,0:T(8,128)S(1)} %get-tuple-element.203.refs_2_), channel_id=1, source_target_pairs={{0,2},{2,0},{4,6},{6,4},{1,3},{3,1},{5,7},{7,5},{8,10},{10,8},{12,... | collective-permute-start | bytes 835592 | tf_op jit(solution)/shard_map/ppermute | solution.py:549
  175.0 11.4 %collective-permute-start.57 = (f32[128,512]{1,0:T(8,128)S(1)}, f32[128,512]{1,0:T(8,128)S(1)}, u32[]{:S(2)}, u32[]{:S(2)}) collective-permute-start(f32[128,512]{1,0:T(8,128)S(1)} %get-tuple-element.204.refs_2_), channel_id=1, source_target_pairs={{0,2},{2,0},{4,6},{6,4},{1,3},{3,1},{5,7},{7,5},{8,10},{10,8},{12,... | collective-permute-start | bytes 786440 | tf_op jit(solution)/shard_map/ppermute | solution.py:549
  180.9 9.5 %collective-permute-start.56 = (f32[128,512]{1,0:T(8,128)S(1)}, f32[128,512]{1,0:T(8,128)S(1)}, u32[]{:S(2)}, u32[]{:S(2)}) collective-permute-start(f32[128,512]{1,0:T(8,128)S(1)} %get-tuple-element.205.refs_5_), channel_id=1, source_target_pairs={{0,2},{2,0},{4,6},{6,4},{1,3},{3,1},{5,7},{7,5},{8,10},{10,8},{12,... | collective-permute-start | bytes 786440 | tf_op jit(solution)/shard_map/ppermute | solution.py:549
  186.5 12.7 %collective-permute-start.60 = (f32[128,512]{1,0:T(8,128)S(1)}, f32[128,512]{1,0:T(8,128)S(1)}, u32[]{:S(2)}, u32[]{:S(2)}) collective-permute-start(f32[128,512]{1,0:T(8,128)S(1)} %shard_map.225.refs_7_.refs_3_), channel_id=1, source_target_pairs={{2,0},{4,6},{3,1},{5,7},{10,8},{12,14},{11,9},{13,15},{18,16},{20,... | collective-permute-start | bytes 786440 | tf_op jit(solution)/shard_map/ppermute | solution.py:555
  190.5 9.2 %collective-permute-start.59 = (f32[128,512]{1,0:T(8,128)S(1)}, f32[128,512]{1,0:T(8,128)S(1)}, u32[]{:S(2)}, u32[]{:S(2)}) collective-permute-start(f32[128,512]{1,0:T(8,128)S(1)} %shard_map.227.refs_2_.refs_0_), channel_id=1, source_target_pairs={{2,4},{4,2},{3,5},{5,3},{0,1},{1,0},{6,7},{7,6},{10,12},{12,10},{1... | collective-permute-start | bytes 786440 | tf_op jit(solution)/shard_map/ppermute | solution.py:559
  190.6 14.1 %collective-permute-start.63 = (f32[128,512]{1,0:T(8,128)S(1)}, f32[128,512]{1,0:T(8,128)S(1)}, u32[]{:S(2)}, u32[]{:S(2)}) collective-permute-start(f32[128,512]{1,0:T(8,128)S(1)} %shard_map.228.refs_7_.refs_3_), channel_id=1, source_target_pairs={{0,2},{2,0},{4,6},{6,4},{1,3},{3,1},{5,7},{7,5},{8,10},{10,8},{12,... | collective-permute-start | bytes 786440 | tf_op jit(solution)/shard_map/ppermute | solution.py:549
  199.7 8.6 %collective-permute-start.62 = (f32[128,512]{1,0:T(8,128)S(1)}, f32[128,512]{1,0:T(8,128)S(1)}, u32[]{:S(2)}, u32[]{:S(2)}) collective-permute-start(f32[128,512]{1,0:T(8,128)S(1)} %shard_map.231.refs_7_.refs_3_), channel_id=1, source_target_pairs={{0,2},{2,0},{4,6},{6,4},{1,3},{3,1},{5,7},{7,5},{8,10},{10,8},{12,... | collective-permute-start | bytes 786440 | tf_op jit(solution)/shard_map/ppermute | solution.py:549
  221.8 9.6 %collective-permute-start.70 = (f32[136,512]{1,0:T(8,128)S(1)}, f32[136,512]{1,0:T(8,128)S(1)}, u32[]{:S(2)}, u32[]{:S(2)}) collective-permute-start(f32[136,512]{1,0:T(8,128)S(1)} %shard_map.236.refs_3_.refs_0_), channel_id=1, source_target_pairs={{0,2},{2,0},{4,6},{6,4},{1,3},{3,1},{5,7},{7,5},{8,10},{10,8},{12,... | collective-permute-start | bytes 835592 | tf_op jit(solution)/shard_map/ppermute | solution.py:549
  224.5 11.7 %collective-permute-start.73 = (f32[128,512]{1,0:T(8,128)S(1)}, f32[128,512]{1,0:T(8,128)S(1)}, u32[]{:S(2)}, u32[]{:S(2)}) collective-permute-start(f32[128,512]{1,0:T(8,128)S(1)} %shard_map.241.refs_2_.refs_0_), channel_id=1, source_target_pairs={{0,2},{2,0},{4,6},{6,4},{1,3},{3,1},{5,7},{7,5},{8,10},{10,8},{12,... | collective-permute-start | bytes 786440 | tf_op jit(solution)/shard_map/ppermute | solution.py:549
  231.5 10.2 %collective-permute-start.69 = (f32[128,512]{1,0:T(8,128)S(1)}, f32[128,512]{1,0:T(8,128)S(1)}, u32[]{:S(2)}, u32[]{:S(2)}) collective-permute-start(f32[128,512]{1,0:T(8,128)S(1)} %shard_map.237.refs_3_.refs_0_), channel_id=1, source_target_pairs={{0,2},{6,4},{1,3},{7,5},{8,10},{14,12},{9,11},{15,13},{16,18},{22,... | collective-permute-start | bytes 786440 | tf_op jit(solution)/shard_map/ppermute | solution.py:552
  236.4 11.0 %collective-permute-start.75 = (f32[136,512]{1,0:T(8,128)S(1)}, f32[136,512]{1,0:T(8,128)S(1)}, u32[]{:S(2)}, u32[]{:S(2)}) collective-permute-start(f32[136,512]{1,0:T(8,128)S(1)} %get-tuple-element.230.refs_2_), channel_id=1, source_target_pairs={{0,2},{2,0},{4,6},{6,4},{1,3},{3,1},{5,7},{7,5},{8,10},{10,8},{12,... | collective-permute-start | bytes 835592 | tf_op jit(solution)/shard_map/ppermute | solution.py:549
  241.8 11.2 %collective-permute-start.78 = (f32[128,512]{1,0:T(8,128)S(1)}, f32[128,512]{1,0:T(8,128)S(1)}, u32[]{:S(2)}, u32[]{:S(2)}) collective-permute-start(f32[128,512]{1,0:T(8,128)S(1)} %get-tuple-element.231.refs_2_), channel_id=1, source_target_pairs={{0,2},{2,0},{4,6},{6,4},{1,3},{3,1},{5,7},{7,5},{8,10},{10,8},{12,... | collective-permute-start | bytes 786440 | tf_op jit(solution)/shard_map/ppermute | solution.py:549
  247.6 9.2 %collective-permute-start.77 = (f32[128,512]{1,0:T(8,128)S(1)}, f32[128,512]{1,0:T(8,128)S(1)}, u32[]{:S(2)}, u32[]{:S(2)}) collective-permute-start(f32[128,512]{1,0:T(8,128)S(1)} %get-tuple-element.232.refs_5_), channel_id=1, source_target_pairs={{0,2},{2,0},{4,6},{6,4},{1,3},{3,1},{5,7},{7,5},{8,10},{10,8},{12,... | collective-permute-start | bytes 786440 | tf_op jit(solution)/shard_map/ppermute | solution.py:549
  253.1 13.1 %collective-permute-start.81 = (f32[128,512]{1,0:T(8,128)S(1)}, f32[128,512]{1,0:T(8,128)S(1)}, u32[]{:S(2)}, u32[]{:S(2)}) collective-permute-start(f32[128,512]{1,0:T(8,128)S(1)} %shard_map.251.refs_7_.refs_3_), channel_id=1, source_target_pairs={{2,0},{4,6},{3,1},{5,7},{10,8},{12,14},{11,9},{13,15},{18,16},{20,... | collective-permute-start | bytes 786440 | tf_op jit(solution)/shard_map/ppermute | solution.py:555
  256.8 9.8 %collective-permute-start.80 = (f32[128,512]{1,0:T(8,128)S(1)}, f32[128,512]{1,0:T(8,128)S(1)}, u32[]{:S(2)}, u32[]{:S(2)}) collective-permute-start(f32[128,512]{1,0:T(8,128)S(1)} %shard_map.253.refs_2_.refs_0_), channel_id=1, source_target_pairs={{2,4},{4,2},{3,5},{5,3},{0,1},{1,0},{6,7},{7,6},{10,12},{12,10},{1... | collective-permute-start | bytes 786440 | tf_op jit(solution)/shard_map/ppermute | solution.py:559
  256.9 14.5 %collective-permute-start.84 = (f32[128,512]{1,0:T(8,128)S(1)}, f32[128,512]{1,0:T(8,128)S(1)}, u32[]{:S(2)}, u32[]{:S(2)}) collective-permute-start(f32[128,512]{1,0:T(8,128)S(1)} %shard_map.254.refs_7_.refs_3_), channel_id=1, source_target_pairs={{0,2},{2,0},{4,6},{6,4},{1,3},{3,1},{5,7},{7,5},{8,10},{10,8},{12,... | collective-permute-start | bytes 786440 | tf_op jit(solution)/shard_map/ppermute | solution.py:549
  266.7 8.3 %collective-permute-start.83 = (f32[128,512]{1,0:T(8,128)S(1)}, f32[128,512]{1,0:T(8,128)S(1)}, u32[]{:S(2)}, u32[]{:S(2)}) collective-permute-start(f32[128,512]{1,0:T(8,128)S(1)} %shard_map.257.refs_7_.refs_3_), channel_id=1, source_target_pairs={{0,2},{2,0},{4,6},{6,4},{1,3},{3,1},{5,7},{7,5},{8,10},{10,8},{12,... | collective-permute-start | bytes 786440 | tf_op jit(solution)/shard_map/ppermute | solution.py:549
  (69 other events, 290.4 us)
